TPU v7x, 32 devices: a whole 2x2x4 slice. The times are simulated.
32 devices in a mesh: lat: 8 (over z, x), lon: 4 (over y, core).
Axes of the slice: x: 2, y: 2, z: 4, core: 2. Of those that a mesh axis runs over, the one named last changes fastest.
Arguments:
- tracers: float32 [4, 8, 32, 5760], P(None, None, 'lat', 'lon'), may hold values from -6 to 6
- merid_courant: float32 [8, 32, 5760], P(None, 'lat', 'lon'), may hold values from -0.45 to 0.45
- zonal_shift: int32 [8, 32], P(None, 'lat'), may hold values from 0 to 64, as said below
- zonal_fraction: float32 [8, 32], P(None, 'lat'), may hold values from 0 to 1
- cutoff: int32 [32], replicated, may hold values from 1 to 1023
- damping: float32 [32], replicated, may hold values from 0.1 to 0.6
Outputs:
- tracer_out: float32 [4, 8, 32, 5760], P(None, None, 'lat', 'lon')
Inputs may be any that keep to these rules, and one draw needn't show every extreme that they name: `zonal_shift`: in row j no displacement exceeds 1 + (64 * |2j - 31|) // 32, a limit that grows toward the poles; below it the values are random.
All inputs are finite; a program needn't handle non-finite values.
Results may differ from a plain program's by a relative error of at most 0.00005.
Values sent between devices are 32-bit elements; how exact they have to be, the bound alone decides.
No kernel may reach another device: no remote copies, remote signals or barrier semaphores. Data moves between devices by JAX's collectives and lax.ppermute only.
A program may use at most 64 MiB of HBM per device.

v0:
```python
import math

import jax
import jax.numpy as jnp
from jax import lax
from jax.sharding import PartitionSpec as P

MODES = 1024
SMAX = 64


def passed_along(block, axis, distance):
    devices = range(lax.axis_size(axis))
    route = [(i - distance, i) for i in devices if i - distance in devices]
    return lax.ppermute(block, axis, route)


def passed_along_2(value, axis, steps):
    count = lax.axis_size(axis)
    pairs = [(source, (source + steps) % count) for source in range(count)]
    return lax.ppermute(value, axis, pairs)


def make_basis(columns, wavenumber, lon_cells):
    phase_index = columns[:, None] * wavenumber[None, :] % lon_cells
    angles = phase_index.astype(jnp.float32) * (2.0 * math.pi / lon_cells)
    return jnp.concatenate([jnp.cos(angles), jnp.sin(angles)], axis=1)


def body(tracers, merid_courant, zonal_shift, zonal_fraction, cutoff, damping):
    tracer_count, level_count, row_count, column_count = tracers.shape
    lat_count = lax.axis_size("lat")
    lat_index = lax.axis_index("lat")
    lon_count = lax.axis_size("lon")
    lon_index = lax.axis_index("lon")
    lat_rows = row_count * lat_count
    lon_cells = column_count * lon_count
    below_row = passed_along(tracers[:, :, row_count - 1 :], "lat", 1)
    stacked_edge = jnp.concatenate([tracers[:, :, :1], merid_courant[None, :, :1]], axis=0)
    above_row = passed_along(stacked_edge, "lat", -1)
    face_speed = jnp.concatenate([merid_courant, above_row[tracer_count]], axis=1)
    south_cells = jnp.concatenate([below_row, tracers], axis=2)
    north_cells = jnp.concatenate([tracers, above_row[:tracer_count]], axis=2)
    face_flux = (
        jnp.maximum(face_speed, 0.0)[None] * south_cells
        + jnp.minimum(face_speed, 0.0)[None] * north_cells
    )
    face_row = lat_index * row_count + jnp.arange(row_count + 1, dtype=jnp.int32)
    open_face = (face_row > 0) & (face_row < lat_rows)
    face_flux = jnp.where(open_face[None, None, :, None], face_flux, 0.0)
    advected = tracers + face_flux[:, :, :-1] - face_flux[:, :, 1:]
    rim_width = SMAX + 1
    west_rim = passed_along_2(advected[:, :, :, column_count - rim_width :], "lon", 1)
    extended = jnp.concatenate([west_rim, advected], axis=3)
    moved = extended
    shift_grid = zonal_shift[None, :, :, None]
    for bit_level in range(SMAX.bit_length()):
        stride = 1 << bit_level
        padding = jnp.zeros(moved.shape[:3] + (stride,), moved.dtype)
        pushed = jnp.concatenate([padding, moved[:, :, :, :-stride]], axis=3)
        selected = shift_grid >> bit_level & 1 == 1
        moved = jnp.where(selected, pushed, moved)
    current = moved[:, :, :, rim_width : rim_width + column_count]
    earlier = moved[:, :, :, rim_width - 1 : rim_width - 1 + column_count]
    fraction_here = zonal_fraction[None, :, :, None]
    shifted = (1.0 - fraction_here) * current + fraction_here * earlier
    wavenumber = jnp.arange(MODES, dtype=jnp.int32)
    local_columns = lon_index * column_count + jnp.arange(column_count, dtype=jnp.int32)
    scale_mode = jnp.where(wavenumber == 0, 1.0, 2.0).astype(jnp.float32) / lon_cells
    quarter = lat_count // 4
    is_cap = (lat_index < quarter) | (lat_index >= lat_count - quarter)
    row_base = lat_index * row_count
    cut_rows = lax.dynamic_slice_in_dim(cutoff, row_base, row_count)
    damp_rows = lax.dynamic_slice_in_dim(damping, row_base, row_count)
    weight = jnp.where(wavenumber[None, :] <= cut_rows[:, None], scale_mode[None, :], 0.0)
    weight = jnp.concatenate([weight, weight], axis=1)
    flat_rows = shifted.reshape(-1, column_count)
    basis_table = make_basis(local_columns, wavenumber, lon_cells)
    coeffs = jnp.dot(
        flat_rows, basis_table, precision=lax.Precision.HIGHEST, preferred_element_type=jnp.float32
    )
    coeffs = lax.psum(coeffs, "lon")
    coeffs = (
        coeffs.reshape(shifted.shape[0], level_count, row_count, 2 * MODES) * weight[None, None]
    )
    low_part = jnp.dot(
        coeffs.reshape(-1, 2 * MODES),
        basis_table.T,
        precision=lax.Precision.HIGHEST,
        preferred_element_type=jnp.float32,
    )
    low_part = low_part.reshape(shifted.shape)
    damp_factor = damp_rows[None, None, :, None]
    filtered = damp_factor * shifted + (1.0 - damp_factor) * low_part
    result = jnp.where(is_cap, filtered, shifted)
    return result


def solution(mesh):
    placed = (
        P(None, None, "lat", "lon"),
        P(None, "lat", "lon"),
        P(None, "lat"),
        P(None, "lat"),
        P(),
        P(),
    )
    return jax.shard_map(
        body, mesh=mesh, in_specs=placed, out_specs=P(None, None, "lat", "lon"), check_vma=False
    )
```

profile of v0, /device:TPU:3, one launch (start us, length us, event | category | flops | bytes accessed | tf_op | source)
XLA Modules:
  0.0 126.5 jit_solution(10585470301114779105)
XLA Ops:
  6.5 0.0 all-reduce.9.cloned.1.call-start
  6.5 1.4 %copy.36 = f32[4,8,4,1440]{3,1,2,0:T(8,128)S(1)} copy(f32[4,8,4,1440]{3,2,1,0:T(4,128)} %param.6) | data formatting | bytes 1474560 | tf_op args[0]
  8.0 1.0 copy.32
  9.0 1.9 %collective-permute-start = (f32[5,8,1,1440]{3,1,2,0:T(8,128)S(1)}, f32[5,8,1,1440]{3,1,2,0:T(8,128)S(1)}, u32[]{:S(2)}, u32[]{:S(2)}) collective-permute-start(f32[5,8,1,1440]{3,1,2,0:T(8,128)S(1)} %pad_maximum_fusion.4), channel_id=1, source_target_pairs={{4,0},{8,4},{12,8},{16,12},{20,16},{24,20},{28,24},{5,1},{9,5},{13... | collective-permute-start | bytes 691208 | tf_op jit(solution)/shard_map/ppermute | solution.py:15
  10.9 4.3 %collective-permute-start.1 = (f32[4,8,1,1440]{3,1,2,0:T(8,128)S(1)}, f32[4,8,1,1440]{3,1,2,0:T(8,128)S(1)}, u32[]{:S(2)}, u32[]{:S(2)}) collective-permute-start(f32[4,8,1,1440]{3,1,2,0:T(8,128)S(1)} %get-tuple-element.8), channel_id=1, source_target_pairs={{0,4},{4,8},{8,12},{12,16},{16,20},{20,24},{24,28},{1,5},{5,9},{9,... | collective-permute-start | bytes 552968 | tf_op jit(solution)/shard_map/ppermute | solution.py:15
  15.2 0.7 broadcast_subtract_fusion
  15.9 0.0 copy-start.2
  15.9 0.0 copy-start
  15.9 27.2 %fusion.8 = (f32[1440,1024]{1,0:T(8,128)}, f32[1440,1024]{1,0:T(8,128)}) fusion(s32[1440]{0:T(1024)S(1)} %iota_add_fusion), kind=kLoop, calls=%fused_computation.11 | loop fusion | flops 13271040 | bytes 11802240 | tf_op jit(solution)/shard_map/cos | solution.py:27
  43.1 0.0 copy-start.4
  43.1 0.0 copy-done.2
  43.1 0.0 collective-permute-done
  43.2 0.0 collective-permute-done.1
  43.2 0.2 fusion.21
  43.5 0.0 copy-done
  43.5 0.4 slice_subtract_fusion
  43.9 0.1 slice.75
  43.9 2.6 %collective-permute-start.2 = (f32[4,8,4,65]{3,1,2,0:T(8,128)S(1)}, f32[4,8,4,65]{3,1,2,0:T(8,128)S(1)}, u32[]{:S(2)}, u32[]{:S(2)}) collective-permute-start(f32[4,8,4,65]{3,1,2,0:T(8,128)S(1)} %slice.75), channel_id=1, source_target_pairs={{0,1},{1,2},{2,3},{3,0},{4,5},{5,6},{6,7},{7,4},{8,9},{9,10},{10,1... | collective-permute-start | bytes 99848 | tf_op jit(solution)/shard_map/ppermute | solution.py:21
  46.5 0.0 copy-done.4
  46.5 0.1 dynamic_slice.7
  46.6 1.3 collective-permute-done.2
  47.8 0.3 fusion.23
  48.1 0.5 fusion.22
  48.6 0.3 pad_select_fusion.5
  48.9 0.0 copy-start.1
  48.9 0.3 pad_select_fusion.4
  49.2 0.3 pad_select_fusion.3
  49.4 0.3 pad_select_fusion.2
  49.7 0.3 pad_select_fusion.1
  50.0 0.3 pad_select_fusion
  50.3 0.0 copy-done.1
  50.3 0.5 fusion.24
  50.8 0.5 copy.37
  51.3 0.3 reshape.91
  51.6 0.0 copy-start.3
  51.6 11.9 %fusion.2 = f32[128,2048]{1,0:T(8,128)} fusion(f32[128,1440]{1,0:T(8,128)S(1)} %reshape.91, f32[1440,1024]{1,0:T(8,128)} %get-tuple-element.12, f32[1440,1024]{1,0:T(8,128)} %get-tuple-element.11), kind=kOutput, calls=%fused_computation.3 | convolution fusion | flops 4532797440 | bytes 13582336 | tf_op jit(solution)/shard_map/dot_general | solution.py:79
  63.5 0.0 all-reduce.9.cloned.1.call-update
  63.5 0.1 fusion.27
  63.6 0.2 mul.103
  63.8 0.4 mul.104
  64.2 0.0 copy-done.3
  64.2 0.1 broadcast_subtract_fusion.1
  64.3 35.8 %all-reduce.9.cloned.1.call-done = f32[128,2048]{1,0:T(8,128)} async-done(((f32[128,2048]{1,0:T(8,128)}), f32[128,2048]{1,0:T(8,128)}) %all-reduce.9.cloned.1.call-update) | async-done | bytes 1048592 | tf_op jit(solution)/shard_map/psum | solution.py:82
  100.1 1.3 %mul.105 = f32[128,2048]{1,0:T(8,128)S(1)} multiply(f32[128,2048]{1,0:T(8,128)} %all-reduce.9.cloned.1.call-done, f32[128,2048]{1,0:T(8,128)S(1)} %mul.104) | non-fusion elementwise | flops 262144 | bytes 3145728 | tf_op jit(solution)/shard_map/mul | solution.py:84
  101.4 0.3 dot_general.9
  101.7 16.6 %fusion.16 = f32[4,8,4,1440]{3,1,2,0:T(8,128)S(1)} fusion(f32[4,8,4,1440]{3,1,2,0:T(8,128)S(1)} %fusion.24, f32[1440,1024]{1,0:T(8,128)} %get-tuple-element.12, f32[1440,1024]{1,0:T(8,128)} %get-tuple-element.11, f32[4,8,4,2048]{3,2,1,0:T(4,128)S(1)} %dot_general.9, f32[4]{0:T(128)S(1)} %get-tuple-element.5, f32[4]{0:T(128)S(1)} %get-tuple-element.6, ...), kind=kOutput, calls=%fused_computation.15 | convolution fusion | flops 4533534720 | bytes 14319649 | tf_op jit(solution)/shard_map/dot_general | solution.py:86
  118.3 1.4 %copy.39 = f32[4,8,4,1440]{3,2,1,0:T(4,128)} copy(f32[4,8,4,1440]{3,1,2,0:T(8,128)S(1)} %fusion.16) | data formatting | bytes 1474560 | tf_op jit(solution)/shard_map/jit(_where)/select_n | solution.py:95
  (11 shorter events, 0.1 us)
Async XLA Ops:
  6.5 93.5 %all-reduce.9.cloned.1.call-start = ((), (), s32[]{:S(2)}) async-start(), calls=%async_computation | async-start | bytes 2097152 | tf_op jit(solution)/shard_map/psum | solution.py:82
  9.0 34.1 %collective-permute-start = (f32[5,8,1,1440]{3,1,2,0:T(8,128)S(1)}, f32[5,8,1,1440]{3,1,2,0:T(8,128)S(1)}, u32[]{:S(2)}, u32[]{:S(2)}) collective-permute-start(f32[5,8,1,1440]{3,1,2,0:T(8,128)S(1)} %pad_maximum_fusion.4), channel_id=1, source_target_pairs={{4,0},{8,4},{12,8},{16,12},{20,16},{24,20},{28,24},{5,1},{9,5},{13... | collective-permute-start | bytes 691208 | tf_op jit(solution)/shard_map/ppermute | solution.py:15
  10.9 32.3 %collective-permute-start.1 = (f32[4,8,1,1440]{3,1,2,0:T(8,128)S(1)}, f32[4,8,1,1440]{3,1,2,0:T(8,128)S(1)}, u32[]{:S(2)}, u32[]{:S(2)}) collective-permute-start(f32[4,8,1,1440]{3,1,2,0:T(8,128)S(1)} %get-tuple-element.8), channel_id=1, source_target_pairs={{0,4},{4,8},{8,12},{12,16},{16,20},{20,24},{24,28},{1,5},{5,9},{9,... | collective-permute-start | bytes 552968 | tf_op jit(solution)/shard_map/ppermute | solution.py:15
  15.9 27.2 %copy-start.2 = (s32[8,4]{0,1:T(4,128)S(1)}, s32[8,4]{0,1:T(4,128)}, u32[]{:S(2)}) copy-start(s32[8,4]{0,1:T(4,128)} %param.8) | copy-start | bytes 388
  15.9 27.6 %copy-start = (f32[4,8,4,1440]{3,2,1,0:T(4,128)S(1)}, f32[4,8,4,1440]{3,2,1,0:T(4,128)}, u32[]{:S(2)}) copy-start(f32[4,8,4,1440]{3,2,1,0:T(4,128)} %param.6) | copy-start | bytes 2211844
  43.1 3.4 %copy-start.4 = (s32[32]{0:T(128)S(1)}, s32[32]{0:T(128)}, u32[]{:S(2)}) copy-start(s32[32]{0:T(128)} %param.10) | copy-start | bytes 388
  43.9 3.9 %collective-permute-start.2 = (f32[4,8,4,65]{3,1,2,0:T(8,128)S(1)}, f32[4,8,4,65]{3,1,2,0:T(8,128)S(1)}, u32[]{:S(2)}, u32[]{:S(2)}) collective-permute-start(f32[4,8,4,65]{3,1,2,0:T(8,128)S(1)} %slice.75), channel_id=1, source_target_pairs={{0,1},{1,2},{2,3},{3,0},{4,5},{5,6},{6,7},{7,4},{8,9},{9,10},{10,1... | collective-permute-start | bytes 99848 | tf_op jit(solution)/shard_map/ppermute | solution.py:21
  48.9 1.4 %copy-start.1 = (f32[8,4]{0,1:T(4,128)S(1)}, f32[8,4]{0,1:T(4,128)}, u32[]{:S(2)}) copy-start(f32[8,4]{0,1:T(4,128)} %param.9) | copy-start | bytes 388
  51.6 12.6 %copy-start.3 = (f32[32]{0:T(128)S(1)}, f32[32]{0:T(128)}, u32[]{:S(2)}) copy-start(f32[32]{0:T(128)} %param.11) | copy-start | bytes 388
Sparse Core Ops, SparseCore 0:
  63.6 36.3 all-reduce.8
where the time goes:
time: 129 us; the launch traced here: 127 us
  waiting for transfers between devices  37 us (29%)
  other arithmetic  33 us (26%)
  matrix products  28.4 us (22%)
  between operations  13.7 us (11%)
  starting transfers between devices  8.75 us (7%)
  local copies, waits for them, and re-layouts  5.67 us (4%)
    psum x1, waiting for transfers between devices, body(): coeffs = lax.psum(coeffs, 'lon')  35.8 us
    cos x1, other arithmetic, make_basis(): return jnp.concatenate([jnp.cos(angles), jnp.sin(angles)], axis=1)  27.2 us
    dot_general x1, matrix products, body(): jnp.dot(coeffs.reshape(-1, 2 * MODES), basis_table.T, precision=lax.Preci...  16.6 us
    dot_general x1, matrix products, body(): jnp.dot(flat_rows, basis_table, precision=lax.Precision.HIGHEST, preferre...  11.9 us
    ppermute x2, starting transfers between devices, passed_along(): return lax.ppermute(block, axis, route)  6.18 us
  transfers between devices with their start and end apart: 4, of which 2 were waited for; matrix products, arithmetic and copies ran while one was open for 23% of the time, Pallas kernels for 0%

commit v1 on v0

v1 whole, which is shorter than its diff:
```python
import functools
import math

import jax
import jax.numpy as jnp
import numpy as np
from jax import lax
from jax.experimental import pallas as pl
from jax.experimental.pallas import tpu as pltpu
from jax.sharding import PartitionSpec as P

MODES = 1024
SMAX = 64
RADIX = 16
HALF = RADIX // 2
LANES = 128


def passed_along(block, axis, distance):
    devices = range(lax.axis_size(axis))
    route = [(i - distance, i) for i in devices if i - distance in devices]
    return lax.ppermute(block, axis, route)


def passed_around(value, axis, steps):
    count = lax.axis_size(axis)
    pairs = [(source, (source + steps) % count) for source in range(count)]
    return lax.ppermute(value, axis, pairs)


def times_phase(value, numerator, denominator):
    re, im = value
    eighth = (8 * numerator % (8 * denominator)) / denominator
    if eighth == 0:
        return re, im
    if eighth == 2:
        return -im, re
    if eighth == 4:
        return -re, -im
    if eighth == 6:
        return im, -re
    c = math.cos(2 * math.pi * numerator / denominator)
    s = math.sin(2 * math.pi * numerator / denominator)
    if eighth == 7:
        return (re + im) * c, (im - re) * c
    if eighth == 1:
        return (re - im) * c, (re + im) * c
    return re * c - im * s, re * s + im * c


def real_dft(values):
    n = len(values)
    if n == 2:
        return [(values[0] + values[1], None), (values[0] - values[1], None)]
    even, odd = real_dft(values[0::2]), real_dft(values[1::2])
    out = [None] * (n // 2 + 1)
    for r in range(n // 4 + 1):
        (er, ei), (tr, ti) = even[r], odd[r]
        if r == 0:
            out[0] = (er + tr, None)
            out[n // 2] = (er - tr, None)
        elif r == n // 4:
            out[r] = (er, -tr)
        else:
            tr, ti = times_phase((tr, ti), -r, n)
            out[r] = (er + tr, ei + ti)
            out[n // 2 - r] = (er - tr, ti - ei)
    return out


def real_inverse(spectrum):
    n = 2 * (len(spectrum) - 1)
    if n == 2:
        a, b = spectrum[0][0], spectrum[1][0]
        return [a + b, a - b]
    even, odd = [None] * (n // 4 + 1), [None] * (n // 4 + 1)
    for r in range(n // 4 + 1):
        (ar, ai), (br, bi) = spectrum[r], spectrum[n // 2 - r]
        if r == 0:
            even[0] = (ar + br, None)
            odd[0] = (ar - br, None)
        elif r == n // 4:
            even[r] = (ar + ar, None)
            odd[r] = (-(ai + ai), None)
        else:
            even[r] = (ar + br, ai - bi)
            odd[r] = times_phase((ar - br, ai + bi), r, n)
    out = [None] * n
    out[0::2] = real_inverse(even)
    out[1::2] = real_inverse(odd)
    return out


def split(value):
    high = value.astype(jnp.bfloat16)
    return high, (value - high.astype(jnp.float32)).astype(jnp.bfloat16)


def product(left, right_high, right_low):
    high, low = split(left)
    dot = functools.partial(jnp.dot, preferred_element_type=jnp.float32)
    return dot(high, right_high) + (dot(high, right_low) + dot(low, right_high))


def filter_kernel(
    cap_ref, cutoff_ref, shift_ref, fraction_ref, damping_ref, phase_ref,
    fwd_high, fwd_low, inv_high, inv_low, *refs
):
    parts = (len(refs) - 3) // 2
    ins, outs = refs[:parts], refs[parts : 2 * parts]
    moved_ref, stack_ref, back_ref = refs[2 * parts :]
    row_count, levels, columns = ins[0].shape
    lon_cells = parts * columns
    piece = lon_cells // RADIX
    padded = stack_ref.shape[1]
    modes = fwd_high.shape[1] // 2
    group = levels * 2 * (HALF + 1)

    for row in range(row_count):
        circle = jnp.concatenate([ref[row] for ref in ins], axis=1)
        distance = shift_ref[row][:, :1]
        for bit in range(SMAX.bit_length()):
            pushed = pltpu.roll(circle, 1 << bit, 1)
            circle = jnp.where((distance >> bit) & 1 == 1, pushed, circle)
        share = fraction_ref[row][:, :1]
        circle = (1.0 - share) * circle + share * pltpu.roll(circle, 1, 1)
        moved_ref[row, :, :lon_cells] = circle
        moved_ref[row, :, lon_cells:] = circle[:, :LANES]

    @pl.when(cap_ref[0] == 0)
    def _():
        for row in range(row_count):
            for part in range(parts):
                start = part * columns
                outs[part][row] = moved_ref[row, :, start : start + columns]

    @pl.when(cap_ref[0] != 0)
    def _():
        for row in range(row_count):
            for tile in range(0, padded, LANES):
                lanes = slice(tile, tile + LANES)
                starts = [piece * u + tile for u in range(RADIX)]
                spectrum = real_dft([moved_ref[row, :, s : s + LANES] for s in starts])
                for r, (re, im) in enumerate(spectrum):
                    base = row * group + 2 * r * levels
                    if r == 0:
                        im = jnp.zeros_like(re)
                    else:
                        c, s = phase_ref[2 * r : 2 * r + 1, lanes], phase_ref[2 * r + 1 : 2 * r + 2, lanes]
                        if im is None:
                            re, im = re * c, -(re * s)
                        else:
                            re, im = re * c + im * s, im * c - re * s
                    stack_ref[base : base + levels, lanes] = re
                    stack_ref[base + levels : base + 2 * levels, lanes] = im
        coeffs = product(stack_ref[...], fwd_high[...], fwd_low[...])
        mode = lax.broadcasted_iota(jnp.int32, (levels, modes), 1) - modes // 2
        for row in range(row_count):
            for r in range(HALF + 1):
                base = row * group + 2 * r * levels
                re, im = coeffs[base : base + levels], coeffs[base + levels : base + 2 * levels]
                wavenumber = jnp.abs(RADIX * mode + r)
                weight = jnp.where(wavenumber <= cutoff_ref[row], 1.0 / lon_cells, 0.0)
                x_re = (re[:, :modes] + im[:, modes:]) * weight
                x_im = (im[:, :modes] - re[:, modes:]) * weight
                back_ref[base : base + levels, :modes] = x_re
                back_ref[base : base + levels, modes:] = -x_im
                back_ref[base + levels : base + 2 * levels, :modes] = x_im
                back_ref[base + levels : base + 2 * levels, modes:] = x_re
        stack_ref[...] = product(back_ref[...], inv_high[...], inv_low[...])
        for row in range(row_count):
            keep = damping_ref[row]
            for tile in range(0, padded, LANES):
                lanes = slice(tile, tile + LANES)
                spectrum = []
                for r in range(HALF + 1):
                    base = row * group + 2 * r * levels
                    re = stack_ref[base : base + levels, lanes]
                    im = stack_ref[base + levels : base + 2 * levels, lanes]
                    if r > 0:
                        c, s = phase_ref[2 * r : 2 * r + 1, lanes], phase_ref[2 * r + 1 : 2 * r + 2, lanes]
                        re, im = re * c - im * s, re * s + im * c
                    spectrum.append((re, im))
                width = min(LANES, piece - tile)
                for u, low in enumerate(real_inverse(spectrum)):
                    start = piece * u + tile
                    shifted = moved_ref[row, :, start : start + LANES]
                    result = keep * shifted + (1.0 - keep) * low
                    part, offset = start // columns, start % columns
                    outs[part][row, :, offset : offset + width] = result[:, :width]


def filter_tables(lon_cells):
    piece = lon_cells // RADIX
    padded = -(-piece // LANES) * LANES
    modes = 2 * MODES // RADIX
    q = np.arange(modes) - modes // 2
    angle = 2 * np.pi * (np.arange(piece)[:, None] * q[None, :] % piece) / piece
    table = np.zeros((padded, 2 * modes))
    table[:piece, :modes] = np.cos(angle)
    table[:piece, modes:] = np.sin(angle)
    high = table.astype(jnp.bfloat16)
    low = (table - high.astype(np.float64)).astype(jnp.bfloat16)
    r = np.arange(HALF + 1)
    turn = 2 * np.pi * r[:, None] * np.arange(padded)[None, :] / lon_cells
    phase = np.stack([np.cos(turn), np.sin(turn)], axis=1).reshape(-1, padded)
    return phase.astype(np.float32), high, low, np.ascontiguousarray(high.T), np.ascontiguousarray(low.T)


def filtered(chunks, is_cap, cut_rows, shift_rows, fraction_rows, damp_rows):
    row_count, levels, columns = chunks[0].shape
    parts = len(chunks)
    lon_cells = parts * columns
    tables = filter_tables(lon_cells)
    padded, double = tables[1].shape
    group = levels * 2 * (HALF + 1)
    spread = lambda v: jnp.broadcast_to(v[:, :, None], v.shape + (LANES,))
    vmem = pl.BlockSpec(memory_space=pltpu.VMEM)
    smem = pl.BlockSpec(memory_space=pltpu.SMEM)
    return pl.pallas_call(
        filter_kernel,
        out_shape=[jax.ShapeDtypeStruct(c.shape, jnp.float32) for c in chunks],
        in_specs=[smem, smem, vmem, vmem, smem] + [vmem] * (5 + parts),
        out_specs=[vmem] * parts,
        scratch_shapes=[
            pltpu.VMEM((row_count, levels, lon_cells + LANES), jnp.float32),
            pltpu.VMEM((row_count * group, padded), jnp.float32),
            pltpu.VMEM((row_count * group, double), jnp.float32),
        ],
        compiler_params=pltpu.CompilerParams(vmem_limit_bytes=24 << 20),
    )(
        is_cap, cut_rows, spread(shift_rows), spread(fraction_rows), damp_rows,
        *[jnp.asarray(t) for t in tables], *chunks,
    )


def body(tracers, merid_courant, zonal_shift, zonal_fraction, cutoff, damping):
    tracer_count, level_count, row_count, column_count = tracers.shape
    lat_count = lax.axis_size("lat")
    lat_index = lax.axis_index("lat")
    lon_count = lax.axis_size("lon")
    lon_index = lax.axis_index("lon")
    share = tracer_count // lon_count

    cells = tracers.transpose(0, 2, 1, 3)
    speed = merid_courant.transpose(1, 0, 2)
    below = passed_along(cells[:, row_count - 1], "lat", 1)
    above = passed_along(jnp.concatenate([cells[:, 0], speed[:1]], axis=0), "lat", -1)

    def flux_of(face_speed, south, north):
        return jnp.maximum(face_speed, 0.0)[None] * south + jnp.minimum(face_speed, 0.0)[None] * north

    first = jnp.where(lat_index > 0, flux_of(speed[0], below, cells[:, 0]), 0.0)
    last = flux_of(above[tracer_count], cells[:, row_count - 1], above[:tracer_count])
    last = jnp.where(lat_index < lat_count - 1, last, 0.0)
    fluxes = [first]
    fluxes += [flux_of(speed[j], cells[:, j - 1], cells[:, j]) for j in range(1, row_count)]
    fluxes.append(last)
    advected = jnp.stack(
        [cells[:, j] + fluxes[j] - fluxes[j + 1] for j in range(row_count)], axis=1
    ).reshape(lon_count, share * row_count, level_count, column_count)

    chunks = [None] * lon_count
    for step in range(lon_count):
        mine = lax.dynamic_index_in_dim(advected, (lon_index + step) % lon_count, 0, False)
        chunks[-step % lon_count] = passed_around(mine, "lon", step) if step else mine

    quarter = lat_count // 4
    is_cap = (lat_index < quarter) | (lat_index >= lat_count - quarter)
    row_base = lat_index * row_count
    cut_rows = jnp.tile(lax.dynamic_slice_in_dim(cutoff, row_base, row_count), share)
    damp_rows = jnp.tile(lax.dynamic_slice_in_dim(damping, row_base, row_count), share)
    shift_rows = jnp.tile(zonal_shift.T, (share, 1))
    fraction_rows = jnp.tile(zonal_fraction.T, (share, 1))
    results = filtered(
        chunks, is_cap.astype(jnp.int32)[None], cut_rows, shift_rows, fraction_rows, damp_rows
    )
    back = [passed_around(r, "lon", step) if step else r for step, r in enumerate(results)]
    stacked = jnp.stack(back, axis=0)
    order = (lon_index - jnp.arange(lon_count)) % lon_count
    stacked = jnp.concatenate(
        [lax.dynamic_slice_in_dim(stacked, order[t], 1, 0) for t in range(lon_count)], axis=0
    )
    stacked = stacked.reshape(tracer_count, row_count, level_count, column_count)
    return stacked.transpose(0, 2, 1, 3)


def solution(mesh):
    placed = (
        P(None, None, "lat", "lon"),
        P(None, "lat", "lon"),
        P(None, "lat"),
        P(None, "lat"),
        P(),
        P(),
    )
    return jax.shard_map(
        body, mesh=mesh, in_specs=placed, out_specs=P(None, None, "lat", "lon"), check_vma=False
    )
```

time: 129 us -> 56.3 us (0.44); the launches traced: 127 us -> 55.4 us
  other arithmetic: 33 us -> 2.59 us
  matrix products: 28.4 us -> 0 us
  waiting for transfers between devices: 37 us -> 18.3 us
  Pallas kernels: 0 us -> 7.86 us
  between operations: 13.7 us -> 8.01 us
  starting transfers between devices: 8.75 us -> 12.6 us
    psum x1 -> x0, waiting for transfers between devices: 35.8 us -> none  [body(): coeffs = lax.psum(coeffs, 'lon')]
    dot_general x2 -> x0, matrix products: 28.4 us -> none  [the longest x1 16.6 us: body(): jnp.dot(coeffs.reshape(-1, 2 * MODES), basis_table.T, precision=lax.Preci...]
    cos x1 -> x0, other arithmetic: 27.2 us -> none  [make_basis(): return jnp.concatenate([jnp.cos(angles), jnp.sin(angles)], axis=1)]
    ppermute x2, waiting for transfers between devices: 0.01 us -> 11.6 us  [passed_along(): return lax.ppermute(block, axis, route)]
    pallas_call x0 -> x1, Pallas kernels: none -> 7.86 us  [filtered(): pl.pallas_call(filter_kernel, out_shape=[jax.ShapeDtypeStruct(c.shape, jn...]
    ppermute x1 -> x6, waiting for transfers between devices: 1.25 us -> 6.61 us  [passed_around(): return lax.ppermute(value, axis, pairs)]
    ppermute x1 -> x6, starting transfers between devices: 2.56 us -> 6.44 us  [passed_around(): return lax.ppermute(value, axis, pairs)]
    select_n x9 -> x1, other arithmetic: 2.43 us -> 0.01 us  [body(): order = (lon_index - jnp.arange(lon_count)) % lon_count]
  transfers between devices with their start and end apart: 4 -> 8, of which waited for: 2 -> 6; matrix products, arithmetic and copies ran while one was open for 23% -> 2% of each run, Pallas kernels for 0% -> 0%
where the time goes in v1:
time: 56.3 us; the launch traced here: 55.4 us
  waiting for transfers between devices  18.3 us (33%)
  starting transfers between devices  12.6 us (22%)
  between operations  8.01 us (14%)
  Pallas kernels  7.86 us (14%)
  local copies, waits for them, and re-layouts  6.11 us (11%)
  other arithmetic  2.59 us (5%)
    ppermute x2, waiting for transfers between devices, passed_along(): return lax.ppermute(block, axis, route)  11.6 us
    pallas_call x1, Pallas kernels, filtered(): pl.pallas_call(filter_kernel, out_shape=[jax.ShapeDtypeStruct(c.shape, jn...  7.86 us
    ppermute x6, waiting for transfers between devices, passed_around(): return lax.ppermute(value, axis, pairs)  6.61 us
    ppermute x6, starting transfers between devices, passed_around(): return lax.ppermute(value, axis, pairs)  6.44 us
    ppermute x2, starting transfers between devices, passed_along(): return lax.ppermute(block, axis, route)  6.18 us
    unnamed x29, local copies, waits for them, and re-layouts  3.01 us
    max x2, other arithmetic, flux_of(): jnp.maximum(face_speed, 0.0)[None] * south  1.64 us
    transpose x1, local copies, waits for them, and re-layouts, body(): return stacked.transpose(0, 2, 1, 3)  1.39 us
  transfers between devices with their start and end apart: 8, of which 6 were waited for; matrix products, arithmetic and copies ran while one was open for 2% of the time, Pallas kernels for 0%

profile of v1, /device:TPU:3, one launch (start us, length us, event | category | flops | bytes accessed | tf_op | source)
XLA Modules:
  0.0 55.4 jit_solution(5093841183348805783)
XLA Ops:
  0.0 1.6 %broadcast_maximum_fusion = (f32[1,8,1440]{2,0,1:T(1,128)S(1)}, f32[1,8,1440]{2,0,1:T(1,128)S(1)}, f32[1,8,1440]{2,0,1:T(1,128)S(1)}, f32[1,8,1440]{2,0,1:T(1,12...) fusion(f32[4,8,1440]{2,0,1:T(4,128)} %bitcast.89), kind=kLoop, calls=%fused_computation.45 | loop fusion | flops 92160 | bytes 599040 | tf_op jit(solution)/shard_map/max | solution.py:251
  1.6 1.6 %copy.43 = f32[4,8,4,1440]{3,0,1,2:T(4,128)S(1)} copy(f32[4,8,4,1440]{3,2,1,0:T(4,128)} %param.11) | data formatting | bytes 1474560 | tf_op args[0]
  3.3 0.2 add_subtract_fusion.1
  3.5 0.1 pad_maximum_fusion.2
  3.6 1.9 %collective-permute-start.1 = (f32[5,8,1440]{2,0,1:T(8,128)S(1)}, f32[5,8,1440]{2,0,1:T(8,128)S(1)}, u32[]{:S(2)}, u32[]{:S(2)}) collective-permute-start(f32[5,8,1440]{2,0,1:T(8,128)S(1)} %pad_maximum_fusion.2), channel_id=1, source_target_pairs={{4,0},{8,4},{12,8},{16,12},{20,16},{24,20},{28,24},{5,1},{9,5},{13... | collective-permute-start | bytes 691208 | tf_op jit(solution)/shard_map/ppermute | solution.py:22
  5.5 4.3 %collective-permute-start = (f32[4,8,1440]{2,0,1:T(4,128)S(1)}, f32[4,8,1440]{2,0,1:T(4,128)S(1)}, u32[]{:S(2)}, u32[]{:S(2)}) collective-permute-start(f32[4,8,1440]{2,0,1:T(4,128)S(1)} %get-tuple-element.25), channel_id=1, source_target_pairs={{0,4},{4,8},{8,12},{12,16},{16,20},{20,24},{24,28},{1,5},{5,9},{9,... | collective-permute-start | bytes 552968 | tf_op jit(solution)/shard_map/ppermute | solution.py:22
  9.9 6.5 %collective-permute-done.1 = f32[5,8,1440]{2,0,1:T(8,128)S(1)} collective-permute-done((f32[5,8,1440]{2,0,1:T(8,128)S(1)}, f32[5,8,1440]{2,0,1:T(8,128)S(1)}, u32[]{:S(2)}, u32[]{:S(2)}) %collective-permute-start.1) | collective-permute-done | bytes 230432 | tf_op jit(solution)/shard_map/ppermute | solution.py:22
  16.4 0.1 slice_maximum_fusion
  16.5 5.1 %collective-permute-done = f32[4,8,1440]{2,0,1:T(4,128)S(1)} collective-permute-done((f32[4,8,1440]{2,0,1:T(4,128)S(1)}, f32[4,8,1440]{2,0,1:T(4,128)S(1)}, u32[]{:S(2)}, u32[]{:S(2)}) %collective-permute-start) | collective-permute-done | bytes 184352 | tf_op jit(solution)/shard_map/ppermute | solution.py:22
  21.6 0.3 fusion.8
  22.0 0.2 pad_maximum_fusion
  22.2 0.7 %constant_dynamic-slice_fusion.4 = (f32[1,4,8,1440]{3,0,2,1:T(1,128)S(1)}, f32[1,4,8,1440]{3,0,2,1:T(1,128)S(1)}, f32[1,4,8,1440]{3,0,2,1:T(1,128)S(1)}, f32[1,4,8,1440]{3,0,2,1:T(1,128)S(1)}) fusion(f32[4,4,8,1440]{3,0,2,1:T(4,128)S(1)} %pad_maximum_fusion, s32[]{:T(128)S(6)} %select_n.80, s32[]{:T(128)S(6)} %select_n.78, s32[]{:T(128)S(6)} %select_n.76, ...), kind=kLoop, calls=%fused_computation.52 | loop fusion | bytes 1474576 | tf_op jit(solution)/shard_map/jit(dynamic_index_in_dim)/dynamic_slice | solution.py:265
  22.9 0.5 collective-permute-start.2
  23.4 1.3 %collective-permute-start.3 = (f32[4,8,1440]{2,1,0:T(8,128)S(1)}, f32[4,8,1440]{2,1,0:T(8,128)S(1)}, u32[]{:S(2)}, u32[]{:S(2)}) collective-permute-start(f32[4,8,1440]{2,1,0:T(8,128)S(1)} %bitcast.87), channel_id=1, source_target_pairs={{0,2},{1,3},{2,0},{3,1},{4,6},{5,7},{6,4},{7,5},{8,10},{9,11},{10,... | collective-permute-start | bytes 552968 | tf_op jit(solution)/shard_map/ppermute | solution.py:28
  24.8 0.0 copy-start.2
  24.8 0.0 copy-start.3
  24.8 1.6 %collective-permute-start.4 = (f32[4,8,1440]{2,1,0:T(8,128)S(1)}, f32[4,8,1440]{2,1,0:T(8,128)S(1)}, u32[]{:S(2)}, u32[]{:S(2)}) collective-permute-start(f32[4,8,1440]{2,1,0:T(8,128)S(1)} %bitcast.88), channel_id=1, source_target_pairs={{0,1},{1,2},{2,3},{3,0},{4,5},{5,6},{6,7},{7,4},{8,9},{9,10},{10,1... | collective-permute-start | bytes 552968 | tf_op jit(solution)/shard_map/ppermute | solution.py:28
  26.4 0.0 copy-start.7
  26.4 0.7 %copy-done.7 = s32[32]{0:T(128)S(1)} copy-done((s32[32]{0:T(128)S(1)}, s32[32]{0:T(128)}, u32[]{:S(2)}) %copy-start.7) | copy-done | bytes 152
  27.0 0.0 copy-start.8
  27.0 0.1 dynamic_slice.31.cutoff_ref
  27.1 0.6 %copy-done.8 = f32[32]{0:T(128)S(1)} copy-done((f32[32]{0:T(128)S(1)}, f32[32]{0:T(128)}, u32[]{:S(2)}) %copy-start.8) | copy-done | bytes 152
  27.7 0.1 dynamic_slice.32.damping_ref
  27.8 0.0 copy-start.4
  27.8 2.3 %collective-permute-done.2.refs_1_ = f32[4,8,1440]{2,1,0:T(8,128)S(1)} collective-permute-done((f32[4,8,1440]{2,1,0:T(8,128)S(1)}, f32[4,8,1440]{2,1,0:T(8,128)S(1)}, u32[]{:S(2)}, u32[]{:S(2)}) %collective-permute-start.2) | collective-permute-done | bytes 184352 | tf_op jit(solution)/shard_map/ppermute | solution.py:28
  30.1 0.0 collective-permute-done.3.refs_2_
  30.1 3.5 %collective-permute-done.4.refs_3_ = f32[4,8,1440]{2,1,0:T(8,128)S(1)} collective-permute-done((f32[4,8,1440]{2,1,0:T(8,128)S(1)}, f32[4,8,1440]{2,1,0:T(8,128)S(1)}, u32[]{:S(2)}, u32[]{:S(2)}) %collective-permute-start.4) | collective-permute-done | bytes 184352 | tf_op jit(solution)/shard_map/ppermute | solution.py:28
  33.7 0.0 copy-done.5
  33.7 0.1 broadcast_in_dim.15.shift_ref
  33.8 0.0 copy-done.6
  33.8 0.1 broadcast_in_dim.16.fraction_ref
  33.8 0.0 copy-done.2
  33.8 0.0 copy-done.3
  33.8 0.0 copy-done
  33.8 0.0 copy-done.1
  33.9 0.0 copy-done.4
  33.9 7.9 %shard_map.109 = (f32[4,8,1440]{2,1,0:T(8,128)S(1)}, f32[4,8,1440]{2,1,0:T(8,128)S(1)}, f32[4,8,1440]{2,1,0:T(8,128)S(1)}, f32[4,8,1440]{2,1,0:T(8,128)S(1)}) custom-call(s32[1]{0:T(128)} %bitcast.cap_ref, s32[4]{0:T(128)S(1)} %dynamic_slice.31.cutoff_ref, s32[4,8,128]{2,1,0:T(8,128)S(1)} %broadcast_in_dim.15.shift_ref, ...), custom_call_target="tpu_custom_call" | custom-call | tf_op jit(solution)/shard_map/pallas_call | solution.py:220
  41.7 2.5 %collective-permute-start.5 = (f32[4,8,1440]{2,1,0:T(8,128)S(1)}, f32[4,8,1440]{2,1,0:T(8,128)S(1)}, u32[]{:S(2)}, u32[]{:S(2)}) collective-permute-start(f32[4,8,1440]{2,1,0:T(8,128)S(1)} %get-tuple-element.10), channel_id=1, source_target_pairs={{0,1},{1,2},{2,3},{3,0},{4,5},{5,6},{6,7},{7,4},{8,9},{9,10},{10,1... | collective-permute-start | bytes 552968 | tf_op jit(solution)/shard_map/ppermute | solution.py:28
  44.3 0.2 collective-permute-start.6
  44.5 0.2 collective-permute-start.7
  44.8 0.7 %fusion.10 = (s32[1]{0:T(128)}, s32[1]{0:T(128)}, s32[1]{0:T(128)}, s32[1]{0:T(128)}) fusion(s32[4]{0:T(128)S(1)} %and_select_fusion), kind=kLoop, calls=%fused_computation.58 | loop fusion | bytes 32 | tf_op jit(solution)/shard_map/slice | solution.py:282
  53.2 0.0 collective-permute-done.5
  53.2 0.1 collective-permute-done.6
  53.3 0.6 %collective-permute-done.7 = f32[4,8,1440]{2,1,0:T(8,128)S(1)} collective-permute-done((f32[4,8,1440]{2,1,0:T(8,128)S(1)}, f32[4,8,1440]{2,1,0:T(8,128)S(1)}, u32[]{:S(2)}, u32[]{:S(2)}) %collective-permute-start.7) | collective-permute-done | bytes 184352 | tf_op jit(solution)/shard_map/ppermute | solution.py:28
  53.9 0.1 pad_maximum_fusion.1
  53.9 0.1 constant_dynamic-slice_fusion.3
  54.0 0.1 maximum_bitcast_fusion
  54.1 1.4 %copy.13 = f32[4,8,4,1440]{3,2,1,0:T(4,128)} copy(f32[4,8,4,1440]{3,1,2,0:T(8,128)S(1)} %maximum_bitcast_fusion) | data formatting | bytes 1474560 | tf_op jit(solution)/shard_map/transpose | solution.py:285
  (15 shorter events, 0.1 us)
Async XLA Ops:
  3.6 12.8 %collective-permute-start.1 = (f32[5,8,1440]{2,0,1:T(8,128)S(1)}, f32[5,8,1440]{2,0,1:T(8,128)S(1)}, u32[]{:S(2)}, u32[]{:S(2)}) collective-permute-start(f32[5,8,1440]{2,0,1:T(8,128)S(1)} %pad_maximum_fusion.2), channel_id=1, source_target_pairs={{4,0},{8,4},{12,8},{16,12},{20,16},{24,20},{28,24},{5,1},{9,5},{13... | collective-permute-start | bytes 691208 | tf_op jit(solution)/shard_map/ppermute | solution.py:22
  5.5 16.1 %collective-permute-start = (f32[4,8,1440]{2,0,1:T(4,128)S(1)}, f32[4,8,1440]{2,0,1:T(4,128)S(1)}, u32[]{:S(2)}, u32[]{:S(2)}) collective-permute-start(f32[4,8,1440]{2,0,1:T(4,128)S(1)} %get-tuple-element.25), channel_id=1, source_target_pairs={{0,4},{4,8},{8,12},{12,16},{16,20},{20,24},{24,28},{1,5},{5,9},{9,... | collective-permute-start | bytes 552968 | tf_op jit(solution)/shard_map/ppermute | solution.py:22
  22.9 7.2 %collective-permute-start.2 = (f32[4,8,1440]{2,1,0:T(8,128)S(1)}, f32[4,8,1440]{2,1,0:T(8,128)S(1)}, u32[]{:S(2)}, u32[]{:S(2)}) collective-permute-start(f32[4,8,1440]{2,1,0:T(8,128)S(1)} %bitcast.86), channel_id=1, source_target_pairs={{0,3},{1,0},{2,1},{3,2},{4,7},{5,4},{6,5},{7,6},{8,11},{9,8},{10,9... | collective-permute-start | bytes 552968 | tf_op jit(solution)/shard_map/ppermute | solution.py:28
  23.4 6.7 %collective-permute-start.3 = (f32[4,8,1440]{2,1,0:T(8,128)S(1)}, f32[4,8,1440]{2,1,0:T(8,128)S(1)}, u32[]{:S(2)}, u32[]{:S(2)}) collective-permute-start(f32[4,8,1440]{2,1,0:T(8,128)S(1)} %bitcast.87), channel_id=1, source_target_pairs={{0,2},{1,3},{2,0},{3,1},{4,6},{5,7},{6,4},{7,5},{8,10},{9,11},{10,... | collective-permute-start | bytes 552968 | tf_op jit(solution)/shard_map/ppermute | solution.py:28
  24.8 9.1 %copy-start.2 = (bf16[256,384]{1,0:T(8,128)(2,1)S(1)}, bf16[256,384]{1,0:T(8,128)(2,1)}, u32[]{:S(2)}) copy-start(bf16[256,384]{1,0:T(8,128)(2,1)} %constant.80.clone.inv_high) | copy-start | bytes 589828
  24.8 9.1 %copy-start.3 = (bf16[256,384]{1,0:T(8,128)(2,1)S(1)}, bf16[256,384]{1,0:T(8,128)(2,1)}, u32[]{:S(2)}) copy-start(bf16[256,384]{1,0:T(8,128)(2,1)} %constant.81.clone.inv_low) | copy-start | bytes 589828
  24.8 8.9 %collective-permute-start.4 = (f32[4,8,1440]{2,1,0:T(8,128)S(1)}, f32[4,8,1440]{2,1,0:T(8,128)S(1)}, u32[]{:S(2)}, u32[]{:S(2)}) collective-permute-start(f32[4,8,1440]{2,1,0:T(8,128)S(1)} %bitcast.88), channel_id=1, source_target_pairs={{0,1},{1,2},{2,3},{3,0},{4,5},{5,6},{6,7},{7,4},{8,9},{9,10},{10,1... | collective-permute-start | bytes 552968 | tf_op jit(solution)/shard_map/ppermute | solution.py:28
  26.4 0.7 %copy-start.7 = (s32[32]{0:T(128)S(1)}, s32[32]{0:T(128)}, u32[]{:S(2)}) copy-start(s32[32]{0:T(128)} %param.15) | copy-start | bytes 388
  27.0 0.7 %copy-start.8 = (f32[32]{0:T(128)S(1)}, f32[32]{0:T(128)}, u32[]{:S(2)}) copy-start(f32[32]{0:T(128)} %param.16) | copy-start | bytes 388
  27.7 5.9 %copy-start.5 = (s32[8,4]{0,1:T(4,128)S(1)}, s32[8,4]{0,1:T(4,128)}, u32[]{:S(2)}) copy-start(s32[8,4]{0,1:T(4,128)} %param.13) | copy-start | bytes 388
  27.7 6.0 %copy-start.6 = (f32[8,4]{0,1:T(4,128)S(1)}, f32[8,4]{0,1:T(4,128)}, u32[]{:S(2)}) copy-start(f32[8,4]{0,1:T(4,128)} %param.14) | copy-start | bytes 388
  27.7 6.1 %copy-start = (bf16[384,256]{1,0:T(8,128)(2,1)S(1)}, bf16[384,256]{1,0:T(8,128)(2,1)}, u32[]{:S(2)}) copy-start(bf16[384,256]{1,0:T(8,128)(2,1)} %constant.78.clone.fwd_high) | copy-start | bytes 589828
  27.8 6.1 %copy-start.1 = (bf16[384,256]{1,0:T(8,128)(2,1)S(1)}, bf16[384,256]{1,0:T(8,128)(2,1)}, u32[]{:S(2)}) copy-start(bf16[384,256]{1,0:T(8,128)(2,1)} %constant.79.clone.fwd_low) | copy-start | bytes 589828
  27.8 6.1 %copy-start.4 = (f32[18,384]{1,0:T(8,128)S(1)}, f32[18,384]{1,0:T(8,128)}, u32[]{:S(2)}) copy-start(f32[18,384]{1,0:T(8,128)} %constant.77.clone.phase_ref) | copy-start | bytes 82948
  41.7 11.4 %collective-permute-start.5 = (f32[4,8,1440]{2,1,0:T(8,128)S(1)}, f32[4,8,1440]{2,1,0:T(8,128)S(1)}, u32[]{:S(2)}, u32[]{:S(2)}) collective-permute-start(f32[4,8,1440]{2,1,0:T(8,128)S(1)} %get-tuple-element.10), channel_id=1, source_target_pairs={{0,1},{1,2},{2,3},{3,0},{4,5},{5,6},{6,7},{7,4},{8,9},{9,10},{10,1... | collective-permute-start | bytes 552968 | tf_op jit(solution)/shard_map/ppermute | solution.py:28
  44.3 9.0 %collective-permute-start.6 = (f32[4,8,1440]{2,1,0:T(8,128)S(1)}, f32[4,8,1440]{2,1,0:T(8,128)S(1)}, u32[]{:S(2)}, u32[]{:S(2)}) collective-permute-start(f32[4,8,1440]{2,1,0:T(8,128)S(1)} %get-tuple-element.11), channel_id=1, source_target_pairs={{0,2},{1,3},{2,0},{3,1},{4,6},{5,7},{6,4},{7,5},{8,10},{9,11},{10,... | collective-permute-start | bytes 552968 | tf_op jit(solution)/shard_map/ppermute | solution.py:28
  44.5 9.4 %collective-permute-start.7 = (f32[4,8,1440]{2,1,0:T(8,128)S(1)}, f32[4,8,1440]{2,1,0:T(8,128)S(1)}, u32[]{:S(2)}, u32[]{:S(2)}) collective-permute-start(f32[4,8,1440]{2,1,0:T(8,128)S(1)} %get-tuple-element.12), channel_id=1, source_target_pairs={{0,3},{1,0},{2,1},{3,2},{4,7},{5,4},{6,5},{7,6},{8,11},{9,8},{10,9... | collective-permute-start | bytes 552968 | tf_op jit(solution)/shard_map/ppermute | solution.py:28

commit v2 on v1

--- a/solution.py
+++ b/solution.py
@@ -14,18 +14,7 @@
 RADIX = 16
 HALF = RADIX // 2
 LANES = 128
-
-
-def passed_along(block, axis, distance):
-    devices = range(lax.axis_size(axis))
-    route = [(i - distance, i) for i in devices if i - distance in devices]
-    return lax.ppermute(block, axis, route)
-
-
-def passed_around(value, axis, steps):
-    count = lax.axis_size(axis)
-    pairs = [(source, (source + steps) % count) for source in range(count)]
-    return lax.ppermute(value, axis, pairs)
+SPAN = 9 * LANES
 
 
 def times_phase(value, numerator, denominator):
@@ -104,12 +93,11 @@
 
 def filter_kernel(
     cap_ref, cutoff_ref, shift_ref, fraction_ref, damping_ref, phase_ref,
-    fwd_high, fwd_low, inv_high, inv_low, *refs
+    fwd_high, fwd_low, inv_high, inv_low, in_ref, out_ref,
+    circle_ref, moved_ref, stack_ref, back_ref,
 ):
-    parts = (len(refs) - 3) // 2
-    ins, outs = refs[:parts], refs[parts : 2 * parts]
-    moved_ref, stack_ref, back_ref = refs[2 * parts :]
-    row_count, levels, columns = ins[0].shape
+    parts, height, columns = in_ref.shape
+    row_count, levels = shift_ref.shape[:2]
     lon_cells = parts * columns
     piece = lon_cells // RADIX
     padded = stack_ref.shape[1]
@@ -117,22 +105,33 @@
     group = levels * 2 * (HALF + 1)
 
     for row in range(row_count):
-        circle = jnp.concatenate([ref[row] for ref in ins], axis=1)
-        distance = shift_ref[row][:, :1]
-        for bit in range(SMAX.bit_length()):
-            pushed = pltpu.roll(circle, 1 << bit, 1)
-            circle = jnp.where((distance >> bit) & 1 == 1, pushed, circle)
-        share = fraction_ref[row][:, :1]
-        circle = (1.0 - share) * circle + share * pltpu.roll(circle, 1, 1)
-        moved_ref[row, :, :lon_cells] = circle
-        moved_ref[row, :, lon_cells:] = circle[:, :LANES]
+        own = slice(row * levels, (row + 1) * levels)
+        for part in range(parts):
+            start = LANES + part * columns
+            circle_ref[row, :, start : start + columns] = in_ref[part, own]
+        circle_ref[row, :, :LANES] = in_ref[parts - 1, own, columns - LANES :]
+        distance = shift_ref[row]
+        share = fraction_ref[row]
+        for start in range(0, lon_cells, SPAN):
+            width = min(SPAN, lon_cells - start) + LANES
+            block = circle_ref[row, :, start : start + width]
+            distances = jnp.concatenate([distance] * (width // LANES), axis=1)
+            shares = jnp.concatenate([share] * (width // LANES), axis=1)
+            for bit in range(SMAX.bit_length()):
+                pushed = pltpu.roll(block, 1 << bit, 1)
+                block = jnp.where((distances >> bit) & 1 == 1, pushed, block)
+            block = (1.0 - shares) * block + shares * pltpu.roll(block, 1, 1)
+            moved_ref[row, :, start : start + width - LANES] = block[:, LANES:]
+            if start == 0:
+                moved_ref[row, :, lon_cells:] = block[:, LANES : 2 * LANES]
 
     @pl.when(cap_ref[0] == 0)
     def _():
         for row in range(row_count):
+            own = slice(row * levels, (row + 1) * levels)
             for part in range(parts):
                 start = part * columns
-                outs[part][row] = moved_ref[row, :, start : start + columns]
+                out_ref[part, own] = moved_ref[row, :, start : start + columns]
 
     @pl.when(cap_ref[0] != 0)
     def _():
@@ -169,6 +168,7 @@
                 back_ref[base + levels : base + 2 * levels, modes:] = x_re
         stack_ref[...] = product(back_ref[...], inv_high[...], inv_low[...])
         for row in range(row_count):
+            own = slice(row * levels, (row + 1) * levels)
             keep = damping_ref[row]
             for tile in range(0, padded, LANES):
                 lanes = slice(tile, tile + LANES)
@@ -187,7 +187,7 @@
                     shifted = moved_ref[row, :, start : start + LANES]
                     result = keep * shifted + (1.0 - keep) * low
                     part, offset = start // columns, start % columns
-                    outs[part][row, :, offset : offset + width] = result[:, :width]
+                    out_ref[part, own, offset : offset + width] = result[:, :width]
 
 
 def filter_tables(lon_cells):
@@ -208,8 +208,8 @@
 
 
 def filtered(chunks, is_cap, cut_rows, shift_rows, fraction_rows, damp_rows):
-    row_count, levels, columns = chunks[0].shape
-    parts = len(chunks)
+    parts, height, columns = chunks.shape
+    row_count, levels = shift_rows.shape
     lon_cells = parts * columns
     tables = filter_tables(lon_cells)
     padded, double = tables[1].shape
@@ -219,19 +219,33 @@
     smem = pl.BlockSpec(memory_space=pltpu.SMEM)
     return pl.pallas_call(
         filter_kernel,
-        out_shape=[jax.ShapeDtypeStruct(c.shape, jnp.float32) for c in chunks],
-        in_specs=[smem, smem, vmem, vmem, smem] + [vmem] * (5 + parts),
-        out_specs=[vmem] * parts,
+        out_shape=jax.ShapeDtypeStruct(chunks.shape, jnp.float32),
+        in_specs=[smem, smem, vmem, vmem, smem] + [vmem] * 6,
+        out_specs=vmem,
         scratch_shapes=[
+            pltpu.VMEM((row_count, levels, lon_cells + LANES), jnp.float32),
             pltpu.VMEM((row_count, levels, lon_cells + LANES), jnp.float32),
             pltpu.VMEM((row_count * group, padded), jnp.float32),
             pltpu.VMEM((row_count * group, double), jnp.float32),
         ],
         compiler_params=pltpu.CompilerParams(vmem_limit_bytes=24 << 20),
+        cost_estimate=pl.CostEstimate(flops=int(2e9), bytes_accessed=1 << 20, transcendentals=0),
     )(
         is_cap, cut_rows, spread(shift_rows), spread(fraction_rows), damp_rows,
-        *[jnp.asarray(t) for t in tables], *chunks,
+        *[jnp.asarray(t) for t in tables], chunks,
     )
+
+
+def swapped(value, axis, first):
+    count = lax.axis_size(axis)
+    pairs = []
+    for low in range(first, count - 1, 2):
+        pairs += [(low, low + 1), (low + 1, low)]
+    return lax.ppermute(value, axis, pairs)
+
+
+def exchanged(value, axis):
+    return lax.all_to_all(value, axis, 0, 0)
 
 
 def body(tracers, merid_courant, zonal_shift, zonal_fraction, cutoff, damping):
@@ -239,50 +253,57 @@
     lat_count = lax.axis_size("lat")
     lat_index = lax.axis_index("lat")
     lon_count = lax.axis_size("lon")
-    lon_index = lax.axis_index("lon")
     share = tracer_count // lon_count
-
-    cells = tracers.transpose(0, 2, 1, 3)
+    top = row_count - 1
+
+    cells = tracers.transpose(2, 0, 1, 3)
     speed = merid_courant.transpose(1, 0, 2)
-    below = passed_along(cells[:, row_count - 1], "lat", 1)
-    above = passed_along(jnp.concatenate([cells[:, 0], speed[:1]], axis=0), "lat", -1)
+    south_edge = jnp.concatenate([cells[0], speed[:1]], axis=0).reshape(-1, column_count)
+    north_edge = jnp.concatenate([cells[top], speed[:1]], axis=0).reshape(-1, column_count)
+    is_even = lat_index % 2 == 0
+    near = swapped(jnp.where(is_even, north_edge, south_edge), "lat", 0)
+    far = swapped(jnp.where(is_even, south_edge, north_edge), "lat", 1)
 
     def flux_of(face_speed, south, north):
         return jnp.maximum(face_speed, 0.0)[None] * south + jnp.minimum(face_speed, 0.0)[None] * north
 
-    first = jnp.where(lat_index > 0, flux_of(speed[0], below, cells[:, 0]), 0.0)
-    last = flux_of(above[tracer_count], cells[:, row_count - 1], above[:tracer_count])
-    last = jnp.where(lat_index < lat_count - 1, last, 0.0)
-    fluxes = [first]
-    fluxes += [flux_of(speed[j], cells[:, j - 1], cells[:, j]) for j in range(1, row_count)]
-    fluxes.append(last)
-    advected = jnp.stack(
-        [cells[:, j] + fluxes[j] - fluxes[j + 1] for j in range(row_count)], axis=1
-    ).reshape(lon_count, share * row_count, level_count, column_count)
-
-    chunks = [None] * lon_count
-    for step in range(lon_count):
-        mine = lax.dynamic_index_in_dim(advected, (lon_index + step) % lon_count, 0, False)
-        chunks[-step % lon_count] = passed_around(mine, "lon", step) if step else mine
+    def packed(rows):
+        block = jnp.stack(rows, axis=1)
+        return block.reshape(lon_count, share * len(rows) * level_count, column_count)
+
+    def unpacked(block, count):
+        return block.reshape(tracer_count, count, level_count, column_count)
 
     quarter = lat_count // 4
     is_cap = (lat_index < quarter) | (lat_index >= lat_count - quarter)
+    is_cap = is_cap.astype(jnp.int32)[None]
     row_base = lat_index * row_count
-    cut_rows = jnp.tile(lax.dynamic_slice_in_dim(cutoff, row_base, row_count), share)
-    damp_rows = jnp.tile(lax.dynamic_slice_in_dim(damping, row_base, row_count), share)
-    shift_rows = jnp.tile(zonal_shift.T, (share, 1))
-    fraction_rows = jnp.tile(zonal_fraction.T, (share, 1))
-    results = filtered(
-        chunks, is_cap.astype(jnp.int32)[None], cut_rows, shift_rows, fraction_rows, damp_rows
+    cut_rows = lax.dynamic_slice_in_dim(cutoff, row_base, row_count)
+    damp_rows = lax.dynamic_slice_in_dim(damping, row_base, row_count)
+
+    def stepped(rows, numbers):
+        pick = lambda v: jnp.concatenate([v[j : j + 1] for j in numbers] * share, axis=0)
+        chunks = exchanged(packed(rows), "lon")
+        result = filtered(
+            chunks, is_cap, pick(cut_rows), pick(zonal_shift.T), pick(zonal_fraction.T), pick(damp_rows)
+        )
+        return unpacked(exchanged(result, "lon"), len(numbers))
+
+    fluxes = [None] + [flux_of(speed[j], cells[j - 1], cells[j]) for j in range(1, row_count)] + [None]
+    inner = stepped(
+        [cells[j] + fluxes[j] - fluxes[j + 1] for j in range(1, top)], list(range(1, top))
     )
-    back = [passed_around(r, "lon", step) if step else r for step, r in enumerate(results)]
-    stacked = jnp.stack(back, axis=0)
-    order = (lon_index - jnp.arange(lon_count)) % lon_count
-    stacked = jnp.concatenate(
-        [lax.dynamic_slice_in_dim(stacked, order[t], 1, 0) for t in range(lon_count)], axis=0
-    )
-    stacked = stacked.reshape(tracer_count, row_count, level_count, column_count)
-    return stacked.transpose(0, 2, 1, 3)
+
+    near = near.reshape(tracer_count + 1, level_count, column_count)
+    far = far.reshape(tracer_count + 1, level_count, column_count)
+    below = jnp.where(is_even, far, near)
+    above = jnp.where(is_even, near, far)
+    first = jnp.where(lat_index > 0, flux_of(speed[0], below[:tracer_count], cells[0]), 0.0)
+    last = flux_of(above[tracer_count], cells[top], above[:tracer_count])
+    last = jnp.where(lat_index < lat_count - 1, last, 0.0)
+    outer = stepped([cells[0] + first - fluxes[1], cells[top] + fluxes[top] - last], [0, top])
+    result = jnp.concatenate([outer[:, :1], inner, outer[:, 1:]], axis=1)
+    return result.transpose(0, 2, 1, 3)
 
 
 def solution(mesh):

time: 56.3 us -> 57.8 us (1.027)
  waiting for transfers between devices: 18.3 us -> 8.3 us
  starting transfers between devices: 12.6 us -> 21.2 us
  between operations: 8.01 us -> 0.29 us
  other arithmetic: 2.59 us -> 7.91 us
  Pallas kernels: 7.86 us -> 11.2 us
  local copies, waits for them, and re-layouts: 6.11 us -> 8.2 us
    ppermute x8 -> x2, waiting for transfers between devices: 18.3 us -> 0.01 us  [swapped(): return lax.ppermute(value, axis, pairs)]
    all_to_all x0 -> x4, starting transfers between devices: none -> 16.8 us  [exchanged(): return lax.all_to_all(value, axis, 0, 0)]
    all_to_all x0 -> x4, waiting for transfers between devices: none -> 8.3 us  [exchanged(): return lax.all_to_all(value, axis, 0, 0)]
    ppermute x8 -> x2, starting transfers between devices: 12.6 us -> 4.43 us  [swapped(): return lax.ppermute(value, axis, pairs)]
    slice x1 -> x7, local copies, waits for them, and re-layouts: 0.67 us -> 4.1 us  [the longest x1 2.83 us: body(): cells[j]]
    pallas_call x1 -> x2, Pallas kernels: 7.86 us -> 11.2 us  [filtered(): pl.pallas_call(filter_kernel, out_shape=jax.ShapeDtypeStruct(chunks.shape...]
    concatenate x1 -> x4, other arithmetic: 0.09 us -> 2.58 us  [stepped(): jnp.concatenate([v[j:j + 1] for j in numbers] * share, axis=0)]
    transpose x1 -> x0, local copies, waits for them, and re-layouts: 1.39 us -> none  [body(): return stacked.transpose(0, 2, 1, 3)]
  transfers between devices with their start and end apart: 8 -> 6, of which waited for: 6 -> 2; matrix products, arithmetic and copies ran while one was open for 2% -> 14% of each run, Pallas kernels for 0% -> 20%
where the time goes in v2:
time: 57.8 us; the launch traced here: 57.1 us
  starting transfers between devices  21.2 us (37%)
  Pallas kernels  11.2 us (19%)
  waiting for transfers between devices  8.3 us (14%)
  local copies, waits for them, and re-layouts  8.2 us (14%)
  other arithmetic  7.91 us (14%)
    all_to_all x4, starting transfers between devices, exchanged(): return lax.all_to_all(value, axis, 0, 0)  16.8 us
    pallas_call x2, Pallas kernels, filtered(): pl.pallas_call(filter_kernel, out_shape=jax.ShapeDtypeStruct(chunks.shape...  11.2 us
    all_to_all x4, waiting for transfers between devices, exchanged(): return lax.all_to_all(value, axis, 0, 0)  8.3 us
    ppermute x2, starting transfers between devices, swapped(): return lax.ppermute(value, axis, pairs)  4.43 us
    slice x1, local copies, waits for them, and re-layouts, body(): cells[j]  2.83 us
    concatenate x4, other arithmetic, stepped(): jnp.concatenate([v[j:j + 1] for j in numbers] * share, axis=0)  2.58 us
    unnamed x28, local copies, waits for them, and re-layouts  2.41 us
    max x2, other arithmetic, flux_of(): jnp.maximum(face_speed, 0.0)[None] * south  1.72 us
  transfers between devices with their start and end apart: 6, of which 2 were waited for; matrix products, arithmetic and copies ran while one was open for 14% of the time, Pallas kernels for 20%

profile of v2, /device:TPU:3, one launch (start us, length us, event | category | flops | bytes accessed | tf_op | source)
XLA Modules:
  0.0 57.1 jit_solution(16303722392471126238)
XLA Ops:
  0.0 1.7 %slice_maximum_fusion.1 = (f32[1,8,1440]{2,0,1:T(1,128)S(1)}, f32[1,8,1440]{2,0,1:T(1,128)S(1)}, f32[1,8,1440]{2,0,1:T(1,128)S(1)}, f32[1,8,1440]{2,0,1:T(1,128)...) fusion(f32[4,8,1440]{2,0,1:T(4,128)} %bitcast.134), kind=kLoop, calls=%fused_computation.56 | loop fusion | flops 92160 | bytes 599040 | tf_op jit(solution)/shard_map/max | solution.py:268
  1.7 2.8 %fusion.21 = (f32[1,4,8,1440]{3,0,2,1:T(1,128)S(1)}, f32[1,4,8,1440]{3,0,2,1:T(1,128)S(1)}, f32[1,4,8,1440]{3,0,2,1:T(1,128)S(1)}, f32[1,4,8,1440]{3,0,2,1:T(1,128)S(1)}) fusion(f32[4,4,8,1440]{3,0,2,1:T(4,128)} %bitcast.128), kind=kLoop, calls=%fused_computation.67 | loop fusion | bytes 1474560 | tf_op jit(solution)/shard_map/slice | solution.py:292
  4.6 0.0 copy-start.5
  4.7 0.1 collective-permute-start.1
  4.8 4.4 %collective-permute-start = (f32[40,1440]{1,0:T(8,128)S(1)}, f32[40,1440]{1,0:T(8,128)S(1)}, u32[]{:S(2)}, u32[]{:S(2)}) collective-permute-start(f32[40,1440]{1,0:T(8,128)S(1)} %get-tuple-element.11), channel_id=1, source_target_pairs={{4,8},{8,4},{12,16},{16,12},{20,24},{24,20},{5,9},{9,5},{13,17},{1... | collective-permute-start | bytes 691208 | tf_op jit(solution)/shard_map/ppermute | solution.py:244
  9.2 0.0 copy-done.5
  9.2 0.8 %fusion.13 = (f32[4,1,8,1440]{3,1,2,0:T(1,128)S(1)}, f32[4,1,8,1440]{3,1,2,0:T(1,128)S(1)}) fusion(f32[8,1440]{1,0:T(8,128)S(1)} %get-tuple-element.38, f32[8,1440]{1,0:T(8,128)S(1)} %get-tuple-element.39, f32[8,1440]{1,0:T(8,128)S(1)} %get-tuple-element.34, f32[8,1440]{1,0:T(8,128)S(1)} %get-tuple-element.35, f32[4,4,8,1440]{3,0,2,1:T(4,128)S(1)} %bitcast.129, ...), kind=kLoop, calls=%fused_computation.27 | loop fusion | flops 552960 | bytes 1336320 | tf_op jit(solution)/shard_map/sub | solution.py:294
  10.0 0.4 pad_maximum_fusion.1
  10.4 0.8 %copy.67 = f32[4,2,8,1440]{3,2,1,0:T(8,128)} copy(f32[4,2,8,1440]{3,1,2,0:T(2,128)S(1)} %pad_maximum_fusion.1) | data formatting | bytes 737280 | tf_op jit(solution)/shard_map/stack | solution.py:271
  11.2 4.8 %all-to-all-start.2 = ((f32[4,16,1440]{2,1,0:T(8,128)}), f32[4,16,1440]{2,1,0:T(8,128)S(1)}, u32[]{:S(2)}, u32[]{:S(2)}) async-start(f32[4,16,1440]{2,1,0:T(8,128)} %bitcast.125), calls=%async_computation.2 | async-start | bytes 786432 | tf_op jit(solution)/shard_map/all_to_all | solution.py:248
  16.0 0.0 copy-done.6
  16.0 0.7 %copy-done.7 = f32[8,4]{0,1:T(4,128)S(1)} copy-done((f32[8,4]{0,1:T(4,128)S(1)}, f32[8,4]{0,1:T(4,128)}, u32[]{:S(2)}) %copy-start.7) | copy-done | bytes 152
  16.8 0.0 copy-start.8
  16.8 0.6 %copy-done.8 = s32[32]{0:T(128)S(1)} copy-done((s32[32]{0:T(128)S(1)}, s32[32]{0:T(128)}, u32[]{:S(2)}) %copy-start.8) | copy-done | bytes 152
  17.5 0.1 dynamic_slice.6
  17.5 0.6 %copy-done.9 = f32[32]{0:T(128)S(1)} copy-done((f32[32]{0:T(128)S(1)}, f32[32]{0:T(128)}, u32[]{:S(2)}) %copy-start.9) | copy-done | bytes 152
  18.1 0.1 dynamic_slice.7
  18.2 0.1 concatenate.39.cutoff_ref
  18.3 0.1 concatenate.42.damping_ref
  18.3 0.6 %fusion.26 = (s32[1]{0:T(128)}, s32[1]{0:T(128)}) fusion(s32[4]{0:T(128)S(1)} %dynamic_slice.6), kind=kLoop, calls=%fused_computation.72 | loop fusion | bytes 16 | tf_op jit(solution)/shard_map/slice | solution.py:285
  18.9 0.6 %fusion.25 = (f32[1]{0:T(128)}, f32[1]{0:T(128)}) fusion(f32[4]{0:T(128)S(1)} %dynamic_slice.7), kind=kLoop, calls=%fused_computation.71 | loop fusion | bytes 16 | tf_op jit(solution)/shard_map/slice | solution.py:285
  19.6 0.0 collective-permute-done.1
  19.6 0.0 collective-permute-done
  19.6 0.1 fusion.11
  19.7 0.1 fusion.4
  19.8 0.0 copy-start.4
  19.8 0.8 %copy_bitcast_fusion.1 = f32[4,16,1440]{2,1,0:T(8,128)} fusion(f32[4,1,8,1440]{3,2,0,1:T(8,128)S(1)} %fusion.4, f32[4,1,8,1440]{3,2,0,1:T(8,128)S(1)} %fusion.11), kind=kLoop, calls=%fused_computation.4 | loop fusion | flops 92160 | bytes 737280 | tf_op jit(solution)/shard_map/reshape | solution.py:272
  20.6 2.0 %all-to-all-done.2.in_ref = f32[4,16,1440]{2,1,0:T(8,128)S(1)} async-done(((f32[4,16,1440]{2,1,0:T(8,128)}), f32[4,16,1440]{2,1,0:T(8,128)S(1)}, u32[]{:S(2)}, u32[]{:S(2)}) %all-to-all-start.2) | async-done | bytes 368672 | tf_op jit(solution)/shard_map/all_to_all | solution.py:248
  22.6 4.3 %all-to-all-start = ((f32[4,16,1440]{2,1,0:T(8,128)}), f32[4,16,1440]{2,1,0:T(8,128)S(1)}, u32[]{:S(2)}, u32[]{:S(2)}) async-start(f32[4,16,1440]{2,1,0:T(8,128)} %copy_bitcast_fusion.1), calls=%async_computation | async-start | bytes 786432 | tf_op jit(solution)/shard_map/all_to_all | solution.py:248
  26.9 1.2 %pad_add_fusion.1.cutoff_ref = s32[2]{0:T(128)S(1)} fusion(s32[1]{0:T(128)} %get-tuple-element.33, s32[1]{0:T(128)} %get-tuple-element.32), kind=kLoop, calls=%fused_computation.65 | loop fusion | flops 2 | bytes 16 | tf_op jit(solution)/shard_map/concatenate | solution.py:285
  28.1 0.1 broadcast_in_dim.22.shift_ref
  28.2 0.1 broadcast_in_dim.23.fraction_ref
  28.2 0.0 copy-done.4
  28.2 0.0 copy-done.1
  28.3 5.6 %shard_map.155 = f32[4,16,1440]{2,1,0:T(8,128)} custom-call(s32[1]{0:T(128)} %bitcast.cap_ref, s32[2]{0:T(128)S(1)} %concatenate.39.cutoff_ref, s32[2,8,128]{2,1,0:T(8,128)S(1)} %broadcast_in_dim.22.shift_ref, f32[2,8,128]{2,1,0:T(8,128)S(1)} %broadcast_in_dim.23.fraction_ref, f32[2]{0:T(128)S(1)} %concatenate.42.damping_ref, f32[18,384]{1,0:T(8,128)S(1)} %copy-done.4, ...), custom_call_target="tpu_custom_call" | custom-call | flops 2000000000 | bytes 1048576 | tf_op jit(solution)/shard_map/pallas_call | solution.py:220
  33.8 0.0 all-to-all-done.in_ref
  33.8 3.9 %all-to-all-start.3 = ((f32[4,16,1440]{2,1,0:T(8,128)}), f32[4,16,1440]{2,1,0:T(8,128)S(1)}, u32[]{:S(2)}, u32[]{:S(2)}) async-start(f32[4,16,1440]{2,1,0:T(8,128)} %shard_map.155), calls=%async_computation.3 | async-start | bytes 786432 | tf_op jit(solution)/shard_map/all_to_all | solution.py:248
  37.8 1.4 %pad_maximum_fusion.5.damping_ref = f32[2]{0:T(128)S(1)} fusion(f32[1]{0:T(128)} %get-tuple-element.31, f32[1]{0:T(128)} %get-tuple-element.30), kind=kLoop, calls=%fused_computation.66 | loop fusion | flops 2 | bytes 16 | tf_op jit(solution)/shard_map/concatenate | solution.py:285
  39.2 0.1 broadcast_in_dim.19.shift_ref
  39.2 0.1 broadcast_in_dim.20.fraction_ref
  39.3 5.6 %shard_map.154 = f32[4,16,1440]{2,1,0:T(8,128)} custom-call(s32[1]{0:T(128)} %bitcast.cap_ref, s32[2]{0:T(128)S(1)} %pad_add_fusion.1.cutoff_ref, s32[2,8,128]{2,1,0:T(8,128)S(1)} %broadcast_in_dim.19.shift_ref, f32[2,8,128]{2,1,0:T(8,128)S(1)} %broadcast_in_dim.20.fraction_ref, f32[2]{0:T(128)S(1)} %pad_maximum_fusion.5.damping_ref, ...), custom_call_target="tpu_custom_call" | custom-call | flops 2000000000 | bytes 1048576 | tf_op jit(solution)/shard_map/pallas_call | solution.py:220
  44.9 0.0 all-to-all-done.3
  44.9 3.8 %all-to-all-start.1 = ((f32[4,16,1440]{2,1,0:T(8,128)}), f32[4,16,1440]{2,1,0:T(8,128)S(1)}, u32[]{:S(2)}, u32[]{:S(2)}) async-start(f32[4,16,1440]{2,1,0:T(8,128)} %shard_map.154), calls=%async_computation.1 | async-start | bytes 786432 | tf_op jit(solution)/shard_map/all_to_all | solution.py:248
  48.7 0.3 copy.26
  49.0 6.3 %all-to-all-done.1 = f32[4,16,1440]{2,1,0:T(8,128)S(1)} async-done(((f32[4,16,1440]{2,1,0:T(8,128)}), f32[4,16,1440]{2,1,0:T(8,128)S(1)}, u32[]{:S(2)}, u32[]{:S(2)}) %all-to-all-start.1) | async-done | bytes 368672 | tf_op jit(solution)/shard_map/all_to_all | solution.py:248
  55.3 0.2 copy.40
  55.5 0.2 copy.39
  55.7 1.4 %maximum_bitcast_fusion = f32[4,8,4,1440]{3,2,1,0:T(4,128)} fusion(f32[4,1,8,1440]{3,1,2,0:T(1,128)S(1)} %copy.40, f32[4,2,8,1440]{3,1,2,0:T(2,128)S(1)} %copy.26, f32[4,1,8,1440]{3,1,2,0:T(1,128)S(1)} %copy.39), kind=kLoop, calls=%fused_computation | loop fusion | flops 368640 | bytes 1474560 | tf_op jit(solution)/shard_map/transpose | solution.py:306
  (28 shorter events, 0.2 us)
Async XLA Ops:
  4.6 4.6 %copy-start.5 = (f32[4,8,4,1440]{3,2,1,0:T(4,128)S(1)}, f32[4,8,4,1440]{3,2,1,0:T(4,128)}, u32[]{:S(2)}) copy-start(f32[4,8,4,1440]{3,2,1,0:T(4,128)} %param.16) | copy-start | bytes 2211844
  4.7 14.9 %collective-permute-start.1 = (f32[40,1440]{1,0:T(8,128)S(1)}, f32[40,1440]{1,0:T(8,128)S(1)}, u32[]{:S(2)}, u32[]{:S(2)}) collective-permute-start(f32[40,1440]{1,0:T(8,128)S(1)} %get-tuple-element.12), channel_id=1, source_target_pairs={{0,4},{4,0},{8,12},{12,8},{16,20},{20,16},{24,28},{28,24},{1,5},{5... | collective-permute-start | bytes 691208 | tf_op jit(solution)/shard_map/ppermute | solution.py:244
  4.8 14.8 %collective-permute-start = (f32[40,1440]{1,0:T(8,128)S(1)}, f32[40,1440]{1,0:T(8,128)S(1)}, u32[]{:S(2)}, u32[]{:S(2)}) collective-permute-start(f32[40,1440]{1,0:T(8,128)S(1)} %get-tuple-element.11), channel_id=1, source_target_pairs={{4,8},{8,4},{12,16},{16,12},{20,24},{24,20},{5,9},{9,5},{13,17},{1... | collective-permute-start | bytes 691208 | tf_op jit(solution)/shard_map/ppermute | solution.py:244
  11.2 4.8 %copy-start.6 = (s32[8,4]{0,1:T(4,128)S(1)}, s32[8,4]{0,1:T(4,128)}, u32[]{:S(2)}) copy-start(s32[8,4]{0,1:T(4,128)} %param.18) | copy-start | bytes 388
  11.2 11.4 %all-to-all-start.2 = ((f32[4,16,1440]{2,1,0:T(8,128)}), f32[4,16,1440]{2,1,0:T(8,128)S(1)}, u32[]{:S(2)}, u32[]{:S(2)}) async-start(f32[4,16,1440]{2,1,0:T(8,128)} %bitcast.125), calls=%async_computation.2 | async-start | bytes 786432 | tf_op jit(solution)/shard_map/all_to_all | solution.py:248
  16.0 0.7 %copy-start.7 = (f32[8,4]{0,1:T(4,128)S(1)}, f32[8,4]{0,1:T(4,128)}, u32[]{:S(2)}) copy-start(f32[8,4]{0,1:T(4,128)} %param.19) | copy-start | bytes 388
  16.8 0.7 %copy-start.8 = (s32[32]{0:T(128)S(1)}, s32[32]{0:T(128)}, u32[]{:S(2)}) copy-start(s32[32]{0:T(128)} %param.20) | copy-start | bytes 388
  17.5 0.7 %copy-start.9 = (f32[32]{0:T(128)S(1)}, f32[32]{0:T(128)}, u32[]{:S(2)}) copy-start(f32[32]{0:T(128)} %param.21) | copy-start | bytes 388
  19.8 8.4 %copy-start.4 = (f32[18,384]{1,0:T(8,128)S(1)}, f32[18,384]{1,0:T(8,128)}, u32[]{:S(2)}) copy-start(f32[18,384]{1,0:T(8,128)} %constant.41.clone.phase_ref) | copy-start | bytes 82948
  20.6 7.7 %copy-start = (bf16[384,256]{1,0:T(8,128)(2,1)S(1)}, bf16[384,256]{1,0:T(8,128)(2,1)}, u32[]{:S(2)}) copy-start(bf16[384,256]{1,0:T(8,128)(2,1)} %constant.42.clone.fwd_high) | copy-start | bytes 589828
  20.6 7.7 %copy-start.1 = (bf16[384,256]{1,0:T(8,128)(2,1)S(1)}, bf16[384,256]{1,0:T(8,128)(2,1)}, u32[]{:S(2)}) copy-start(bf16[384,256]{1,0:T(8,128)(2,1)} %constant.43.clone.fwd_low) | copy-start | bytes 589828
  20.6 7.7 %copy-start.2 = (bf16[256,384]{1,0:T(8,128)(2,1)S(1)}, bf16[256,384]{1,0:T(8,128)(2,1)}, u32[]{:S(2)}) copy-start(bf16[256,384]{1,0:T(8,128)(2,1)} %constant.44.clone.inv_high) | copy-start | bytes 589828
  20.6 7.7 %copy-start.3 = (bf16[256,384]{1,0:T(8,128)(2,1)S(1)}, bf16[256,384]{1,0:T(8,128)(2,1)}, u32[]{:S(2)}) copy-start(bf16[256,384]{1,0:T(8,128)(2,1)} %constant.45.clone.inv_low) | copy-start | bytes 589828
  22.6 11.2 %all-to-all-start = ((f32[4,16,1440]{2,1,0:T(8,128)}), f32[4,16,1440]{2,1,0:T(8,128)S(1)}, u32[]{:S(2)}, u32[]{:S(2)}) async-start(f32[4,16,1440]{2,1,0:T(8,128)} %copy_bitcast_fusion.1), calls=%async_computation | async-start | bytes 786432 | tf_op jit(solution)/shard_map/all_to_all | solution.py:248
  33.8 11.0 %all-to-all-start.3 = ((f32[4,16,1440]{2,1,0:T(8,128)}), f32[4,16,1440]{2,1,0:T(8,128)S(1)}, u32[]{:S(2)}, u32[]{:S(2)}) async-start(f32[4,16,1440]{2,1,0:T(8,128)} %shard_map.155), calls=%async_computation.3 | async-start | bytes 786432 | tf_op jit(solution)/shard_map/all_to_all | solution.py:248
  44.9 10.3 %all-to-all-start.1 = ((f32[4,16,1440]{2,1,0:T(8,128)}), f32[4,16,1440]{2,1,0:T(8,128)S(1)}, u32[]{:S(2)}, u32[]{:S(2)}) async-start(f32[4,16,1440]{2,1,0:T(8,128)} %shard_map.154), calls=%async_computation.1 | async-start | bytes 786432 | tf_op jit(solution)/shard_map/all_to_all | solution.py:248

commit v3 on v1

v3 whole, which is shorter than its diff:
```python
import functools
import math

import jax
import jax.numpy as jnp
import numpy as np
from jax import lax
from jax.experimental import pallas as pl
from jax.experimental.pallas import tpu as pltpu
from jax.sharding import PartitionSpec as P

MODES = 1024
SMAX = 64
RADIX = 16
HALF = RADIX // 2
LANES = 128
SPAN = 6 * LANES
PAIR = 2


def times_phase(value, numerator, denominator):
    re, im = value
    eighth = (8 * numerator % (8 * denominator)) / denominator
    if eighth == 0:
        return re, im
    if eighth == 2:
        return -im, re
    if eighth == 4:
        return -re, -im
    if eighth == 6:
        return im, -re
    c = math.cos(2 * math.pi * numerator / denominator)
    s = math.sin(2 * math.pi * numerator / denominator)
    if eighth == 7:
        return (re + im) * c, (im - re) * c
    if eighth == 1:
        return (re - im) * c, (re + im) * c
    return re * c - im * s, re * s + im * c


def real_dft(values):
    n = len(values)
    if n == 2:
        return [(values[0] + values[1], None), (values[0] - values[1], None)]
    even, odd = real_dft(values[0::2]), real_dft(values[1::2])
    out = [None] * (n // 2 + 1)
    for r in range(n // 4 + 1):
        (er, ei), (tr, ti) = even[r], odd[r]
        if r == 0:
            out[0] = (er + tr, None)
            out[n // 2] = (er - tr, None)
        elif r == n // 4:
            out[r] = (er, -tr)
        else:
            tr, ti = times_phase((tr, ti), -r, n)
            out[r] = (er + tr, ei + ti)
            out[n // 2 - r] = (er - tr, ti - ei)
    return out


def real_inverse(spectrum):
    n = 2 * (len(spectrum) - 1)
    if n == 2:
        a, b = spectrum[0][0], spectrum[1][0]
        return [a + b, a - b]
    even, odd = [None] * (n // 4 + 1), [None] * (n // 4 + 1)
    for r in range(n // 4 + 1):
        (ar, ai), (br, bi) = spectrum[r], spectrum[n // 2 - r]
        if r == 0:
            even[0] = (ar + br, None)
            odd[0] = (ar - br, None)
        elif r == n // 4:
            even[r] = (ar + ar, None)
            odd[r] = (-(ai + ai), None)
        else:
            even[r] = (ar + br, ai - bi)
            odd[r] = times_phase((ar - br, ai + bi), r, n)
    out = [None] * n
    out[0::2] = real_inverse(even)
    out[1::2] = real_inverse(odd)
    return out


def four(values, sign):
    (ar, ai), (br, bi), (cr, ci), (dr, di) = values
    pr, pi, mr, mi = ar + cr, ai + ci, ar - cr, ai - ci
    qr, qi, nr, ni = br + dr, bi + di, br - dr, bi - di
    if sign > 0:
        nr, ni = -nr, -ni
    return [(pr + qr, pi + qi), (mr + ni, mi - nr), (pr - qr, pi - qi), (mr - ni, mi + nr)]


def half_dft(x):
    out = [None] * 9
    out[0::2] = real_dft(x)
    odd = four([times_phase((x[v], -x[v + 4]), -v, 16) for v in range(4)], -1)
    out[1], out[5] = odd[0], odd[1]
    out[7] = (odd[2][0], -odd[2][1])
    out[3] = (odd[3][0], -odd[3][1])
    return out


def half_inverse(w):
    even = real_inverse(w[0::2])
    odd = four([w[1], w[5], (w[7][0], -w[7][1]), (w[3][0], -w[3][1])], 1)
    odd = [times_phase(value, v, 16) for v, value in enumerate(odd)]
    return [even[v] + odd[v][0] for v in range(4)] + [even[v + 4] - odd[v][1] for v in range(4)]


def split(value):
    high = value.astype(jnp.bfloat16)
    return high, (value - high.astype(jnp.float32)).astype(jnp.bfloat16)


def product(left, right_high, right_low):
    high, low = split(left)
    dot = functools.partial(jnp.dot, preferred_element_type=jnp.float32)
    return dot(high, right_high) + (dot(high, right_low) + dot(low, right_high))


def spans(columns, width):
    return [slice(start, min(start + width, columns)) for start in range(0, columns, width)]


def is_cap(lat):
    count = lax.axis_size("lat")
    return (lat < count // 4) | (lat >= count - count // 4)


def flux_of(face_speed, south, north):
    return jnp.maximum(face_speed, 0.0) * south + jnp.minimum(face_speed, 0.0) * north


def begin_kernel(cells_ref, speed_ref, near_ref, far_ref, mine_ref, send_ref, edge_mine_ref, edge_send_ref):
    tracer_count, levels, row_count, columns = cells_ref.shape
    share = tracer_count // PAIR
    core = lax.rem(lax.axis_index("lon"), PAIR)
    is_even = lax.rem(lax.axis_index("lat"), 2) == 0
    for lanes in spans(columns, 3 * LANES):
        speed = [speed_ref[:, j, lanes] for j in range(row_count)]
        near_ref[tracer_count * levels :, lanes] = speed[0]
        far_ref[tracer_count * levels :, lanes] = speed[0]
        for which, (inner_ref, outer_ref) in enumerate(
            [(mine_ref, edge_mine_ref), (send_ref, edge_send_ref)]
        ):
            for i in range(share):
                t = lax.rem(core + which, PAIR) * share + i
                x = [cells_ref[t, :, j, lanes] for j in range(row_count)]
                place = pl.ds(pl.multiple_of(t * levels, levels), levels)
                near_ref[place, lanes] = jnp.where(is_even, x[-1], x[0])
                far_ref[place, lanes] = jnp.where(is_even, x[0], x[-1])
                flux = [flux_of(speed[j], x[j - 1], x[j]) for j in range(1, row_count)]
                for j in range(1, row_count - 1):
                    inner_ref[i, j - 1, :, lanes] = x[j] + flux[j - 1] - flux[j]
                outer_ref[i, 0, :, lanes] = x[0] - flux[0]
                outer_ref[i, 1, :, lanes] = x[-1] + flux[-1]


def edge_kernel(
    near_out_ref, far_out_ref, near_first_ref, near_later_ref, far_first_ref, far_later_ref,
    edge_mine_ref, edge_send_ref, mine_ref, send_ref,
):
    share, _, levels, columns = edge_mine_ref.shape
    total = share * PAIR * levels
    core = lax.rem(lax.axis_index("lon"), PAIR)
    lat = lax.axis_index("lat")
    is_even = lax.rem(lat, 2) == 0
    cap = is_cap(lat)
    for lanes in spans(columns, 3 * LANES):

        def received(place):
            near = jnp.where(cap, near_first_ref[place, lanes], near_later_ref[place, lanes])
            far = jnp.where(cap, far_first_ref[place, lanes], far_later_ref[place, lanes])
            return jnp.where(is_even, far, near), jnp.where(is_even, near, far)

        speed_below = near_out_ref[total:, lanes]
        speed_above = received(slice(total, total + levels))[1]
        speed_below = jnp.where(lat > 0, speed_below, 0.0)
        speed_above = jnp.where(lat < lax.axis_size("lat") - 1, speed_above, 0.0)
        for which, (partial_ref, out_ref) in enumerate(
            [(edge_mine_ref, mine_ref), (edge_send_ref, send_ref)]
        ):
            for i in range(share):
                t = lax.rem(core + which, PAIR) * share + i
                place = pl.ds(pl.multiple_of(t * levels, levels), levels)
                below, above = received(place)
                near_own, far_own = near_out_ref[place, lanes], far_out_ref[place, lanes]
                south = jnp.where(is_even, far_own, near_own)
                north = jnp.where(is_even, near_own, far_own)
                out_ref[i, 0, :, lanes] = partial_ref[i, 0, :, lanes] + flux_of(speed_below, below, south)
                out_ref[i, 1, :, lanes] = partial_ref[i, 1, :, lanes] - flux_of(speed_above, north, above)


def forward_kernel(mine_ref, theirs_ref, phase_ref, high_ref, low_ref, message_ref, held_ref, stack_ref):
    share, number, levels, columns = mine_ref.shape
    piece = columns * PAIR // HALF
    padded = stack_ref.shape[1]
    modes = high_ref.shape[1] // 2
    group = levels * 2 * (HALF + 1)
    core = lax.rem(lax.axis_index("lon"), PAIR)
    count = share * number
    for n in range(count):
        i, j = divmod(n, number)
        held_ref[core, n, :, :columns] = mine_ref[i, j]
        held_ref[1 - core, n, :, :columns] = theirs_ref[i, j]
        for pos in range(PAIR):
            held_ref[pos, n, :, columns:] = jnp.zeros((levels, held_ref.shape[3] - columns), jnp.float32)
        message_ref[n, :, 2 * MODES :] = held_ref[PAIR - 1, n, :, columns - LANES : columns]

    @pl.when(is_cap(lax.axis_index("lat")))
    def _():
        for n in range(count):
            for tile in range(0, padded, LANES):
                lanes = slice(tile, tile + LANES)
                x = []
                for u in range(HALF):
                    pos, start = divmod(u * piece, columns)
                    x.append(held_ref[pos, n, :, start + tile : start + tile + LANES])
                for r, (re, im) in enumerate(half_dft(x)):
                    base = n * group + 2 * r * levels
                    if r == 0:
                        im = jnp.zeros_like(re)
                    else:
                        c, s = phase_ref[2 * r : 2 * r + 1, lanes], phase_ref[2 * r + 1 : 2 * r + 2, lanes]
                        if im is None:
                            re, im = re * c, -(re * s)
                        else:
                            re, im = re * c + im * s, im * c - re * s
                    stack_ref[base : base + levels, lanes] = re
                    stack_ref[base + levels : base + 2 * levels, lanes] = im
        coeffs = product(stack_ref[...], high_ref[...], low_ref[...])
        upper = lax.broadcasted_iota(jnp.int32, (levels, modes), 1) >= modes // 2
        for n in range(count):
            first = None
            for r in [0, HALF] + list(range(1, HALF)):
                base = n * group + 2 * r * levels
                re, im = coeffs[base : base + levels], coeffs[base + levels : base + 2 * levels]
                x_re = re[:, :modes] + im[:, modes:]
                x_im = im[:, :modes] - re[:, modes:]
                if r == 0:
                    first = x_re, x_im
                    continue
                slot = r
                if r == HALF:
                    x_re = jnp.where(upper, first[0], pltpu.roll(x_re, modes // 2, 1))
                    x_im = jnp.where(upper, first[1], pltpu.roll(x_im, modes // 2, 1))
                    slot = 0
                message_ref[n, :, 2 * slot * modes : (2 * slot + 1) * modes] = x_re
                message_ref[n, :, (2 * slot + 1) * modes : (2 * slot + 2) * modes] = x_im


def row_vector(ref, row, levels):
    level = lax.broadcasted_iota(jnp.int32, (levels, LANES), 0)
    out = jnp.full((levels, LANES), ref[row, 0])
    for i in range(1, levels):
        out = jnp.where(level == i, ref[row, i], out)
    return out


def displaced(block, distance, share):
    repeat = block.shape[1] // LANES
    distances = jnp.concatenate([distance] * repeat, axis=1)
    shares = jnp.concatenate([share] * repeat, axis=1)
    for bit in range(SMAX.bit_length()):
        pushed = pltpu.roll(block, 1 << bit, 1)
        block = jnp.where((distances >> bit) & 1 == 1, pushed, block)
    return (1.0 - shares) * block + shares * pltpu.roll(block, 1, 1)


def wave_angle(steps, lon_cells):
    steps = lax.rem(steps, lon_cells)
    return steps.astype(jnp.float32) * (2.0 * math.pi / lon_cells)


def shift_kernel(
    rows, columns, shift_ref, fraction_ref, cutoff_ref, wave_ref, held_ref, moved_ref, gain_ref
):
    _, count, levels, padded = held_ref.shape
    number = len(rows)
    lon_cells = columns * PAIR * PAIR
    modes = gain_ref.shape[3]
    lat = lax.axis_index("lat")
    for j, row in enumerate(rows):
        distance = row_vector(shift_ref, row, levels)
        share = row_vector(fraction_ref, row, levels)
        for n in range(j, count, number):
            for pos in range(PAIR):
                for lanes in spans(padded, SPAN):
                    if lanes.start:
                        block = held_ref[pos, n, :, lanes.start - LANES : lanes.stop]
                    else:
                        tail = held_ref[PAIR - 1 - pos, n, :, columns - LANES : columns]
                        block = jnp.concatenate([tail, held_ref[pos, n, :, lanes]], axis=1)
                    moved_ref[n, pos, :, lanes] = displaced(block, distance, share)[:, LANES:]

    @pl.when(is_cap(lat))
    def _():
        lane = lax.broadcasted_iota(jnp.int32, (levels, modes), 1)
        mode = lane - modes // 2
        for j, row in enumerate(rows):
            distance = row_vector(shift_ref, row, levels)
            share = row_vector(fraction_ref, row, levels)
            limit = cutoff_ref[lat * shift_ref.shape[0] + row]
            wide = wave_angle(RADIX * mode * distance, lon_cells)
            wide_re, wide_im = jnp.cos(wide), -jnp.sin(wide)
            fine = wave_angle(lane * distance, lon_cells)
            fine_re, fine_im = jnp.cos(fine), -jnp.sin(fine)
            for r in range(HALF + 1):
                wavenumber = RADIX * mode + r
                kept = jnp.abs(wavenumber) <= limit
                if r in (0, HALF):
                    kept = kept & (wavenumber >= 0)
                weight = jnp.full((levels, modes), (1.0 if r % 2 == 0 and r not in (0, HALF) else 2.0) / lon_cells)
                if r == 0:
                    weight = jnp.where(wavenumber == 0, 1.0 / lon_cells, weight)
                weight = jnp.where(kept, weight, 0.0)
                mix_re = (1.0 - share) + share * wave_ref[2 * r : 2 * r + 1]
                mix_im = -share * wave_ref[2 * r + 1 : 2 * r + 2]
                turn_re, turn_im = fine_re[:, r : r + 1], fine_im[:, r : r + 1]
                re, im = wide_re * turn_re - wide_im * turn_im, wide_re * turn_im + wide_im * turn_re
                gain_ref[j, 2 * r] = (re * mix_re - im * mix_im) * weight
                gain_ref[j, 2 * r + 1] = (re * mix_im + im * mix_re) * weight


def inverse_kernel(
    rows, columns, shift_ref, fraction_ref, damping_ref, phase_ref, high_ref, low_ref,
    held_ref, moved_ref, gain_ref, own_ref, other_ref, mine_ref, send_ref,
    stack_ref, back_ref, pair_ref,
):
    _, count, levels, _ = held_ref.shape
    number = len(rows)
    piece = columns * PAIR // HALF
    padded = stack_ref.shape[1]
    modes = gain_ref.shape[3]
    group = levels * 2 * (HALF + 1)
    lat = lax.axis_index("lat")
    core = lax.rem(lax.axis_index("lon"), PAIR)
    cap = is_cap(lat)
    for j, row in enumerate(rows):
        distance = row_vector(shift_ref, row, levels)
        share = row_vector(fraction_ref, row, levels)
        for n in range(j, count, number):
            rim = other_ref[n, :, 2 * MODES :]
            block = jnp.concatenate([rim, held_ref[0, n, :, :LANES]], axis=1)
            moved_ref[n, 0, :, :LANES] = displaced(block, distance, share)[:, LANES:]

    @pl.when(jnp.logical_not(cap))
    def _():
        for n in range(count):
            i, j = divmod(n, number)
            mine_ref[i, j] = moved_ref[n, core, :, :columns]
            send_ref[i, j] = moved_ref[n, 1 - core, :, :columns]

    @pl.when(cap)
    def _():
        for n in range(count):
            j = n % number
            for r in range(HALF + 1):
                slot = r % HALF
                ours, theirs = (
                    [ref[n, :, (2 * slot + part) * modes : (2 * slot + part + 1) * modes] for part in range(2)]
                    for ref in (own_ref, other_ref)
                )
                if r % 2:
                    re, im = ours[0] - theirs[0], ours[1] - theirs[1]
                else:
                    re, im = ours[0] + theirs[0], ours[1] + theirs[1]
                if r == HALF:
                    re, im = pltpu.roll(re, modes // 2, 1), pltpu.roll(im, modes // 2, 1)
                g_re, g_im = gain_ref[j, 2 * r], gain_ref[j, 2 * r + 1]
                re, im = re * g_re - im * g_im, re * g_im + im * g_re
                base = n * group + 2 * r * levels
                back_ref[base : base + levels, :modes] = re
                back_ref[base : base + levels, modes:] = -im
                back_ref[base + levels : base + 2 * levels, :modes] = im
                back_ref[base + levels : base + 2 * levels, modes:] = re
        stack_ref[...] = product(back_ref[...], high_ref[...], low_ref[...])
        for n in range(count):
            i, j = divmod(n, number)
            keep = damping_ref[lat * shift_ref.shape[0] + rows[j]]
            for tile in range(0, padded, LANES):
                lanes = slice(tile, tile + LANES)
                spectrum = []
                for r in range(HALF + 1):
                    base = n * group + 2 * r * levels
                    re = stack_ref[base : base + levels, lanes]
                    im = stack_ref[base + levels : base + 2 * levels, lanes]
                    if r > 0:
                        c, s = phase_ref[2 * r : 2 * r + 1, lanes], phase_ref[2 * r + 1 : 2 * r + 2, lanes]
                        re, im = re * c - im * s, re * s + im * c
                    spectrum.append((re, im))
                width = min(LANES, piece - tile)
                for u, value in enumerate(half_inverse(spectrum)):
                    pos, start = divmod(u * piece, columns)
                    start += tile
                    shifted = moved_ref[n, pos, :, start : start + LANES]
                    result = keep * shifted + (1.0 - keep) * value
                    pair_ref[pos, n, :, start : start + width] = result[:, :width]
        for n in range(count):
            i, j = divmod(n, number)
            mine_ref[i, j] = pair_ref[core, n, :, :columns]
            send_ref[i, j] = pair_ref[1 - core, n, :, :columns]


def end_kernel(inner_ref, inner_back_ref, outer_ref, outer_back_ref, out_ref):
    tracer_count, levels, row_count, columns = out_ref.shape
    share = tracer_count // PAIR
    core = lax.rem(lax.axis_index("lon"), PAIR)
    for which, (inner, outer) in enumerate([(inner_ref, outer_ref), (inner_back_ref, outer_back_ref)]):
        for i in range(share):
            t = lax.rem(core + which, PAIR) * share + i
            for j in range(row_count):
                if j in (0, row_count - 1):
                    out_ref[t, :, j, :] = outer[i, min(j, 1)]
                else:
                    out_ref[t, :, j, :] = inner[i, j - 1]


def filter_tables(lon_cells):
    piece = lon_cells // RADIX
    padded = -(-piece // LANES) * LANES
    modes = 2 * MODES // RADIX
    q = np.arange(modes) - modes // 2
    angle = 2 * np.pi * (np.arange(piece)[:, None] * q[None, :] % piece) / piece
    table = np.zeros((padded, 2 * modes))
    table[:piece, :modes] = np.cos(angle)
    table[:piece, modes:] = np.sin(angle)
    high = table.astype(jnp.bfloat16)
    low = (table - high.astype(np.float64)).astype(jnp.bfloat16)
    r = np.arange(HALF + 1)[:, None]

    def waves(steps):
        angle = 2 * np.pi * steps / lon_cells
        pairs = np.stack([np.cos(angle), np.sin(angle)], axis=1)
        return pairs.reshape(-1, steps.shape[1]).astype(np.float32)

    phase = waves(r * np.arange(padded)[None, :])
    wave = waves(RADIX * q[None, :] + r)
    return phase, wave, high, low, np.ascontiguousarray(high.T), np.ascontiguousarray(low.T)


def call(kernel, outs, operands, scratch=(), flops=0):
    vmem = pl.BlockSpec(memory_space=pltpu.VMEM)
    smem = pl.BlockSpec(memory_space=pltpu.SMEM)
    scalars = [v for v, place in operands if place]
    specs = [smem if place else vmem for v, place in operands]
    shapes = [jax.ShapeDtypeStruct(shape, jnp.float32) for shape in outs]
    size = sum(4 * math.prod(shape) for shape in outs)
    return pl.pallas_call(
        kernel,
        out_shape=shapes,
        in_specs=specs,
        out_specs=[vmem] * len(shapes),
        scratch_shapes=[pltpu.VMEM(shape, jnp.float32) for shape in scratch],
        compiler_params=pltpu.CompilerParams(vmem_limit_bytes=24 << 20),
        cost_estimate=pl.CostEstimate(flops=flops, bytes_accessed=2 * size, transcendentals=0),
    )(*[v for v, place in operands])


def permuted(value, axis, pairs):
    return lax.ppermute(value, axis, pairs)


def body(tracers, merid_courant, zonal_shift, zonal_fraction, cutoff, damping):
    tracer_count, level_count, row_count, column_count = tracers.shape
    lat_count = lax.axis_size("lat")
    lon_count = lax.axis_size("lon")
    assert lon_count == PAIR * PAIR and tracer_count % PAIR == 0 and row_count > 2
    share = tracer_count // PAIR
    top = row_count - 1
    lon_cells = column_count * lon_count
    phase, wave, fwd_high, fwd_low, inv_high, inv_low = [jnp.asarray(t) for t in filter_tables(lon_cells)]
    padded, double = fwd_high.shape
    width = -(-column_count // LANES) * LANES
    assert column_count - lon_cells // RADIX + padded <= width
    group = level_count * 2 * (HALF + 1)
    shift_rows, fraction_rows = zonal_shift.T, zonal_fraction.T

    swap_core = lambda v: permuted(v, "lon", [(p, p ^ 1) for p in range(lon_count)])
    swap_half = lambda v: permuted(v, "lon", [(p, p ^ 2) for p in range(lon_count)])
    caps = [b for b in range(lat_count) if b < lat_count // 4 or b >= lat_count - lat_count // 4]

    edge_shape = ((tracer_count + 1) * level_count, column_count)
    inner_shape = (share, row_count - 2, level_count, column_count)
    outer_shape = (share, 2, level_count, column_count)
    near_out, far_out, inner_mine, inner_send, outer_mine, outer_send = call(
        begin_kernel,
        [edge_shape] * 2 + [inner_shape] * 2 + [outer_shape] * 2,
        [(tracers, 0), (merid_courant, 0)],
    )
    inner_theirs = swap_core(inner_send)

    def halo(value, first, to_caps):
        pairs = []
        for b in range(first, lat_count - 1, 2):
            pairs += [(s, d) for s, d in ((b, b + 1), (b + 1, b)) if (d in caps) == to_caps]
        return permuted(value, "lat", pairs)

    near_first, far_first = halo(near_out, 0, True), halo(far_out, 1, True)

    def forward(mine, theirs):
        count = mine.shape[0] * mine.shape[1]
        message, held = call(
            forward_kernel,
            [(count, level_count, 2 * MODES + LANES), (PAIR, count, level_count, width)],
            [(v, 0) for v in (mine, theirs, phase, fwd_high, fwd_low)],
            [(count * group, padded)],
            2 * 3 * count * group * padded * double,
        )
        return message, held

    def shifted(rows, held):
        count = held.shape[1]
        return call(
            functools.partial(shift_kernel, rows, column_count),
            [(count, PAIR, level_count, width), (len(rows), 2 * (HALF + 1), level_count, double // 2)],
            [(shift_rows, 1), (fraction_rows, 1), (cutoff, 1), (wave, 0), (held, 0)],
        )

    def inverse(rows, held, moved, gain, own, other):
        count = held.shape[1]
        shape = (share, len(rows), level_count, column_count)
        return call(
            functools.partial(inverse_kernel, rows, column_count),
            [shape, shape],
            [(shift_rows, 1), (fraction_rows, 1), (damping, 1)]
            + [(v, 0) for v in (phase, inv_high, inv_low, held, moved, gain, own, other)],
            [(count * group, padded), (count * group, double), (PAIR, count, level_count, width)],
            2 * 3 * count * group * padded * double,
        )

    inner_rows, outer_rows = list(range(1, top)), [0, top]
    inner_own, inner_held = forward(inner_mine, inner_theirs)
    inner_other = swap_half(inner_own)
    near_later, far_later = halo(near_out, 0, False), halo(far_out, 1, False)
    inner_moved, inner_gain = shifted(inner_rows, inner_held)

    outer_mine, outer_send = call(
        edge_kernel,
        [outer_shape] * 2,
        [(v, 0) for v in (near_out, far_out, near_first, near_later, far_first, far_later, outer_mine, outer_send)],
    )
    outer_theirs = swap_core(outer_send)
    outer_own, outer_held = forward(outer_mine, outer_theirs)
    outer_other = swap_half(outer_own)
    outer_moved, outer_gain = shifted(outer_rows, outer_held)

    inner_mine, inner_send = inverse(
        inner_rows, inner_held, inner_moved, inner_gain, inner_own, inner_other
    )
    inner_back = swap_core(inner_send)
    outer_mine, outer_send = inverse(
        outer_rows, outer_held, outer_moved, outer_gain, outer_own, outer_other
    )
    outer_back = swap_core(outer_send)
    (result,) = call(
        end_kernel,
        [tracers.shape],
        [(v, 0) for v in (inner_mine, inner_back, outer_mine, outer_back)],
    )
    return result


def solution(mesh):
    placed = (
        P(None, None, "lat", "lon"),
        P(None, "lat", "lon"),
        P(None, "lat"),
        P(None, "lat"),
        P(),
        P(),
    )
    return jax.shard_map(
        body, mesh=mesh, in_specs=placed, out_specs=P(None, None, "lat", "lon"), check_vma=False
    )
```

time: 56.3 us -> 41.8 us (0.74)
  the two profiles are of different devices: /device:TPU:3 before, /device:TPU:25 now
where the time goes in v3:
time: 41.8 us; the launch traced here: 41.5 us
  Pallas kernels  17.3 us (41%)
  starting transfers between devices  16.8 us (40%)
  waiting for transfers between devices  3.82 us (9%)
  local copies, waits for them, and re-layouts  3.41 us (8%)
    pallas_call x9, Pallas kernels, call(): pl.pallas_call(kernel, out_shape=shapes, in_specs=specs, out_specs=[vmem]...  17.3 us
    ppermute x10, starting transfers between devices, permuted(): return lax.ppermute(value, axis, pairs)  16.8 us
    ppermute x10, waiting for transfers between devices, permuted(): return lax.ppermute(value, axis, pairs)  3.82 us
    unnamed x24, local copies, waits for them, and re-layouts  3.41 us
  transfers between devices with their start and end apart: 10, of which 3 were waited for; matrix products, arithmetic and copies ran while one was open for 0% of the time, Pallas kernels for 38%

profile of v3, /device:TPU:25, one launch (start us, length us, event | category | flops | bytes accessed | tf_op | source)
XLA Modules:
  0.0 41.5 jit_solution(17700882747097531976)
XLA Ops:
  0.0 0.0 copy-start.2
  0.0 1.1 %copy-done.2 = f32[4,8,4,1440]{3,2,1,0:T(4,128)S(1)} copy-done((f32[4,8,4,1440]{3,2,1,0:T(4,128)S(1)}, f32[4,8,4,1440]{3,2,1,0:T(4,128)}, u32[]{:S(2)}) %copy-start.2) | copy-done | bytes 737304
  1.1 0.0 copy-start.3
  1.1 0.9 %copy-done.3 = f32[8,4,1440]{2,1,0:T(4,128)S(1)} copy-done((f32[8,4,1440]{2,1,0:T(4,128)S(1)}, f32[8,4,1440]{2,1,0:T(4,128)}, u32[]{:S(2)}) %copy-start.3) | copy-done | bytes 184344
  2.1 0.6 %shard_map.118 = (f32[40,1440]{1,0:T(8,128)S(1)}, f32[40,1440]{1,0:T(8,128)S(1)}, f32[2,2,8,1440]{3,2,1,0:T(8,128)S(1)}, f32[2,2,8,1440]{3,2,1,0:T(8,128)S(1)}, ...) custom-call(f32[4,8,4,1440]{3,2,1,0:T(4,128)S(1)} %copy-done.2, f32[8,4,1440]{2,1,0:T(4,128)S(1)} %copy-done.3), custom_call_target="tpu_custom_call" | custom-call | bytes 2396160 | tf_op jit(solution)/shard_map/pallas_call | solution.py:449
  2.7 3.1 %collective-permute-start.3 = (f32[40,1440]{1,0:T(8,128)S(1)}, f32[40,1440]{1,0:T(8,128)S(1)}, u32[]{:S(2)}, u32[]{:S(2)}) collective-permute-start(f32[40,1440]{1,0:T(8,128)S(1)} %get-tuple-element.33.near_out_ref), channel_id=1, source_target_pairs={{0,4},{4,0},{24,28},{28,24},{1,5},{5,1},{25,29},{29,25},{2,6},{6,2... | collective-permute-start | bytes 691208 | tf_op jit(solution)/shard_map/ppermute | solution.py:461
  5.8 0.7 %collective-permute-start.4 = (f32[40,1440]{1,0:T(8,128)S(1)}, f32[40,1440]{1,0:T(8,128)S(1)}, u32[]{:S(2)}, u32[]{:S(2)}) collective-permute-start(f32[40,1440]{1,0:T(8,128)S(1)} %get-tuple-element.33.near_out_ref), channel_id=1, source_target_pairs={{8,12},{12,8},{16,20},{20,16},{9,13},{13,9},{17,21},{21,17},{10,14... | collective-permute-start | bytes 691208 | tf_op jit(solution)/shard_map/ppermute | solution.py:461
  6.5 1.3 %collective-permute-start.5 = (f32[40,1440]{1,0:T(8,128)S(1)}, f32[40,1440]{1,0:T(8,128)S(1)}, u32[]{:S(2)}, u32[]{:S(2)}) collective-permute-start(f32[40,1440]{1,0:T(8,128)S(1)} %get-tuple-element.34.far_out_ref), channel_id=1, source_target_pairs={{8,4},{20,24},{9,5},{21,25},{10,6},{22,26},{11,7},{23,27}} | collective-permute-start | bytes 691208 | tf_op jit(solution)/shard_map/ppermute | solution.py:461
  7.8 4.9 %collective-permute-start.6 = (f32[40,1440]{1,0:T(8,128)S(1)}, f32[40,1440]{1,0:T(8,128)S(1)}, u32[]{:S(2)}, u32[]{:S(2)}) collective-permute-start(f32[40,1440]{1,0:T(8,128)S(1)} %get-tuple-element.34.far_out_ref), channel_id=1, source_target_pairs={{4,8},{12,16},{16,12},{24,20},{5,9},{13,17},{17,13},{25,21},{6,10}... | collective-permute-start | bytes 691208 | tf_op jit(solution)/shard_map/ppermute | solution.py:461
  12.7 1.6 %collective-permute-start = (f32[2,2,8,1440]{3,2,1,0:T(8,128)S(1)}, f32[2,2,8,1440]{3,2,1,0:T(8,128)S(1)}, u32[]{:S(2)}, u32[]{:S(2)}) collective-permute-start(f32[2,2,8,1440]{3,2,1,0:T(8,128)S(1)} %get-tuple-element.26), channel_id=1, source_target_pairs={{0,1},{1,0},{2,3},{3,2},{4,5},{5,4},{6,7},{7,6},{8,9},{9,8},{10,11... | collective-permute-start | bytes 552968 | tf_op jit(solution)/shard_map/ppermute | solution.py:461
  14.3 0.0 collective-permute-done.3.near_first_ref
  14.3 0.0 collective-permute-done.4.near_later_ref
  14.3 1.6 %collective-permute-done.5.far_first_ref = f32[40,1440]{1,0:T(8,128)S(1)} collective-permute-done((f32[40,1440]{1,0:T(8,128)S(1)}, f32[40,1440]{1,0:T(8,128)S(1)}, u32[]{:S(2)}, u32[]{:S(2)}) %collective-permute-start.5) | collective-permute-done | bytes 230432 | tf_op jit(solution)/shard_map/ppermute | solution.py:461
  15.9 0.8 %collective-permute-done.6.far_later_ref = f32[40,1440]{1,0:T(8,128)S(1)} collective-permute-done((f32[40,1440]{1,0:T(8,128)S(1)}, f32[40,1440]{1,0:T(8,128)S(1)}, u32[]{:S(2)}, u32[]{:S(2)}) %collective-permute-start.6) | collective-permute-done | bytes 230432 | tf_op jit(solution)/shard_map/ppermute | solution.py:461
  16.7 0.0 copy-start.4
  16.7 0.0 copy-start.10
  16.7 0.1 shard_map.122
  16.8 2.2 %collective-permute-start.7 = (f32[2,2,8,1440]{3,2,1,0:T(8,128)S(1)}, f32[2,2,8,1440]{3,2,1,0:T(8,128)S(1)}, u32[]{:S(2)}, u32[]{:S(2)}) collective-permute-start(f32[2,2,8,1440]{3,2,1,0:T(8,128)S(1)} %get-tuple-element.38), channel_id=1, source_target_pairs={{0,1},{1,0},{2,3},{3,2},{4,5},{5,4},{6,7},{7,6},{8,9},{9,8},{10,11... | collective-permute-start | bytes 552968 | tf_op jit(solution)/shard_map/ppermute | solution.py:461
  19.0 0.0 collective-permute-done.theirs_ref
  19.0 0.0 copy-done.4
  19.0 0.0 copy-done.10
  19.1 0.0 copy-done.11
  19.1 1.5 %shard_map.119 = (f32[4,8,2176]{2,1,0:T(8,128)S(1)}, f32[2,4,8,1536]{3,2,1,0:T(8,128)S(1)}) custom-call(f32[2,2,8,1440]{3,2,1,0:T(8,128)S(1)} %get-tuple-element.25.mine_ref, f32[2,2,8,1440]{3,2,1,0:T(8,128)S(1)} %collective-permute-done.theirs_ref, f32[18,384]{1,0:T(8,128)S(1)} %copy-done.4, bf16[384,256]{1,0:T(8,128)(2,1)S(1)} %copy-done.10, ...), custom_call_target="tpu_custom_call" | custom-call | flops 339738624 | bytes 1343488 | tf_op jit(solution)/shard_map/pallas_call | solution.py:449
  20.5 1.3 %collective-permute-start.1 = (f32[4,8,2176]{2,1,0:T(8,128)S(1)}, f32[4,8,2176]{2,1,0:T(8,128)S(1)}, u32[]{:S(2)}, u32[]{:S(2)}) collective-permute-start(f32[4,8,2176]{2,1,0:T(8,128)S(1)} %get-tuple-element.30.own_ref), channel_id=1, source_target_pairs={{0,2},{1,3},{2,0},{3,1},{4,6},{5,7},{6,4},{7,5},{8,10},{9,11},{10,... | collective-permute-start | bytes 835592 | tf_op jit(solution)/shard_map/ppermute | solution.py:461
  21.8 0.0 collective-permute-done.7.theirs_ref
  21.8 1.5 %shard_map.123 = (f32[4,8,2176]{2,1,0:T(8,128)S(1)}, f32[2,4,8,1536]{3,2,1,0:T(8,128)S(1)}) custom-call(f32[2,2,8,1440]{3,2,1,0:T(8,128)S(1)} %get-tuple-element.37.mine_ref, f32[2,2,8,1440]{3,2,1,0:T(8,128)S(1)} %collective-permute-done.7.theirs_ref, f32[18,384]{1,0:T(8,128)S(1)} %copy-done.4, bf16[384,256]{1,0:T(8,128)(2,1)S(1)} %copy-done.10, ...), custom_call_target="tpu_custom_call" | custom-call | flops 339738624 | bytes 1343488 | tf_op jit(solution)/shard_map/pallas_call | solution.py:449
  23.2 0.2 collective-permute-start.8
  23.5 0.0 copy-done.5
  23.5 0.7 %copy-done.7 = f32[8,4]{0,1:T(4,128)S(1)} copy-done((f32[8,4]{0,1:T(4,128)S(1)}, f32[8,4]{0,1:T(4,128)}, u32[]{:S(2)}) %copy-start.7) | copy-done | bytes 152
  24.1 0.0 copy-done.6
  24.2 0.0 copy-done.8
  24.2 4.3 %shard_map.120 = (f32[4,2,8,1536]{3,2,1,0:T(8,128)S(1)}, f32[2,18,8,128]{3,2,1,0:T(8,128)S(1)}) custom-call(s32[4,8]{1,0:T(4,128)S(1)} %bitcast.2, f32[4,8]{1,0:T(4,128)S(1)} %bitcast.6, s32[32]{0:T(128)S(1)} %copy-done.8, f32[18,128]{1,0:T(8,128)S(1)} %copy-done.5, f32[2,4,8,1536]{3,2,1,0:T(8,128)S(1)} %get-tuple-element.27.held_ref), custom_call_target="tpu_custom_call" | custom-call | bytes 1081344 | tf_op jit(solution)/shard_map/pallas_call | solution.py:449
  28.4 0.0 copy-start
  28.4 0.0 copy-start.1
  28.5 4.3 %shard_map.124 = (f32[4,2,8,1536]{3,2,1,0:T(8,128)S(1)}, f32[2,18,8,128]{3,2,1,0:T(8,128)S(1)}) custom-call(s32[4,8]{1,0:T(4,128)S(1)} %bitcast.3, f32[4,8]{1,0:T(4,128)S(1)} %bitcast.7, s32[32]{0:T(128)S(1)} %copy-done.8, f32[18,128]{1,0:T(8,128)S(1)} %copy-done.5, f32[2,4,8,1536]{3,2,1,0:T(8,128)S(1)} %get-tuple-element.39.held_ref), custom_call_target="tpu_custom_call" | custom-call | bytes 1081344 | tf_op jit(solution)/shard_map/pallas_call | solution.py:449
  32.7 0.0 collective-permute-done.1.other_ref
  32.7 0.0 copy-start.9
  32.7 0.0 copy-done
  32.7 0.0 copy-done.1
  32.8 0.6 %copy-done.9 = f32[32]{0:T(128)S(1)} copy-done((f32[32]{0:T(128)S(1)}, f32[32]{0:T(128)}, u32[]{:S(2)}) %copy-start.9) | copy-done | bytes 152
  33.4 2.1 %shard_map.121 = (f32[2,2,8,1440]{3,2,1,0:T(8,128)S(1)}, f32[2,2,8,1440]{3,2,1,0:T(8,128)S(1)}) custom-call(s32[4,8]{1,0:T(4,128)S(1)} %bitcast.4, f32[4,8]{1,0:T(4,128)S(1)} %bitcast.8, f32[32]{0:T(128)S(1)} %copy-done.9, f32[18,384]{1,0:T(8,128)S(1)} %copy-done.4, bf16[256,384]{1,0:T(8,128)(2,1)S(1)} %copy-done, bf16[256,384]{1,0:T(8,128)(2,1)S(1)} %copy-done.1, ...), custom_call_target="tpu_custom_call" | custom-call | flops 339738624 | bytes 737280 | tf_op jit(solution)/shard_map/pallas_call | solution.py:449
  35.4 1.4 %collective-permute-start.2 = (f32[2,2,8,1440]{3,2,1,0:T(8,128)S(1)}, f32[2,2,8,1440]{3,2,1,0:T(8,128)S(1)}, u32[]{:S(2)}, u32[]{:S(2)}) collective-permute-start(f32[2,2,8,1440]{3,2,1,0:T(8,128)S(1)} %get-tuple-element.32), channel_id=1, source_target_pairs={{0,1},{1,0},{2,3},{3,2},{4,5},{5,4},{6,7},{7,6},{8,9},{9,8},{10,11... | collective-permute-start | bytes 552968 | tf_op jit(solution)/shard_map/ppermute | solution.py:461
  36.9 0.0 collective-permute-done.8.other_ref
  36.9 2.1 %shard_map.125 = (f32[2,2,8,1440]{3,2,1,0:T(8,128)S(1)}, f32[2,2,8,1440]{3,2,1,0:T(8,128)S(1)}) custom-call(s32[4,8]{1,0:T(4,128)S(1)} %bitcast.5, f32[4,8]{1,0:T(4,128)S(1)} %bitcast.9, f32[32]{0:T(128)S(1)} %copy-done.9, f32[18,384]{1,0:T(8,128)S(1)} %copy-done.4, bf16[256,384]{1,0:T(8,128)(2,1)S(1)} %copy-done, bf16[256,384]{1,0:T(8,128)(2,1)S(1)} %copy-done.1, ...), custom_call_target="tpu_custom_call" | custom-call | flops 339738624 | bytes 737280 | tf_op jit(solution)/shard_map/pallas_call | solution.py:449
  39.0 0.1 collective-permute-start.9
  39.0 0.0 collective-permute-done.2.inner_back_ref
  39.0 1.4 %collective-permute-done.9.outer_back_ref = f32[2,2,8,1440]{3,2,1,0:T(8,128)S(1)} collective-permute-done((f32[2,2,8,1440]{3,2,1,0:T(8,128)S(1)}, f32[2,2,8,1440]{3,2,1,0:T(8,128)S(1)}, u32[]{:S(2)}, u32[]{:S(2)}) %collective-permute-start.9) | collective-permute-done | bytes 184352 | tf_op jit(solution)/shard_map/ppermute | solution.py:461
  40.5 1.0 %shard_map.126 = f32[4,8,4,1440]{3,2,1,0:T(4,128)} custom-call(f32[2,2,8,1440]{3,2,1,0:T(8,128)S(1)} %get-tuple-element.31.inner_ref, f32[2,2,8,1440]{3,2,1,0:T(8,128)S(1)} %collective-permute-done.2.inner_back_ref, f32[2,2,8,1440]{3,2,1,0:T(8,128)S(1)} %get-tuple-element.43.outer_ref, f32[2,2,8,1440]{3,2,1,0:T(8,128)S(1)} %collective-permute-done.9.outer_back_ref), custom_call_target="tpu_custom_call" | custom-call | bytes 1474560 | tf_op jit(solution)/shard_map/pallas_call | solution.py:449
  (5 shorter events, 0.0 us)
Async XLA Ops:
  0.0 1.1 %copy-start.2 = (f32[4,8,4,1440]{3,2,1,0:T(4,128)S(1)}, f32[4,8,4,1440]{3,2,1,0:T(4,128)}, u32[]{:S(2)}) copy-start(f32[4,8,4,1440]{3,2,1,0:T(4,128)} %cells_ref.1) | copy-start | bytes 2211844
  1.1 0.9 %copy-start.3 = (f32[8,4,1440]{2,1,0:T(4,128)S(1)}, f32[8,4,1440]{2,1,0:T(4,128)}, u32[]{:S(2)}) copy-start(f32[8,4,1440]{2,1,0:T(4,128)} %speed_ref.1) | copy-start | bytes 552964
  2.7 11.6 %collective-permute-start.3 = (f32[40,1440]{1,0:T(8,128)S(1)}, f32[40,1440]{1,0:T(8,128)S(1)}, u32[]{:S(2)}, u32[]{:S(2)}) collective-permute-start(f32[40,1440]{1,0:T(8,128)S(1)} %get-tuple-element.33.near_out_ref), channel_id=1, source_target_pairs={{0,4},{4,0},{24,28},{28,24},{1,5},{5,1},{25,29},{29,25},{2,6},{6,2... | collective-permute-start | bytes 691208 | tf_op jit(solution)/shard_map/ppermute | solution.py:461
  5.8 8.5 %collective-permute-start.4 = (f32[40,1440]{1,0:T(8,128)S(1)}, f32[40,1440]{1,0:T(8,128)S(1)}, u32[]{:S(2)}, u32[]{:S(2)}) collective-permute-start(f32[40,1440]{1,0:T(8,128)S(1)} %get-tuple-element.33.near_out_ref), channel_id=1, source_target_pairs={{8,12},{12,8},{16,20},{20,16},{9,13},{13,9},{17,21},{21,17},{10,14... | collective-permute-start | bytes 691208 | tf_op jit(solution)/shard_map/ppermute | solution.py:461
  6.5 9.4 %collective-permute-start.5 = (f32[40,1440]{1,0:T(8,128)S(1)}, f32[40,1440]{1,0:T(8,128)S(1)}, u32[]{:S(2)}, u32[]{:S(2)}) collective-permute-start(f32[40,1440]{1,0:T(8,128)S(1)} %get-tuple-element.34.far_out_ref), channel_id=1, source_target_pairs={{8,4},{20,24},{9,5},{21,25},{10,6},{22,26},{11,7},{23,27}} | collective-permute-start | bytes 691208 | tf_op jit(solution)/shard_map/ppermute | solution.py:461
  7.8 8.9 %collective-permute-start.6 = (f32[40,1440]{1,0:T(8,128)S(1)}, f32[40,1440]{1,0:T(8,128)S(1)}, u32[]{:S(2)}, u32[]{:S(2)}) collective-permute-start(f32[40,1440]{1,0:T(8,128)S(1)} %get-tuple-element.34.far_out_ref), channel_id=1, source_target_pairs={{4,8},{12,16},{16,12},{24,20},{5,9},{13,17},{17,13},{25,21},{6,10}... | collective-permute-start | bytes 691208 | tf_op jit(solution)/shard_map/ppermute | solution.py:461
  12.7 6.3 %collective-permute-start = (f32[2,2,8,1440]{3,2,1,0:T(8,128)S(1)}, f32[2,2,8,1440]{3,2,1,0:T(8,128)S(1)}, u32[]{:S(2)}, u32[]{:S(2)}) collective-permute-start(f32[2,2,8,1440]{3,2,1,0:T(8,128)S(1)} %get-tuple-element.26), channel_id=1, source_target_pairs={{0,1},{1,0},{2,3},{3,2},{4,5},{5,4},{6,7},{7,6},{8,9},{9,8},{10,11... | collective-permute-start | bytes 552968 | tf_op jit(solution)/shard_map/ppermute | solution.py:461
  16.7 2.4 %copy-start.4 = (f32[18,384]{1,0:T(8,128)S(1)}, f32[18,384]{1,0:T(8,128)}, u32[]{:S(2)}) copy-start(f32[18,384]{1,0:T(8,128)} %constant.12.clone.phase_ref) | copy-start | bytes 82948
  16.7 2.4 %copy-start.10 = (bf16[384,256]{1,0:T(8,128)(2,1)S(1)}, bf16[384,256]{1,0:T(8,128)(2,1)}, u32[]{:S(2)}) copy-start(bf16[384,256]{1,0:T(8,128)(2,1)} %constant.14.clone.high_ref) | copy-start | bytes 589828
  16.7 2.4 %copy-start.11 = (bf16[384,256]{1,0:T(8,128)(2,1)S(1)}, bf16[384,256]{1,0:T(8,128)(2,1)}, u32[]{:S(2)}) copy-start(bf16[384,256]{1,0:T(8,128)(2,1)} %constant.15.clone.low_ref) | copy-start | bytes 589828
  16.8 5.0 %collective-permute-start.7 = (f32[2,2,8,1440]{3,2,1,0:T(8,128)S(1)}, f32[2,2,8,1440]{3,2,1,0:T(8,128)S(1)}, u32[]{:S(2)}, u32[]{:S(2)}) collective-permute-start(f32[2,2,8,1440]{3,2,1,0:T(8,128)S(1)} %get-tuple-element.38), channel_id=1, source_target_pairs={{0,1},{1,0},{2,3},{3,2},{4,5},{5,4},{6,7},{7,6},{8,9},{9,8},{10,11... | collective-permute-start | bytes 552968 | tf_op jit(solution)/shard_map/ppermute | solution.py:461
  20.5 12.2 %collective-permute-start.1 = (f32[4,8,2176]{2,1,0:T(8,128)S(1)}, f32[4,8,2176]{2,1,0:T(8,128)S(1)}, u32[]{:S(2)}, u32[]{:S(2)}) collective-permute-start(f32[4,8,2176]{2,1,0:T(8,128)S(1)} %get-tuple-element.30.own_ref), channel_id=1, source_target_pairs={{0,2},{1,3},{2,0},{3,1},{4,6},{5,7},{6,4},{7,5},{8,10},{9,11},{10,... | collective-permute-start | bytes 835592 | tf_op jit(solution)/shard_map/ppermute | solution.py:461
  21.8 1.7 %copy-start.5 = (f32[18,128]{1,0:T(8,128)S(1)}, f32[18,128]{1,0:T(8,128)}, u32[]{:S(2)}) copy-start(f32[18,128]{1,0:T(8,128)} %constant.13.clone.wave_ref) | copy-start | bytes 27652
  23.2 13.7 %collective-permute-start.8 = (f32[4,8,2176]{2,1,0:T(8,128)S(1)}, f32[4,8,2176]{2,1,0:T(8,128)S(1)}, u32[]{:S(2)}, u32[]{:S(2)}) collective-permute-start(f32[4,8,2176]{2,1,0:T(8,128)S(1)} %get-tuple-element.42.own_ref), channel_id=1, source_target_pairs={{0,2},{1,3},{2,0},{3,1},{4,6},{5,7},{6,4},{7,5},{8,10},{9,11},{10,... | collective-permute-start | bytes 835592 | tf_op jit(solution)/shard_map/ppermute | solution.py:461
  23.5 0.7 %copy-start.7 = (f32[8,4]{0,1:T(4,128)S(1)}, f32[8,4]{0,1:T(4,128)}, u32[]{:S(2)}) copy-start(f32[8,4]{0,1:T(4,128)} %param.15) | copy-start | bytes 388
  23.5 0.7 %copy-start.6 = (s32[8,4]{0,1:T(4,128)S(1)}, s32[8,4]{0,1:T(4,128)}, u32[]{:S(2)}) copy-start(s32[8,4]{0,1:T(4,128)} %param.14) | copy-start | bytes 388
  23.5 0.7 %copy-start.8 = (s32[32]{0:T(128)S(1)}, s32[32]{0:T(128)}, u32[]{:S(2)}) copy-start(s32[32]{0:T(128)} %cutoff_ref.3) | copy-start | bytes 388
  28.4 4.3 %copy-start = (bf16[256,384]{1,0:T(8,128)(2,1)S(1)}, bf16[256,384]{1,0:T(8,128)(2,1)}, u32[]{:S(2)}) copy-start(bf16[256,384]{1,0:T(8,128)(2,1)} %constant.16.clone.high_ref) | copy-start | bytes 589828
  28.4 4.3 %copy-start.1 = (bf16[256,384]{1,0:T(8,128)(2,1)S(1)}, bf16[256,384]{1,0:T(8,128)(2,1)}, u32[]{:S(2)}) copy-start(bf16[256,384]{1,0:T(8,128)(2,1)} %constant.17.clone.low_ref) | copy-start | bytes 589828
  32.7 0.7 %copy-start.9 = (f32[32]{0:T(128)S(1)}, f32[32]{0:T(128)}, u32[]{:S(2)}) copy-start(f32[32]{0:T(128)} %damping_ref.3) | copy-start | bytes 388
  35.4 3.6 %collective-permute-start.2 = (f32[2,2,8,1440]{3,2,1,0:T(8,128)S(1)}, f32[2,2,8,1440]{3,2,1,0:T(8,128)S(1)}, u32[]{:S(2)}, u32[]{:S(2)}) collective-permute-start(f32[2,2,8,1440]{3,2,1,0:T(8,128)S(1)} %get-tuple-element.32), channel_id=1, source_target_pairs={{0,1},{1,0},{2,3},{3,2},{4,5},{5,4},{6,7},{7,6},{8,9},{9,8},{10,11... | collective-permute-start | bytes 552968 | tf_op jit(solution)/shard_map/ppermute | solution.py:461
  39.0 1.5 %collective-permute-start.9 = (f32[2,2,8,1440]{3,2,1,0:T(8,128)S(1)}, f32[2,2,8,1440]{3,2,1,0:T(8,128)S(1)}, u32[]{:S(2)}, u32[]{:S(2)}) collective-permute-start(f32[2,2,8,1440]{3,2,1,0:T(8,128)S(1)} %get-tuple-element.44), channel_id=1, source_target_pairs={{0,1},{1,0},{2,3},{3,2},{4,5},{5,4},{6,7},{7,6},{8,9},{9,8},{10,11... | collective-permute-start | bytes 552968 | tf_op jit(solution)/shard_map/ppermute | solution.py:461

commit v4 on v3

--- a/solution.py
+++ b/solution.py
@@ -14,7 +14,6 @@
 RADIX = 16
 HALF = RADIX // 2
 LANES = 128
-SPAN = 6 * LANES
 PAIR = 2
 
 
@@ -112,10 +111,13 @@
     return high, (value - high.astype(jnp.float32)).astype(jnp.bfloat16)
 
 
-def product(left, right_high, right_low):
+def product(left, table_high, table_low, side):
     high, low = split(left)
-    dot = functools.partial(jnp.dot, preferred_element_type=jnp.float32)
-    return dot(high, right_high) + (dot(high, right_low) + dot(low, right_high))
+
+    def dot(x, y):
+        return lax.dot_general(x, y, (((1,), (side,)), ((), ())), preferred_element_type=jnp.float32)
+
+    return dot(high, table_high) + (dot(high, table_low) + dot(low, table_high))
 
 
 def spans(columns, width):
@@ -131,67 +133,72 @@
     return jnp.maximum(face_speed, 0.0) * south + jnp.minimum(face_speed, 0.0) * north
 
 
-def begin_kernel(cells_ref, speed_ref, near_ref, far_ref, mine_ref, send_ref, edge_mine_ref, edge_send_ref):
+def near_is_north():
+    return lax.rem(lax.axis_index("lat"), 2) == 0
+
+
+def inner_kernel(cells_ref, speed_ref, mine_ref, send_ref):
     tracer_count, levels, row_count, columns = cells_ref.shape
     share = tracer_count // PAIR
     core = lax.rem(lax.axis_index("lon"), PAIR)
-    is_even = lax.rem(lax.axis_index("lat"), 2) == 0
     for lanes in spans(columns, 3 * LANES):
         speed = [speed_ref[:, j, lanes] for j in range(row_count)]
-        near_ref[tracer_count * levels :, lanes] = speed[0]
-        far_ref[tracer_count * levels :, lanes] = speed[0]
-        for which, (inner_ref, outer_ref) in enumerate(
-            [(mine_ref, edge_mine_ref), (send_ref, edge_send_ref)]
-        ):
+        for which, out_ref in enumerate([mine_ref, send_ref]):
             for i in range(share):
                 t = lax.rem(core + which, PAIR) * share + i
                 x = [cells_ref[t, :, j, lanes] for j in range(row_count)]
-                place = pl.ds(pl.multiple_of(t * levels, levels), levels)
-                near_ref[place, lanes] = jnp.where(is_even, x[-1], x[0])
-                far_ref[place, lanes] = jnp.where(is_even, x[0], x[-1])
                 flux = [flux_of(speed[j], x[j - 1], x[j]) for j in range(1, row_count)]
                 for j in range(1, row_count - 1):
-                    inner_ref[i, j - 1, :, lanes] = x[j] + flux[j - 1] - flux[j]
-                outer_ref[i, 0, :, lanes] = x[0] - flux[0]
-                outer_ref[i, 1, :, lanes] = x[-1] + flux[-1]
-
-
-def edge_kernel(
-    near_out_ref, far_out_ref, near_first_ref, near_later_ref, far_first_ref, far_later_ref,
-    edge_mine_ref, edge_send_ref, mine_ref, send_ref,
-):
-    share, _, levels, columns = edge_mine_ref.shape
-    total = share * PAIR * levels
+                    out_ref[i, j - 1, :, lanes] = x[j] + flux[j - 1] - flux[j]
+
+
+def outer_kernel(cells_ref, speed_ref, after_ref, near_ref, far_ref, near_part_ref, far_part_ref):
+    tracer_count, levels, row_count, columns = cells_ref.shape
+    north = near_is_north()
+    for lanes in spans(columns, 3 * LANES):
+        speed = [speed_ref[:, j, lanes] for j in (0, 1, row_count - 1)]
+        near_ref[tracer_count * levels :, lanes] = speed[0]
+        far_ref[tracer_count * levels :, lanes] = speed[0]
+        for t in range(tracer_count):
+            first, second = cells_ref[t, :, 0, lanes], cells_ref[t, :, 1, lanes]
+            third, last = cells_ref[t, :, row_count - 2, lanes], cells_ref[t, :, row_count - 1, lanes]
+            place = slice(t * levels, (t + 1) * levels)
+            near_ref[place, lanes] = jnp.where(north, last, first)
+            far_ref[place, lanes] = jnp.where(north, first, last)
+            south_part = first - flux_of(speed[1], first, second)
+            north_part = last + flux_of(speed[2], third, last)
+            near_part_ref[t, :, lanes] = jnp.where(north, north_part, south_part)
+            far_part_ref[t, :, lanes] = jnp.where(north, south_part, north_part)
+
+
+def edge_kernel(is_near, own_ref, got_ref, part_ref, after_ref, mine_ref, send_ref):
+    tracer_count, levels, columns = part_ref.shape
+    share = tracer_count // PAIR
+    total = tracer_count * levels
     core = lax.rem(lax.axis_index("lon"), PAIR)
     lat = lax.axis_index("lat")
-    is_even = lax.rem(lat, 2) == 0
-    cap = is_cap(lat)
+    north = near_is_north() if is_near else jnp.logical_not(near_is_north())
+    wall = jnp.where(north, lat == lax.axis_size("lat") - 1, lat == 0)
     for lanes in spans(columns, 3 * LANES):
-
-        def received(place):
-            near = jnp.where(cap, near_first_ref[place, lanes], near_later_ref[place, lanes])
-            far = jnp.where(cap, far_first_ref[place, lanes], far_later_ref[place, lanes])
-            return jnp.where(is_even, far, near), jnp.where(is_even, near, far)
-
-        speed_below = near_out_ref[total:, lanes]
-        speed_above = received(slice(total, total + levels))[1]
-        speed_below = jnp.where(lat > 0, speed_below, 0.0)
-        speed_above = jnp.where(lat < lax.axis_size("lat") - 1, speed_above, 0.0)
-        for which, (partial_ref, out_ref) in enumerate(
-            [(edge_mine_ref, mine_ref), (edge_send_ref, send_ref)]
-        ):
+        speed = jnp.where(north, got_ref[total:, lanes], own_ref[total:, lanes])
+        speed = jnp.where(wall, 0.0, speed)
+        for which, out_ref in enumerate([mine_ref, send_ref]):
             for i in range(share):
                 t = lax.rem(core + which, PAIR) * share + i
                 place = pl.ds(pl.multiple_of(t * levels, levels), levels)
-                below, above = received(place)
-                near_own, far_own = near_out_ref[place, lanes], far_out_ref[place, lanes]
-                south = jnp.where(is_even, far_own, near_own)
-                north = jnp.where(is_even, near_own, far_own)
-                out_ref[i, 0, :, lanes] = partial_ref[i, 0, :, lanes] + flux_of(speed_below, below, south)
-                out_ref[i, 1, :, lanes] = partial_ref[i, 1, :, lanes] - flux_of(speed_above, north, above)
-
-
-def forward_kernel(mine_ref, theirs_ref, phase_ref, high_ref, low_ref, message_ref, held_ref, stack_ref):
+                own, got = own_ref[place, lanes], got_ref[place, lanes]
+                flux = flux_of(speed, jnp.where(north, own, got), jnp.where(north, got, own))
+                out_ref[i, 0, :, lanes] = part_ref[t, :, lanes] + jnp.where(north, -flux, flux)
+
+
+def forward_kernel(relay, *refs):
+    if relay:
+        *refs, relay_ref, stack_ref = refs
+        *refs, source_ref, message_ref, held_ref = refs
+        relay_ref[...] = source_ref[...]
+    else:
+        *refs, message_ref, held_ref, stack_ref = refs
+    mine_ref, theirs_ref, phase_ref, high_ref, low_ref = refs[:5]
     share, number, levels, columns = mine_ref.shape
     piece = columns * PAIR // HALF
     padded = stack_ref.shape[1]
@@ -228,7 +235,7 @@
                             re, im = re * c + im * s, im * c - re * s
                     stack_ref[base : base + levels, lanes] = re
                     stack_ref[base + levels : base + 2 * levels, lanes] = im
-        coeffs = product(stack_ref[...], high_ref[...], low_ref[...])
+        coeffs = product(stack_ref[...], high_ref[...], low_ref[...], 0)
         upper = lax.broadcasted_iota(jnp.int32, (levels, modes), 1) >= modes // 2
         for n in range(count):
             first = None
@@ -257,14 +264,24 @@
     return out
 
 
-def displaced(block, distance, share):
-    repeat = block.shape[1] // LANES
-    distances = jnp.concatenate([distance] * repeat, axis=1)
-    shares = jnp.concatenate([share] * repeat, axis=1)
-    for bit in range(SMAX.bit_length()):
-        pushed = pltpu.roll(block, 1 << bit, 1)
-        block = jnp.where((distances >> bit) & 1 == 1, pushed, block)
-    return (1.0 - shares) * block + shares * pltpu.roll(block, 1, 1)
+def displaced(tiles, distance, share):
+    lane = lax.broadcasted_iota(jnp.int32, distance.shape, 1)
+
+    def moved(steps):
+        index = (lane - steps) & (LANES - 1)
+        turned = [jnp.take_along_axis(v, index, axis=1, mode="promise_in_bounds") for v in tiles]
+        from_left = lane < steps
+        return [jnp.where(from_left, a, b) for a, b in zip(turned, turned[1:])]
+
+    pairs = zip(moved(distance), moved(distance + 1))
+    return [(1.0 - share) * here + share * earlier for here, earlier in pairs]
+
+
+def rows_of(which, row_count):
+    if which == "inner":
+        return list(range(1, row_count - 1))
+    north = near_is_north() if which == "near" else jnp.logical_not(near_is_north())
+    return [jnp.where(north, row_count - 1, 0)]
 
 
 def wave_angle(steps, lon_cells):
@@ -273,9 +290,10 @@
 
 
 def shift_kernel(
-    rows, columns, shift_ref, fraction_ref, cutoff_ref, wave_ref, held_ref, moved_ref, gain_ref
+    which, columns, shift_ref, fraction_ref, cutoff_ref, wave_ref, held_ref, after_ref, moved_ref, gain_ref
 ):
     _, count, levels, padded = held_ref.shape
+    rows = rows_of(which, shift_ref.shape[0])
     number = len(rows)
     lon_cells = columns * PAIR * PAIR
     modes = gain_ref.shape[3]
@@ -285,13 +303,10 @@
         share = row_vector(fraction_ref, row, levels)
         for n in range(j, count, number):
             for pos in range(PAIR):
-                for lanes in spans(padded, SPAN):
-                    if lanes.start:
-                        block = held_ref[pos, n, :, lanes.start - LANES : lanes.stop]
-                    else:
-                        tail = held_ref[PAIR - 1 - pos, n, :, columns - LANES : columns]
-                        block = jnp.concatenate([tail, held_ref[pos, n, :, lanes]], axis=1)
-                    moved_ref[n, pos, :, lanes] = displaced(block, distance, share)[:, LANES:]
+                tiles = [held_ref[PAIR - 1 - pos, n, :, columns - LANES : columns]]
+                tiles += [held_ref[pos, n, :, lanes] for lanes in spans(padded, LANES)]
+                for lanes, tile in zip(spans(padded, LANES), displaced(tiles, distance, share)):
+                    moved_ref[n, pos, :, lanes] = tile
 
     @pl.when(is_cap(lat))
     def _():
@@ -323,11 +338,12 @@
 
 
 def inverse_kernel(
-    rows, columns, shift_ref, fraction_ref, damping_ref, phase_ref, high_ref, low_ref,
-    held_ref, moved_ref, gain_ref, own_ref, other_ref, mine_ref, send_ref,
+    which, columns, shift_ref, fraction_ref, damping_ref, phase_ref, high_ref, low_ref,
+    held_ref, moved_ref, gain_ref, own_ref, other_ref, after_ref, mine_ref, send_ref,
     stack_ref, back_ref, pair_ref,
 ):
     _, count, levels, _ = held_ref.shape
+    rows = rows_of(which, shift_ref.shape[0])
     number = len(rows)
     piece = columns * PAIR // HALF
     padded = stack_ref.shape[1]
@@ -340,9 +356,8 @@
         distance = row_vector(shift_ref, row, levels)
         share = row_vector(fraction_ref, row, levels)
         for n in range(j, count, number):
-            rim = other_ref[n, :, 2 * MODES :]
-            block = jnp.concatenate([rim, held_ref[0, n, :, :LANES]], axis=1)
-            moved_ref[n, 0, :, :LANES] = displaced(block, distance, share)[:, LANES:]
+            tiles = [other_ref[n, :, 2 * MODES :], held_ref[0, n, :, :LANES]]
+            (moved_ref[n, 0, :, :LANES],) = displaced(tiles, distance, share)
 
     @pl.when(jnp.logical_not(cap))
     def _():
@@ -374,7 +389,7 @@
                 back_ref[base : base + levels, modes:] = -im
                 back_ref[base + levels : base + 2 * levels, :modes] = im
                 back_ref[base + levels : base + 2 * levels, modes:] = re
-        stack_ref[...] = product(back_ref[...], high_ref[...], low_ref[...])
+        stack_ref[...] = product(back_ref[...], high_ref[...], low_ref[...], 1)
         for n in range(count):
             i, j = divmod(n, number)
             keep = damping_ref[lat * shift_ref.shape[0] + rows[j]]
@@ -402,18 +417,21 @@
             send_ref[i, j] = pair_ref[1 - core, n, :, :columns]
 
 
-def end_kernel(inner_ref, inner_back_ref, outer_ref, outer_back_ref, out_ref):
+def end_kernel(*refs):
+    *refs, out_ref = refs
     tracer_count, levels, row_count, columns = out_ref.shape
     share = tracer_count // PAIR
     core = lax.rem(lax.axis_index("lon"), PAIR)
-    for which, (inner, outer) in enumerate([(inner_ref, outer_ref), (inner_back_ref, outer_back_ref)]):
+    north = near_is_north()
+    for place, (inner, near, far) in enumerate([refs[:3], refs[3:]]):
         for i in range(share):
-            t = lax.rem(core + which, PAIR) * share + i
-            for j in range(row_count):
-                if j in (0, row_count - 1):
-                    out_ref[t, :, j, :] = outer[i, min(j, 1)]
-                else:
-                    out_ref[t, :, j, :] = inner[i, j - 1]
+            t = lax.rem(core + place, PAIR) * share + i
+            for lanes in spans(columns, 4 * LANES):
+                a, b = near[i, 0, :, lanes], far[i, 0, :, lanes]
+                out_ref[t, :, 0, lanes] = jnp.where(north, b, a)
+                out_ref[t, :, row_count - 1, lanes] = jnp.where(north, a, b)
+                for j in range(1, row_count - 1):
+                    out_ref[t, :, j, lanes] = inner[i, j - 1, :, lanes]
 
 
 def filter_tables(lon_cells):
@@ -436,29 +454,27 @@
 
     phase = waves(r * np.arange(padded)[None, :])
     wave = waves(RADIX * q[None, :] + r)
-    return phase, wave, high, low, np.ascontiguousarray(high.T), np.ascontiguousarray(low.T)
+    return phase, wave, high, low
+
+
+SMALL, WHOLE, UNREAD = pltpu.SMEM, pltpu.VMEM, pl.ANY
 
 
 def call(kernel, outs, operands, scratch=(), flops=0):
-    vmem = pl.BlockSpec(memory_space=pltpu.VMEM)
-    smem = pl.BlockSpec(memory_space=pltpu.SMEM)
-    scalars = [v for v, place in operands if place]
-    specs = [smem if place else vmem for v, place in operands]
-    shapes = [jax.ShapeDtypeStruct(shape, jnp.float32) for shape in outs]
     size = sum(4 * math.prod(shape) for shape in outs)
     return pl.pallas_call(
         kernel,
-        out_shape=shapes,
-        in_specs=specs,
-        out_specs=[vmem] * len(shapes),
+        out_shape=[jax.ShapeDtypeStruct(shape, jnp.float32) for shape in outs],
+        in_specs=[pl.BlockSpec(memory_space=place) for _, place in operands],
+        out_specs=[pl.BlockSpec(memory_space=WHOLE)] * len(outs),
         scratch_shapes=[pltpu.VMEM(shape, jnp.float32) for shape in scratch],
         compiler_params=pltpu.CompilerParams(vmem_limit_bytes=24 << 20),
         cost_estimate=pl.CostEstimate(flops=flops, bytes_accessed=2 * size, transcendentals=0),
-    )(*[v for v, place in operands])
-
-
-def permuted(value, axis, pairs):
-    return lax.ppermute(value, axis, pairs)
+    )(*[v for v, _ in operands])
+
+
+def whole(*values):
+    return [(v, WHOLE) for v in values]
 
 
 def body(tracers, merid_courant, zonal_shift, zonal_fraction, cutoff, damping):
@@ -467,96 +483,114 @@
     lon_count = lax.axis_size("lon")
     assert lon_count == PAIR * PAIR and tracer_count % PAIR == 0 and row_count > 2
     share = tracer_count // PAIR
-    top = row_count - 1
     lon_cells = column_count * lon_count
-    phase, wave, fwd_high, fwd_low, inv_high, inv_low = [jnp.asarray(t) for t in filter_tables(lon_cells)]
-    padded, double = fwd_high.shape
+    phase, wave, high, low = [jnp.asarray(t) for t in filter_tables(lon_cells)]
+    padded, double = high.shape
     width = -(-column_count // LANES) * LANES
     assert column_count - lon_cells // RADIX + padded <= width
     group = level_count * 2 * (HALF + 1)
     shift_rows, fraction_rows = zonal_shift.T, zonal_fraction.T
 
-    swap_core = lambda v: permuted(v, "lon", [(p, p ^ 1) for p in range(lon_count)])
-    swap_half = lambda v: permuted(v, "lon", [(p, p ^ 2) for p in range(lon_count)])
-    caps = [b for b in range(lat_count) if b < lat_count // 4 or b >= lat_count - lat_count // 4]
-
-    edge_shape = ((tracer_count + 1) * level_count, column_count)
-    inner_shape = (share, row_count - 2, level_count, column_count)
-    outer_shape = (share, 2, level_count, column_count)
-    near_out, far_out, inner_mine, inner_send, outer_mine, outer_send = call(
-        begin_kernel,
-        [edge_shape] * 2 + [inner_shape] * 2 + [outer_shape] * 2,
-        [(tracers, 0), (merid_courant, 0)],
-    )
-    inner_theirs = swap_core(inner_send)
-
-    def halo(value, first, to_caps):
+    def swap_core(value):
+        return lax.ppermute(value, "lon", [(p, p ^ 1) for p in range(lon_count)])
+
+    def swap_half(value):
+        return lax.ppermute(value, "lon", [(p, p ^ 2) for p in range(lon_count)])
+
+    def swap_band(value, first):
         pairs = []
         for b in range(first, lat_count - 1, 2):
-            pairs += [(s, d) for s, d in ((b, b + 1), (b + 1, b)) if (d in caps) == to_caps]
-        return permuted(value, "lat", pairs)
-
-    near_first, far_first = halo(near_out, 0, True), halo(far_out, 1, True)
-
-    def forward(mine, theirs):
+            pairs += [(b, b + 1), (b + 1, b)]
+        return lax.ppermute(value, "lat", pairs)
+
+    def set_shape(number):
+        return (share, number, level_count, column_count)
+
+    def forward(mine, theirs, after, relay=None):
         count = mine.shape[0] * mine.shape[1]
-        message, held = call(
-            forward_kernel,
-            [(count, level_count, 2 * MODES + LANES), (PAIR, count, level_count, width)],
-            [(v, 0) for v in (mine, theirs, phase, fwd_high, fwd_low)],
+        outs = [(count, level_count, 2 * MODES + LANES), (PAIR, count, level_count, width)]
+        operands = whole(mine, theirs, phase, high, low) + [(after, UNREAD)]
+        if relay is not None:
+            outs.append(relay.shape)
+            operands += whole(relay)
+        return call(
+            functools.partial(forward_kernel, relay is not None),
+            outs,
+            operands,
             [(count * group, padded)],
             2 * 3 * count * group * padded * double,
         )
-        return message, held
-
-    def shifted(rows, held):
+
+    def shifted(which, held, after):
+        count = held.shape[1]
+        number = count // share
+        return call(
+            functools.partial(shift_kernel, which, column_count),
+            [(count, PAIR, level_count, width), (number, 2 * (HALF + 1), level_count, double // 2)],
+            [(shift_rows, SMALL), (fraction_rows, SMALL), (cutoff, SMALL)]
+            + whole(wave, held)
+            + [(after, UNREAD)],
+        )
+
+    def inverse(which, held, moved, gain, own, other, after):
         count = held.shape[1]
         return call(
-            functools.partial(shift_kernel, rows, column_count),
-            [(count, PAIR, level_count, width), (len(rows), 2 * (HALF + 1), level_count, double // 2)],
-            [(shift_rows, 1), (fraction_rows, 1), (cutoff, 1), (wave, 0), (held, 0)],
-        )
-
-    def inverse(rows, held, moved, gain, own, other):
-        count = held.shape[1]
-        shape = (share, len(rows), level_count, column_count)
-        return call(
-            functools.partial(inverse_kernel, rows, column_count),
-            [shape, shape],
-            [(shift_rows, 1), (fraction_rows, 1), (damping, 1)]
-            + [(v, 0) for v in (phase, inv_high, inv_low, held, moved, gain, own, other)],
+            functools.partial(inverse_kernel, which, column_count),
+            [set_shape(count // share)] * 2,
+            [(shift_rows, SMALL), (fraction_rows, SMALL), (damping, SMALL)]
+            + whole(phase, high, low, held, moved, gain, own, other)
+            + [(after, UNREAD)],
             [(count * group, padded), (count * group, double), (PAIR, count, level_count, width)],
             2 * 3 * count * group * padded * double,
         )
 
-    inner_rows, outer_rows = list(range(1, top)), [0, top]
-    inner_own, inner_held = forward(inner_mine, inner_theirs)
+    inner_mine, inner_send = call(
+        inner_kernel, [set_shape(row_count - 2)] * 2, whole(tracers, merid_courant)
+    )
+    inner_theirs = swap_core(inner_send)
+    edge_shape = ((tracer_count + 1) * level_count, column_count)
+    part_shape = (tracer_count, level_count, column_count)
+    near_own, far_own, near_part, far_part = call(
+        outer_kernel,
+        [edge_shape] * 2 + [part_shape] * 2,
+        whole(tracers, merid_courant) + [(inner_mine, UNREAD)],
+    )
+    near_got = swap_band(near_own, 0)
+    inner_own, inner_held, far_relay = forward(inner_mine, inner_theirs, near_part, far_own)
     inner_other = swap_half(inner_own)
-    near_later, far_later = halo(near_out, 0, False), halo(far_out, 1, False)
-    inner_moved, inner_gain = shifted(inner_rows, inner_held)
-
-    outer_mine, outer_send = call(
-        edge_kernel,
-        [outer_shape] * 2,
-        [(v, 0) for v in (near_out, far_out, near_first, near_later, far_first, far_later, outer_mine, outer_send)],
+    far_got = swap_band(far_relay, 1)
+    inner_moved, inner_gain = shifted("inner", inner_held, inner_own)
+
+    near_mine, near_send = call(
+        functools.partial(edge_kernel, True),
+        [set_shape(1)] * 2,
+        whole(near_own, near_got, near_part) + [(inner_moved, UNREAD)],
     )
-    outer_theirs = swap_core(outer_send)
-    outer_own, outer_held = forward(outer_mine, outer_theirs)
-    outer_other = swap_half(outer_own)
-    outer_moved, outer_gain = shifted(outer_rows, outer_held)
-
-    inner_mine, inner_send = inverse(
-        inner_rows, inner_held, inner_moved, inner_gain, inner_own, inner_other
+    near_theirs = swap_core(near_send)
+    near_own, near_held, = forward(near_mine, near_theirs, inner_moved)
+    near_other = swap_half(near_own)
+    near_moved, near_gain = shifted("near", near_held, near_own)
+
+    far_mine, far_send = call(
+        functools.partial(edge_kernel, False),
+        [set_shape(1)] * 2,
+        whole(far_own, far_got, far_part) + [(near_moved, UNREAD)],
     )
-    inner_back = swap_core(inner_send)
-    outer_mine, outer_send = inverse(
-        outer_rows, outer_held, outer_moved, outer_gain, outer_own, outer_other
-    )
-    outer_back = swap_core(outer_send)
+    far_theirs = swap_core(far_send)
+    far_own, far_held = forward(far_mine, far_theirs, near_moved)
+    far_other = swap_half(far_own)
+    far_moved, far_gain = shifted("far", far_held, far_own)
+
+    inner = inverse("inner", inner_held, inner_moved, inner_gain, inner_own, inner_other, far_moved)
+    inner_back = swap_core(inner[1])
+    near = inverse("near", near_held, near_moved, near_gain, near_own, near_other, inner[0])
+    near_back = swap_core(near[1])
+    far = inverse("far", far_held, far_moved, far_gain, far_own, far_other, near[0])
+    far_back = swap_core(far[1])
     (result,) = call(
         end_kernel,
         [tracers.shape],
-        [(v, 0) for v in (inner_mine, inner_back, outer_mine, outer_back)],
+        whole(inner[0], near[0], far[0], inner_back, near_back, far_back),
     )
     return result
 

time: 41.8 us -> 33.7 us (0.81)
  the two profiles are of different devices: /device:TPU:25 before, /device:TPU:3 now
where the time goes in v4:
time: 33.7 us; the launch traced here: 33.3 us
  starting transfers between devices  14.3 us (42%)
  Pallas kernels  13 us (39%)
  local copies, waits for them, and re-layouts  3.42 us (10%)
  waiting for transfers between devices  2.47 us (7%)
    pallas_call x14, Pallas kernels, call(): pl.pallas_call(kernel, out_shape=[jax.ShapeDtypeStruct(shape, jnp.float32...  13 us
    ppermute x6, starting transfers between devices, swap_core(): return lax.ppermute(value, 'lon', [(p, p ^ 1) for p in range(lon_count)])  8.22 us
    ppermute x3, starting transfers between devices, swap_half(): return lax.ppermute(value, 'lon', [(p, p ^ 2) for p in range(lon_count)])  3.5 us
    unnamed x20, local copies, waits for them, and re-layouts  3.42 us
    ppermute x2, starting transfers between devices, swap_band(): return lax.ppermute(value, 'lat', pairs)  2.56 us
    ppermute x6, waiting for transfers between devices, swap_core(): return lax.ppermute(value, 'lon', [(p, p ^ 1) for p in range(lon_count)])  2.46 us
  transfers between devices with their start and end apart: 11, of which 3 were waited for; matrix products, arithmetic and copies ran while one was open for 0% of the time, Pallas kernels for 35%

profile of v4, /device:TPU:3, one launch (start us, length us, event | category | flops | bytes accessed | tf_op | source)
XLA Modules:
  0.0 33.3 jit_solution(12042947892626957255)
XLA Ops:
  0.0 0.0 copy-start.2
  0.0 1.1 %copy-done.2 = f32[4,8,4,1440]{3,2,1,0:T(4,128)S(1)} copy-done((f32[4,8,4,1440]{3,2,1,0:T(4,128)S(1)}, f32[4,8,4,1440]{3,2,1,0:T(4,128)}, u32[]{:S(2)}) %copy-start.2) | copy-done | bytes 737304
  1.1 0.9 %copy-done.4 = f32[8,4,1440]{2,1,0:T(4,128)S(1)} copy-done((f32[8,4,1440]{2,1,0:T(4,128)S(1)}, f32[8,4,1440]{2,1,0:T(4,128)}, u32[]{:S(2)}) %copy-start.4) | copy-done | bytes 184344
  2.1 0.4 %shard_map.100 = (f32[2,2,8,1440]{3,2,1,0:T(8,128)S(1)}, f32[2,2,8,1440]{3,2,1,0:T(8,128)S(1)}) custom-call(f32[4,8,4,1440]{3,2,1,0:T(4,128)S(1)} %copy-done.2, f32[8,4,1440]{2,1,0:T(4,128)S(1)} %copy-done.4), custom_call_target="tpu_custom_call" | custom-call | bytes 737280 | tf_op jit(solution)/shard_map/pallas_call | solution.py:465
  2.4 0.7 %collective-permute-start = (f32[2,2,8,1440]{3,2,1,0:T(8,128)S(1)}, f32[2,2,8,1440]{3,2,1,0:T(8,128)S(1)}, u32[]{:S(2)}, u32[]{:S(2)}) collective-permute-start(f32[2,2,8,1440]{3,2,1,0:T(8,128)S(1)} %get-tuple-element.35), channel_id=1, source_target_pairs={{0,1},{1,0},{2,3},{3,2},{4,5},{5,4},{6,7},{7,6},{8,9},{9,8},{10,11... | collective-permute-start | bytes 552968 | tf_op jit(solution)/shard_map/ppermute | solution.py:495
  3.2 0.4 %shard_map.101 = (f32[40,1440]{1,0:T(8,128)S(1)}, f32[40,1440]{1,0:T(8,128)S(1)}, f32[4,8,1440]{2,1,0:T(8,128)S(1)}, f32[4,8,1440]{2,1,0:T(8,128)S(1)}) custom-call(f32[4,8,4,1440]{3,2,1,0:T(4,128)S(1)} %copy-done.2, f32[8,4,1440]{2,1,0:T(4,128)S(1)} %copy-done.4, f32[2,2,8,1440]{3,2,1,0:T(8,128)S(1)} %get-tuple-element.34.after_ref.refs_0_), custom_call_target="tpu_custom_call" | custom-call | bytes 1658880 | tf_op jit(solution)/shard_map/pallas_call | solution.py:465
  3.6 0.1 collective-permute-start.3
  3.7 0.6 %collective-permute-done.refs_1_ = f32[2,2,8,1440]{3,2,1,0:T(8,128)S(1)} collective-permute-done((f32[2,2,8,1440]{3,2,1,0:T(8,128)S(1)}, f32[2,2,8,1440]{3,2,1,0:T(8,128)S(1)}, u32[]{:S(2)}, u32[]{:S(2)}) %collective-permute-start) | collective-permute-done | bytes 184352 | tf_op jit(solution)/shard_map/ppermute | solution.py:495
  4.2 0.0 copy-done
  4.2 0.0 copy-done.1
  4.2 0.0 copy-done.3
  4.2 1.5 %shard_map.102 = (f32[4,8,2176]{2,1,0:T(8,128)S(1)}, f32[2,4,8,1536]{3,2,1,0:T(8,128)S(1)}, f32[40,1440]{1,0:T(8,128)S(1)}) custom-call(f32[2,2,8,1440]{3,2,1,0:T(8,128)S(1)} %get-tuple-element.34.after_ref.refs_0_, f32[2,2,8,1440]{3,2,1,0:T(8,128)S(1)} %collective-permute-done.refs_1_, f32[18,384]{1,0:T(8,128)S(1)} %copy-done.3, ...), custom_call_target="tpu_custom_call" | custom-call | flops 339738624 | bytes 1804288 | tf_op jit(solution)/shard_map/pallas_call | solution.py:465
  5.7 2.5 %collective-permute-start.2 = (f32[40,1440]{1,0:T(8,128)S(1)}, f32[40,1440]{1,0:T(8,128)S(1)}, u32[]{:S(2)}, u32[]{:S(2)}) collective-permute-start(f32[40,1440]{1,0:T(8,128)S(1)} %get-tuple-element.42), channel_id=1, source_target_pairs={{4,8},{8,4},{12,16},{16,12},{20,24},{24,20},{5,9},{9,5},{13,17},{1... | collective-permute-start | bytes 691208 | tf_op jit(solution)/shard_map/ppermute | solution.py:504
  8.2 1.3 %collective-permute-start.1 = (f32[4,8,2176]{2,1,0:T(8,128)S(1)}, f32[4,8,2176]{2,1,0:T(8,128)S(1)}, u32[]{:S(2)}, u32[]{:S(2)}) collective-permute-start(f32[4,8,2176]{2,1,0:T(8,128)S(1)} %get-tuple-element.39.after_ref.own_ref), channel_id=1, source_target_pairs={{0,2},{1,3},{2,0},{3,1},{4,6},{5,7},{6,4},{7,5},{8,10},{9,11},{10,... | collective-permute-start | bytes 835592 | tf_op jit(solution)/shard_map/ppermute | solution.py:498
  9.5 0.0 copy-done.5
  9.5 0.7 %copy-done.7 = f32[8,4]{0,1:T(4,128)S(1)} copy-done((f32[8,4]{0,1:T(4,128)S(1)}, f32[8,4]{0,1:T(4,128)}, u32[]{:S(2)}) %copy-start.7) | copy-done | bytes 152
  10.2 0.0 copy-done.6
  10.2 0.0 copy-done.9
  10.2 1.5 %shard_map.103 = (f32[4,2,8,1536]{3,2,1,0:T(8,128)S(1)}, f32[2,18,8,128]{3,2,1,0:T(8,128)S(1)}) custom-call(s32[4,8]{1,0:T(4,128)S(1)} %bitcast.2, f32[4,8]{1,0:T(4,128)S(1)} %bitcast.8, s32[32]{0:T(128)S(1)} %copy-done.9, f32[18,128]{1,0:T(8,128)S(1)} %copy-done.5, f32[2,4,8,1536]{3,2,1,0:T(8,128)S(1)} %get-tuple-element.38.held_ref, ...), custom_call_target="tpu_custom_call" | custom-call | bytes 1081344 | tf_op jit(solution)/shard_map/pallas_call | solution.py:465
  11.7 0.0 collective-permute-done.3.got_ref
  11.7 0.1 shard_map.104
  11.8 5.6 %collective-permute-start.4 = (f32[2,1,8,1440]{3,2,1,0:T(8,128)S(1)}, f32[2,1,8,1440]{3,2,1,0:T(8,128)S(1)}, u32[]{:S(2)}, u32[]{:S(2)}) collective-permute-start(f32[2,1,8,1440]{3,2,1,0:T(8,128)S(1)} %get-tuple-element.46), channel_id=1, source_target_pairs={{0,1},{1,0},{2,3},{3,2},{4,5},{5,4},{6,7},{7,6},{8,9},{9,8},{10,11... | collective-permute-start | bytes 276488 | tf_op jit(solution)/shard_map/ppermute | solution.py:495
  17.4 0.9 %collective-permute-done.4.refs_1_ = f32[2,1,8,1440]{3,2,1,0:T(8,128)S(1)} collective-permute-done((f32[2,1,8,1440]{3,2,1,0:T(8,128)S(1)}, f32[2,1,8,1440]{3,2,1,0:T(8,128)S(1)}, u32[]{:S(2)}, u32[]{:S(2)}) %collective-permute-start.4) | collective-permute-done | bytes 92192 | tf_op jit(solution)/shard_map/ppermute | solution.py:495
  18.4 0.9 %shard_map.105 = (f32[2,8,2176]{2,1,0:T(8,128)S(1)}, f32[2,2,8,1536]{3,2,1,0:T(8,128)S(1)}) custom-call(f32[2,1,8,1440]{3,2,1,0:T(8,128)S(1)} %get-tuple-element.45.refs_0_, f32[2,1,8,1440]{3,2,1,0:T(8,128)S(1)} %collective-permute-done.4.refs_1_, f32[18,384]{1,0:T(8,128)S(1)} %copy-done.3, bf16[384,256]{1,0:T(8,128)(2,1)S(1)} %copy-done, ...), custom_call_target="tpu_custom_call" | custom-call | flops 169869312 | bytes 671744 | tf_op jit(solution)/shard_map/pallas_call | solution.py:465
  19.3 1.1 %shard_map.106 = (f32[2,2,8,1536]{3,2,1,0:T(8,128)S(1)}, f32[1,18,8,128]{3,2,1,0:T(8,128)S(1)}) custom-call(s32[4,8]{1,0:T(4,128)S(1)} %bitcast.3, f32[4,8]{1,0:T(4,128)S(1)} %bitcast.9, s32[32]{0:T(128)S(1)} %copy-done.9, f32[18,128]{1,0:T(8,128)S(1)} %copy-done.5, f32[2,2,8,1536]{3,2,1,0:T(8,128)S(1)} %get-tuple-element.47.held_ref, ...), custom_call_target="tpu_custom_call" | custom-call | bytes 540672 | tf_op jit(solution)/shard_map/pallas_call | solution.py:465
  20.4 0.0 collective-permute-done.2.got_ref
  20.4 0.1 shard_map.107
  20.5 0.4 %collective-permute-start.5 = (f32[2,1,8,1440]{3,2,1,0:T(8,128)S(1)}, f32[2,1,8,1440]{3,2,1,0:T(8,128)S(1)}, u32[]{:S(2)}, u32[]{:S(2)}) collective-permute-start(f32[2,1,8,1440]{3,2,1,0:T(8,128)S(1)} %get-tuple-element.51), channel_id=1, source_target_pairs={{0,1},{1,0},{2,3},{3,2},{4,5},{5,4},{6,7},{7,6},{8,9},{9,8},{10,11... | collective-permute-start | bytes 276488 | tf_op jit(solution)/shard_map/ppermute | solution.py:495
  20.9 1.2 %collective-permute-start.6 = (f32[2,8,2176]{2,1,0:T(8,128)S(1)}, f32[2,8,2176]{2,1,0:T(8,128)S(1)}, u32[]{:S(2)}, u32[]{:S(2)}) collective-permute-start(f32[2,8,2176]{2,1,0:T(8,128)S(1)} %get-tuple-element.48.after_ref.own_ref), channel_id=1, source_target_pairs={{0,2},{1,3},{2,0},{3,1},{4,6},{5,7},{6,4},{7,5},{8,10},{9,11},{10,... | collective-permute-start | bytes 417800 | tf_op jit(solution)/shard_map/ppermute | solution.py:498
  22.1 0.0 collective-permute-done.5.refs_1_
  22.1 0.9 %shard_map.108 = (f32[2,8,2176]{2,1,0:T(8,128)S(1)}, f32[2,2,8,1536]{3,2,1,0:T(8,128)S(1)}) custom-call(f32[2,1,8,1440]{3,2,1,0:T(8,128)S(1)} %get-tuple-element.50.refs_0_, f32[2,1,8,1440]{3,2,1,0:T(8,128)S(1)} %collective-permute-done.5.refs_1_, f32[18,384]{1,0:T(8,128)S(1)} %copy-done.3, bf16[384,256]{1,0:T(8,128)(2,1)S(1)} %copy-done, ...), custom_call_target="tpu_custom_call" | custom-call | flops 169869312 | bytes 671744 | tf_op jit(solution)/shard_map/pallas_call | solution.py:465
  23.0 1.0 %collective-permute-start.7 = (f32[2,8,2176]{2,1,0:T(8,128)S(1)}, f32[2,8,2176]{2,1,0:T(8,128)S(1)}, u32[]{:S(2)}, u32[]{:S(2)}) collective-permute-start(f32[2,8,2176]{2,1,0:T(8,128)S(1)} %get-tuple-element.53.after_ref.own_ref), channel_id=1, source_target_pairs={{0,2},{1,3},{2,0},{3,1},{4,6},{5,7},{6,4},{7,5},{8,10},{9,11},{10,... | collective-permute-start | bytes 417800 | tf_op jit(solution)/shard_map/ppermute | solution.py:498
  24.0 1.1 %shard_map.109 = (f32[2,2,8,1536]{3,2,1,0:T(8,128)S(1)}, f32[1,18,8,128]{3,2,1,0:T(8,128)S(1)}) custom-call(s32[4,8]{1,0:T(4,128)S(1)} %bitcast.4, f32[4,8]{1,0:T(4,128)S(1)} %bitcast.10, s32[32]{0:T(128)S(1)} %copy-done.9, f32[18,128]{1,0:T(8,128)S(1)} %copy-done.5, f32[2,2,8,1536]{3,2,1,0:T(8,128)S(1)} %get-tuple-element.52.held_ref, ...), custom_call_target="tpu_custom_call" | custom-call | bytes 540672 | tf_op jit(solution)/shard_map/pallas_call | solution.py:465
  25.1 0.0 collective-permute-done.1.other_ref
  25.1 0.0 copy-start.8
  25.1 0.6 %copy-done.8 = f32[32]{0:T(128)S(1)} copy-done((f32[32]{0:T(128)S(1)}, f32[32]{0:T(128)}, u32[]{:S(2)}) %copy-start.8) | copy-done | bytes 152
  25.7 1.6 %shard_map.110 = (f32[2,2,8,1440]{3,2,1,0:T(8,128)S(1)}, f32[2,2,8,1440]{3,2,1,0:T(8,128)S(1)}) custom-call(s32[4,8]{1,0:T(4,128)S(1)} %bitcast.5, f32[4,8]{1,0:T(4,128)S(1)} %bitcast.11, f32[32]{0:T(128)S(1)} %copy-done.8, f32[18,384]{1,0:T(8,128)S(1)} %copy-done.3, bf16[384,256]{1,0:T(8,128)(2,1)S(1)} %copy-done, bf16[384,256]{1,0:T(8,128)(2,1)S(1)} %copy-done.1, ...), custom_call_target="tpu_custom_call" | custom-call | flops 339738624 | bytes 737280 | tf_op jit(solution)/shard_map/pallas_call | solution.py:465
  27.3 0.7 %collective-permute-start.8 = (f32[2,2,8,1440]{3,2,1,0:T(8,128)S(1)}, f32[2,2,8,1440]{3,2,1,0:T(8,128)S(1)}, u32[]{:S(2)}, u32[]{:S(2)}) collective-permute-start(f32[2,2,8,1440]{3,2,1,0:T(8,128)S(1)} %get-tuple-element.60), channel_id=1, source_target_pairs={{0,1},{1,0},{2,3},{3,2},{4,5},{5,4},{6,7},{7,6},{8,9},{9,8},{10,11... | collective-permute-start | bytes 552968 | tf_op jit(solution)/shard_map/ppermute | solution.py:495
  28.0 0.0 collective-permute-done.6.other_ref
  28.0 1.2 %shard_map.111 = (f32[2,1,8,1440]{3,2,1,0:T(8,128)S(1)}, f32[2,1,8,1440]{3,2,1,0:T(8,128)S(1)}) custom-call(s32[4,8]{1,0:T(4,128)S(1)} %bitcast.6, f32[4,8]{1,0:T(4,128)S(1)} %bitcast.12, f32[32]{0:T(128)S(1)} %copy-done.8, f32[18,384]{1,0:T(8,128)S(1)} %copy-done.3, bf16[384,256]{1,0:T(8,128)(2,1)S(1)} %copy-done, bf16[384,256]{1,0:T(8,128)(2,1)S(1)} %copy-done.1, ...), custom_call_target="tpu_custom_call" | custom-call | flops 169869312 | bytes 368640 | tf_op jit(solution)/shard_map/pallas_call | solution.py:465
  29.3 0.1 collective-permute-start.9
  29.4 0.0 collective-permute-done.7.other_ref
  29.4 1.3 %shard_map.112 = (f32[2,1,8,1440]{3,2,1,0:T(8,128)S(1)}, f32[2,1,8,1440]{3,2,1,0:T(8,128)S(1)}) custom-call(s32[4,8]{1,0:T(4,128)S(1)} %bitcast.7, f32[4,8]{1,0:T(4,128)S(1)} %bitcast.13, f32[32]{0:T(128)S(1)} %copy-done.8, f32[18,384]{1,0:T(8,128)S(1)} %copy-done.3, bf16[384,256]{1,0:T(8,128)(2,1)S(1)} %copy-done, bf16[384,256]{1,0:T(8,128)(2,1)S(1)} %copy-done.1, ...), custom_call_target="tpu_custom_call" | custom-call | flops 169869312 | bytes 368640 | tf_op jit(solution)/shard_map/pallas_call | solution.py:465
  30.6 0.7 %collective-permute-start.10 = (f32[2,1,8,1440]{3,2,1,0:T(8,128)S(1)}, f32[2,1,8,1440]{3,2,1,0:T(8,128)S(1)}, u32[]{:S(2)}, u32[]{:S(2)}) collective-permute-start(f32[2,1,8,1440]{3,2,1,0:T(8,128)S(1)} %get-tuple-element.62), channel_id=1, source_target_pairs={{0,1},{1,0},{2,3},{3,2},{4,5},{5,4},{6,7},{7,6},{8,9},{9,8},{10,11... | collective-permute-start | bytes 276488 | tf_op jit(solution)/shard_map/ppermute | solution.py:495
  31.3 0.0 collective-permute-done.9.refs_4_
  31.3 0.0 collective-permute-done.8.refs_3_
  31.3 0.9 %collective-permute-done.10.refs_5_ = f32[2,1,8,1440]{3,2,1,0:T(8,128)S(1)} collective-permute-done((f32[2,1,8,1440]{3,2,1,0:T(8,128)S(1)}, f32[2,1,8,1440]{3,2,1,0:T(8,128)S(1)}, u32[]{:S(2)}, u32[]{:S(2)}) %collective-permute-start.10) | collective-permute-done | bytes 92192 | tf_op jit(solution)/shard_map/ppermute | solution.py:495
  32.2 1.0 %shard_map.113 = f32[4,8,4,1440]{3,2,1,0:T(4,128)} custom-call(f32[2,2,8,1440]{3,2,1,0:T(8,128)S(1)} %get-tuple-element.55.after_ref.refs_0_, f32[2,1,8,1440]{3,2,1,0:T(8,128)S(1)} %get-tuple-element.57.after_ref.refs_1_, f32[2,1,8,1440]{3,2,1,0:T(8,128)S(1)} %get-tuple-element.59.refs_2_, f32[2,2,8,1440]{3,2,1,0:T(8,128)S(1)} %collective-permute-done.8.refs_3_, ...), custom_call_target="tpu_custom_call" | custom-call | bytes 1474560 | tf_op jit(solution)/shard_map/pallas_call | solution.py:465
  (8 shorter events, 0.0 us)
Async XLA Ops:
  0.0 1.1 %copy-start.2 = (f32[4,8,4,1440]{3,2,1,0:T(4,128)S(1)}, f32[4,8,4,1440]{3,2,1,0:T(4,128)}, u32[]{:S(2)}) copy-start(f32[4,8,4,1440]{3,2,1,0:T(4,128)} %cells_ref.3) | copy-start | bytes 2211844
  1.1 0.9 %copy-start.4 = (f32[8,4,1440]{2,1,0:T(4,128)S(1)}, f32[8,4,1440]{2,1,0:T(4,128)}, u32[]{:S(2)}) copy-start(f32[8,4,1440]{2,1,0:T(4,128)} %speed_ref.3) | copy-start | bytes 552964
  2.4 1.8 %collective-permute-start = (f32[2,2,8,1440]{3,2,1,0:T(8,128)S(1)}, f32[2,2,8,1440]{3,2,1,0:T(8,128)S(1)}, u32[]{:S(2)}, u32[]{:S(2)}) collective-permute-start(f32[2,2,8,1440]{3,2,1,0:T(8,128)S(1)} %get-tuple-element.35), channel_id=1, source_target_pairs={{0,1},{1,0},{2,3},{3,2},{4,5},{5,4},{6,7},{7,6},{8,9},{9,8},{10,11... | collective-permute-start | bytes 552968 | tf_op jit(solution)/shard_map/ppermute | solution.py:495
  3.2 1.1 %copy-start = (bf16[384,256]{1,0:T(8,128)(2,1)S(1)}, bf16[384,256]{1,0:T(8,128)(2,1)}, u32[]{:S(2)}) copy-start(bf16[384,256]{1,0:T(8,128)(2,1)} %constant.10.clone.refs_3_.high_ref) | copy-start | bytes 589828
  3.2 1.1 %copy-start.1 = (bf16[384,256]{1,0:T(8,128)(2,1)S(1)}, bf16[384,256]{1,0:T(8,128)(2,1)}, u32[]{:S(2)}) copy-start(bf16[384,256]{1,0:T(8,128)(2,1)} %constant.11.clone.refs_4_.low_ref) | copy-start | bytes 589828
  3.2 1.1 %copy-start.3 = (f32[18,384]{1,0:T(8,128)S(1)}, f32[18,384]{1,0:T(8,128)}, u32[]{:S(2)}) copy-start(f32[18,384]{1,0:T(8,128)} %constant.8.clone.refs_2_.phase_ref) | copy-start | bytes 82948
  3.6 8.1 %collective-permute-start.3 = (f32[40,1440]{1,0:T(8,128)S(1)}, f32[40,1440]{1,0:T(8,128)S(1)}, u32[]{:S(2)}, u32[]{:S(2)}) collective-permute-start(f32[40,1440]{1,0:T(8,128)S(1)} %get-tuple-element.44.own_ref), channel_id=1, source_target_pairs={{0,4},{4,0},{8,12},{12,8},{16,20},{20,16},{24,28},{28,24},{1,5},{5... | collective-permute-start | bytes 691208 | tf_op jit(solution)/shard_map/ppermute | solution.py:504
  4.2 5.3 %copy-start.5 = (f32[18,128]{1,0:T(8,128)S(1)}, f32[18,128]{1,0:T(8,128)}, u32[]{:S(2)}) copy-start(f32[18,128]{1,0:T(8,128)} %constant.9.clone.wave_ref) | copy-start | bytes 27652
  5.7 14.7 %collective-permute-start.2 = (f32[40,1440]{1,0:T(8,128)S(1)}, f32[40,1440]{1,0:T(8,128)S(1)}, u32[]{:S(2)}, u32[]{:S(2)}) collective-permute-start(f32[40,1440]{1,0:T(8,128)S(1)} %get-tuple-element.42), channel_id=1, source_target_pairs={{4,8},{8,4},{12,16},{16,12},{20,24},{24,20},{5,9},{9,5},{13,17},{1... | collective-permute-start | bytes 691208 | tf_op jit(solution)/shard_map/ppermute | solution.py:504
  8.2 16.9 %collective-permute-start.1 = (f32[4,8,2176]{2,1,0:T(8,128)S(1)}, f32[4,8,2176]{2,1,0:T(8,128)S(1)}, u32[]{:S(2)}, u32[]{:S(2)}) collective-permute-start(f32[4,8,2176]{2,1,0:T(8,128)S(1)} %get-tuple-element.39.after_ref.own_ref), channel_id=1, source_target_pairs={{0,2},{1,3},{2,0},{3,1},{4,6},{5,7},{6,4},{7,5},{8,10},{9,11},{10,... | collective-permute-start | bytes 835592 | tf_op jit(solution)/shard_map/ppermute | solution.py:498
  9.5 0.7 %copy-start.7 = (f32[8,4]{0,1:T(4,128)S(1)}, f32[8,4]{0,1:T(4,128)}, u32[]{:S(2)}) copy-start(f32[8,4]{0,1:T(4,128)} %param.13) | copy-start | bytes 388
  9.5 0.7 %copy-start.6 = (s32[8,4]{0,1:T(4,128)S(1)}, s32[8,4]{0,1:T(4,128)}, u32[]{:S(2)}) copy-start(s32[8,4]{0,1:T(4,128)} %param.12) | copy-start | bytes 388
  9.5 0.7 %copy-start.9 = (s32[32]{0:T(128)S(1)}, s32[32]{0:T(128)}, u32[]{:S(2)}) copy-start(s32[32]{0:T(128)} %cutoff_ref.5) | copy-start | bytes 388
  11.8 6.6 %collective-permute-start.4 = (f32[2,1,8,1440]{3,2,1,0:T(8,128)S(1)}, f32[2,1,8,1440]{3,2,1,0:T(8,128)S(1)}, u32[]{:S(2)}, u32[]{:S(2)}) collective-permute-start(f32[2,1,8,1440]{3,2,1,0:T(8,128)S(1)} %get-tuple-element.46), channel_id=1, source_target_pairs={{0,1},{1,0},{2,3},{3,2},{4,5},{5,4},{6,7},{7,6},{8,9},{9,8},{10,11... | collective-permute-start | bytes 276488 | tf_op jit(solution)/shard_map/ppermute | solution.py:495
  20.5 1.7 %collective-permute-start.5 = (f32[2,1,8,1440]{3,2,1,0:T(8,128)S(1)}, f32[2,1,8,1440]{3,2,1,0:T(8,128)S(1)}, u32[]{:S(2)}, u32[]{:S(2)}) collective-permute-start(f32[2,1,8,1440]{3,2,1,0:T(8,128)S(1)} %get-tuple-element.51), channel_id=1, source_target_pairs={{0,1},{1,0},{2,3},{3,2},{4,5},{5,4},{6,7},{7,6},{8,9},{9,8},{10,11... | collective-permute-start | bytes 276488 | tf_op jit(solution)/shard_map/ppermute | solution.py:495
  20.9 7.1 %collective-permute-start.6 = (f32[2,8,2176]{2,1,0:T(8,128)S(1)}, f32[2,8,2176]{2,1,0:T(8,128)S(1)}, u32[]{:S(2)}, u32[]{:S(2)}) collective-permute-start(f32[2,8,2176]{2,1,0:T(8,128)S(1)} %get-tuple-element.48.after_ref.own_ref), channel_id=1, source_target_pairs={{0,2},{1,3},{2,0},{3,1},{4,6},{5,7},{6,4},{7,5},{8,10},{9,11},{10,... | collective-permute-start | bytes 417800 | tf_op jit(solution)/shard_map/ppermute | solution.py:498
  23.0 6.3 %collective-permute-start.7 = (f32[2,8,2176]{2,1,0:T(8,128)S(1)}, f32[2,8,2176]{2,1,0:T(8,128)S(1)}, u32[]{:S(2)}, u32[]{:S(2)}) collective-permute-start(f32[2,8,2176]{2,1,0:T(8,128)S(1)} %get-tuple-element.53.after_ref.own_ref), channel_id=1, source_target_pairs={{0,2},{1,3},{2,0},{3,1},{4,6},{5,7},{6,4},{7,5},{8,10},{9,11},{10,... | collective-permute-start | bytes 417800 | tf_op jit(solution)/shard_map/ppermute | solution.py:498
  25.1 0.7 %copy-start.8 = (f32[32]{0:T(128)S(1)}, f32[32]{0:T(128)}, u32[]{:S(2)}) copy-start(f32[32]{0:T(128)} %damping_ref.5) | copy-start | bytes 388
  27.3 4.0 %collective-permute-start.8 = (f32[2,2,8,1440]{3,2,1,0:T(8,128)S(1)}, f32[2,2,8,1440]{3,2,1,0:T(8,128)S(1)}, u32[]{:S(2)}, u32[]{:S(2)}) collective-permute-start(f32[2,2,8,1440]{3,2,1,0:T(8,128)S(1)} %get-tuple-element.60), channel_id=1, source_target_pairs={{0,1},{1,0},{2,3},{3,2},{4,5},{5,4},{6,7},{7,6},{8,9},{9,8},{10,11... | collective-permute-start | bytes 552968 | tf_op jit(solution)/shard_map/ppermute | solution.py:495
  29.3 2.0 %collective-permute-start.9 = (f32[2,1,8,1440]{3,2,1,0:T(8,128)S(1)}, f32[2,1,8,1440]{3,2,1,0:T(8,128)S(1)}, u32[]{:S(2)}, u32[]{:S(2)}) collective-permute-start(f32[2,1,8,1440]{3,2,1,0:T(8,128)S(1)} %get-tuple-element.61), channel_id=1, source_target_pairs={{0,1},{1,0},{2,3},{3,2},{4,5},{5,4},{6,7},{7,6},{8,9},{9,8},{10,11... | collective-permute-start | bytes 276488 | tf_op jit(solution)/shard_map/ppermute | solution.py:495
  30.6 1.6 %collective-permute-start.10 = (f32[2,1,8,1440]{3,2,1,0:T(8,128)S(1)}, f32[2,1,8,1440]{3,2,1,0:T(8,128)S(1)}, u32[]{:S(2)}, u32[]{:S(2)}) collective-permute-start(f32[2,1,8,1440]{3,2,1,0:T(8,128)S(1)} %get-tuple-element.62), channel_id=1, source_target_pairs={{0,1},{1,0},{2,3},{3,2},{4,5},{5,4},{6,7},{7,6},{8,9},{9,8},{10,11... | collective-permute-start | bytes 276488 | tf_op jit(solution)/shard_map/ppermute | solution.py:495

commit v5 on v4

--- a/solution.py
+++ b/solution.py
@@ -137,41 +137,47 @@
     return lax.rem(lax.axis_index("lat"), 2) == 0
 
 
-def inner_kernel(cells_ref, speed_ref, mine_ref, send_ref):
+def begin_kernel(
+    cells_hbm, speed_hbm, mine_ref, send_ref, near_ref, far_ref, near_part_ref, far_part_ref,
+    cells_ref, speed_ref, sems,
+):
     tracer_count, levels, row_count, columns = cells_ref.shape
     share = tracer_count // PAIR
     core = lax.rem(lax.axis_index("lon"), PAIR)
-    for lanes in spans(columns, 3 * LANES):
+    north = near_is_north()
+    copies = [pltpu.make_async_copy(speed_hbm, speed_ref, sems.at[tracer_count])]
+    copies += [
+        pltpu.make_async_copy(cells_hbm.at[t], cells_ref.at[t], sems.at[t]) for t in range(tracer_count)
+    ]
+    for copy in copies:
+        copy.start()
+    for copy in copies:
+        copy.wait()
+    for lanes in spans(columns, 2 * LANES):
         speed = [speed_ref[:, j, lanes] for j in range(row_count)]
+        near_ref[tracer_count * levels :, lanes] = speed[0]
+        far_ref[tracer_count * levels :, lanes] = speed[0]
         for which, out_ref in enumerate([mine_ref, send_ref]):
             for i in range(share):
                 t = lax.rem(core + which, PAIR) * share + i
+                place = pl.ds(pl.multiple_of(t * levels, levels), levels)
                 x = [cells_ref[t, :, j, lanes] for j in range(row_count)]
                 flux = [flux_of(speed[j], x[j - 1], x[j]) for j in range(1, row_count)]
                 for j in range(1, row_count - 1):
                     out_ref[i, j - 1, :, lanes] = x[j] + flux[j - 1] - flux[j]
-
-
-def outer_kernel(cells_ref, speed_ref, after_ref, near_ref, far_ref, near_part_ref, far_part_ref):
-    tracer_count, levels, row_count, columns = cells_ref.shape
-    north = near_is_north()
-    for lanes in spans(columns, 3 * LANES):
-        speed = [speed_ref[:, j, lanes] for j in (0, 1, row_count - 1)]
-        near_ref[tracer_count * levels :, lanes] = speed[0]
-        far_ref[tracer_count * levels :, lanes] = speed[0]
-        for t in range(tracer_count):
-            first, second = cells_ref[t, :, 0, lanes], cells_ref[t, :, 1, lanes]
-            third, last = cells_ref[t, :, row_count - 2, lanes], cells_ref[t, :, row_count - 1, lanes]
-            place = slice(t * levels, (t + 1) * levels)
-            near_ref[place, lanes] = jnp.where(north, last, first)
-            far_ref[place, lanes] = jnp.where(north, first, last)
-            south_part = first - flux_of(speed[1], first, second)
-            north_part = last + flux_of(speed[2], third, last)
-            near_part_ref[t, :, lanes] = jnp.where(north, north_part, south_part)
-            far_part_ref[t, :, lanes] = jnp.where(north, south_part, north_part)
-
-
-def edge_kernel(is_near, own_ref, got_ref, part_ref, after_ref, mine_ref, send_ref):
+                near_ref[place, lanes] = jnp.where(north, x[-1], x[0])
+                far_ref[place, lanes] = jnp.where(north, x[0], x[-1])
+                south_part, north_part = x[0] - flux[0], x[-1] + flux[-1]
+                near_part_ref[t, :, lanes] = jnp.where(north, north_part, south_part)
+                far_part_ref[t, :, lanes] = jnp.where(north, south_part, north_part)
+
+
+def edge_kernel(is_near, own_ref, got_ref, part_ref, after_ref, *refs):
+    if is_near:
+        source_ref, mine_ref, send_ref, relay_ref = refs
+        relay_ref[...] = source_ref[...]
+    else:
+        mine_ref, send_ref = refs
     tracer_count, levels, columns = part_ref.shape
     share = tracer_count // PAIR
     total = tracer_count * levels
@@ -191,14 +197,9 @@
                 out_ref[i, 0, :, lanes] = part_ref[t, :, lanes] + jnp.where(north, -flux, flux)
 
 
-def forward_kernel(relay, *refs):
-    if relay:
-        *refs, relay_ref, stack_ref = refs
-        *refs, source_ref, message_ref, held_ref = refs
-        relay_ref[...] = source_ref[...]
-    else:
-        *refs, message_ref, held_ref, stack_ref = refs
-    mine_ref, theirs_ref, phase_ref, high_ref, low_ref = refs[:5]
+def forward_kernel(
+    mine_ref, theirs_ref, phase_ref, high_ref, low_ref, after_ref, message_ref, held_ref, stack_ref
+):
     share, number, levels, columns = mine_ref.shape
     piece = columns * PAIR // HALF
     padded = stack_ref.shape[1]
@@ -289,33 +290,27 @@
     return steps.astype(jnp.float32) * (2.0 * math.pi / lon_cells)
 
 
-def shift_kernel(
-    which, columns, shift_ref, fraction_ref, cutoff_ref, wave_ref, held_ref, after_ref, moved_ref, gain_ref
+def row_kernel(
+    columns, shift_ref, fraction_ref, cutoff_ref, damping_ref, wave_ref, after_ref,
+    distance_ref, share_ref, keep_ref, gain_ref,
 ):
-    _, count, levels, padded = held_ref.shape
-    rows = rows_of(which, shift_ref.shape[0])
-    number = len(rows)
+    row_count, levels = shift_ref.shape
     lon_cells = columns * PAIR * PAIR
     modes = gain_ref.shape[3]
     lat = lax.axis_index("lat")
-    for j, row in enumerate(rows):
-        distance = row_vector(shift_ref, row, levels)
-        share = row_vector(fraction_ref, row, levels)
-        for n in range(j, count, number):
-            for pos in range(PAIR):
-                tiles = [held_ref[PAIR - 1 - pos, n, :, columns - LANES : columns]]
-                tiles += [held_ref[pos, n, :, lanes] for lanes in spans(padded, LANES)]
-                for lanes, tile in zip(spans(padded, LANES), displaced(tiles, distance, share)):
-                    moved_ref[n, pos, :, lanes] = tile
+    for row in range(row_count):
+        distance_ref[row] = row_vector(shift_ref, row, levels).astype(jnp.float32)
+        share_ref[row] = row_vector(fraction_ref, row, levels)
+        keep_ref[row] = jnp.full((levels, LANES), damping_ref[lat * row_count + row])
 
     @pl.when(is_cap(lat))
     def _():
         lane = lax.broadcasted_iota(jnp.int32, (levels, modes), 1)
         mode = lane - modes // 2
-        for j, row in enumerate(rows):
-            distance = row_vector(shift_ref, row, levels)
-            share = row_vector(fraction_ref, row, levels)
-            limit = cutoff_ref[lat * shift_ref.shape[0] + row]
+        for row in range(row_count):
+            distance = distance_ref[row].astype(jnp.int32)
+            share = share_ref[row]
+            limit = cutoff_ref[lat * row_count + row]
             wide = wave_angle(RADIX * mode * distance, lon_cells)
             wide_re, wide_im = jnp.cos(wide), -jnp.sin(wide)
             fine = wave_angle(lane * distance, lon_cells)
@@ -325,7 +320,8 @@
                 kept = jnp.abs(wavenumber) <= limit
                 if r in (0, HALF):
                     kept = kept & (wavenumber >= 0)
-                weight = jnp.full((levels, modes), (1.0 if r % 2 == 0 and r not in (0, HALF) else 2.0) / lon_cells)
+                once = r % 2 == 0 and r not in (0, HALF)
+                weight = jnp.full((levels, modes), (1.0 if once else 2.0) / lon_cells)
                 if r == 0:
                     weight = jnp.where(wavenumber == 0, 1.0 / lon_cells, weight)
                 weight = jnp.where(kept, weight, 0.0)
@@ -333,28 +329,40 @@
                 mix_im = -share * wave_ref[2 * r + 1 : 2 * r + 2]
                 turn_re, turn_im = fine_re[:, r : r + 1], fine_im[:, r : r + 1]
                 re, im = wide_re * turn_re - wide_im * turn_im, wide_re * turn_im + wide_im * turn_re
-                gain_ref[j, 2 * r] = (re * mix_re - im * mix_im) * weight
-                gain_ref[j, 2 * r + 1] = (re * mix_im + im * mix_re) * weight
+                gain_ref[row, 2 * r] = (re * mix_re - im * mix_im) * weight
+                gain_ref[row, 2 * r + 1] = (re * mix_im + im * mix_re) * weight
+
+
+def shift_kernel(which, columns, distance_ref, share_ref, held_ref, after_ref, moved_ref):
+    _, count, levels, padded = held_ref.shape
+    rows = rows_of(which, share_ref.shape[0])
+    number = len(rows)
+    for j, row in enumerate(rows):
+        distance, share = distance_ref[row].astype(jnp.int32), share_ref[row]
+        for n in range(j, count, number):
+            for pos in range(PAIR):
+                tiles = [held_ref[PAIR - 1 - pos, n, :, columns - LANES : columns]]
+                tiles += [held_ref[pos, n, :, lanes] for lanes in spans(padded, LANES)]
+                for lanes, tile in zip(spans(padded, LANES), displaced(tiles, distance, share)):
+                    moved_ref[n, pos, :, lanes] = tile
 
 
 def inverse_kernel(
-    which, columns, shift_ref, fraction_ref, damping_ref, phase_ref, high_ref, low_ref,
-    held_ref, moved_ref, gain_ref, own_ref, other_ref, after_ref, mine_ref, send_ref,
+    which, columns, distance_ref, share_ref, keep_ref, gain_ref, phase_ref, high_ref, low_ref,
+    held_ref, moved_ref, own_ref, other_ref, after_ref, mine_ref, send_ref,
     stack_ref, back_ref, pair_ref,
 ):
     _, count, levels, _ = held_ref.shape
-    rows = rows_of(which, shift_ref.shape[0])
+    rows = rows_of(which, share_ref.shape[0])
     number = len(rows)
     piece = columns * PAIR // HALF
     padded = stack_ref.shape[1]
     modes = gain_ref.shape[3]
     group = levels * 2 * (HALF + 1)
-    lat = lax.axis_index("lat")
     core = lax.rem(lax.axis_index("lon"), PAIR)
-    cap = is_cap(lat)
+    cap = is_cap(lax.axis_index("lat"))
     for j, row in enumerate(rows):
-        distance = row_vector(shift_ref, row, levels)
-        share = row_vector(fraction_ref, row, levels)
+        distance, share = distance_ref[row].astype(jnp.int32), share_ref[row]
         for n in range(j, count, number):
             tiles = [other_ref[n, :, 2 * MODES :], held_ref[0, n, :, :LANES]]
             (moved_ref[n, 0, :, :LANES],) = displaced(tiles, distance, share)
@@ -369,7 +377,7 @@
     @pl.when(cap)
     def _():
         for n in range(count):
-            j = n % number
+            row = rows[n % number]
             for r in range(HALF + 1):
                 slot = r % HALF
                 ours, theirs = (
@@ -382,7 +390,7 @@
                     re, im = ours[0] + theirs[0], ours[1] + theirs[1]
                 if r == HALF:
                     re, im = pltpu.roll(re, modes // 2, 1), pltpu.roll(im, modes // 2, 1)
-                g_re, g_im = gain_ref[j, 2 * r], gain_ref[j, 2 * r + 1]
+                g_re, g_im = gain_ref[row, 2 * r], gain_ref[row, 2 * r + 1]
                 re, im = re * g_re - im * g_im, re * g_im + im * g_re
                 base = n * group + 2 * r * levels
                 back_ref[base : base + levels, :modes] = re
@@ -392,7 +400,7 @@
         stack_ref[...] = product(back_ref[...], high_ref[...], low_ref[...], 1)
         for n in range(count):
             i, j = divmod(n, number)
-            keep = damping_ref[lat * shift_ref.shape[0] + rows[j]]
+            keep = keep_ref[rows[j]]
             for tile in range(0, padded, LANES):
                 lanes = slice(tile, tile + LANES)
                 spectrum = []
@@ -418,20 +426,26 @@
 
 
 def end_kernel(*refs):
-    *refs, out_ref = refs
+    *refs, out_hbm, out_ref, sems = refs
     tracer_count, levels, row_count, columns = out_ref.shape
     share = tracer_count // PAIR
     core = lax.rem(lax.axis_index("lon"), PAIR)
     north = near_is_north()
+    copies = []
     for place, (inner, near, far) in enumerate([refs[:3], refs[3:]]):
         for i in range(share):
-            t = lax.rem(core + place, PAIR) * share + i
+            slot = place * share + i
             for lanes in spans(columns, 4 * LANES):
                 a, b = near[i, 0, :, lanes], far[i, 0, :, lanes]
-                out_ref[t, :, 0, lanes] = jnp.where(north, b, a)
-                out_ref[t, :, row_count - 1, lanes] = jnp.where(north, a, b)
+                out_ref[slot, :, 0, lanes] = jnp.where(north, b, a)
+                out_ref[slot, :, row_count - 1, lanes] = jnp.where(north, a, b)
                 for j in range(1, row_count - 1):
-                    out_ref[t, :, j, lanes] = inner[i, j - 1, :, lanes]
+                    out_ref[slot, :, j, lanes] = inner[i, j - 1, :, lanes]
+            t = lax.rem(core + place, PAIR) * share + i
+            copies.append(pltpu.make_async_copy(out_ref.at[slot], out_hbm.at[t], sems.at[slot]))
+            copies[-1].start()
+    for copy in copies:
+        copy.wait()
 
 
 def filter_tables(lon_cells):
@@ -460,16 +474,16 @@
 SMALL, WHOLE, UNREAD = pltpu.SMEM, pltpu.VMEM, pl.ANY
 
 
-def call(kernel, outs, operands, scratch=(), flops=0):
-    size = sum(4 * math.prod(shape) for shape in outs)
+def call(kernel, outs, operands, scratch=(), sems=0, place=None):
     return pl.pallas_call(
         kernel,
         out_shape=[jax.ShapeDtypeStruct(shape, jnp.float32) for shape in outs],
         in_specs=[pl.BlockSpec(memory_space=place) for _, place in operands],
-        out_specs=[pl.BlockSpec(memory_space=WHOLE)] * len(outs),
-        scratch_shapes=[pltpu.VMEM(shape, jnp.float32) for shape in scratch],
+        out_specs=[pl.BlockSpec(memory_space=place or WHOLE)] * len(outs),
+        scratch_shapes=[pltpu.VMEM(shape, jnp.float32) for shape in scratch]
+        + ([pltpu.SemaphoreType.DMA((sems,))] if sems else []),
         compiler_params=pltpu.CompilerParams(vmem_limit_bytes=24 << 20),
-        cost_estimate=pl.CostEstimate(flops=flops, bytes_accessed=2 * size, transcendentals=0),
+        cost_estimate=pl.CostEstimate(flops=1, bytes_accessed=1, transcendentals=0),
     )(*[v for v, _ in operands])
 
 
@@ -506,91 +520,90 @@
     def set_shape(number):
         return (share, number, level_count, column_count)
 
-    def forward(mine, theirs, after, relay=None):
+    def forward(mine, theirs, after):
         count = mine.shape[0] * mine.shape[1]
-        outs = [(count, level_count, 2 * MODES + LANES), (PAIR, count, level_count, width)]
-        operands = whole(mine, theirs, phase, high, low) + [(after, UNREAD)]
-        if relay is not None:
-            outs.append(relay.shape)
-            operands += whole(relay)
         return call(
-            functools.partial(forward_kernel, relay is not None),
-            outs,
-            operands,
+            forward_kernel,
+            [(count, level_count, 2 * MODES + LANES), (PAIR, count, level_count, width)],
+            whole(mine, theirs, phase, high, low) + [(after, UNREAD)],
             [(count * group, padded)],
-            2 * 3 * count * group * padded * double,
         )
 
     def shifted(which, held, after):
         count = held.shape[1]
-        number = count // share
-        return call(
+        (moved,) = call(
             functools.partial(shift_kernel, which, column_count),
-            [(count, PAIR, level_count, width), (number, 2 * (HALF + 1), level_count, double // 2)],
-            [(shift_rows, SMALL), (fraction_rows, SMALL), (cutoff, SMALL)]
-            + whole(wave, held)
-            + [(after, UNREAD)],
+            [(count, PAIR, level_count, width)],
+            whole(distance, fraction, held) + [(after, UNREAD)],
         )
-
-    def inverse(which, held, moved, gain, own, other, after):
+        return moved
+
+    def inverse(which, held, moved, own, other, after):
         count = held.shape[1]
         return call(
             functools.partial(inverse_kernel, which, column_count),
             [set_shape(count // share)] * 2,
-            [(shift_rows, SMALL), (fraction_rows, SMALL), (damping, SMALL)]
-            + whole(phase, high, low, held, moved, gain, own, other)
+            whole(distance, fraction, keep, gain, phase, high, low, held, moved, own, other)
             + [(after, UNREAD)],
             [(count * group, padded), (count * group, double), (PAIR, count, level_count, width)],
-            2 * 3 * count * group * padded * double,
         )
 
-    inner_mine, inner_send = call(
-        inner_kernel, [set_shape(row_count - 2)] * 2, whole(tracers, merid_courant)
+    edge_shape = ((tracer_count + 1) * level_count, column_count)
+    part_shape = (tracer_count, level_count, column_count)
+    inner_mine, inner_send, near_edge, far_edge, near_part, far_part = call(
+        begin_kernel,
+        [set_shape(row_count - 2)] * 2 + [edge_shape] * 2 + [part_shape] * 2,
+        [(tracers, pltpu.HBM), (merid_courant, pltpu.HBM)],
+        [tracers.shape, merid_courant.shape],
+        tracer_count + 1,
     )
     inner_theirs = swap_core(inner_send)
-    edge_shape = ((tracer_count + 1) * level_count, column_count)
-    part_shape = (tracer_count, level_count, column_count)
-    near_own, far_own, near_part, far_part = call(
-        outer_kernel,
-        [edge_shape] * 2 + [part_shape] * 2,
-        whole(tracers, merid_courant) + [(inner_mine, UNREAD)],
+    near_got = swap_band(near_edge, 0)
+    inner_own, inner_held = forward(inner_mine, inner_theirs, near_part)
+    inner_other = swap_half(inner_own)
+    row_shape = (row_count, level_count, LANES)
+    distance, fraction, keep, gain = call(
+        functools.partial(row_kernel, column_count),
+        [row_shape] * 3 + [(row_count, 2 * (HALF + 1), level_count, double // 2)],
+        [(v, SMALL) for v in (shift_rows, fraction_rows, cutoff, damping)]
+        + whole(wave)
+        + [(inner_own, UNREAD)],
     )
-    near_got = swap_band(near_own, 0)
-    inner_own, inner_held, far_relay = forward(inner_mine, inner_theirs, near_part, far_own)
-    inner_other = swap_half(inner_own)
-    far_got = swap_band(far_relay, 1)
-    inner_moved, inner_gain = shifted("inner", inner_held, inner_own)
-
-    near_mine, near_send = call(
+    inner_moved = shifted("inner", inner_held, inner_own)
+
+    near_mine, near_send, far_relay = call(
         functools.partial(edge_kernel, True),
-        [set_shape(1)] * 2,
-        whole(near_own, near_got, near_part) + [(inner_moved, UNREAD)],
+        [set_shape(1)] * 2 + [edge_shape],
+        whole(near_edge, near_got, near_part) + [(inner_moved, UNREAD)] + whole(far_edge),
     )
     near_theirs = swap_core(near_send)
-    near_own, near_held, = forward(near_mine, near_theirs, inner_moved)
+    far_got = swap_band(far_relay, 1)
+    near_own, near_held = forward(near_mine, near_theirs, inner_moved)
     near_other = swap_half(near_own)
-    near_moved, near_gain = shifted("near", near_held, near_own)
+    near_moved = shifted("near", near_held, near_own)
+    inner = inverse("inner", inner_held, inner_moved, inner_own, inner_other, near_moved)
+    inner_back = swap_core(inner[1])
 
     far_mine, far_send = call(
         functools.partial(edge_kernel, False),
         [set_shape(1)] * 2,
-        whole(far_own, far_got, far_part) + [(near_moved, UNREAD)],
+        whole(far_edge, far_got, far_part) + [(inner[0], UNREAD)],
     )
     far_theirs = swap_core(far_send)
-    far_own, far_held = forward(far_mine, far_theirs, near_moved)
+    near = inverse("near", near_held, near_moved, near_own, near_other, far_mine)
+    near_back = swap_core(near[1])
+    far_own, far_held = forward(far_mine, far_theirs, near[0])
     far_other = swap_half(far_own)
-    far_moved, far_gain = shifted("far", far_held, far_own)
-
-    inner = inverse("inner", inner_held, inner_moved, inner_gain, inner_own, inner_other, far_moved)
-    inner_back = swap_core(inner[1])
-    near = inverse("near", near_held, near_moved, near_gain, near_own, near_other, inner[0])
-    near_back = swap_core(near[1])
-    far = inverse("far", far_held, far_moved, far_gain, far_own, far_other, near[0])
+    far_moved = shifted("far", far_held, far_own)
+    far = inverse("far", far_held, far_moved, far_own, far_other, far_moved)
     far_back = swap_core(far[1])
     (result,) = call(
         end_kernel,
         [tracers.shape],
         whole(inner[0], near[0], far[0], inner_back, near_back, far_back),
+        [tracers.shape],
+        tracer_count,
+        pltpu.HBM,
     )
     return result
 

time: 33.7 us -> 34.8 us (1.033)
  waiting for transfers between devices: 2.47 us -> 7.21 us
  Pallas kernels: 13 us -> 11 us
  starting transfers between devices: 14.3 us -> 13.4 us
  local copies, waits for them, and re-layouts: 3.42 us -> 2.78 us
    ppermute x2, waiting for transfers between devices: 0.01 us -> 2.08 us  [swap_band(): return lax.ppermute(value, 'lat', pairs)]
    pallas_call x14, Pallas kernels: 13 us -> 11 us  [call(): pl.pallas_call(kernel, out_shape=[jax.ShapeDtypeStruct(shape, jnp.float32...]
    ppermute x3, waiting for transfers between devices: 0.01 us -> 1.89 us  [swap_half(): return lax.ppermute(value, 'lon', [(p, p ^ 2) for p in range(lon_count)])]
    ppermute x6, starting transfers between devices: 8.22 us -> 6.46 us  [swap_core(): return lax.ppermute(value, 'lon', [(p, p ^ 1) for p in range(lon_count)])]
    ppermute x6, waiting for transfers between devices: 2.46 us -> 3.24 us  [swap_core(): return lax.ppermute(value, 'lon', [(p, p ^ 1) for p in range(lon_count)])]
    unnamed x20, local copies, waits for them, and re-layouts: 3.42 us -> 2.78 us
    ppermute x2, starting transfers between devices: 2.56 us -> 3.18 us  [swap_band(): return lax.ppermute(value, 'lat', pairs)]
  transfers between devices with their start and end apart: 11 -> 11, of which waited for: 3 -> 7; matrix products, arithmetic and copies ran while one was open for 0% -> 0% of each run, Pallas kernels for 35% -> 20%
where the time goes in v5:
time: 34.8 us; the launch traced here: 34.6 us
  starting transfers between devices  13.4 us (39%)
  Pallas kernels  11 us (32%)
  waiting for transfers between devices  7.21 us (21%)
  local copies, waits for them, and re-layouts  2.78 us (8%)
    pallas_call x14, Pallas kernels, call(): pl.pallas_call(kernel, out_shape=[jax.ShapeDtypeStruct(shape, jnp.float32...  11 us
    ppermute x6, starting transfers between devices, swap_core(): return lax.ppermute(value, 'lon', [(p, p ^ 1) for p in range(lon_count)])  6.46 us
    ppermute x3, starting transfers between devices, swap_half(): return lax.ppermute(value, 'lon', [(p, p ^ 2) for p in range(lon_count)])  3.78 us
    ppermute x6, waiting for transfers between devices, swap_core(): return lax.ppermute(value, 'lon', [(p, p ^ 1) for p in range(lon_count)])  3.24 us
    ppermute x2, starting transfers between devices, swap_band(): return lax.ppermute(value, 'lat', pairs)  3.18 us
    unnamed x20, local copies, waits for them, and re-layouts  2.78 us
    ppermute x2, waiting for transfers between devices, swap_band(): return lax.ppermute(value, 'lat', pairs)  2.08 us
    ppermute x3, waiting for transfers between devices, swap_half(): return lax.ppermute(value, 'lon', [(p, p ^ 2) for p in range(lon_count)])  1.89 us
  transfers between devices with their start and end apart: 11, of which 7 were waited for; matrix products, arithmetic and copies ran while one was open for 0% of the time, Pallas kernels for 20%

profile of v5, /device:TPU:3, one launch (start us, length us, event | category | flops | bytes accessed | tf_op | source)
XLA Modules:
  0.0 34.6 jit_solution(6709987608880105179)
XLA Ops:
  0.0 0.0 copy-start
  0.0 0.0 copy-start.3
  0.0 1.2 %copy-done.3 = f32[4,8,4,1440]{3,2,1,0:T(4,128)S(1)} copy-done((f32[4,8,4,1440]{3,2,1,0:T(4,128)S(1)}, f32[4,8,4,1440]{3,2,1,0:T(4,128)}, u32[]{:S(2)}) %copy-start.3) | copy-done | bytes 737304
  1.2 0.9 %copy-done.4 = f32[8,4,1440]{2,1,0:T(4,128)S(1)} copy-done((f32[8,4,1440]{2,1,0:T(4,128)S(1)}, f32[8,4,1440]{2,1,0:T(4,128)}, u32[]{:S(2)}) %copy-start.4) | copy-done | bytes 184344
  2.1 2.2 %shard_map.100 = (f32[2,2,8,1440]{3,2,1,0:T(8,128)S(1)}, f32[2,2,8,1440]{3,2,1,0:T(8,128)S(1)}, f32[40,1440]{1,0:T(8,128)S(1)}, f32[40,1440]{1,0:T(8,128)S(1)}, ...) custom-call(f32[4,8,4,1440]{3,2,1,0:T(4,128)S(1)} %copy-done.3, f32[8,4,1440]{2,1,0:T(4,128)S(1)} %copy-done.4), custom_call_target="tpu_custom_call" | custom-call | flops 1 | bytes 1 | tf_op jit(solution)/shard_map/pallas_call | solution.py:478
  4.3 0.7 %collective-permute-start = (f32[2,2,8,1440]{3,2,1,0:T(8,128)S(1)}, f32[2,2,8,1440]{3,2,1,0:T(8,128)S(1)}, u32[]{:S(2)}, u32[]{:S(2)}) collective-permute-start(f32[2,2,8,1440]{3,2,1,0:T(8,128)S(1)} %get-tuple-element.33), channel_id=1, source_target_pairs={{0,1},{1,0},{2,3},{3,2},{4,5},{5,4},{6,7},{7,6},{8,9},{9,8},{10,11... | collective-permute-start | bytes 552968 | tf_op jit(solution)/shard_map/ppermute | solution.py:509
  5.1 0.0 collective-permute-start.2
  5.1 1.1 %collective-permute-done.theirs_ref = f32[2,2,8,1440]{3,2,1,0:T(8,128)S(1)} collective-permute-done((f32[2,2,8,1440]{3,2,1,0:T(8,128)S(1)}, f32[2,2,8,1440]{3,2,1,0:T(8,128)S(1)}, u32[]{:S(2)}, u32[]{:S(2)}) %collective-permute-start) | collective-permute-done | bytes 184352 | tf_op jit(solution)/shard_map/ppermute | solution.py:509
  6.2 0.0 copy-done
  6.2 0.0 copy-done.1
  6.2 0.0 copy-done.2
  6.2 1.5 %shard_map.101 = (f32[4,8,2176]{2,1,0:T(8,128)S(1)}, f32[2,4,8,1536]{3,2,1,0:T(8,128)S(1)}) custom-call(f32[2,2,8,1440]{3,2,1,0:T(8,128)S(1)} %get-tuple-element.32.mine_ref, f32[2,2,8,1440]{3,2,1,0:T(8,128)S(1)} %collective-permute-done.theirs_ref, f32[18,384]{1,0:T(8,128)S(1)} %copy-done.2, bf16[384,256]{1,0:T(8,128)(2,1)S(1)} %copy-done, ...), custom_call_target="tpu_custom_call" | custom-call | flops 1 | bytes 1 | tf_op jit(solution)/shard_map/pallas_call | solution.py:478
  7.6 1.3 %collective-permute-start.1 = (f32[4,8,2176]{2,1,0:T(8,128)S(1)}, f32[4,8,2176]{2,1,0:T(8,128)S(1)}, u32[]{:S(2)}, u32[]{:S(2)}) collective-permute-start(f32[4,8,2176]{2,1,0:T(8,128)S(1)} %get-tuple-element.35.after_ref.own_ref), channel_id=1, source_target_pairs={{0,2},{1,3},{2,0},{3,1},{4,6},{5,7},{6,4},{7,5},{8,10},{9,11},{10,... | collective-permute-start | bytes 835592 | tf_op jit(solution)/shard_map/ppermute | solution.py:512
  8.9 0.0 copy-done.5
  8.9 0.0 copy-done.7
  8.9 0.0 copy-done.6
  8.9 0.6 %copy-done.8 = s32[32]{0:T(128)S(1)} copy-done((s32[32]{0:T(128)S(1)}, s32[32]{0:T(128)}, u32[]{:S(2)}) %copy-start.8) | copy-done | bytes 152
  9.6 0.0 copy-done.9
  9.6 0.9 %shard_map.102 = (f32[4,8,128]{2,1,0:T(8,128)S(1)}, f32[4,8,128]{2,1,0:T(8,128)S(1)}, f32[4,8,128]{2,1,0:T(8,128)S(1)}, f32[4,18,8,128]{3,2,1,0:T(8,128)S(1)}) custom-call(s32[4,8]{1,0:T(4,128)S(1)} %bitcast.2, f32[4,8]{1,0:T(4,128)S(1)} %bitcast.3, s32[32]{0:T(128)S(1)} %copy-done.8, f32[32]{0:T(128)S(1)} %copy-done.9, f32[18,128]{1,0:T(8,128)S(1)} %copy-done.5, ...), custom_call_target="tpu_custom_call" | custom-call | flops 1 | bytes 1 | tf_op jit(solution)/shard_map/pallas_call | solution.py:478
  10.5 0.7 %shard_map.103.after_ref.moved_ref = f32[4,2,8,1536]{3,2,1,0:T(8,128)S(1)} custom-call(f32[4,8,128]{2,1,0:T(8,128)S(1)} %get-tuple-element.36.distance_ref, f32[4,8,128]{2,1,0:T(8,128)S(1)} %get-tuple-element.37.share_ref, f32[2,4,8,1536]{3,2,1,0:T(8,128)S(1)} %get-tuple-element.40.held_ref, f32[4,8,2176]{2,1,0:T(8,128)S(1)} %get-tuple-element.35.after_ref.own_ref), custom_call_target="tpu_custom_call" | custom-call | flops 1 | bytes 1 | tf_op jit(solution)/shard_map/pallas_call | solution.py:478
  11.2 1.5 %collective-permute-done.2.got_ref = f32[40,1440]{1,0:T(8,128)S(1)} collective-permute-done((f32[40,1440]{1,0:T(8,128)S(1)}, f32[40,1440]{1,0:T(8,128)S(1)}, u32[]{:S(2)}, u32[]{:S(2)}) %collective-permute-start.2) | collective-permute-done | bytes 230432 | tf_op jit(solution)/shard_map/ppermute | solution.py:518
  12.6 0.1 shard_map.104
  12.7 3.2 %collective-permute-start.5 = (f32[40,1440]{1,0:T(8,128)S(1)}, f32[40,1440]{1,0:T(8,128)S(1)}, u32[]{:S(2)}, u32[]{:S(2)}) collective-permute-start(f32[40,1440]{1,0:T(8,128)S(1)} %get-tuple-element.48), channel_id=1, source_target_pairs={{4,8},{8,4},{12,16},{16,12},{20,24},{24,20},{5,9},{9,5},{13,17},{1... | collective-permute-start | bytes 691208 | tf_op jit(solution)/shard_map/ppermute | solution.py:518
  15.9 1.2 %collective-permute-start.3 = (f32[2,1,8,1440]{3,2,1,0:T(8,128)S(1)}, f32[2,1,8,1440]{3,2,1,0:T(8,128)S(1)}, u32[]{:S(2)}, u32[]{:S(2)}) collective-permute-start(f32[2,1,8,1440]{3,2,1,0:T(8,128)S(1)} %get-tuple-element.44), channel_id=1, source_target_pairs={{0,1},{1,0},{2,3},{3,2},{4,5},{5,4},{6,7},{7,6},{8,9},{9,8},{10,11... | collective-permute-start | bytes 276488 | tf_op jit(solution)/shard_map/ppermute | solution.py:509
  17.1 0.9 %collective-permute-done.3.theirs_ref = f32[2,1,8,1440]{3,2,1,0:T(8,128)S(1)} collective-permute-done((f32[2,1,8,1440]{3,2,1,0:T(8,128)S(1)}, f32[2,1,8,1440]{3,2,1,0:T(8,128)S(1)}, u32[]{:S(2)}, u32[]{:S(2)}) %collective-permute-start.3) | collective-permute-done | bytes 92192 | tf_op jit(solution)/shard_map/ppermute | solution.py:509
  18.0 0.9 %shard_map.105 = (f32[2,8,2176]{2,1,0:T(8,128)S(1)}, f32[2,2,8,1536]{3,2,1,0:T(8,128)S(1)}) custom-call(f32[2,1,8,1440]{3,2,1,0:T(8,128)S(1)} %get-tuple-element.43.mine_ref, f32[2,1,8,1440]{3,2,1,0:T(8,128)S(1)} %collective-permute-done.3.theirs_ref, f32[18,384]{1,0:T(8,128)S(1)} %copy-done.2, bf16[384,256]{1,0:T(8,128)(2,1)S(1)} %copy-done, ...), custom_call_target="tpu_custom_call" | custom-call | flops 1 | bytes 1 | tf_op jit(solution)/shard_map/pallas_call | solution.py:478
  18.9 1.3 %collective-permute-start.4 = (f32[2,8,2176]{2,1,0:T(8,128)S(1)}, f32[2,8,2176]{2,1,0:T(8,128)S(1)}, u32[]{:S(2)}, u32[]{:S(2)}) collective-permute-start(f32[2,8,2176]{2,1,0:T(8,128)S(1)} %get-tuple-element.46.after_ref.own_ref), channel_id=1, source_target_pairs={{0,2},{1,3},{2,0},{3,1},{4,6},{5,7},{6,4},{7,5},{8,10},{9,11},{10,... | collective-permute-start | bytes 417800 | tf_op jit(solution)/shard_map/ppermute | solution.py:512
  20.2 0.3 shard_map.106.after_ref.moved_ref
  20.5 0.0 collective-permute-done.1.other_ref
  20.5 1.0 %shard_map.107 = (f32[2,2,8,1440]{3,2,1,0:T(8,128)S(1)}, f32[2,2,8,1440]{3,2,1,0:T(8,128)S(1)}) custom-call(f32[4,8,128]{2,1,0:T(8,128)S(1)} %get-tuple-element.36.distance_ref, f32[4,8,128]{2,1,0:T(8,128)S(1)} %get-tuple-element.37.share_ref, f32[4,8,128]{2,1,0:T(8,128)S(1)} %get-tuple-element.38.keep_ref, ...), custom_call_target="tpu_custom_call" | custom-call | flops 1 | bytes 1 | tf_op jit(solution)/shard_map/pallas_call | solution.py:478
  21.5 0.6 %collective-permute-done.5.got_ref = f32[40,1440]{1,0:T(8,128)S(1)} collective-permute-done((f32[40,1440]{1,0:T(8,128)S(1)}, f32[40,1440]{1,0:T(8,128)S(1)}, u32[]{:S(2)}, u32[]{:S(2)}) %collective-permute-start.5) | collective-permute-done | bytes 230432 | tf_op jit(solution)/shard_map/ppermute | solution.py:518
  22.1 0.1 shard_map.108
  22.2 1.8 %collective-permute-start.6 = (f32[2,1,8,1440]{3,2,1,0:T(8,128)S(1)}, f32[2,1,8,1440]{3,2,1,0:T(8,128)S(1)}, u32[]{:S(2)}, u32[]{:S(2)}) collective-permute-start(f32[2,1,8,1440]{3,2,1,0:T(8,128)S(1)} %get-tuple-element.52), channel_id=1, source_target_pairs={{0,1},{1,0},{2,3},{3,2},{4,5},{5,4},{6,7},{7,6},{8,9},{9,8},{10,11... | collective-permute-start | bytes 276488 | tf_op jit(solution)/shard_map/ppermute | solution.py:509
  24.0 0.0 collective-permute-done.4.other_ref
  24.0 0.6 %shard_map.109 = (f32[2,1,8,1440]{3,2,1,0:T(8,128)S(1)}, f32[2,1,8,1440]{3,2,1,0:T(8,128)S(1)}) custom-call(f32[4,8,128]{2,1,0:T(8,128)S(1)} %get-tuple-element.36.distance_ref, f32[4,8,128]{2,1,0:T(8,128)S(1)} %get-tuple-element.37.share_ref, f32[4,8,128]{2,1,0:T(8,128)S(1)} %get-tuple-element.38.keep_ref, ...), custom_call_target="tpu_custom_call" | custom-call | flops 1 | bytes 1 | tf_op jit(solution)/shard_map/pallas_call | solution.py:478
  24.7 0.3 collective-permute-done.6.theirs_ref
  24.9 0.9 %shard_map.110 = (f32[2,8,2176]{2,1,0:T(8,128)S(1)}, f32[2,2,8,1536]{3,2,1,0:T(8,128)S(1)}) custom-call(f32[2,1,8,1440]{3,2,1,0:T(8,128)S(1)} %get-tuple-element.50.after_ref.mine_ref, f32[2,1,8,1440]{3,2,1,0:T(8,128)S(1)} %collective-permute-done.6.theirs_ref, f32[18,384]{1,0:T(8,128)S(1)} %copy-done.2, bf16[384,256]{1,0:T(8,128)(2,1)S(1)} %copy-done, ...), custom_call_target="tpu_custom_call" | custom-call | flops 1 | bytes 1 | tf_op jit(solution)/shard_map/pallas_call | solution.py:478
  25.8 1.3 %collective-permute-start.7 = (f32[2,8,2176]{2,1,0:T(8,128)S(1)}, f32[2,8,2176]{2,1,0:T(8,128)S(1)}, u32[]{:S(2)}, u32[]{:S(2)}) collective-permute-start(f32[2,8,2176]{2,1,0:T(8,128)S(1)} %get-tuple-element.54.after_ref.own_ref), channel_id=1, source_target_pairs={{0,2},{1,3},{2,0},{3,1},{4,6},{5,7},{6,4},{7,5},{8,10},{9,11},{10,... | collective-permute-start | bytes 417800 | tf_op jit(solution)/shard_map/ppermute | solution.py:512
  27.1 1.0 %collective-permute-start.8 = (f32[2,2,8,1440]{3,2,1,0:T(8,128)S(1)}, f32[2,2,8,1440]{3,2,1,0:T(8,128)S(1)}, u32[]{:S(2)}, u32[]{:S(2)}) collective-permute-start(f32[2,2,8,1440]{3,2,1,0:T(8,128)S(1)} %get-tuple-element.56), channel_id=1, source_target_pairs={{0,1},{1,0},{2,3},{3,2},{4,5},{5,4},{6,7},{7,6},{8,9},{9,8},{10,11... | collective-permute-start | bytes 552968 | tf_op jit(solution)/shard_map/ppermute | solution.py:509
  28.1 0.0 collective-permute-start.9
  28.1 0.3 shard_map.111.moved_ref.after_ref
  28.4 1.9 %collective-permute-done.7.other_ref = f32[2,8,2176]{2,1,0:T(8,128)S(1)} collective-permute-done((f32[2,8,2176]{2,1,0:T(8,128)S(1)}, f32[2,8,2176]{2,1,0:T(8,128)S(1)}, u32[]{:S(2)}, u32[]{:S(2)}) %collective-permute-start.7) | collective-permute-done | bytes 139296 | tf_op jit(solution)/shard_map/ppermute | solution.py:512
  30.3 0.7 %shard_map.112 = (f32[2,1,8,1440]{3,2,1,0:T(8,128)S(1)}, f32[2,1,8,1440]{3,2,1,0:T(8,128)S(1)}) custom-call(f32[4,8,128]{2,1,0:T(8,128)S(1)} %get-tuple-element.36.distance_ref, f32[4,8,128]{2,1,0:T(8,128)S(1)} %get-tuple-element.37.share_ref, f32[4,8,128]{2,1,0:T(8,128)S(1)} %get-tuple-element.38.keep_ref, ...), custom_call_target="tpu_custom_call" | custom-call | flops 1 | bytes 1 | tf_op jit(solution)/shard_map/pallas_call | solution.py:478
  31.0 1.7 %collective-permute-start.10 = (f32[2,1,8,1440]{3,2,1,0:T(8,128)S(1)}, f32[2,1,8,1440]{3,2,1,0:T(8,128)S(1)}, u32[]{:S(2)}, u32[]{:S(2)}) collective-permute-start(f32[2,1,8,1440]{3,2,1,0:T(8,128)S(1)} %get-tuple-element.58), channel_id=1, source_target_pairs={{0,1},{1,0},{2,3},{3,2},{4,5},{5,4},{6,7},{7,6},{8,9},{9,8},{10,11... | collective-permute-start | bytes 276488 | tf_op jit(solution)/shard_map/ppermute | solution.py:509
  32.7 0.0 collective-permute-done.9.refs_4_
  32.7 0.0 collective-permute-done.8.refs_3_
  32.7 0.9 %collective-permute-done.10.refs_5_ = f32[2,1,8,1440]{3,2,1,0:T(8,128)S(1)} collective-permute-done((f32[2,1,8,1440]{3,2,1,0:T(8,128)S(1)}, f32[2,1,8,1440]{3,2,1,0:T(8,128)S(1)}, u32[]{:S(2)}, u32[]{:S(2)}) %collective-permute-start.10) | collective-permute-done | bytes 92192 | tf_op jit(solution)/shard_map/ppermute | solution.py:509
  33.6 1.0 %shard_map.113 = f32[4,8,4,1440]{3,2,1,0:T(4,128)} custom-call(f32[2,2,8,1440]{3,2,1,0:T(8,128)S(1)} %get-tuple-element.47.after_ref.refs_0_, f32[2,1,8,1440]{3,2,1,0:T(8,128)S(1)} %get-tuple-element.51.after_ref.refs_1_, f32[2,1,8,1440]{3,2,1,0:T(8,128)S(1)} %get-tuple-element.55.refs_2_, f32[2,2,8,1440]{3,2,1,0:T(8,128)S(1)} %collective-permute-done.8.refs_3_, ...), custom_call_target="tpu_custom_call" | custom-call | flops 1 | bytes 1 | tf_op jit(solution)/shard_map/pallas_call | solution.py:478
  (8 shorter events, 0.0 us)
Async XLA Ops:
  0.0 6.2 %copy-start = (bf16[384,256]{1,0:T(8,128)(2,1)S(1)}, bf16[384,256]{1,0:T(8,128)(2,1)}, u32[]{:S(2)}) copy-start(bf16[384,256]{1,0:T(8,128)(2,1)} %constant.10.clone.high_ref) | copy-start | bytes 589828
  0.0 6.2 %copy-start.1 = (bf16[384,256]{1,0:T(8,128)(2,1)S(1)}, bf16[384,256]{1,0:T(8,128)(2,1)}, u32[]{:S(2)}) copy-start(bf16[384,256]{1,0:T(8,128)(2,1)} %constant.11.clone.low_ref) | copy-start | bytes 589828
  0.0 6.2 %copy-start.2 = (f32[18,384]{1,0:T(8,128)S(1)}, f32[18,384]{1,0:T(8,128)}, u32[]{:S(2)}) copy-start(f32[18,384]{1,0:T(8,128)} %constant.8.clone.phase_ref) | copy-start | bytes 82948
  0.0 1.2 %copy-start.3 = (f32[4,8,4,1440]{3,2,1,0:T(4,128)S(1)}, f32[4,8,4,1440]{3,2,1,0:T(4,128)}, u32[]{:S(2)}) copy-start(f32[4,8,4,1440]{3,2,1,0:T(4,128)} %cells_hbm.1) | copy-start | bytes 2211844
  1.2 0.9 %copy-start.4 = (f32[8,4,1440]{2,1,0:T(4,128)S(1)}, f32[8,4,1440]{2,1,0:T(4,128)}, u32[]{:S(2)}) copy-start(f32[8,4,1440]{2,1,0:T(4,128)} %speed_hbm.1) | copy-start | bytes 552964
  4.3 1.8 %collective-permute-start = (f32[2,2,8,1440]{3,2,1,0:T(8,128)S(1)}, f32[2,2,8,1440]{3,2,1,0:T(8,128)S(1)}, u32[]{:S(2)}, u32[]{:S(2)}) collective-permute-start(f32[2,2,8,1440]{3,2,1,0:T(8,128)S(1)} %get-tuple-element.33), channel_id=1, source_target_pairs={{0,1},{1,0},{2,3},{3,2},{4,5},{5,4},{6,7},{7,6},{8,9},{9,8},{10,11... | collective-permute-start | bytes 552968 | tf_op jit(solution)/shard_map/ppermute | solution.py:509
  5.1 7.5 %collective-permute-start.2 = (f32[40,1440]{1,0:T(8,128)S(1)}, f32[40,1440]{1,0:T(8,128)S(1)}, u32[]{:S(2)}, u32[]{:S(2)}) collective-permute-start(f32[40,1440]{1,0:T(8,128)S(1)} %get-tuple-element.41.own_ref), channel_id=1, source_target_pairs={{0,4},{4,0},{8,12},{12,8},{16,20},{20,16},{24,28},{28,24},{1,5},{5... | collective-permute-start | bytes 691208 | tf_op jit(solution)/shard_map/ppermute | solution.py:518
  6.2 2.8 %copy-start.5 = (f32[18,128]{1,0:T(8,128)S(1)}, f32[18,128]{1,0:T(8,128)}, u32[]{:S(2)}) copy-start(f32[18,128]{1,0:T(8,128)} %constant.9.clone.wave_ref) | copy-start | bytes 27652
  7.6 1.3 %copy-start.7 = (f32[8,4]{0,1:T(4,128)S(1)}, f32[8,4]{0,1:T(4,128)}, u32[]{:S(2)}) copy-start(f32[8,4]{0,1:T(4,128)} %param.13) | copy-start | bytes 388
  7.6 1.3 %copy-start.6 = (s32[8,4]{0,1:T(4,128)S(1)}, s32[8,4]{0,1:T(4,128)}, u32[]{:S(2)}) copy-start(s32[8,4]{0,1:T(4,128)} %param.12) | copy-start | bytes 388
  7.6 12.9 %collective-permute-start.1 = (f32[4,8,2176]{2,1,0:T(8,128)S(1)}, f32[4,8,2176]{2,1,0:T(8,128)S(1)}, u32[]{:S(2)}, u32[]{:S(2)}) collective-permute-start(f32[4,8,2176]{2,1,0:T(8,128)S(1)} %get-tuple-element.35.after_ref.own_ref), channel_id=1, source_target_pairs={{0,2},{1,3},{2,0},{3,1},{4,6},{5,7},{6,4},{7,5},{8,10},{9,11},{10,... | collective-permute-start | bytes 835592 | tf_op jit(solution)/shard_map/ppermute | solution.py:512
  8.9 0.7 %copy-start.8 = (s32[32]{0:T(128)S(1)}, s32[32]{0:T(128)}, u32[]{:S(2)}) copy-start(s32[32]{0:T(128)} %cutoff_ref.1) | copy-start | bytes 388
  8.9 0.7 %copy-start.9 = (f32[32]{0:T(128)S(1)}, f32[32]{0:T(128)}, u32[]{:S(2)}) copy-start(f32[32]{0:T(128)} %damping_ref.1) | copy-start | bytes 388
  12.7 9.4 %collective-permute-start.5 = (f32[40,1440]{1,0:T(8,128)S(1)}, f32[40,1440]{1,0:T(8,128)S(1)}, u32[]{:S(2)}, u32[]{:S(2)}) collective-permute-start(f32[40,1440]{1,0:T(8,128)S(1)} %get-tuple-element.48), channel_id=1, source_target_pairs={{4,8},{8,4},{12,16},{16,12},{20,24},{24,20},{5,9},{9,5},{13,17},{1... | collective-permute-start | bytes 691208 | tf_op jit(solution)/shard_map/ppermute | solution.py:518
  15.9 2.1 %collective-permute-start.3 = (f32[2,1,8,1440]{3,2,1,0:T(8,128)S(1)}, f32[2,1,8,1440]{3,2,1,0:T(8,128)S(1)}, u32[]{:S(2)}, u32[]{:S(2)}) collective-permute-start(f32[2,1,8,1440]{3,2,1,0:T(8,128)S(1)} %get-tuple-element.44), channel_id=1, source_target_pairs={{0,1},{1,0},{2,3},{3,2},{4,5},{5,4},{6,7},{7,6},{8,9},{9,8},{10,11... | collective-permute-start | bytes 276488 | tf_op jit(solution)/shard_map/ppermute | solution.py:509
  18.9 5.1 %collective-permute-start.4 = (f32[2,8,2176]{2,1,0:T(8,128)S(1)}, f32[2,8,2176]{2,1,0:T(8,128)S(1)}, u32[]{:S(2)}, u32[]{:S(2)}) collective-permute-start(f32[2,8,2176]{2,1,0:T(8,128)S(1)} %get-tuple-element.46.after_ref.own_ref), channel_id=1, source_target_pairs={{0,2},{1,3},{2,0},{3,1},{4,6},{5,7},{6,4},{7,5},{8,10},{9,11},{10,... | collective-permute-start | bytes 417800 | tf_op jit(solution)/shard_map/ppermute | solution.py:512
  22.2 2.8 %collective-permute-start.6 = (f32[2,1,8,1440]{3,2,1,0:T(8,128)S(1)}, f32[2,1,8,1440]{3,2,1,0:T(8,128)S(1)}, u32[]{:S(2)}, u32[]{:S(2)}) collective-permute-start(f32[2,1,8,1440]{3,2,1,0:T(8,128)S(1)} %get-tuple-element.52), channel_id=1, source_target_pairs={{0,1},{1,0},{2,3},{3,2},{4,5},{5,4},{6,7},{7,6},{8,9},{9,8},{10,11... | collective-permute-start | bytes 276488 | tf_op jit(solution)/shard_map/ppermute | solution.py:509
  25.8 4.5 %collective-permute-start.7 = (f32[2,8,2176]{2,1,0:T(8,128)S(1)}, f32[2,8,2176]{2,1,0:T(8,128)S(1)}, u32[]{:S(2)}, u32[]{:S(2)}) collective-permute-start(f32[2,8,2176]{2,1,0:T(8,128)S(1)} %get-tuple-element.54.after_ref.own_ref), channel_id=1, source_target_pairs={{0,2},{1,3},{2,0},{3,1},{4,6},{5,7},{6,4},{7,5},{8,10},{9,11},{10,... | collective-permute-start | bytes 417800 | tf_op jit(solution)/shard_map/ppermute | solution.py:512
  27.1 5.6 %collective-permute-start.8 = (f32[2,2,8,1440]{3,2,1,0:T(8,128)S(1)}, f32[2,2,8,1440]{3,2,1,0:T(8,128)S(1)}, u32[]{:S(2)}, u32[]{:S(2)}) collective-permute-start(f32[2,2,8,1440]{3,2,1,0:T(8,128)S(1)} %get-tuple-element.56), channel_id=1, source_target_pairs={{0,1},{1,0},{2,3},{3,2},{4,5},{5,4},{6,7},{7,6},{8,9},{9,8},{10,11... | collective-permute-start | bytes 552968 | tf_op jit(solution)/shard_map/ppermute | solution.py:509
  28.1 4.6 %collective-permute-start.9 = (f32[2,1,8,1440]{3,2,1,0:T(8,128)S(1)}, f32[2,1,8,1440]{3,2,1,0:T(8,128)S(1)}, u32[]{:S(2)}, u32[]{:S(2)}) collective-permute-start(f32[2,1,8,1440]{3,2,1,0:T(8,128)S(1)} %get-tuple-element.57), channel_id=1, source_target_pairs={{0,1},{1,0},{2,3},{3,2},{4,5},{5,4},{6,7},{7,6},{8,9},{9,8},{10,11... | collective-permute-start | bytes 276488 | tf_op jit(solution)/shard_map/ppermute | solution.py:509
  31.0 2.6 %collective-permute-start.10 = (f32[2,1,8,1440]{3,2,1,0:T(8,128)S(1)}, f32[2,1,8,1440]{3,2,1,0:T(8,128)S(1)}, u32[]{:S(2)}, u32[]{:S(2)}) collective-permute-start(f32[2,1,8,1440]{3,2,1,0:T(8,128)S(1)} %get-tuple-element.58), channel_id=1, source_target_pairs={{0,1},{1,0},{2,3},{3,2},{4,5},{5,4},{6,7},{7,6},{8,9},{9,8},{10,11... | collective-permute-start | bytes 276488 | tf_op jit(solution)/shard_map/ppermute | solution.py:509

commit v6 on v5

--- a/solution.py
+++ b/solution.py
@@ -138,21 +138,12 @@
 
 
 def begin_kernel(
-    cells_hbm, speed_hbm, mine_ref, send_ref, near_ref, far_ref, near_part_ref, far_part_ref,
-    cells_ref, speed_ref, sems,
+    cells_ref, speed_ref, mine_ref, send_ref, near_ref, far_ref, near_part_ref, far_part_ref
 ):
     tracer_count, levels, row_count, columns = cells_ref.shape
     share = tracer_count // PAIR
     core = lax.rem(lax.axis_index("lon"), PAIR)
     north = near_is_north()
-    copies = [pltpu.make_async_copy(speed_hbm, speed_ref, sems.at[tracer_count])]
-    copies += [
-        pltpu.make_async_copy(cells_hbm.at[t], cells_ref.at[t], sems.at[t]) for t in range(tracer_count)
-    ]
-    for copy in copies:
-        copy.start()
-    for copy in copies:
-        copy.wait()
     for lanes in spans(columns, 2 * LANES):
         speed = [speed_ref[:, j, lanes] for j in range(row_count)]
         near_ref[tracer_count * levels :, lanes] = speed[0]
@@ -172,12 +163,7 @@
                 far_part_ref[t, :, lanes] = jnp.where(north, south_part, north_part)
 
 
-def edge_kernel(is_near, own_ref, got_ref, part_ref, after_ref, *refs):
-    if is_near:
-        source_ref, mine_ref, send_ref, relay_ref = refs
-        relay_ref[...] = source_ref[...]
-    else:
-        mine_ref, send_ref = refs
+def edge_kernel(is_near, own_ref, got_ref, part_ref, after_ref, mine_ref, send_ref):
     tracer_count, levels, columns = part_ref.shape
     share = tracer_count // PAIR
     total = tracer_count * levels
@@ -333,7 +319,12 @@
                 gain_ref[row, 2 * r + 1] = (re * mix_im + im * mix_re) * weight
 
 
-def shift_kernel(which, columns, distance_ref, share_ref, held_ref, after_ref, moved_ref):
+def shift_kernel(which, columns, distance_ref, share_ref, held_ref, after_ref, *refs):
+    if which == "inner":
+        source_ref, moved_ref, relay_ref = refs
+        relay_ref[...] = source_ref[...]
+    else:
+        (moved_ref,) = refs
     _, count, levels, padded = held_ref.shape
     rows = rows_of(which, share_ref.shape[0])
     number = len(rows)
@@ -529,14 +520,13 @@
             [(count * group, padded)],
         )
 
-    def shifted(which, held, after):
+    def shifted(which, held, after, *relay):
         count = held.shape[1]
-        (moved,) = call(
+        return call(
             functools.partial(shift_kernel, which, column_count),
-            [(count, PAIR, level_count, width)],
-            whole(distance, fraction, held) + [(after, UNREAD)],
+            [(count, PAIR, level_count, width)] + [v.shape for v in relay],
+            whole(distance, fraction, held) + [(after, UNREAD)] + whole(*relay),
         )
-        return moved
 
     def inverse(which, held, moved, own, other, after):
         count = held.shape[1]
@@ -553,9 +543,7 @@
     inner_mine, inner_send, near_edge, far_edge, near_part, far_part = call(
         begin_kernel,
         [set_shape(row_count - 2)] * 2 + [edge_shape] * 2 + [part_shape] * 2,
-        [(tracers, pltpu.HBM), (merid_courant, pltpu.HBM)],
-        [tracers.shape, merid_courant.shape],
-        tracer_count + 1,
+        whole(tracers, merid_courant),
     )
     inner_theirs = swap_core(inner_send)
     near_got = swap_band(near_edge, 0)
@@ -569,18 +557,18 @@
         + whole(wave)
         + [(inner_own, UNREAD)],
     )
-    inner_moved = shifted("inner", inner_held, inner_own)
-
-    near_mine, near_send, far_relay = call(
+    inner_moved, far_relay = shifted("inner", inner_held, inner_own, far_edge)
+    far_got = swap_band(far_relay, 1)
+
+    near_mine, near_send = call(
         functools.partial(edge_kernel, True),
-        [set_shape(1)] * 2 + [edge_shape],
-        whole(near_edge, near_got, near_part) + [(inner_moved, UNREAD)] + whole(far_edge),
+        [set_shape(1)] * 2,
+        whole(near_edge, near_got, near_part) + [(inner_moved, UNREAD)],
     )
     near_theirs = swap_core(near_send)
-    far_got = swap_band(far_relay, 1)
     near_own, near_held = forward(near_mine, near_theirs, inner_moved)
     near_other = swap_half(near_own)
-    near_moved = shifted("near", near_held, near_own)
+    (near_moved,) = shifted("near", near_held, near_own)
     inner = inverse("inner", inner_held, inner_moved, inner_own, inner_other, near_moved)
     inner_back = swap_core(inner[1])
 
@@ -590,12 +578,12 @@
         whole(far_edge, far_got, far_part) + [(inner[0], UNREAD)],
     )
     far_theirs = swap_core(far_send)
-    near = inverse("near", near_held, near_moved, near_own, near_other, far_mine)
+    far_own, far_held = forward(far_mine, far_theirs, inner[0])
+    far_other = swap_half(far_own)
+    (far_moved,) = shifted("far", far_held, far_own)
+    near = inverse("near", near_held, near_moved, near_own, near_other, far_moved)
     near_back = swap_core(near[1])
-    far_own, far_held = forward(far_mine, far_theirs, near[0])
-    far_other = swap_half(far_own)
-    far_moved = shifted("far", far_held, far_own)
-    far = inverse("far", far_held, far_moved, far_own, far_other, far_moved)
+    far = inverse("far", far_held, far_moved, far_own, far_other, near[0])
     far_back = swap_core(far[1])
     (result,) = call(
         end_kernel,

time: 34.8 us -> 33.2 us (0.954)
  starting transfers between devices: 13.4 us -> 10.1 us
  waiting for transfers between devices: 7.21 us -> 10.1 us
  Pallas kernels: 11 us -> 9.77 us
    ppermute x3, starting transfers between devices: 3.78 us -> 2.07 us  [swap_half(): return lax.ppermute(value, 'lon', [(p, p ^ 2) for p in range(lon_count)])]
    ppermute x2, waiting for transfers between devices: 2.08 us -> 3.59 us  [swap_band(): return lax.ppermute(value, 'lat', pairs)]
    pallas_call x14, Pallas kernels: 11 us -> 9.77 us  [call(): pl.pallas_call(kernel, out_shape=[jax.ShapeDtypeStruct(shape, jnp.float32...]
    ppermute x2, starting transfers between devices: 3.18 us -> 1.92 us  [swap_band(): return lax.ppermute(value, 'lat', pairs)]
    ppermute x3, waiting for transfers between devices: 1.89 us -> 2.89 us  [swap_half(): return lax.ppermute(value, 'lon', [(p, p ^ 2) for p in range(lon_count)])]
    ppermute x6, waiting for transfers between devices: 3.24 us -> 3.66 us  [swap_core(): return lax.ppermute(value, 'lon', [(p, p ^ 1) for p in range(lon_count)])]
    ppermute x6, starting transfers between devices: 6.46 us -> 6.08 us  [swap_core(): return lax.ppermute(value, 'lon', [(p, p ^ 1) for p in range(lon_count)])]
  transfers between devices with their start and end apart: 11 -> 11, of which waited for: 7 -> 7; matrix products, arithmetic and copies ran while one was open for 0% -> 0% of each run, Pallas kernels for 20% -> 24%
where the time goes in v6:
time: 33.2 us; the launch traced here: 32.9 us
  starting transfers between devices  10.1 us (30%)
  waiting for transfers between devices  10.1 us (30%)
  Pallas kernels  9.77 us (29%)
  local copies, waits for them, and re-layouts  2.78 us (8%)
    pallas_call x14, Pallas kernels, call(): pl.pallas_call(kernel, out_shape=[jax.ShapeDtypeStruct(shape, jnp.float32...  9.77 us
    ppermute x6, starting transfers between devices, swap_core(): return lax.ppermute(value, 'lon', [(p, p ^ 1) for p in range(lon_count)])  6.08 us
    ppermute x6, waiting for transfers between devices, swap_core(): return lax.ppermute(value, 'lon', [(p, p ^ 1) for p in range(lon_count)])  3.66 us
    ppermute x2, waiting for transfers between devices, swap_band(): return lax.ppermute(value, 'lat', pairs)  3.59 us
    ppermute x3, waiting for transfers between devices, swap_half(): return lax.ppermute(value, 'lon', [(p, p ^ 2) for p in range(lon_count)])  2.89 us
    unnamed x20, local copies, waits for them, and re-layouts  2.78 us
    ppermute x3, starting transfers between devices, swap_half(): return lax.ppermute(value, 'lon', [(p, p ^ 2) for p in range(lon_count)])  2.07 us
    ppermute x2, starting transfers between devices, swap_band(): return lax.ppermute(value, 'lat', pairs)  1.92 us
  transfers between devices with their start and end apart: 11, of which 7 were waited for; matrix products, arithmetic and copies ran while one was open for 0% of the time, Pallas kernels for 24%

profile of v6, /device:TPU:3, one launch (start us, length us, event | category | flops | bytes accessed | tf_op | source)
XLA Modules:
  0.0 32.9 jit_solution(4998854027506729214)
XLA Ops:
  0.0 0.0 copy-start
  0.0 0.0 copy-start.3
  0.0 1.2 %copy-done.3 = f32[4,8,4,1440]{3,2,1,0:T(4,128)S(1)} copy-done((f32[4,8,4,1440]{3,2,1,0:T(4,128)S(1)}, f32[4,8,4,1440]{3,2,1,0:T(4,128)}, u32[]{:S(2)}) %copy-start.3) | copy-done | bytes 737304
  1.2 0.9 %copy-done.4 = f32[8,4,1440]{2,1,0:T(4,128)S(1)} copy-done((f32[8,4,1440]{2,1,0:T(4,128)S(1)}, f32[8,4,1440]{2,1,0:T(4,128)}, u32[]{:S(2)}) %copy-start.4) | copy-done | bytes 184344
  2.1 0.9 %shard_map.100 = (f32[2,2,8,1440]{3,2,1,0:T(8,128)S(1)}, f32[2,2,8,1440]{3,2,1,0:T(8,128)S(1)}, f32[40,1440]{1,0:T(8,128)S(1)}, f32[40,1440]{1,0:T(8,128)S(1)}, ...) custom-call(f32[4,8,4,1440]{3,2,1,0:T(4,128)S(1)} %copy-done.3, f32[8,4,1440]{2,1,0:T(4,128)S(1)} %copy-done.4), custom_call_target="tpu_custom_call" | custom-call | flops 1 | bytes 1 | tf_op jit(solution)/shard_map/pallas_call | solution.py:469
  3.1 0.7 %collective-permute-start = (f32[2,2,8,1440]{3,2,1,0:T(8,128)S(1)}, f32[2,2,8,1440]{3,2,1,0:T(8,128)S(1)}, u32[]{:S(2)}, u32[]{:S(2)}) collective-permute-start(f32[2,2,8,1440]{3,2,1,0:T(8,128)S(1)} %get-tuple-element.34), channel_id=1, source_target_pairs={{0,1},{1,0},{2,3},{3,2},{4,5},{5,4},{6,7},{7,6},{8,9},{9,8},{10,11... | collective-permute-start | bytes 552968 | tf_op jit(solution)/shard_map/ppermute | solution.py:500
  3.8 0.0 collective-permute-start.2
  3.8 1.1 %collective-permute-done.theirs_ref = f32[2,2,8,1440]{3,2,1,0:T(8,128)S(1)} collective-permute-done((f32[2,2,8,1440]{3,2,1,0:T(8,128)S(1)}, f32[2,2,8,1440]{3,2,1,0:T(8,128)S(1)}, u32[]{:S(2)}, u32[]{:S(2)}) %collective-permute-start) | collective-permute-done | bytes 184352 | tf_op jit(solution)/shard_map/ppermute | solution.py:500
  4.9 0.0 copy-done
  4.9 0.0 copy-done.1
  4.9 0.0 copy-done.2
  4.9 1.5 %shard_map.101 = (f32[4,8,2176]{2,1,0:T(8,128)S(1)}, f32[2,4,8,1536]{3,2,1,0:T(8,128)S(1)}) custom-call(f32[2,2,8,1440]{3,2,1,0:T(8,128)S(1)} %get-tuple-element.33.mine_ref, f32[2,2,8,1440]{3,2,1,0:T(8,128)S(1)} %collective-permute-done.theirs_ref, f32[18,384]{1,0:T(8,128)S(1)} %copy-done.2, bf16[384,256]{1,0:T(8,128)(2,1)S(1)} %copy-done, ...), custom_call_target="tpu_custom_call" | custom-call | flops 1 | bytes 1 | tf_op jit(solution)/shard_map/pallas_call | solution.py:469
  6.3 1.3 %collective-permute-start.1 = (f32[4,8,2176]{2,1,0:T(8,128)S(1)}, f32[4,8,2176]{2,1,0:T(8,128)S(1)}, u32[]{:S(2)}, u32[]{:S(2)}) collective-permute-start(f32[4,8,2176]{2,1,0:T(8,128)S(1)} %get-tuple-element.36.after_ref.own_ref), channel_id=1, source_target_pairs={{0,2},{1,3},{2,0},{3,1},{4,6},{5,7},{6,4},{7,5},{8,10},{9,11},{10,... | collective-permute-start | bytes 835592 | tf_op jit(solution)/shard_map/ppermute | solution.py:503
  7.6 0.0 copy-done.5
  7.6 0.0 copy-done.7
  7.6 0.0 copy-done.6
  7.6 0.6 %copy-done.8 = s32[32]{0:T(128)S(1)} copy-done((s32[32]{0:T(128)S(1)}, s32[32]{0:T(128)}, u32[]{:S(2)}) %copy-start.8) | copy-done | bytes 152
  8.3 0.0 copy-done.9
  8.3 0.9 %shard_map.102 = (f32[4,8,128]{2,1,0:T(8,128)S(1)}, f32[4,8,128]{2,1,0:T(8,128)S(1)}, f32[4,8,128]{2,1,0:T(8,128)S(1)}, f32[4,18,8,128]{3,2,1,0:T(8,128)S(1)}) custom-call(s32[4,8]{1,0:T(4,128)S(1)} %bitcast.2, f32[4,8]{1,0:T(4,128)S(1)} %bitcast.3, s32[32]{0:T(128)S(1)} %copy-done.8, f32[32]{0:T(128)S(1)} %copy-done.9, f32[18,128]{1,0:T(8,128)S(1)} %copy-done.5, ...), custom_call_target="tpu_custom_call" | custom-call | flops 1 | bytes 1 | tf_op jit(solution)/shard_map/pallas_call | solution.py:469
  9.2 0.7 %shard_map.103 = (f32[4,2,8,1536]{3,2,1,0:T(8,128)S(1)}, f32[40,1440]{1,0:T(8,128)S(1)}) custom-call(f32[4,8,128]{2,1,0:T(8,128)S(1)} %get-tuple-element.37.distance_ref, f32[4,8,128]{2,1,0:T(8,128)S(1)} %get-tuple-element.38.share_ref, f32[2,4,8,1536]{3,2,1,0:T(8,128)S(1)} %get-tuple-element.41.held_ref, ...), custom_call_target="tpu_custom_call" | custom-call | flops 1 | bytes 1 | tf_op jit(solution)/shard_map/pallas_call | solution.py:469
  9.9 1.9 %collective-permute-start.5 = (f32[40,1440]{1,0:T(8,128)S(1)}, f32[40,1440]{1,0:T(8,128)S(1)}, u32[]{:S(2)}, u32[]{:S(2)}) collective-permute-start(f32[40,1440]{1,0:T(8,128)S(1)} %get-tuple-element.50), channel_id=1, source_target_pairs={{4,8},{8,4},{12,16},{16,12},{20,24},{24,20},{5,9},{9,5},{13,17},{1... | collective-permute-start | bytes 691208 | tf_op jit(solution)/shard_map/ppermute | solution.py:509
  11.8 0.0 collective-permute-done.2.got_ref
  11.8 0.1 shard_map.104
  11.9 0.8 %collective-permute-start.3 = (f32[2,1,8,1440]{3,2,1,0:T(8,128)S(1)}, f32[2,1,8,1440]{3,2,1,0:T(8,128)S(1)}, u32[]{:S(2)}, u32[]{:S(2)}) collective-permute-start(f32[2,1,8,1440]{3,2,1,0:T(8,128)S(1)} %get-tuple-element.46), channel_id=1, source_target_pairs={{0,1},{1,0},{2,3},{3,2},{4,5},{5,4},{6,7},{7,6},{8,9},{9,8},{10,11... | collective-permute-start | bytes 276488 | tf_op jit(solution)/shard_map/ppermute | solution.py:500
  12.8 0.9 %collective-permute-done.3.theirs_ref = f32[2,1,8,1440]{3,2,1,0:T(8,128)S(1)} collective-permute-done((f32[2,1,8,1440]{3,2,1,0:T(8,128)S(1)}, f32[2,1,8,1440]{3,2,1,0:T(8,128)S(1)}, u32[]{:S(2)}, u32[]{:S(2)}) %collective-permute-start.3) | collective-permute-done | bytes 92192 | tf_op jit(solution)/shard_map/ppermute | solution.py:500
  13.7 0.9 %shard_map.105 = (f32[2,8,2176]{2,1,0:T(8,128)S(1)}, f32[2,2,8,1536]{3,2,1,0:T(8,128)S(1)}) custom-call(f32[2,1,8,1440]{3,2,1,0:T(8,128)S(1)} %get-tuple-element.45.mine_ref, f32[2,1,8,1440]{3,2,1,0:T(8,128)S(1)} %collective-permute-done.3.theirs_ref, f32[18,384]{1,0:T(8,128)S(1)} %copy-done.2, bf16[384,256]{1,0:T(8,128)(2,1)S(1)} %copy-done, ...), custom_call_target="tpu_custom_call" | custom-call | flops 1 | bytes 1 | tf_op jit(solution)/shard_map/pallas_call | solution.py:469
  14.6 0.3 shard_map.106.after_ref.moved_ref
  14.9 0.0 collective-permute-done.1.other_ref
  14.9 1.0 %shard_map.107 = (f32[2,2,8,1440]{3,2,1,0:T(8,128)S(1)}, f32[2,2,8,1440]{3,2,1,0:T(8,128)S(1)}) custom-call(f32[4,8,128]{2,1,0:T(8,128)S(1)} %get-tuple-element.37.distance_ref, f32[4,8,128]{2,1,0:T(8,128)S(1)} %get-tuple-element.38.share_ref, f32[4,8,128]{2,1,0:T(8,128)S(1)} %get-tuple-element.39.keep_ref, ...), custom_call_target="tpu_custom_call" | custom-call | flops 1 | bytes 1 | tf_op jit(solution)/shard_map/pallas_call | solution.py:469
  15.9 3.6 %collective-permute-done.5.got_ref = f32[40,1440]{1,0:T(8,128)S(1)} collective-permute-done((f32[40,1440]{1,0:T(8,128)S(1)}, f32[40,1440]{1,0:T(8,128)S(1)}, u32[]{:S(2)}, u32[]{:S(2)}) %collective-permute-start.5) | collective-permute-done | bytes 230432 | tf_op jit(solution)/shard_map/ppermute | solution.py:509
  19.5 0.1 shard_map.108
  19.6 1.6 %collective-permute-start.6 = (f32[2,1,8,1440]{3,2,1,0:T(8,128)S(1)}, f32[2,1,8,1440]{3,2,1,0:T(8,128)S(1)}, u32[]{:S(2)}, u32[]{:S(2)}) collective-permute-start(f32[2,1,8,1440]{3,2,1,0:T(8,128)S(1)} %get-tuple-element.53), channel_id=1, source_target_pairs={{0,1},{1,0},{2,3},{3,2},{4,5},{5,4},{6,7},{7,6},{8,9},{9,8},{10,11... | collective-permute-start | bytes 276488 | tf_op jit(solution)/shard_map/ppermute | solution.py:500
  21.2 0.2 collective-permute-start.4
  21.4 0.7 %collective-permute-done.6.theirs_ref = f32[2,1,8,1440]{3,2,1,0:T(8,128)S(1)} collective-permute-done((f32[2,1,8,1440]{3,2,1,0:T(8,128)S(1)}, f32[2,1,8,1440]{3,2,1,0:T(8,128)S(1)}, u32[]{:S(2)}, u32[]{:S(2)}) %collective-permute-start.6) | collective-permute-done | bytes 92192 | tf_op jit(solution)/shard_map/ppermute | solution.py:500
  22.1 0.9 %shard_map.109 = (f32[2,8,2176]{2,1,0:T(8,128)S(1)}, f32[2,2,8,1536]{3,2,1,0:T(8,128)S(1)}) custom-call(f32[2,1,8,1440]{3,2,1,0:T(8,128)S(1)} %get-tuple-element.52.mine_ref, f32[2,1,8,1440]{3,2,1,0:T(8,128)S(1)} %collective-permute-done.6.theirs_ref, f32[18,384]{1,0:T(8,128)S(1)} %copy-done.2, bf16[384,256]{1,0:T(8,128)(2,1)S(1)} %copy-done, ...), custom_call_target="tpu_custom_call" | custom-call | flops 1 | bytes 1 | tf_op jit(solution)/shard_map/pallas_call | solution.py:469
  23.0 0.6 %collective-permute-start.7 = (f32[2,8,2176]{2,1,0:T(8,128)S(1)}, f32[2,8,2176]{2,1,0:T(8,128)S(1)}, u32[]{:S(2)}, u32[]{:S(2)}) collective-permute-start(f32[2,8,2176]{2,1,0:T(8,128)S(1)} %get-tuple-element.55.after_ref.own_ref), channel_id=1, source_target_pairs={{0,2},{1,3},{2,0},{3,1},{4,6},{5,7},{6,4},{7,5},{8,10},{9,11},{10,... | collective-permute-start | bytes 417800 | tf_op jit(solution)/shard_map/ppermute | solution.py:503
  23.6 0.6 %collective-permute-start.8 = (f32[2,2,8,1440]{3,2,1,0:T(8,128)S(1)}, f32[2,2,8,1440]{3,2,1,0:T(8,128)S(1)}, u32[]{:S(2)}, u32[]{:S(2)}) collective-permute-start(f32[2,2,8,1440]{3,2,1,0:T(8,128)S(1)} %get-tuple-element.58), channel_id=1, source_target_pairs={{0,1},{1,0},{2,3},{3,2},{4,5},{5,4},{6,7},{7,6},{8,9},{9,8},{10,11... | collective-permute-start | bytes 552968 | tf_op jit(solution)/shard_map/ppermute | solution.py:500
  24.2 0.3 shard_map.110.after_ref.moved_ref
  24.5 1.9 %collective-permute-done.4.other_ref = f32[2,8,2176]{2,1,0:T(8,128)S(1)} collective-permute-done((f32[2,8,2176]{2,1,0:T(8,128)S(1)}, f32[2,8,2176]{2,1,0:T(8,128)S(1)}, u32[]{:S(2)}, u32[]{:S(2)}) %collective-permute-start.4) | collective-permute-done | bytes 139296 | tf_op jit(solution)/shard_map/ppermute | solution.py:503
  26.4 0.6 %shard_map.111 = (f32[2,1,8,1440]{3,2,1,0:T(8,128)S(1)}, f32[2,1,8,1440]{3,2,1,0:T(8,128)S(1)}) custom-call(f32[4,8,128]{2,1,0:T(8,128)S(1)} %get-tuple-element.37.distance_ref, f32[4,8,128]{2,1,0:T(8,128)S(1)} %get-tuple-element.38.share_ref, f32[4,8,128]{2,1,0:T(8,128)S(1)} %get-tuple-element.39.keep_ref, ...), custom_call_target="tpu_custom_call" | custom-call | flops 1 | bytes 1 | tf_op jit(solution)/shard_map/pallas_call | solution.py:469
  27.1 1.4 %collective-permute-start.9 = (f32[2,1,8,1440]{3,2,1,0:T(8,128)S(1)}, f32[2,1,8,1440]{3,2,1,0:T(8,128)S(1)}, u32[]{:S(2)}, u32[]{:S(2)}) collective-permute-start(f32[2,1,8,1440]{3,2,1,0:T(8,128)S(1)} %get-tuple-element.59), channel_id=1, source_target_pairs={{0,1},{1,0},{2,3},{3,2},{4,5},{5,4},{6,7},{7,6},{8,9},{9,8},{10,11... | collective-permute-start | bytes 276488 | tf_op jit(solution)/shard_map/ppermute | solution.py:500
  28.5 1.0 %collective-permute-done.7.other_ref = f32[2,8,2176]{2,1,0:T(8,128)S(1)} collective-permute-done((f32[2,8,2176]{2,1,0:T(8,128)S(1)}, f32[2,8,2176]{2,1,0:T(8,128)S(1)}, u32[]{:S(2)}, u32[]{:S(2)}) %collective-permute-start.7) | collective-permute-done | bytes 139296 | tf_op jit(solution)/shard_map/ppermute | solution.py:503
  29.4 0.6 %shard_map.112 = (f32[2,1,8,1440]{3,2,1,0:T(8,128)S(1)}, f32[2,1,8,1440]{3,2,1,0:T(8,128)S(1)}) custom-call(f32[4,8,128]{2,1,0:T(8,128)S(1)} %get-tuple-element.37.distance_ref, f32[4,8,128]{2,1,0:T(8,128)S(1)} %get-tuple-element.38.share_ref, f32[4,8,128]{2,1,0:T(8,128)S(1)} %get-tuple-element.39.keep_ref, ...), custom_call_target="tpu_custom_call" | custom-call | flops 1 | bytes 1 | tf_op jit(solution)/shard_map/pallas_call | solution.py:469
  30.1 0.9 %collective-permute-start.10 = (f32[2,1,8,1440]{3,2,1,0:T(8,128)S(1)}, f32[2,1,8,1440]{3,2,1,0:T(8,128)S(1)}, u32[]{:S(2)}, u32[]{:S(2)}) collective-permute-start(f32[2,1,8,1440]{3,2,1,0:T(8,128)S(1)} %get-tuple-element.60), channel_id=1, source_target_pairs={{0,1},{1,0},{2,3},{3,2},{4,5},{5,4},{6,7},{7,6},{8,9},{9,8},{10,11... | collective-permute-start | bytes 276488 | tf_op jit(solution)/shard_map/ppermute | solution.py:500
  31.0 0.0 collective-permute-done.8.refs_3_
  31.0 0.0 collective-permute-done.9.refs_4_
  31.0 0.9 %collective-permute-done.10.refs_5_ = f32[2,1,8,1440]{3,2,1,0:T(8,128)S(1)} collective-permute-done((f32[2,1,8,1440]{3,2,1,0:T(8,128)S(1)}, f32[2,1,8,1440]{3,2,1,0:T(8,128)S(1)}, u32[]{:S(2)}, u32[]{:S(2)}) %collective-permute-start.10) | collective-permute-done | bytes 92192 | tf_op jit(solution)/shard_map/ppermute | solution.py:500
  31.9 1.0 %shard_map.113 = f32[4,8,4,1440]{3,2,1,0:T(4,128)} custom-call(f32[2,2,8,1440]{3,2,1,0:T(8,128)S(1)} %get-tuple-element.49.after_ref.refs_0_, f32[2,1,8,1440]{3,2,1,0:T(8,128)S(1)} %get-tuple-element.56.after_ref.refs_1_, f32[2,1,8,1440]{3,2,1,0:T(8,128)S(1)} %get-tuple-element.57.refs_2_, f32[2,2,8,1440]{3,2,1,0:T(8,128)S(1)} %collective-permute-done.8.refs_3_, ...), custom_call_target="tpu_custom_call" | custom-call | flops 1 | bytes 1 | tf_op jit(solution)/shard_map/pallas_call | solution.py:469
  (8 shorter events, 0.0 us)
Async XLA Ops:
  0.0 4.9 %copy-start = (bf16[384,256]{1,0:T(8,128)(2,1)S(1)}, bf16[384,256]{1,0:T(8,128)(2,1)}, u32[]{:S(2)}) copy-start(bf16[384,256]{1,0:T(8,128)(2,1)} %constant.10.clone.high_ref) | copy-start | bytes 589828
  0.0 4.9 %copy-start.1 = (bf16[384,256]{1,0:T(8,128)(2,1)S(1)}, bf16[384,256]{1,0:T(8,128)(2,1)}, u32[]{:S(2)}) copy-start(bf16[384,256]{1,0:T(8,128)(2,1)} %constant.11.clone.low_ref) | copy-start | bytes 589828
  0.0 4.9 %copy-start.2 = (f32[18,384]{1,0:T(8,128)S(1)}, f32[18,384]{1,0:T(8,128)}, u32[]{:S(2)}) copy-start(f32[18,384]{1,0:T(8,128)} %constant.8.clone.phase_ref) | copy-start | bytes 82948
  0.0 1.2 %copy-start.3 = (f32[4,8,4,1440]{3,2,1,0:T(4,128)S(1)}, f32[4,8,4,1440]{3,2,1,0:T(4,128)}, u32[]{:S(2)}) copy-start(f32[4,8,4,1440]{3,2,1,0:T(4,128)} %cells_ref.1) | copy-start | bytes 2211844
  1.2 0.9 %copy-start.4 = (f32[8,4,1440]{2,1,0:T(4,128)S(1)}, f32[8,4,1440]{2,1,0:T(4,128)}, u32[]{:S(2)}) copy-start(f32[8,4,1440]{2,1,0:T(4,128)} %speed_ref.1) | copy-start | bytes 552964
  3.1 1.8 %collective-permute-start = (f32[2,2,8,1440]{3,2,1,0:T(8,128)S(1)}, f32[2,2,8,1440]{3,2,1,0:T(8,128)S(1)}, u32[]{:S(2)}, u32[]{:S(2)}) collective-permute-start(f32[2,2,8,1440]{3,2,1,0:T(8,128)S(1)} %get-tuple-element.34), channel_id=1, source_target_pairs={{0,1},{1,0},{2,3},{3,2},{4,5},{5,4},{6,7},{7,6},{8,9},{9,8},{10,11... | collective-permute-start | bytes 552968 | tf_op jit(solution)/shard_map/ppermute | solution.py:500
  3.8 8.0 %collective-permute-start.2 = (f32[40,1440]{1,0:T(8,128)S(1)}, f32[40,1440]{1,0:T(8,128)S(1)}, u32[]{:S(2)}, u32[]{:S(2)}) collective-permute-start(f32[40,1440]{1,0:T(8,128)S(1)} %get-tuple-element.44.own_ref), channel_id=1, source_target_pairs={{0,4},{4,0},{8,12},{12,8},{16,20},{20,16},{24,28},{28,24},{1,5},{5... | collective-permute-start | bytes 691208 | tf_op jit(solution)/shard_map/ppermute | solution.py:509
  4.9 2.8 %copy-start.5 = (f32[18,128]{1,0:T(8,128)S(1)}, f32[18,128]{1,0:T(8,128)}, u32[]{:S(2)}) copy-start(f32[18,128]{1,0:T(8,128)} %constant.9.clone.wave_ref) | copy-start | bytes 27652
  6.3 1.3 %copy-start.7 = (f32[8,4]{0,1:T(4,128)S(1)}, f32[8,4]{0,1:T(4,128)}, u32[]{:S(2)}) copy-start(f32[8,4]{0,1:T(4,128)} %param.13) | copy-start | bytes 388
  6.3 1.3 %copy-start.6 = (s32[8,4]{0,1:T(4,128)S(1)}, s32[8,4]{0,1:T(4,128)}, u32[]{:S(2)}) copy-start(s32[8,4]{0,1:T(4,128)} %param.12) | copy-start | bytes 388
  6.3 8.6 %collective-permute-start.1 = (f32[4,8,2176]{2,1,0:T(8,128)S(1)}, f32[4,8,2176]{2,1,0:T(8,128)S(1)}, u32[]{:S(2)}, u32[]{:S(2)}) collective-permute-start(f32[4,8,2176]{2,1,0:T(8,128)S(1)} %get-tuple-element.36.after_ref.own_ref), channel_id=1, source_target_pairs={{0,2},{1,3},{2,0},{3,1},{4,6},{5,7},{6,4},{7,5},{8,10},{9,11},{10,... | collective-permute-start | bytes 835592 | tf_op jit(solution)/shard_map/ppermute | solution.py:503
  7.6 0.7 %copy-start.8 = (s32[32]{0:T(128)S(1)}, s32[32]{0:T(128)}, u32[]{:S(2)}) copy-start(s32[32]{0:T(128)} %cutoff_ref.1) | copy-start | bytes 388
  7.6 0.7 %copy-start.9 = (f32[32]{0:T(128)S(1)}, f32[32]{0:T(128)}, u32[]{:S(2)}) copy-start(f32[32]{0:T(128)} %damping_ref.1) | copy-start | bytes 388
  9.9 9.6 %collective-permute-start.5 = (f32[40,1440]{1,0:T(8,128)S(1)}, f32[40,1440]{1,0:T(8,128)S(1)}, u32[]{:S(2)}, u32[]{:S(2)}) collective-permute-start(f32[40,1440]{1,0:T(8,128)S(1)} %get-tuple-element.50), channel_id=1, source_target_pairs={{4,8},{8,4},{12,16},{16,12},{20,24},{24,20},{5,9},{9,5},{13,17},{1... | collective-permute-start | bytes 691208 | tf_op jit(solution)/shard_map/ppermute | solution.py:509
  11.9 1.8 %collective-permute-start.3 = (f32[2,1,8,1440]{3,2,1,0:T(8,128)S(1)}, f32[2,1,8,1440]{3,2,1,0:T(8,128)S(1)}, u32[]{:S(2)}, u32[]{:S(2)}) collective-permute-start(f32[2,1,8,1440]{3,2,1,0:T(8,128)S(1)} %get-tuple-element.46), channel_id=1, source_target_pairs={{0,1},{1,0},{2,3},{3,2},{4,5},{5,4},{6,7},{7,6},{8,9},{9,8},{10,11... | collective-permute-start | bytes 276488 | tf_op jit(solution)/shard_map/ppermute | solution.py:500
  19.6 2.5 %collective-permute-start.6 = (f32[2,1,8,1440]{3,2,1,0:T(8,128)S(1)}, f32[2,1,8,1440]{3,2,1,0:T(8,128)S(1)}, u32[]{:S(2)}, u32[]{:S(2)}) collective-permute-start(f32[2,1,8,1440]{3,2,1,0:T(8,128)S(1)} %get-tuple-element.53), channel_id=1, source_target_pairs={{0,1},{1,0},{2,3},{3,2},{4,5},{5,4},{6,7},{7,6},{8,9},{9,8},{10,11... | collective-permute-start | bytes 276488 | tf_op jit(solution)/shard_map/ppermute | solution.py:500
  21.2 5.3 %collective-permute-start.4 = (f32[2,8,2176]{2,1,0:T(8,128)S(1)}, f32[2,8,2176]{2,1,0:T(8,128)S(1)}, u32[]{:S(2)}, u32[]{:S(2)}) collective-permute-start(f32[2,8,2176]{2,1,0:T(8,128)S(1)} %get-tuple-element.48.after_ref.own_ref), channel_id=1, source_target_pairs={{0,2},{1,3},{2,0},{3,1},{4,6},{5,7},{6,4},{7,5},{8,10},{9,11},{10,... | collective-permute-start | bytes 417800 | tf_op jit(solution)/shard_map/ppermute | solution.py:503
  23.0 6.4 %collective-permute-start.7 = (f32[2,8,2176]{2,1,0:T(8,128)S(1)}, f32[2,8,2176]{2,1,0:T(8,128)S(1)}, u32[]{:S(2)}, u32[]{:S(2)}) collective-permute-start(f32[2,8,2176]{2,1,0:T(8,128)S(1)} %get-tuple-element.55.after_ref.own_ref), channel_id=1, source_target_pairs={{0,2},{1,3},{2,0},{3,1},{4,6},{5,7},{6,4},{7,5},{8,10},{9,11},{10,... | collective-permute-start | bytes 417800 | tf_op jit(solution)/shard_map/ppermute | solution.py:503
  23.6 7.4 %collective-permute-start.8 = (f32[2,2,8,1440]{3,2,1,0:T(8,128)S(1)}, f32[2,2,8,1440]{3,2,1,0:T(8,128)S(1)}, u32[]{:S(2)}, u32[]{:S(2)}) collective-permute-start(f32[2,2,8,1440]{3,2,1,0:T(8,128)S(1)} %get-tuple-element.58), channel_id=1, source_target_pairs={{0,1},{1,0},{2,3},{3,2},{4,5},{5,4},{6,7},{7,6},{8,9},{9,8},{10,11... | collective-permute-start | bytes 552968 | tf_op jit(solution)/shard_map/ppermute | solution.py:500
  27.1 3.9 %collective-permute-start.9 = (f32[2,1,8,1440]{3,2,1,0:T(8,128)S(1)}, f32[2,1,8,1440]{3,2,1,0:T(8,128)S(1)}, u32[]{:S(2)}, u32[]{:S(2)}) collective-permute-start(f32[2,1,8,1440]{3,2,1,0:T(8,128)S(1)} %get-tuple-element.59), channel_id=1, source_target_pairs={{0,1},{1,0},{2,3},{3,2},{4,5},{5,4},{6,7},{7,6},{8,9},{9,8},{10,11... | collective-permute-start | bytes 276488 | tf_op jit(solution)/shard_map/ppermute | solution.py:500
  30.1 1.9 %collective-permute-start.10 = (f32[2,1,8,1440]{3,2,1,0:T(8,128)S(1)}, f32[2,1,8,1440]{3,2,1,0:T(8,128)S(1)}, u32[]{:S(2)}, u32[]{:S(2)}) collective-permute-start(f32[2,1,8,1440]{3,2,1,0:T(8,128)S(1)} %get-tuple-element.60), channel_id=1, source_target_pairs={{0,1},{1,0},{2,3},{3,2},{4,5},{5,4},{6,7},{7,6},{8,9},{9,8},{10,11... | collective-permute-start | bytes 276488 | tf_op jit(solution)/shard_map/ppermute | solution.py:500

commit v7 on v6

--- a/solution.py
+++ b/solution.py
@@ -572,18 +572,19 @@
     inner = inverse("inner", inner_held, inner_moved, inner_own, inner_other, near_moved)
     inner_back = swap_core(inner[1])
 
+    near = inverse("near", near_held, near_moved, near_own, near_other, inner[0])
+    near_back = swap_core(near[1])
+
     far_mine, far_send = call(
         functools.partial(edge_kernel, False),
         [set_shape(1)] * 2,
-        whole(far_edge, far_got, far_part) + [(inner[0], UNREAD)],
+        whole(far_edge, far_got, far_part) + [(near[0], UNREAD)],
     )
     far_theirs = swap_core(far_send)
-    far_own, far_held = forward(far_mine, far_theirs, inner[0])
+    far_own, far_held = forward(far_mine, far_theirs, near[0])
     far_other = swap_half(far_own)
     (far_moved,) = shifted("far", far_held, far_own)
-    near = inverse("near", near_held, near_moved, near_own, near_other, far_moved)
-    near_back = swap_core(near[1])
-    far = inverse("far", far_held, far_moved, far_own, far_other, near[0])
+    far = inverse("far", far_held, far_moved, far_own, far_other, far_moved)
     far_back = swap_core(far[1])
     (result,) = call(
         end_kernel,

time: 33.2 us -> 34.4 us (1.036)
  starting transfers between devices: 10.1 us -> 11.4 us
    ppermute x3, waiting for transfers between devices: 2.89 us -> 5.11 us  [swap_half(): return lax.ppermute(value, 'lon', [(p, p ^ 2) for p in range(lon_count)])]
    ppermute x3, starting transfers between devices: 2.07 us -> 3.78 us  [swap_half(): return lax.ppermute(value, 'lon', [(p, p ^ 2) for p in range(lon_count)])]
    ppermute x6, starting transfers between devices: 6.08 us -> 4.42 us  [swap_core(): return lax.ppermute(value, 'lon', [(p, p ^ 1) for p in range(lon_count)])]
    ppermute x2, waiting for transfers between devices: 3.59 us -> 2.08 us  [swap_band(): return lax.ppermute(value, 'lat', pairs)]
    ppermute x2, starting transfers between devices: 1.92 us -> 3.17 us  [swap_band(): return lax.ppermute(value, 'lat', pairs)]
    ppermute x6, waiting for transfers between devices: 3.66 us -> 2.96 us  [swap_core(): return lax.ppermute(value, 'lon', [(p, p ^ 1) for p in range(lon_count)])]
  transfers between devices with their start and end apart: 11 -> 11, of which waited for: 7 -> 7; matrix products, arithmetic and copies ran while one was open for 0% -> 0% of each run, Pallas kernels for 24% -> 20%
where the time goes in v7:
time: 34.4 us; the launch traced here: 34.2 us
  starting transfers between devices  11.4 us (33%)
  waiting for transfers between devices  10.2 us (30%)
  Pallas kernels  9.75 us (28%)
  local copies, waits for them, and re-layouts  2.78 us (8%)
    pallas_call x14, Pallas kernels, call(): pl.pallas_call(kernel, out_shape=[jax.ShapeDtypeStruct(shape, jnp.float32...  9.75 us
    ppermute x3, waiting for transfers between devices, swap_half(): return lax.ppermute(value, 'lon', [(p, p ^ 2) for p in range(lon_count)])  5.11 us
    ppermute x6, starting transfers between devices, swap_core(): return lax.ppermute(value, 'lon', [(p, p ^ 1) for p in range(lon_count)])  4.42 us
    ppermute x3, starting transfers between devices, swap_half(): return lax.ppermute(value, 'lon', [(p, p ^ 2) for p in range(lon_count)])  3.78 us
    ppermute x2, starting transfers between devices, swap_band(): return lax.ppermute(value, 'lat', pairs)  3.17 us
    ppermute x6, waiting for transfers between devices, swap_core(): return lax.ppermute(value, 'lon', [(p, p ^ 1) for p in range(lon_count)])  2.96 us
    unnamed x20, local copies, waits for them, and re-layouts  2.78 us
    ppermute x2, waiting for transfers between devices, swap_band(): return lax.ppermute(value, 'lat', pairs)  2.08 us
  transfers between devices with their start and end apart: 11, of which 7 were waited for; matrix products, arithmetic and copies ran while one was open for 0% of the time, Pallas kernels for 20%

profile of v7, /device:TPU:3, one launch (start us, length us, event | category | flops | bytes accessed | tf_op | source)
XLA Modules:
  0.0 34.2 jit_solution(7641277164109157525)
XLA Ops:
  0.0 0.0 copy-start
  0.0 0.0 copy-start.3
  0.0 1.2 %copy-done.3 = f32[4,8,4,1440]{3,2,1,0:T(4,128)S(1)} copy-done((f32[4,8,4,1440]{3,2,1,0:T(4,128)S(1)}, f32[4,8,4,1440]{3,2,1,0:T(4,128)}, u32[]{:S(2)}) %copy-start.3) | copy-done | bytes 737304
  1.2 0.9 %copy-done.4 = f32[8,4,1440]{2,1,0:T(4,128)S(1)} copy-done((f32[8,4,1440]{2,1,0:T(4,128)S(1)}, f32[8,4,1440]{2,1,0:T(4,128)}, u32[]{:S(2)}) %copy-start.4) | copy-done | bytes 184344
  2.1 0.9 %shard_map.100 = (f32[2,2,8,1440]{3,2,1,0:T(8,128)S(1)}, f32[2,2,8,1440]{3,2,1,0:T(8,128)S(1)}, f32[40,1440]{1,0:T(8,128)S(1)}, f32[40,1440]{1,0:T(8,128)S(1)}, ...) custom-call(f32[4,8,4,1440]{3,2,1,0:T(4,128)S(1)} %copy-done.3, f32[8,4,1440]{2,1,0:T(4,128)S(1)} %copy-done.4), custom_call_target="tpu_custom_call" | custom-call | flops 1 | bytes 1 | tf_op jit(solution)/shard_map/pallas_call | solution.py:469
  3.1 0.7 %collective-permute-start = (f32[2,2,8,1440]{3,2,1,0:T(8,128)S(1)}, f32[2,2,8,1440]{3,2,1,0:T(8,128)S(1)}, u32[]{:S(2)}, u32[]{:S(2)}) collective-permute-start(f32[2,2,8,1440]{3,2,1,0:T(8,128)S(1)} %get-tuple-element.34), channel_id=1, source_target_pairs={{0,1},{1,0},{2,3},{3,2},{4,5},{5,4},{6,7},{7,6},{8,9},{9,8},{10,11... | collective-permute-start | bytes 552968 | tf_op jit(solution)/shard_map/ppermute | solution.py:500
  3.8 0.0 collective-permute-start.2
  3.8 1.1 %collective-permute-done.theirs_ref = f32[2,2,8,1440]{3,2,1,0:T(8,128)S(1)} collective-permute-done((f32[2,2,8,1440]{3,2,1,0:T(8,128)S(1)}, f32[2,2,8,1440]{3,2,1,0:T(8,128)S(1)}, u32[]{:S(2)}, u32[]{:S(2)}) %collective-permute-start) | collective-permute-done | bytes 184352 | tf_op jit(solution)/shard_map/ppermute | solution.py:500
  4.9 0.0 copy-done
  4.9 0.0 copy-done.1
  4.9 0.0 copy-done.2
  4.9 1.5 %shard_map.101 = (f32[4,8,2176]{2,1,0:T(8,128)S(1)}, f32[2,4,8,1536]{3,2,1,0:T(8,128)S(1)}) custom-call(f32[2,2,8,1440]{3,2,1,0:T(8,128)S(1)} %get-tuple-element.33.mine_ref, f32[2,2,8,1440]{3,2,1,0:T(8,128)S(1)} %collective-permute-done.theirs_ref, f32[18,384]{1,0:T(8,128)S(1)} %copy-done.2, bf16[384,256]{1,0:T(8,128)(2,1)S(1)} %copy-done, ...), custom_call_target="tpu_custom_call" | custom-call | flops 1 | bytes 1 | tf_op jit(solution)/shard_map/pallas_call | solution.py:469
  6.4 1.3 %collective-permute-start.1 = (f32[4,8,2176]{2,1,0:T(8,128)S(1)}, f32[4,8,2176]{2,1,0:T(8,128)S(1)}, u32[]{:S(2)}, u32[]{:S(2)}) collective-permute-start(f32[4,8,2176]{2,1,0:T(8,128)S(1)} %get-tuple-element.36.after_ref.own_ref), channel_id=1, source_target_pairs={{0,2},{1,3},{2,0},{3,1},{4,6},{5,7},{6,4},{7,5},{8,10},{9,11},{10,... | collective-permute-start | bytes 835592 | tf_op jit(solution)/shard_map/ppermute | solution.py:503
  7.6 0.0 copy-done.5
  7.6 0.0 copy-done.7
  7.6 0.0 copy-done.6
  7.7 0.6 %copy-done.8 = s32[32]{0:T(128)S(1)} copy-done((s32[32]{0:T(128)S(1)}, s32[32]{0:T(128)}, u32[]{:S(2)}) %copy-start.8) | copy-done | bytes 152
  8.3 0.0 copy-done.9
  8.3 0.9 %shard_map.102 = (f32[4,8,128]{2,1,0:T(8,128)S(1)}, f32[4,8,128]{2,1,0:T(8,128)S(1)}, f32[4,8,128]{2,1,0:T(8,128)S(1)}, f32[4,18,8,128]{3,2,1,0:T(8,128)S(1)}) custom-call(s32[4,8]{1,0:T(4,128)S(1)} %bitcast.2, f32[4,8]{1,0:T(4,128)S(1)} %bitcast.3, s32[32]{0:T(128)S(1)} %copy-done.8, f32[32]{0:T(128)S(1)} %copy-done.9, f32[18,128]{1,0:T(8,128)S(1)} %copy-done.5, ...), custom_call_target="tpu_custom_call" | custom-call | flops 1 | bytes 1 | tf_op jit(solution)/shard_map/pallas_call | solution.py:469
  9.2 0.7 %shard_map.103 = (f32[4,2,8,1536]{3,2,1,0:T(8,128)S(1)}, f32[40,1440]{1,0:T(8,128)S(1)}) custom-call(f32[4,8,128]{2,1,0:T(8,128)S(1)} %get-tuple-element.37.distance_ref, f32[4,8,128]{2,1,0:T(8,128)S(1)} %get-tuple-element.38.share_ref, f32[2,4,8,1536]{3,2,1,0:T(8,128)S(1)} %get-tuple-element.41.held_ref, ...), custom_call_target="tpu_custom_call" | custom-call | flops 1 | bytes 1 | tf_op jit(solution)/shard_map/pallas_call | solution.py:469
  9.9 1.4 %collective-permute-done.2.got_ref = f32[40,1440]{1,0:T(8,128)S(1)} collective-permute-done((f32[40,1440]{1,0:T(8,128)S(1)}, f32[40,1440]{1,0:T(8,128)S(1)}, u32[]{:S(2)}, u32[]{:S(2)}) %collective-permute-start.2) | collective-permute-done | bytes 230432 | tf_op jit(solution)/shard_map/ppermute | solution.py:509
  11.3 0.1 shard_map.104
  11.4 0.9 %collective-permute-start.3 = (f32[2,1,8,1440]{3,2,1,0:T(8,128)S(1)}, f32[2,1,8,1440]{3,2,1,0:T(8,128)S(1)}, u32[]{:S(2)}, u32[]{:S(2)}) collective-permute-start(f32[2,1,8,1440]{3,2,1,0:T(8,128)S(1)} %get-tuple-element.46), channel_id=1, source_target_pairs={{0,1},{1,0},{2,3},{3,2},{4,5},{5,4},{6,7},{7,6},{8,9},{9,8},{10,11... | collective-permute-start | bytes 276488 | tf_op jit(solution)/shard_map/ppermute | solution.py:500
  12.3 3.2 %collective-permute-start.5 = (f32[40,1440]{1,0:T(8,128)S(1)}, f32[40,1440]{1,0:T(8,128)S(1)}, u32[]{:S(2)}, u32[]{:S(2)}) collective-permute-start(f32[40,1440]{1,0:T(8,128)S(1)} %get-tuple-element.51), channel_id=1, source_target_pairs={{4,8},{8,4},{12,16},{16,12},{20,24},{24,20},{5,9},{9,5},{13,17},{1... | collective-permute-start | bytes 691208 | tf_op jit(solution)/shard_map/ppermute | solution.py:509
  15.5 0.0 collective-permute-done.3.theirs_ref
  15.5 0.9 %shard_map.105 = (f32[2,8,2176]{2,1,0:T(8,128)S(1)}, f32[2,2,8,1536]{3,2,1,0:T(8,128)S(1)}) custom-call(f32[2,1,8,1440]{3,2,1,0:T(8,128)S(1)} %get-tuple-element.45.mine_ref, f32[2,1,8,1440]{3,2,1,0:T(8,128)S(1)} %collective-permute-done.3.theirs_ref, f32[18,384]{1,0:T(8,128)S(1)} %copy-done.2, bf16[384,256]{1,0:T(8,128)(2,1)S(1)} %copy-done, ...), custom_call_target="tpu_custom_call" | custom-call | flops 1 | bytes 1 | tf_op jit(solution)/shard_map/pallas_call | solution.py:469
  16.4 1.3 %collective-permute-start.4 = (f32[2,8,2176]{2,1,0:T(8,128)S(1)}, f32[2,8,2176]{2,1,0:T(8,128)S(1)}, u32[]{:S(2)}, u32[]{:S(2)}) collective-permute-start(f32[2,8,2176]{2,1,0:T(8,128)S(1)} %get-tuple-element.48.after_ref.own_ref), channel_id=1, source_target_pairs={{0,2},{1,3},{2,0},{3,1},{4,6},{5,7},{6,4},{7,5},{8,10},{9,11},{10,... | collective-permute-start | bytes 417800 | tf_op jit(solution)/shard_map/ppermute | solution.py:503
  17.7 0.3 shard_map.106.after_ref.moved_ref
  18.0 0.0 collective-permute-done.1.other_ref
  18.0 1.0 %shard_map.107 = (f32[2,2,8,1440]{3,2,1,0:T(8,128)S(1)}, f32[2,2,8,1440]{3,2,1,0:T(8,128)S(1)}) custom-call(f32[4,8,128]{2,1,0:T(8,128)S(1)} %get-tuple-element.37.distance_ref, f32[4,8,128]{2,1,0:T(8,128)S(1)} %get-tuple-element.38.share_ref, f32[4,8,128]{2,1,0:T(8,128)S(1)} %get-tuple-element.39.keep_ref, ...), custom_call_target="tpu_custom_call" | custom-call | flops 1 | bytes 1 | tf_op jit(solution)/shard_map/pallas_call | solution.py:469
  19.0 2.4 %collective-permute-done.4.other_ref = f32[2,8,2176]{2,1,0:T(8,128)S(1)} collective-permute-done((f32[2,8,2176]{2,1,0:T(8,128)S(1)}, f32[2,8,2176]{2,1,0:T(8,128)S(1)}, u32[]{:S(2)}, u32[]{:S(2)}) %collective-permute-start.4) | collective-permute-done | bytes 139296 | tf_op jit(solution)/shard_map/ppermute | solution.py:503
  21.4 0.6 %shard_map.108 = (f32[2,1,8,1440]{3,2,1,0:T(8,128)S(1)}, f32[2,1,8,1440]{3,2,1,0:T(8,128)S(1)}) custom-call(f32[4,8,128]{2,1,0:T(8,128)S(1)} %get-tuple-element.37.distance_ref, f32[4,8,128]{2,1,0:T(8,128)S(1)} %get-tuple-element.38.share_ref, f32[4,8,128]{2,1,0:T(8,128)S(1)} %get-tuple-element.39.keep_ref, ...), custom_call_target="tpu_custom_call" | custom-call | flops 1 | bytes 1 | tf_op jit(solution)/shard_map/pallas_call | solution.py:469
  22.0 0.6 %collective-permute-done.5.got_ref = f32[40,1440]{1,0:T(8,128)S(1)} collective-permute-done((f32[40,1440]{1,0:T(8,128)S(1)}, f32[40,1440]{1,0:T(8,128)S(1)}, u32[]{:S(2)}, u32[]{:S(2)}) %collective-permute-start.5) | collective-permute-done | bytes 230432 | tf_op jit(solution)/shard_map/ppermute | solution.py:509
  22.7 0.1 shard_map.109
  22.7 0.9 %collective-permute-start.6 = (f32[2,1,8,1440]{3,2,1,0:T(8,128)S(1)}, f32[2,1,8,1440]{3,2,1,0:T(8,128)S(1)}, u32[]{:S(2)}, u32[]{:S(2)}) collective-permute-start(f32[2,1,8,1440]{3,2,1,0:T(8,128)S(1)} %get-tuple-element.54), channel_id=1, source_target_pairs={{0,1},{1,0},{2,3},{3,2},{4,5},{5,4},{6,7},{7,6},{8,9},{9,8},{10,11... | collective-permute-start | bytes 276488 | tf_op jit(solution)/shard_map/ppermute | solution.py:500
  23.6 0.9 %collective-permute-done.6.theirs_ref = f32[2,1,8,1440]{3,2,1,0:T(8,128)S(1)} collective-permute-done((f32[2,1,8,1440]{3,2,1,0:T(8,128)S(1)}, f32[2,1,8,1440]{3,2,1,0:T(8,128)S(1)}, u32[]{:S(2)}, u32[]{:S(2)}) %collective-permute-start.6) | collective-permute-done | bytes 92192 | tf_op jit(solution)/shard_map/ppermute | solution.py:500
  24.6 0.9 %shard_map.110 = (f32[2,8,2176]{2,1,0:T(8,128)S(1)}, f32[2,2,8,1536]{3,2,1,0:T(8,128)S(1)}) custom-call(f32[2,1,8,1440]{3,2,1,0:T(8,128)S(1)} %get-tuple-element.53.mine_ref, f32[2,1,8,1440]{3,2,1,0:T(8,128)S(1)} %collective-permute-done.6.theirs_ref, f32[18,384]{1,0:T(8,128)S(1)} %copy-done.2, bf16[384,256]{1,0:T(8,128)(2,1)S(1)} %copy-done, ...), custom_call_target="tpu_custom_call" | custom-call | flops 1 | bytes 1 | tf_op jit(solution)/shard_map/pallas_call | solution.py:469
  25.5 1.3 %collective-permute-start.7 = (f32[2,8,2176]{2,1,0:T(8,128)S(1)}, f32[2,8,2176]{2,1,0:T(8,128)S(1)}, u32[]{:S(2)}, u32[]{:S(2)}) collective-permute-start(f32[2,8,2176]{2,1,0:T(8,128)S(1)} %get-tuple-element.56.after_ref.own_ref), channel_id=1, source_target_pairs={{0,2},{1,3},{2,0},{3,1},{4,6},{5,7},{6,4},{7,5},{8,10},{9,11},{10,... | collective-permute-start | bytes 417800 | tf_op jit(solution)/shard_map/ppermute | solution.py:503
  26.7 0.6 %collective-permute-start.8 = (f32[2,2,8,1440]{3,2,1,0:T(8,128)S(1)}, f32[2,2,8,1440]{3,2,1,0:T(8,128)S(1)}, u32[]{:S(2)}, u32[]{:S(2)}) collective-permute-start(f32[2,2,8,1440]{3,2,1,0:T(8,128)S(1)} %get-tuple-element.58), channel_id=1, source_target_pairs={{0,1},{1,0},{2,3},{3,2},{4,5},{5,4},{6,7},{7,6},{8,9},{9,8},{10,11... | collective-permute-start | bytes 552968 | tf_op jit(solution)/shard_map/ppermute | solution.py:500
  27.3 0.0 collective-permute-start.9
  27.4 0.3 shard_map.111.moved_ref.after_ref
  27.7 2.7 %collective-permute-done.7.other_ref = f32[2,8,2176]{2,1,0:T(8,128)S(1)} collective-permute-done((f32[2,8,2176]{2,1,0:T(8,128)S(1)}, f32[2,8,2176]{2,1,0:T(8,128)S(1)}, u32[]{:S(2)}, u32[]{:S(2)}) %collective-permute-start.7) | collective-permute-done | bytes 139296 | tf_op jit(solution)/shard_map/ppermute | solution.py:503
  30.4 0.7 %shard_map.112 = (f32[2,1,8,1440]{3,2,1,0:T(8,128)S(1)}, f32[2,1,8,1440]{3,2,1,0:T(8,128)S(1)}) custom-call(f32[4,8,128]{2,1,0:T(8,128)S(1)} %get-tuple-element.37.distance_ref, f32[4,8,128]{2,1,0:T(8,128)S(1)} %get-tuple-element.38.share_ref, f32[4,8,128]{2,1,0:T(8,128)S(1)} %get-tuple-element.39.keep_ref, ...), custom_call_target="tpu_custom_call" | custom-call | flops 1 | bytes 1 | tf_op jit(solution)/shard_map/pallas_call | solution.py:469
  31.0 1.3 %collective-permute-start.10 = (f32[2,1,8,1440]{3,2,1,0:T(8,128)S(1)}, f32[2,1,8,1440]{3,2,1,0:T(8,128)S(1)}, u32[]{:S(2)}, u32[]{:S(2)}) collective-permute-start(f32[2,1,8,1440]{3,2,1,0:T(8,128)S(1)} %get-tuple-element.60), channel_id=1, source_target_pairs={{0,1},{1,0},{2,3},{3,2},{4,5},{5,4},{6,7},{7,6},{8,9},{9,8},{10,11... | collective-permute-start | bytes 276488 | tf_op jit(solution)/shard_map/ppermute | solution.py:500
  32.3 0.0 collective-permute-done.9.refs_4_
  32.3 0.0 collective-permute-done.8.refs_3_
  32.3 0.9 %collective-permute-done.10.refs_5_ = f32[2,1,8,1440]{3,2,1,0:T(8,128)S(1)} collective-permute-done((f32[2,1,8,1440]{3,2,1,0:T(8,128)S(1)}, f32[2,1,8,1440]{3,2,1,0:T(8,128)S(1)}, u32[]{:S(2)}, u32[]{:S(2)}) %collective-permute-start.10) | collective-permute-done | bytes 92192 | tf_op jit(solution)/shard_map/ppermute | solution.py:500
  33.2 0.9 %shard_map.113 = f32[4,8,4,1440]{3,2,1,0:T(4,128)} custom-call(f32[2,2,8,1440]{3,2,1,0:T(8,128)S(1)} %get-tuple-element.49.after_ref.refs_0_, f32[2,1,8,1440]{3,2,1,0:T(8,128)S(1)} %get-tuple-element.50.after_ref.refs_1_, f32[2,1,8,1440]{3,2,1,0:T(8,128)S(1)} %get-tuple-element.57.refs_2_, f32[2,2,8,1440]{3,2,1,0:T(8,128)S(1)} %collective-permute-done.8.refs_3_, ...), custom_call_target="tpu_custom_call" | custom-call | flops 1 | bytes 1 | tf_op jit(solution)/shard_map/pallas_call | solution.py:469
  (8 shorter events, 0.0 us)
Async XLA Ops:
  0.0 4.9 %copy-start = (bf16[384,256]{1,0:T(8,128)(2,1)S(1)}, bf16[384,256]{1,0:T(8,128)(2,1)}, u32[]{:S(2)}) copy-start(bf16[384,256]{1,0:T(8,128)(2,1)} %constant.10.clone.high_ref) | copy-start | bytes 589828
  0.0 4.9 %copy-start.1 = (bf16[384,256]{1,0:T(8,128)(2,1)S(1)}, bf16[384,256]{1,0:T(8,128)(2,1)}, u32[]{:S(2)}) copy-start(bf16[384,256]{1,0:T(8,128)(2,1)} %constant.11.clone.low_ref) | copy-start | bytes 589828
  0.0 4.9 %copy-start.2 = (f32[18,384]{1,0:T(8,128)S(1)}, f32[18,384]{1,0:T(8,128)}, u32[]{:S(2)}) copy-start(f32[18,384]{1,0:T(8,128)} %constant.8.clone.phase_ref) | copy-start | bytes 82948
  0.0 1.2 %copy-start.3 = (f32[4,8,4,1440]{3,2,1,0:T(4,128)S(1)}, f32[4,8,4,1440]{3,2,1,0:T(4,128)}, u32[]{:S(2)}) copy-start(f32[4,8,4,1440]{3,2,1,0:T(4,128)} %cells_ref.1) | copy-start | bytes 2211844
  1.2 0.9 %copy-start.4 = (f32[8,4,1440]{2,1,0:T(4,128)S(1)}, f32[8,4,1440]{2,1,0:T(4,128)}, u32[]{:S(2)}) copy-start(f32[8,4,1440]{2,1,0:T(4,128)} %speed_ref.1) | copy-start | bytes 552964
  3.1 1.8 %collective-permute-start = (f32[2,2,8,1440]{3,2,1,0:T(8,128)S(1)}, f32[2,2,8,1440]{3,2,1,0:T(8,128)S(1)}, u32[]{:S(2)}, u32[]{:S(2)}) collective-permute-start(f32[2,2,8,1440]{3,2,1,0:T(8,128)S(1)} %get-tuple-element.34), channel_id=1, source_target_pairs={{0,1},{1,0},{2,3},{3,2},{4,5},{5,4},{6,7},{7,6},{8,9},{9,8},{10,11... | collective-permute-start | bytes 552968 | tf_op jit(solution)/shard_map/ppermute | solution.py:500
  3.8 7.5 %collective-permute-start.2 = (f32[40,1440]{1,0:T(8,128)S(1)}, f32[40,1440]{1,0:T(8,128)S(1)}, u32[]{:S(2)}, u32[]{:S(2)}) collective-permute-start(f32[40,1440]{1,0:T(8,128)S(1)} %get-tuple-element.44.own_ref), channel_id=1, source_target_pairs={{0,4},{4,0},{8,12},{12,8},{16,20},{20,16},{24,28},{28,24},{1,5},{5... | collective-permute-start | bytes 691208 | tf_op jit(solution)/shard_map/ppermute | solution.py:509
  4.9 2.8 %copy-start.5 = (f32[18,128]{1,0:T(8,128)S(1)}, f32[18,128]{1,0:T(8,128)}, u32[]{:S(2)}) copy-start(f32[18,128]{1,0:T(8,128)} %constant.9.clone.wave_ref) | copy-start | bytes 27652
  6.3 1.3 %copy-start.7 = (f32[8,4]{0,1:T(4,128)S(1)}, f32[8,4]{0,1:T(4,128)}, u32[]{:S(2)}) copy-start(f32[8,4]{0,1:T(4,128)} %param.13) | copy-start | bytes 388
  6.3 1.3 %copy-start.6 = (s32[8,4]{0,1:T(4,128)S(1)}, s32[8,4]{0,1:T(4,128)}, u32[]{:S(2)}) copy-start(s32[8,4]{0,1:T(4,128)} %param.12) | copy-start | bytes 388
  6.4 11.6 %collective-permute-start.1 = (f32[4,8,2176]{2,1,0:T(8,128)S(1)}, f32[4,8,2176]{2,1,0:T(8,128)S(1)}, u32[]{:S(2)}, u32[]{:S(2)}) collective-permute-start(f32[4,8,2176]{2,1,0:T(8,128)S(1)} %get-tuple-element.36.after_ref.own_ref), channel_id=1, source_target_pairs={{0,2},{1,3},{2,0},{3,1},{4,6},{5,7},{6,4},{7,5},{8,10},{9,11},{10,... | collective-permute-start | bytes 835592 | tf_op jit(solution)/shard_map/ppermute | solution.py:503
  7.6 0.7 %copy-start.8 = (s32[32]{0:T(128)S(1)}, s32[32]{0:T(128)}, u32[]{:S(2)}) copy-start(s32[32]{0:T(128)} %cutoff_ref.1) | copy-start | bytes 388
  7.6 0.7 %copy-start.9 = (f32[32]{0:T(128)S(1)}, f32[32]{0:T(128)}, u32[]{:S(2)}) copy-start(f32[32]{0:T(128)} %damping_ref.1) | copy-start | bytes 388
  11.4 4.1 %collective-permute-start.3 = (f32[2,1,8,1440]{3,2,1,0:T(8,128)S(1)}, f32[2,1,8,1440]{3,2,1,0:T(8,128)S(1)}, u32[]{:S(2)}, u32[]{:S(2)}) collective-permute-start(f32[2,1,8,1440]{3,2,1,0:T(8,128)S(1)} %get-tuple-element.46), channel_id=1, source_target_pairs={{0,1},{1,0},{2,3},{3,2},{4,5},{5,4},{6,7},{7,6},{8,9},{9,8},{10,11... | collective-permute-start | bytes 276488 | tf_op jit(solution)/shard_map/ppermute | solution.py:500
  12.3 10.3 %collective-permute-start.5 = (f32[40,1440]{1,0:T(8,128)S(1)}, f32[40,1440]{1,0:T(8,128)S(1)}, u32[]{:S(2)}, u32[]{:S(2)}) collective-permute-start(f32[40,1440]{1,0:T(8,128)S(1)} %get-tuple-element.51), channel_id=1, source_target_pairs={{4,8},{8,4},{12,16},{16,12},{20,24},{24,20},{5,9},{9,5},{13,17},{1... | collective-permute-start | bytes 691208 | tf_op jit(solution)/shard_map/ppermute | solution.py:509
  16.4 5.0 %collective-permute-start.4 = (f32[2,8,2176]{2,1,0:T(8,128)S(1)}, f32[2,8,2176]{2,1,0:T(8,128)S(1)}, u32[]{:S(2)}, u32[]{:S(2)}) collective-permute-start(f32[2,8,2176]{2,1,0:T(8,128)S(1)} %get-tuple-element.48.after_ref.own_ref), channel_id=1, source_target_pairs={{0,2},{1,3},{2,0},{3,1},{4,6},{5,7},{6,4},{7,5},{8,10},{9,11},{10,... | collective-permute-start | bytes 417800 | tf_op jit(solution)/shard_map/ppermute | solution.py:503
  22.7 1.8 %collective-permute-start.6 = (f32[2,1,8,1440]{3,2,1,0:T(8,128)S(1)}, f32[2,1,8,1440]{3,2,1,0:T(8,128)S(1)}, u32[]{:S(2)}, u32[]{:S(2)}) collective-permute-start(f32[2,1,8,1440]{3,2,1,0:T(8,128)S(1)} %get-tuple-element.54), channel_id=1, source_target_pairs={{0,1},{1,0},{2,3},{3,2},{4,5},{5,4},{6,7},{7,6},{8,9},{9,8},{10,11... | collective-permute-start | bytes 276488 | tf_op jit(solution)/shard_map/ppermute | solution.py:500
  25.5 4.9 %collective-permute-start.7 = (f32[2,8,2176]{2,1,0:T(8,128)S(1)}, f32[2,8,2176]{2,1,0:T(8,128)S(1)}, u32[]{:S(2)}, u32[]{:S(2)}) collective-permute-start(f32[2,8,2176]{2,1,0:T(8,128)S(1)} %get-tuple-element.56.after_ref.own_ref), channel_id=1, source_target_pairs={{0,2},{1,3},{2,0},{3,1},{4,6},{5,7},{6,4},{7,5},{8,10},{9,11},{10,... | collective-permute-start | bytes 417800 | tf_op jit(solution)/shard_map/ppermute | solution.py:503
  26.7 5.6 %collective-permute-start.8 = (f32[2,2,8,1440]{3,2,1,0:T(8,128)S(1)}, f32[2,2,8,1440]{3,2,1,0:T(8,128)S(1)}, u32[]{:S(2)}, u32[]{:S(2)}) collective-permute-start(f32[2,2,8,1440]{3,2,1,0:T(8,128)S(1)} %get-tuple-element.58), channel_id=1, source_target_pairs={{0,1},{1,0},{2,3},{3,2},{4,5},{5,4},{6,7},{7,6},{8,9},{9,8},{10,11... | collective-permute-start | bytes 552968 | tf_op jit(solution)/shard_map/ppermute | solution.py:500
  27.3 4.9 %collective-permute-start.9 = (f32[2,1,8,1440]{3,2,1,0:T(8,128)S(1)}, f32[2,1,8,1440]{3,2,1,0:T(8,128)S(1)}, u32[]{:S(2)}, u32[]{:S(2)}) collective-permute-start(f32[2,1,8,1440]{3,2,1,0:T(8,128)S(1)} %get-tuple-element.59), channel_id=1, source_target_pairs={{0,1},{1,0},{2,3},{3,2},{4,5},{5,4},{6,7},{7,6},{8,9},{9,8},{10,11... | collective-permute-start | bytes 276488 | tf_op jit(solution)/shard_map/ppermute | solution.py:500
  31.0 2.2 %collective-permute-start.10 = (f32[2,1,8,1440]{3,2,1,0:T(8,128)S(1)}, f32[2,1,8,1440]{3,2,1,0:T(8,128)S(1)}, u32[]{:S(2)}, u32[]{:S(2)}) collective-permute-start(f32[2,1,8,1440]{3,2,1,0:T(8,128)S(1)} %get-tuple-element.60), channel_id=1, source_target_pairs={{0,1},{1,0},{2,3},{3,2},{4,5},{5,4},{6,7},{7,6},{8,9},{9,8},{10,11... | collective-permute-start | bytes 276488 | tf_op jit(solution)/shard_map/ppermute | solution.py:500

commit v8 on v7

--- a/solution.py
+++ b/solution.py
@@ -138,12 +138,21 @@
 
 
 def begin_kernel(
-    cells_ref, speed_ref, mine_ref, send_ref, near_ref, far_ref, near_part_ref, far_part_ref
+    cells_hbm, speed_hbm, mine_ref, send_ref, near_ref, far_ref, near_part_ref, far_part_ref,
+    cells_ref, speed_ref, sems,
 ):
     tracer_count, levels, row_count, columns = cells_ref.shape
     share = tracer_count // PAIR
     core = lax.rem(lax.axis_index("lon"), PAIR)
     north = near_is_north()
+    copies = [pltpu.make_async_copy(speed_hbm, speed_ref, sems.at[tracer_count])]
+    copies += [
+        pltpu.make_async_copy(cells_hbm.at[t], cells_ref.at[t], sems.at[t]) for t in range(tracer_count)
+    ]
+    for copy in copies:
+        copy.start()
+    for copy in copies:
+        copy.wait()
     for lanes in spans(columns, 2 * LANES):
         speed = [speed_ref[:, j, lanes] for j in range(row_count)]
         near_ref[tracer_count * levels :, lanes] = speed[0]
@@ -543,7 +552,9 @@
     inner_mine, inner_send, near_edge, far_edge, near_part, far_part = call(
         begin_kernel,
         [set_shape(row_count - 2)] * 2 + [edge_shape] * 2 + [part_shape] * 2,
-        whole(tracers, merid_courant),
+        [(pltpu.with_memory_space_constraint(v, pltpu.HBM), pltpu.HBM) for v in (tracers, merid_courant)],
+        [tracers.shape, merid_courant.shape],
+        tracer_count + 1,
     )
     inner_theirs = swap_core(inner_send)
     near_got = swap_band(near_edge, 0)
@@ -572,15 +583,14 @@
     inner = inverse("inner", inner_held, inner_moved, inner_own, inner_other, near_moved)
     inner_back = swap_core(inner[1])
 
-    near = inverse("near", near_held, near_moved, near_own, near_other, inner[0])
-    near_back = swap_core(near[1])
-
     far_mine, far_send = call(
         functools.partial(edge_kernel, False),
         [set_shape(1)] * 2,
-        whole(far_edge, far_got, far_part) + [(near[0], UNREAD)],
+        whole(far_edge, far_got, far_part) + [(inner[0], UNREAD)],
     )
     far_theirs = swap_core(far_send)
+    near = inverse("near", near_held, near_moved, near_own, near_other, far_mine)
+    near_back = swap_core(near[1])
     far_own, far_held = forward(far_mine, far_theirs, near[0])
     far_other = swap_half(far_own)
     (far_moved,) = shifted("far", far_held, far_own)

time: 34.4 us -> 31.3 us (0.910)
  local copies, waits for them, and re-layouts: 2.78 us -> 0.67 us
  starting transfers between devices: 11.4 us -> 9.34 us
  Pallas kernels: 9.75 us -> 11.1 us
  waiting for transfers between devices: 10.2 us -> 9.74 us
    unnamed x20 -> x16, local copies, waits for them, and re-layouts: 2.78 us -> 0.67 us
    ppermute x3, starting transfers between devices: 3.78 us -> 2.34 us  [swap_half(): return lax.ppermute(value, 'lon', [(p, p ^ 2) for p in range(lon_count)])]
    ppermute x3, waiting for transfers between devices: 5.11 us -> 3.73 us  [swap_half(): return lax.ppermute(value, 'lon', [(p, p ^ 2) for p in range(lon_count)])]
    pallas_call x14, Pallas kernels: 9.75 us -> 11.1 us  [call(): pl.pallas_call(kernel, out_shape=[jax.ShapeDtypeStruct(shape, jnp.float32...]
    ppermute x2, starting transfers between devices: 3.17 us -> 1.92 us  [swap_band(): return lax.ppermute(value, 'lat', pairs)]
    ppermute x2, waiting for transfers between devices: 2.08 us -> 2.77 us  [swap_band(): return lax.ppermute(value, 'lat', pairs)]
    ppermute x6, starting transfers between devices: 4.42 us -> 5.08 us  [swap_core(): return lax.ppermute(value, 'lon', [(p, p ^ 1) for p in range(lon_count)])]
  transfers between devices with their start and end apart: 11 -> 11, of which waited for: 7 -> 6; matrix products, arithmetic and copies ran while one was open for 0% -> 0% of each run, Pallas kernels for 20% -> 23%
where the time goes in v8:
time: 31.3 us; the launch traced here: 31 us
  Pallas kernels  11.1 us (35%)
  waiting for transfers between devices  9.74 us (31%)
  starting transfers between devices  9.34 us (30%)
  local copies, waits for them, and re-layouts  0.67 us (2%)
    pallas_call x14, Pallas kernels, call(): pl.pallas_call(kernel, out_shape=[jax.ShapeDtypeStruct(shape, jnp.float32...  11.1 us
    ppermute x6, starting transfers between devices, swap_core(): return lax.ppermute(value, 'lon', [(p, p ^ 1) for p in range(lon_count)])  5.08 us
    ppermute x3, waiting for transfers between devices, swap_half(): return lax.ppermute(value, 'lon', [(p, p ^ 2) for p in range(lon_count)])  3.73 us
    ppermute x6, waiting for transfers between devices, swap_core(): return lax.ppermute(value, 'lon', [(p, p ^ 1) for p in range(lon_count)])  3.24 us
    ppermute x2, waiting for transfers between devices, swap_band(): return lax.ppermute(value, 'lat', pairs)  2.77 us
    ppermute x3, starting transfers between devices, swap_half(): return lax.ppermute(value, 'lon', [(p, p ^ 2) for p in range(lon_count)])  2.34 us
    ppermute x2, starting transfers between devices, swap_band(): return lax.ppermute(value, 'lat', pairs)  1.92 us
    unnamed x16, local copies, waits for them, and re-layouts  0.67 us
  transfers between devices with their start and end apart: 11, of which 6 were waited for; matrix products, arithmetic and copies ran while one was open for 0% of the time, Pallas kernels for 23%

profile of v8, /device:TPU:3, one launch (start us, length us, event | category | flops | bytes accessed | tf_op | source)
XLA Modules:
  0.0 31.0 jit_solution(18010022485436584882)
XLA Ops:
  0.0 0.0 copy-start
  0.0 0.0 copy-start.1
  0.0 0.0 copy-start.2
  0.0 2.3 %shard_map.100 = (f32[2,2,8,1440]{3,2,1,0:T(8,128)S(1)}, f32[2,2,8,1440]{3,2,1,0:T(8,128)S(1)}, f32[40,1440]{1,0:T(8,128)S(1)}, f32[40,1440]{1,0:T(8,128)S(1)}, ...) custom-call(f32[4,8,4,1440]{3,2,1,0:T(4,128)} %cells_hbm.1, f32[8,4,1440]{2,1,0:T(4,128)} %speed_hbm.1), custom_call_target="tpu_custom_call" | custom-call | flops 1 | bytes 1 | tf_op jit(solution)/shard_map/pallas_call | solution.py:478
  2.3 0.7 %collective-permute-start = (f32[2,2,8,1440]{3,2,1,0:T(8,128)S(1)}, f32[2,2,8,1440]{3,2,1,0:T(8,128)S(1)}, u32[]{:S(2)}, u32[]{:S(2)}) collective-permute-start(f32[2,2,8,1440]{3,2,1,0:T(8,128)S(1)} %get-tuple-element.34), channel_id=1, source_target_pairs={{0,1},{1,0},{2,3},{3,2},{4,5},{5,4},{6,7},{7,6},{8,9},{9,8},{10,11... | collective-permute-start | bytes 552968 | tf_op jit(solution)/shard_map/ppermute | solution.py:509
  3.0 0.0 collective-permute-start.2
  3.1 1.1 %collective-permute-done.theirs_ref = f32[2,2,8,1440]{3,2,1,0:T(8,128)S(1)} collective-permute-done((f32[2,2,8,1440]{3,2,1,0:T(8,128)S(1)}, f32[2,2,8,1440]{3,2,1,0:T(8,128)S(1)}, u32[]{:S(2)}, u32[]{:S(2)}) %collective-permute-start) | collective-permute-done | bytes 184352 | tf_op jit(solution)/shard_map/ppermute | solution.py:509
  4.1 0.0 copy-done
  4.1 0.0 copy-done.1
  4.1 0.0 copy-done.2
  4.1 0.0 copy-start.3
  4.1 1.5 %shard_map.101 = (f32[4,8,2176]{2,1,0:T(8,128)S(1)}, f32[2,4,8,1536]{3,2,1,0:T(8,128)S(1)}) custom-call(f32[2,2,8,1440]{3,2,1,0:T(8,128)S(1)} %get-tuple-element.33.mine_ref, f32[2,2,8,1440]{3,2,1,0:T(8,128)S(1)} %collective-permute-done.theirs_ref, f32[18,384]{1,0:T(8,128)S(1)} %copy-done.2, bf16[384,256]{1,0:T(8,128)(2,1)S(1)} %copy-done, ...), custom_call_target="tpu_custom_call" | custom-call | flops 1 | bytes 1 | tf_op jit(solution)/shard_map/pallas_call | solution.py:478
  5.6 1.3 %collective-permute-start.1 = (f32[4,8,2176]{2,1,0:T(8,128)S(1)}, f32[4,8,2176]{2,1,0:T(8,128)S(1)}, u32[]{:S(2)}, u32[]{:S(2)}) collective-permute-start(f32[4,8,2176]{2,1,0:T(8,128)S(1)} %get-tuple-element.36.after_ref.own_ref), channel_id=1, source_target_pairs={{0,2},{1,3},{2,0},{3,1},{4,6},{5,7},{6,4},{7,5},{8,10},{9,11},{10,... | collective-permute-start | bytes 835592 | tf_op jit(solution)/shard_map/ppermute | solution.py:512
  6.9 0.0 copy-done.3
  6.9 0.0 copy-done.5
  6.9 0.0 copy-done.4
  6.9 0.6 %copy-done.6 = s32[32]{0:T(128)S(1)} copy-done((s32[32]{0:T(128)S(1)}, s32[32]{0:T(128)}, u32[]{:S(2)}) %copy-start.6) | copy-done | bytes 152
  7.5 0.0 copy-done.7
  7.5 0.9 %shard_map.102 = (f32[4,8,128]{2,1,0:T(8,128)S(1)}, f32[4,8,128]{2,1,0:T(8,128)S(1)}, f32[4,8,128]{2,1,0:T(8,128)S(1)}, f32[4,18,8,128]{3,2,1,0:T(8,128)S(1)}) custom-call(s32[4,8]{1,0:T(4,128)S(1)} %bitcast.2, f32[4,8]{1,0:T(4,128)S(1)} %bitcast.3, s32[32]{0:T(128)S(1)} %copy-done.6, f32[32]{0:T(128)S(1)} %copy-done.7, f32[18,128]{1,0:T(8,128)S(1)} %copy-done.3, ...), custom_call_target="tpu_custom_call" | custom-call | flops 1 | bytes 1 | tf_op jit(solution)/shard_map/pallas_call | solution.py:478
  8.4 0.7 %shard_map.103 = (f32[4,2,8,1536]{3,2,1,0:T(8,128)S(1)}, f32[40,1440]{1,0:T(8,128)S(1)}) custom-call(f32[4,8,128]{2,1,0:T(8,128)S(1)} %get-tuple-element.37.distance_ref, f32[4,8,128]{2,1,0:T(8,128)S(1)} %get-tuple-element.38.share_ref, f32[2,4,8,1536]{3,2,1,0:T(8,128)S(1)} %get-tuple-element.41.held_ref, ...), custom_call_target="tpu_custom_call" | custom-call | flops 1 | bytes 1 | tf_op jit(solution)/shard_map/pallas_call | solution.py:478
  9.1 1.9 %collective-permute-start.5 = (f32[40,1440]{1,0:T(8,128)S(1)}, f32[40,1440]{1,0:T(8,128)S(1)}, u32[]{:S(2)}, u32[]{:S(2)}) collective-permute-start(f32[40,1440]{1,0:T(8,128)S(1)} %get-tuple-element.50), channel_id=1, source_target_pairs={{4,8},{8,4},{12,16},{16,12},{20,24},{24,20},{5,9},{9,5},{13,17},{1... | collective-permute-start | bytes 691208 | tf_op jit(solution)/shard_map/ppermute | solution.py:518
  11.1 0.0 collective-permute-done.2.got_ref
  11.1 0.1 shard_map.104
  11.2 0.8 %collective-permute-start.3 = (f32[2,1,8,1440]{3,2,1,0:T(8,128)S(1)}, f32[2,1,8,1440]{3,2,1,0:T(8,128)S(1)}, u32[]{:S(2)}, u32[]{:S(2)}) collective-permute-start(f32[2,1,8,1440]{3,2,1,0:T(8,128)S(1)} %get-tuple-element.46), channel_id=1, source_target_pairs={{0,1},{1,0},{2,3},{3,2},{4,5},{5,4},{6,7},{7,6},{8,9},{9,8},{10,11... | collective-permute-start | bytes 276488 | tf_op jit(solution)/shard_map/ppermute | solution.py:509
  12.0 0.9 %collective-permute-done.3.theirs_ref = f32[2,1,8,1440]{3,2,1,0:T(8,128)S(1)} collective-permute-done((f32[2,1,8,1440]{3,2,1,0:T(8,128)S(1)}, f32[2,1,8,1440]{3,2,1,0:T(8,128)S(1)}, u32[]{:S(2)}, u32[]{:S(2)}) %collective-permute-start.3) | collective-permute-done | bytes 92192 | tf_op jit(solution)/shard_map/ppermute | solution.py:509
  12.9 0.9 %shard_map.105 = (f32[2,8,2176]{2,1,0:T(8,128)S(1)}, f32[2,2,8,1536]{3,2,1,0:T(8,128)S(1)}) custom-call(f32[2,1,8,1440]{3,2,1,0:T(8,128)S(1)} %get-tuple-element.45.mine_ref, f32[2,1,8,1440]{3,2,1,0:T(8,128)S(1)} %collective-permute-done.3.theirs_ref, f32[18,384]{1,0:T(8,128)S(1)} %copy-done.2, bf16[384,256]{1,0:T(8,128)(2,1)S(1)} %copy-done, ...), custom_call_target="tpu_custom_call" | custom-call | flops 1 | bytes 1 | tf_op jit(solution)/shard_map/pallas_call | solution.py:478
  13.8 0.8 %collective-permute-start.4 = (f32[2,8,2176]{2,1,0:T(8,128)S(1)}, f32[2,8,2176]{2,1,0:T(8,128)S(1)}, u32[]{:S(2)}, u32[]{:S(2)}) collective-permute-start(f32[2,8,2176]{2,1,0:T(8,128)S(1)} %get-tuple-element.48.after_ref.own_ref), channel_id=1, source_target_pairs={{0,2},{1,3},{2,0},{3,1},{4,6},{5,7},{6,4},{7,5},{8,10},{9,11},{10,... | collective-permute-start | bytes 417800 | tf_op jit(solution)/shard_map/ppermute | solution.py:512
  14.7 0.3 shard_map.106.after_ref.moved_ref
  15.0 0.0 collective-permute-done.1.other_ref
  15.0 1.0 %shard_map.107 = (f32[2,2,8,1440]{3,2,1,0:T(8,128)S(1)}, f32[2,2,8,1440]{3,2,1,0:T(8,128)S(1)}) custom-call(f32[4,8,128]{2,1,0:T(8,128)S(1)} %get-tuple-element.37.distance_ref, f32[4,8,128]{2,1,0:T(8,128)S(1)} %get-tuple-element.38.share_ref, f32[4,8,128]{2,1,0:T(8,128)S(1)} %get-tuple-element.39.keep_ref, ...), custom_call_target="tpu_custom_call" | custom-call | flops 1 | bytes 1 | tf_op jit(solution)/shard_map/pallas_call | solution.py:478
  16.0 2.8 %collective-permute-done.5.got_ref = f32[40,1440]{1,0:T(8,128)S(1)} collective-permute-done((f32[40,1440]{1,0:T(8,128)S(1)}, f32[40,1440]{1,0:T(8,128)S(1)}, u32[]{:S(2)}, u32[]{:S(2)}) %collective-permute-start.5) | collective-permute-done | bytes 230432 | tf_op jit(solution)/shard_map/ppermute | solution.py:518
  18.8 0.1 shard_map.108
  18.8 1.6 %collective-permute-start.6 = (f32[2,1,8,1440]{3,2,1,0:T(8,128)S(1)}, f32[2,1,8,1440]{3,2,1,0:T(8,128)S(1)}, u32[]{:S(2)}, u32[]{:S(2)}) collective-permute-start(f32[2,1,8,1440]{3,2,1,0:T(8,128)S(1)} %get-tuple-element.54), channel_id=1, source_target_pairs={{0,1},{1,0},{2,3},{3,2},{4,5},{5,4},{6,7},{7,6},{8,9},{9,8},{10,11... | collective-permute-start | bytes 276488 | tf_op jit(solution)/shard_map/ppermute | solution.py:509
  20.4 0.0 collective-permute-done.4.other_ref
  20.4 0.6 %shard_map.109 = (f32[2,1,8,1440]{3,2,1,0:T(8,128)S(1)}, f32[2,1,8,1440]{3,2,1,0:T(8,128)S(1)}) custom-call(f32[4,8,128]{2,1,0:T(8,128)S(1)} %get-tuple-element.37.distance_ref, f32[4,8,128]{2,1,0:T(8,128)S(1)} %get-tuple-element.38.share_ref, f32[4,8,128]{2,1,0:T(8,128)S(1)} %get-tuple-element.39.keep_ref, ...), custom_call_target="tpu_custom_call" | custom-call | flops 1 | bytes 1 | tf_op jit(solution)/shard_map/pallas_call | solution.py:478
  21.1 0.3 collective-permute-done.6.theirs_ref
  21.4 0.9 %shard_map.110 = (f32[2,8,2176]{2,1,0:T(8,128)S(1)}, f32[2,2,8,1536]{3,2,1,0:T(8,128)S(1)}) custom-call(f32[2,1,8,1440]{3,2,1,0:T(8,128)S(1)} %get-tuple-element.52.after_ref.mine_ref, f32[2,1,8,1440]{3,2,1,0:T(8,128)S(1)} %collective-permute-done.6.theirs_ref, f32[18,384]{1,0:T(8,128)S(1)} %copy-done.2, bf16[384,256]{1,0:T(8,128)(2,1)S(1)} %copy-done, ...), custom_call_target="tpu_custom_call" | custom-call | flops 1 | bytes 1 | tf_op jit(solution)/shard_map/pallas_call | solution.py:478
  22.3 0.2 collective-permute-start.7
  22.5 0.6 %collective-permute-start.8 = (f32[2,2,8,1440]{3,2,1,0:T(8,128)S(1)}, f32[2,2,8,1440]{3,2,1,0:T(8,128)S(1)}, u32[]{:S(2)}, u32[]{:S(2)}) collective-permute-start(f32[2,2,8,1440]{3,2,1,0:T(8,128)S(1)} %get-tuple-element.58), channel_id=1, source_target_pairs={{0,1},{1,0},{2,3},{3,2},{4,5},{5,4},{6,7},{7,6},{8,9},{9,8},{10,11... | collective-permute-start | bytes 552968 | tf_op jit(solution)/shard_map/ppermute | solution.py:509
  23.1 0.0 collective-permute-start.9
  23.1 0.3 shard_map.111.moved_ref.after_ref
  23.5 3.7 %collective-permute-done.7.other_ref = f32[2,8,2176]{2,1,0:T(8,128)S(1)} collective-permute-done((f32[2,8,2176]{2,1,0:T(8,128)S(1)}, f32[2,8,2176]{2,1,0:T(8,128)S(1)}, u32[]{:S(2)}, u32[]{:S(2)}) %collective-permute-start.7) | collective-permute-done | bytes 139296 | tf_op jit(solution)/shard_map/ppermute | solution.py:512
  27.2 0.6 %shard_map.112 = (f32[2,1,8,1440]{3,2,1,0:T(8,128)S(1)}, f32[2,1,8,1440]{3,2,1,0:T(8,128)S(1)}) custom-call(f32[4,8,128]{2,1,0:T(8,128)S(1)} %get-tuple-element.37.distance_ref, f32[4,8,128]{2,1,0:T(8,128)S(1)} %get-tuple-element.38.share_ref, f32[4,8,128]{2,1,0:T(8,128)S(1)} %get-tuple-element.39.keep_ref, ...), custom_call_target="tpu_custom_call" | custom-call | flops 1 | bytes 1 | tf_op jit(solution)/shard_map/pallas_call | solution.py:478
  27.8 1.3 %collective-permute-start.10 = (f32[2,1,8,1440]{3,2,1,0:T(8,128)S(1)}, f32[2,1,8,1440]{3,2,1,0:T(8,128)S(1)}, u32[]{:S(2)}, u32[]{:S(2)}) collective-permute-start(f32[2,1,8,1440]{3,2,1,0:T(8,128)S(1)} %get-tuple-element.60), channel_id=1, source_target_pairs={{0,1},{1,0},{2,3},{3,2},{4,5},{5,4},{6,7},{7,6},{8,9},{9,8},{10,11... | collective-permute-start | bytes 276488 | tf_op jit(solution)/shard_map/ppermute | solution.py:509
  29.1 0.0 collective-permute-done.9.refs_4_
  29.1 0.0 collective-permute-done.8.refs_3_
  29.1 0.9 %collective-permute-done.10.refs_5_ = f32[2,1,8,1440]{3,2,1,0:T(8,128)S(1)} collective-permute-done((f32[2,1,8,1440]{3,2,1,0:T(8,128)S(1)}, f32[2,1,8,1440]{3,2,1,0:T(8,128)S(1)}, u32[]{:S(2)}, u32[]{:S(2)}) %collective-permute-start.10) | collective-permute-done | bytes 92192 | tf_op jit(solution)/shard_map/ppermute | solution.py:509
  30.0 1.0 %shard_map.113 = f32[4,8,4,1440]{3,2,1,0:T(4,128)} custom-call(f32[2,2,8,1440]{3,2,1,0:T(8,128)S(1)} %get-tuple-element.49.after_ref.refs_0_, f32[2,1,8,1440]{3,2,1,0:T(8,128)S(1)} %get-tuple-element.53.after_ref.refs_1_, f32[2,1,8,1440]{3,2,1,0:T(8,128)S(1)} %get-tuple-element.57.refs_2_, f32[2,2,8,1440]{3,2,1,0:T(8,128)S(1)} %collective-permute-done.8.refs_3_, ...), custom_call_target="tpu_custom_call" | custom-call | flops 1 | bytes 1 | tf_op jit(solution)/shard_map/pallas_call | solution.py:478
  (4 shorter events, 0.0 us)
Async XLA Ops:
  0.0 4.1 %copy-start = (bf16[384,256]{1,0:T(8,128)(2,1)S(1)}, bf16[384,256]{1,0:T(8,128)(2,1)}, u32[]{:S(2)}) copy-start(bf16[384,256]{1,0:T(8,128)(2,1)} %constant.10.clone.high_ref) | copy-start | bytes 589828
  0.0 4.1 %copy-start.1 = (bf16[384,256]{1,0:T(8,128)(2,1)S(1)}, bf16[384,256]{1,0:T(8,128)(2,1)}, u32[]{:S(2)}) copy-start(bf16[384,256]{1,0:T(8,128)(2,1)} %constant.11.clone.low_ref) | copy-start | bytes 589828
  0.0 4.1 %copy-start.2 = (f32[18,384]{1,0:T(8,128)S(1)}, f32[18,384]{1,0:T(8,128)}, u32[]{:S(2)}) copy-start(f32[18,384]{1,0:T(8,128)} %constant.8.clone.phase_ref) | copy-start | bytes 82948
  2.3 1.8 %collective-permute-start = (f32[2,2,8,1440]{3,2,1,0:T(8,128)S(1)}, f32[2,2,8,1440]{3,2,1,0:T(8,128)S(1)}, u32[]{:S(2)}, u32[]{:S(2)}) collective-permute-start(f32[2,2,8,1440]{3,2,1,0:T(8,128)S(1)} %get-tuple-element.34), channel_id=1, source_target_pairs={{0,1},{1,0},{2,3},{3,2},{4,5},{5,4},{6,7},{7,6},{8,9},{9,8},{10,11... | collective-permute-start | bytes 552968 | tf_op jit(solution)/shard_map/ppermute | solution.py:509
  3.0 8.0 %collective-permute-start.2 = (f32[40,1440]{1,0:T(8,128)S(1)}, f32[40,1440]{1,0:T(8,128)S(1)}, u32[]{:S(2)}, u32[]{:S(2)}) collective-permute-start(f32[40,1440]{1,0:T(8,128)S(1)} %get-tuple-element.44.own_ref), channel_id=1, source_target_pairs={{0,4},{4,0},{8,12},{12,8},{16,20},{20,16},{24,28},{28,24},{1,5},{5... | collective-permute-start | bytes 691208 | tf_op jit(solution)/shard_map/ppermute | solution.py:518
  4.1 2.8 %copy-start.3 = (f32[18,128]{1,0:T(8,128)S(1)}, f32[18,128]{1,0:T(8,128)}, u32[]{:S(2)}) copy-start(f32[18,128]{1,0:T(8,128)} %constant.9.clone.wave_ref) | copy-start | bytes 27652
  5.6 1.3 %copy-start.5 = (f32[8,4]{0,1:T(4,128)S(1)}, f32[8,4]{0,1:T(4,128)}, u32[]{:S(2)}) copy-start(f32[8,4]{0,1:T(4,128)} %param.13) | copy-start | bytes 388
  5.6 1.3 %copy-start.4 = (s32[8,4]{0,1:T(4,128)S(1)}, s32[8,4]{0,1:T(4,128)}, u32[]{:S(2)}) copy-start(s32[8,4]{0,1:T(4,128)} %param.12) | copy-start | bytes 388
  5.6 9.4 %collective-permute-start.1 = (f32[4,8,2176]{2,1,0:T(8,128)S(1)}, f32[4,8,2176]{2,1,0:T(8,128)S(1)}, u32[]{:S(2)}, u32[]{:S(2)}) collective-permute-start(f32[4,8,2176]{2,1,0:T(8,128)S(1)} %get-tuple-element.36.after_ref.own_ref), channel_id=1, source_target_pairs={{0,2},{1,3},{2,0},{3,1},{4,6},{5,7},{6,4},{7,5},{8,10},{9,11},{10,... | collective-permute-start | bytes 835592 | tf_op jit(solution)/shard_map/ppermute | solution.py:512
  6.9 0.7 %copy-start.6 = (s32[32]{0:T(128)S(1)}, s32[32]{0:T(128)}, u32[]{:S(2)}) copy-start(s32[32]{0:T(128)} %cutoff_ref.1) | copy-start | bytes 388
  6.9 0.7 %copy-start.7 = (f32[32]{0:T(128)S(1)}, f32[32]{0:T(128)}, u32[]{:S(2)}) copy-start(f32[32]{0:T(128)} %damping_ref.1) | copy-start | bytes 388
  9.1 9.6 %collective-permute-start.5 = (f32[40,1440]{1,0:T(8,128)S(1)}, f32[40,1440]{1,0:T(8,128)S(1)}, u32[]{:S(2)}, u32[]{:S(2)}) collective-permute-start(f32[40,1440]{1,0:T(8,128)S(1)} %get-tuple-element.50), channel_id=1, source_target_pairs={{4,8},{8,4},{12,16},{16,12},{20,24},{24,20},{5,9},{9,5},{13,17},{1... | collective-permute-start | bytes 691208 | tf_op jit(solution)/shard_map/ppermute | solution.py:518
  11.2 1.8 %collective-permute-start.3 = (f32[2,1,8,1440]{3,2,1,0:T(8,128)S(1)}, f32[2,1,8,1440]{3,2,1,0:T(8,128)S(1)}, u32[]{:S(2)}, u32[]{:S(2)}) collective-permute-start(f32[2,1,8,1440]{3,2,1,0:T(8,128)S(1)} %get-tuple-element.46), channel_id=1, source_target_pairs={{0,1},{1,0},{2,3},{3,2},{4,5},{5,4},{6,7},{7,6},{8,9},{9,8},{10,11... | collective-permute-start | bytes 276488 | tf_op jit(solution)/shard_map/ppermute | solution.py:509
  13.8 6.6 %collective-permute-start.4 = (f32[2,8,2176]{2,1,0:T(8,128)S(1)}, f32[2,8,2176]{2,1,0:T(8,128)S(1)}, u32[]{:S(2)}, u32[]{:S(2)}) collective-permute-start(f32[2,8,2176]{2,1,0:T(8,128)S(1)} %get-tuple-element.48.after_ref.own_ref), channel_id=1, source_target_pairs={{0,2},{1,3},{2,0},{3,1},{4,6},{5,7},{6,4},{7,5},{8,10},{9,11},{10,... | collective-permute-start | bytes 417800 | tf_op jit(solution)/shard_map/ppermute | solution.py:512
  18.8 2.5 %collective-permute-start.6 = (f32[2,1,8,1440]{3,2,1,0:T(8,128)S(1)}, f32[2,1,8,1440]{3,2,1,0:T(8,128)S(1)}, u32[]{:S(2)}, u32[]{:S(2)}) collective-permute-start(f32[2,1,8,1440]{3,2,1,0:T(8,128)S(1)} %get-tuple-element.54), channel_id=1, source_target_pairs={{0,1},{1,0},{2,3},{3,2},{4,5},{5,4},{6,7},{7,6},{8,9},{9,8},{10,11... | collective-permute-start | bytes 276488 | tf_op jit(solution)/shard_map/ppermute | solution.py:509
  22.3 4.9 %collective-permute-start.7 = (f32[2,8,2176]{2,1,0:T(8,128)S(1)}, f32[2,8,2176]{2,1,0:T(8,128)S(1)}, u32[]{:S(2)}, u32[]{:S(2)}) collective-permute-start(f32[2,8,2176]{2,1,0:T(8,128)S(1)} %get-tuple-element.56.after_ref.own_ref), channel_id=1, source_target_pairs={{0,2},{1,3},{2,0},{3,1},{4,6},{5,7},{6,4},{7,5},{8,10},{9,11},{10,... | collective-permute-start | bytes 417800 | tf_op jit(solution)/shard_map/ppermute | solution.py:512
  22.5 6.6 %collective-permute-start.8 = (f32[2,2,8,1440]{3,2,1,0:T(8,128)S(1)}, f32[2,2,8,1440]{3,2,1,0:T(8,128)S(1)}, u32[]{:S(2)}, u32[]{:S(2)}) collective-permute-start(f32[2,2,8,1440]{3,2,1,0:T(8,128)S(1)} %get-tuple-element.58), channel_id=1, source_target_pairs={{0,1},{1,0},{2,3},{3,2},{4,5},{5,4},{6,7},{7,6},{8,9},{9,8},{10,11... | collective-permute-start | bytes 552968 | tf_op jit(solution)/shard_map/ppermute | solution.py:509
  23.1 6.0 %collective-permute-start.9 = (f32[2,1,8,1440]{3,2,1,0:T(8,128)S(1)}, f32[2,1,8,1440]{3,2,1,0:T(8,128)S(1)}, u32[]{:S(2)}, u32[]{:S(2)}) collective-permute-start(f32[2,1,8,1440]{3,2,1,0:T(8,128)S(1)} %get-tuple-element.59), channel_id=1, source_target_pairs={{0,1},{1,0},{2,3},{3,2},{4,5},{5,4},{6,7},{7,6},{8,9},{9,8},{10,11... | collective-permute-start | bytes 276488 | tf_op jit(solution)/shard_map/ppermute | solution.py:509
  27.8 2.2 %collective-permute-start.10 = (f32[2,1,8,1440]{3,2,1,0:T(8,128)S(1)}, f32[2,1,8,1440]{3,2,1,0:T(8,128)S(1)}, u32[]{:S(2)}, u32[]{:S(2)}) collective-permute-start(f32[2,1,8,1440]{3,2,1,0:T(8,128)S(1)} %get-tuple-element.60), channel_id=1, source_target_pairs={{0,1},{1,0},{2,3},{3,2},{4,5},{5,4},{6,7},{7,6},{8,9},{9,8},{10,11... | collective-permute-start | bytes 276488 | tf_op jit(solution)/shard_map/ppermute | solution.py:509

commit v9 on v8

--- a/solution.py
+++ b/solution.py
@@ -328,12 +328,7 @@
                 gain_ref[row, 2 * r + 1] = (re * mix_im + im * mix_re) * weight
 
 
-def shift_kernel(which, columns, distance_ref, share_ref, held_ref, after_ref, *refs):
-    if which == "inner":
-        source_ref, moved_ref, relay_ref = refs
-        relay_ref[...] = source_ref[...]
-    else:
-        (moved_ref,) = refs
+def shift_kernel(which, columns, distance_ref, share_ref, held_ref, after_ref, moved_ref):
     _, count, levels, padded = held_ref.shape
     rows = rows_of(which, share_ref.shape[0])
     number = len(rows)
@@ -529,12 +524,12 @@
             [(count * group, padded)],
         )
 
-    def shifted(which, held, after, *relay):
+    def shifted(which, held, after):
         count = held.shape[1]
         return call(
             functools.partial(shift_kernel, which, column_count),
-            [(count, PAIR, level_count, width)] + [v.shape for v in relay],
-            whole(distance, fraction, held) + [(after, UNREAD)] + whole(*relay),
+            [(count, PAIR, level_count, width)],
+            whole(distance, fraction, held) + [(after, UNREAD)],
         )
 
     def inverse(which, held, moved, own, other, after):
@@ -557,7 +552,7 @@
         tracer_count + 1,
     )
     inner_theirs = swap_core(inner_send)
-    near_got = swap_band(near_edge, 0)
+    far_got = swap_band(far_edge, 1)
     inner_own, inner_held = forward(inner_mine, inner_theirs, near_part)
     inner_other = swap_half(inner_own)
     row_shape = (row_count, level_count, LANES)
@@ -568,34 +563,34 @@
         + whole(wave)
         + [(inner_own, UNREAD)],
     )
-    inner_moved, far_relay = shifted("inner", inner_held, inner_own, far_edge)
-    far_got = swap_band(far_relay, 1)
+    (inner_moved,) = shifted("inner", inner_held, inner_own)
+    near_got = swap_band(near_edge, 0)
+
+    far_mine, far_send = call(
+        functools.partial(edge_kernel, False),
+        [set_shape(1)] * 2,
+        whole(far_edge, far_got, far_part) + [(inner_moved, UNREAD)],
+    )
+    far_theirs = swap_core(far_send)
+    far_own, far_held = forward(far_mine, far_theirs, inner_moved)
+    far_other = swap_half(far_own)
+    (far_moved,) = shifted("far", far_held, far_own)
+    inner = inverse("inner", inner_held, inner_moved, inner_own, inner_other, far_moved)
+    inner_back = swap_core(inner[1])
 
     near_mine, near_send = call(
         functools.partial(edge_kernel, True),
         [set_shape(1)] * 2,
-        whole(near_edge, near_got, near_part) + [(inner_moved, UNREAD)],
+        whole(near_edge, near_got, near_part) + [(inner[0], UNREAD)],
     )
     near_theirs = swap_core(near_send)
-    near_own, near_held = forward(near_mine, near_theirs, inner_moved)
+    near_own, near_held = forward(near_mine, near_theirs, inner[0])
     near_other = swap_half(near_own)
     (near_moved,) = shifted("near", near_held, near_own)
-    inner = inverse("inner", inner_held, inner_moved, inner_own, inner_other, near_moved)
-    inner_back = swap_core(inner[1])
-
-    far_mine, far_send = call(
-        functools.partial(edge_kernel, False),
-        [set_shape(1)] * 2,
-        whole(far_edge, far_got, far_part) + [(inner[0], UNREAD)],
-    )
-    far_theirs = swap_core(far_send)
-    near = inverse("near", near_held, near_moved, near_own, near_other, far_mine)
+    far = inverse("far", far_held, far_moved, far_own, far_other, near_moved)
+    far_back = swap_core(far[1])
+    near = inverse("near", near_held, near_moved, near_own, near_other, far[0])
     near_back = swap_core(near[1])
-    far_own, far_held = forward(far_mine, far_theirs, near[0])
-    far_other = swap_half(far_own)
-    (far_moved,) = shifted("far", far_held, far_own)
-    far = inverse("far", far_held, far_moved, far_own, far_other, far_moved)
-    far_back = swap_core(far[1])
     (result,) = call(
         end_kernel,
         [tracers.shape],

time: 31.3 us -> 31.6 us (level)
  starting transfers between devices: 9.34 us -> 11.8 us
  waiting for transfers between devices: 9.74 us -> 7.56 us
    ppermute x3, waiting for transfers between devices: 3.73 us -> 2.17 us  [swap_half(): return lax.ppermute(value, 'lon', [(p, p ^ 2) for p in range(lon_count)])]
    ppermute x6, waiting for transfers between devices: 3.24 us -> 1.89 us  [swap_core(): return lax.ppermute(value, 'lon', [(p, p ^ 1) for p in range(lon_count)])]
    ppermute x2, starting transfers between devices: 1.92 us -> 3.17 us  [swap_band(): return lax.ppermute(value, 'lat', pairs)]
    ppermute x3, starting transfers between devices: 2.34 us -> 3.45 us  [swap_half(): return lax.ppermute(value, 'lon', [(p, p ^ 2) for p in range(lon_count)])]
    ppermute x2, waiting for transfers between devices: 2.77 us -> 3.49 us  [swap_band(): return lax.ppermute(value, 'lat', pairs)]
  transfers between devices with their start and end apart: 11 -> 11, of which waited for: 6 -> 6; matrix products, arithmetic and copies ran while one was open for 0% -> 0% of each run, Pallas kernels for 23% -> 25%
where the time goes in v9:
time: 31.6 us; the launch traced here: 31.3 us
  starting transfers between devices  11.8 us (37%)
  Pallas kernels  11.1 us (35%)
  waiting for transfers between devices  7.56 us (24%)
  local copies, waits for them, and re-layouts  0.69 us (2%)
    pallas_call x14, Pallas kernels, call(): pl.pallas_call(kernel, out_shape=[jax.ShapeDtypeStruct(shape, jnp.float32...  11.1 us
    ppermute x6, starting transfers between devices, swap_core(): return lax.ppermute(value, 'lon', [(p, p ^ 1) for p in range(lon_count)])  5.17 us
    ppermute x2, waiting for transfers between devices, swap_band(): return lax.ppermute(value, 'lat', pairs)  3.49 us
    ppermute x3, starting transfers between devices, swap_half(): return lax.ppermute(value, 'lon', [(p, p ^ 2) for p in range(lon_count)])  3.45 us
    ppermute x2, starting transfers between devices, swap_band(): return lax.ppermute(value, 'lat', pairs)  3.17 us
    ppermute x3, waiting for transfers between devices, swap_half(): return lax.ppermute(value, 'lon', [(p, p ^ 2) for p in range(lon_count)])  2.17 us
    ppermute x6, waiting for transfers between devices, swap_core(): return lax.ppermute(value, 'lon', [(p, p ^ 1) for p in range(lon_count)])  1.89 us
    unnamed x16, local copies, waits for them, and re-layouts  0.69 us
  transfers between devices with their start and end apart: 11, of which 6 were waited for; matrix products, arithmetic and copies ran while one was open for 0% of the time, Pallas kernels for 25%

profile of v9, /device:TPU:3, one launch (start us, length us, event | category | flops | bytes accessed | tf_op | source)
XLA Modules:
  0.0 31.3 jit_solution(10727566843989052179)
XLA Ops:
  0.0 0.0 copy-start
  0.0 0.0 copy-start.1
  0.0 2.3 %shard_map.100 = (f32[2,2,8,1440]{3,2,1,0:T(8,128)S(1)}, f32[2,2,8,1440]{3,2,1,0:T(8,128)S(1)}, f32[40,1440]{1,0:T(8,128)S(1)}, f32[40,1440]{1,0:T(8,128)S(1)}, ...) custom-call(f32[4,8,4,1440]{3,2,1,0:T(4,128)} %cells_hbm.1, f32[8,4,1440]{2,1,0:T(4,128)} %speed_hbm.1), custom_call_target="tpu_custom_call" | custom-call | flops 1 | bytes 1 | tf_op jit(solution)/shard_map/pallas_call | solution.py:473
  2.3 0.7 %collective-permute-start = (f32[2,2,8,1440]{3,2,1,0:T(8,128)S(1)}, f32[2,2,8,1440]{3,2,1,0:T(8,128)S(1)}, u32[]{:S(2)}, u32[]{:S(2)}) collective-permute-start(f32[2,2,8,1440]{3,2,1,0:T(8,128)S(1)} %get-tuple-element.32), channel_id=1, source_target_pairs={{0,1},{1,0},{2,3},{3,2},{4,5},{5,4},{6,7},{7,6},{8,9},{9,8},{10,11... | collective-permute-start | bytes 552968 | tf_op jit(solution)/shard_map/ppermute | solution.py:504
  3.0 3.2 %collective-permute-start.2 = (f32[40,1440]{1,0:T(8,128)S(1)}, f32[40,1440]{1,0:T(8,128)S(1)}, u32[]{:S(2)}, u32[]{:S(2)}) collective-permute-start(f32[40,1440]{1,0:T(8,128)S(1)} %get-tuple-element.40.own_ref), channel_id=1, source_target_pairs={{4,8},{8,4},{12,16},{16,12},{20,24},{24,20},{5,9},{9,5},{13,17},{1... | collective-permute-start | bytes 691208 | tf_op jit(solution)/shard_map/ppermute | solution.py:513
  6.2 0.0 collective-permute-done.theirs_ref
  6.2 0.0 copy-done
  6.2 0.0 copy-done.1
  6.3 0.0 copy-done.2
  6.3 0.0 copy-start.3
  6.3 1.5 %shard_map.101 = (f32[4,8,2176]{2,1,0:T(8,128)S(1)}, f32[2,4,8,1536]{3,2,1,0:T(8,128)S(1)}) custom-call(f32[2,2,8,1440]{3,2,1,0:T(8,128)S(1)} %get-tuple-element.31.mine_ref, f32[2,2,8,1440]{3,2,1,0:T(8,128)S(1)} %collective-permute-done.theirs_ref, f32[18,384]{1,0:T(8,128)S(1)} %copy-done.2, bf16[384,256]{1,0:T(8,128)(2,1)S(1)} %copy-done, ...), custom_call_target="tpu_custom_call" | custom-call | flops 1 | bytes 1 | tf_op jit(solution)/shard_map/pallas_call | solution.py:473
  7.7 1.3 %collective-permute-start.1 = (f32[4,8,2176]{2,1,0:T(8,128)S(1)}, f32[4,8,2176]{2,1,0:T(8,128)S(1)}, u32[]{:S(2)}, u32[]{:S(2)}) collective-permute-start(f32[4,8,2176]{2,1,0:T(8,128)S(1)} %get-tuple-element.34.after_ref.own_ref), channel_id=1, source_target_pairs={{0,2},{1,3},{2,0},{3,1},{4,6},{5,7},{6,4},{7,5},{8,10},{9,11},{10,... | collective-permute-start | bytes 835592 | tf_op jit(solution)/shard_map/ppermute | solution.py:507
  9.0 0.0 collective-permute-start.4
  9.0 0.0 copy-start.7
  9.0 0.0 copy-done.3
  9.0 0.6 %copy-done.5 = f32[8,4]{0,1:T(4,128)S(1)} copy-done((f32[8,4]{0,1:T(4,128)S(1)}, f32[8,4]{0,1:T(4,128)}, u32[]{:S(2)}) %copy-start.5) | copy-done | bytes 152
  9.7 0.0 copy-done.4
  9.7 0.0 copy-done.6
  9.7 0.0 copy-done.7
  9.7 0.9 %shard_map.102 = (f32[4,8,128]{2,1,0:T(8,128)S(1)}, f32[4,8,128]{2,1,0:T(8,128)S(1)}, f32[4,8,128]{2,1,0:T(8,128)S(1)}, f32[4,18,8,128]{3,2,1,0:T(8,128)S(1)}) custom-call(s32[4,8]{1,0:T(4,128)S(1)} %bitcast.2, f32[4,8]{1,0:T(4,128)S(1)} %bitcast.3, s32[32]{0:T(128)S(1)} %copy-done.6, f32[32]{0:T(128)S(1)} %copy-done.7, f32[18,128]{1,0:T(8,128)S(1)} %copy-done.3, ...), custom_call_target="tpu_custom_call" | custom-call | flops 1 | bytes 1 | tf_op jit(solution)/shard_map/pallas_call | solution.py:473
  10.6 0.7 %shard_map.103.after_ref.moved_ref = f32[4,2,8,1536]{3,2,1,0:T(8,128)S(1)} custom-call(f32[4,8,128]{2,1,0:T(8,128)S(1)} %get-tuple-element.35.distance_ref, f32[4,8,128]{2,1,0:T(8,128)S(1)} %get-tuple-element.36.share_ref, f32[2,4,8,1536]{3,2,1,0:T(8,128)S(1)} %get-tuple-element.39.held_ref, f32[4,8,2176]{2,1,0:T(8,128)S(1)} %get-tuple-element.34.after_ref.own_ref), custom_call_target="tpu_custom_call" | custom-call | flops 1 | bytes 1 | tf_op jit(solution)/shard_map/pallas_call | solution.py:473
  11.3 2.1 %collective-permute-done.2.got_ref = f32[40,1440]{1,0:T(8,128)S(1)} collective-permute-done((f32[40,1440]{1,0:T(8,128)S(1)}, f32[40,1440]{1,0:T(8,128)S(1)}, u32[]{:S(2)}, u32[]{:S(2)}) %collective-permute-start.2) | collective-permute-done | bytes 230432 | tf_op jit(solution)/shard_map/ppermute | solution.py:513
  13.4 0.1 shard_map.104
  13.5 1.0 %collective-permute-start.3 = (f32[2,1,8,1440]{3,2,1,0:T(8,128)S(1)}, f32[2,1,8,1440]{3,2,1,0:T(8,128)S(1)}, u32[]{:S(2)}, u32[]{:S(2)}) collective-permute-start(f32[2,1,8,1440]{3,2,1,0:T(8,128)S(1)} %get-tuple-element.43), channel_id=1, source_target_pairs={{0,1},{1,0},{2,3},{3,2},{4,5},{5,4},{6,7},{7,6},{8,9},{9,8},{10,11... | collective-permute-start | bytes 276488 | tf_op jit(solution)/shard_map/ppermute | solution.py:504
  14.5 0.9 %collective-permute-done.3.theirs_ref = f32[2,1,8,1440]{3,2,1,0:T(8,128)S(1)} collective-permute-done((f32[2,1,8,1440]{3,2,1,0:T(8,128)S(1)}, f32[2,1,8,1440]{3,2,1,0:T(8,128)S(1)}, u32[]{:S(2)}, u32[]{:S(2)}) %collective-permute-start.3) | collective-permute-done | bytes 92192 | tf_op jit(solution)/shard_map/ppermute | solution.py:504
  15.4 0.9 %shard_map.105 = (f32[2,8,2176]{2,1,0:T(8,128)S(1)}, f32[2,2,8,1536]{3,2,1,0:T(8,128)S(1)}) custom-call(f32[2,1,8,1440]{3,2,1,0:T(8,128)S(1)} %get-tuple-element.42.mine_ref, f32[2,1,8,1440]{3,2,1,0:T(8,128)S(1)} %collective-permute-done.3.theirs_ref, f32[18,384]{1,0:T(8,128)S(1)} %copy-done.2, bf16[384,256]{1,0:T(8,128)(2,1)S(1)} %copy-done, ...), custom_call_target="tpu_custom_call" | custom-call | flops 1 | bytes 1 | tf_op jit(solution)/shard_map/pallas_call | solution.py:473
  16.3 0.3 shard_map.106.after_ref.moved_ref
  16.6 0.0 collective-permute-done.1.other_ref
  16.6 1.0 %shard_map.107 = (f32[2,2,8,1440]{3,2,1,0:T(8,128)S(1)}, f32[2,2,8,1440]{3,2,1,0:T(8,128)S(1)}) custom-call(f32[4,8,128]{2,1,0:T(8,128)S(1)} %get-tuple-element.35.distance_ref, f32[4,8,128]{2,1,0:T(8,128)S(1)} %get-tuple-element.36.share_ref, f32[4,8,128]{2,1,0:T(8,128)S(1)} %get-tuple-element.37.keep_ref, ...), custom_call_target="tpu_custom_call" | custom-call | flops 1 | bytes 1 | tf_op jit(solution)/shard_map/pallas_call | solution.py:473
  17.6 1.4 %collective-permute-done.4.got_ref = f32[40,1440]{1,0:T(8,128)S(1)} collective-permute-done((f32[40,1440]{1,0:T(8,128)S(1)}, f32[40,1440]{1,0:T(8,128)S(1)}, u32[]{:S(2)}, u32[]{:S(2)}) %collective-permute-start.4) | collective-permute-done | bytes 230432 | tf_op jit(solution)/shard_map/ppermute | solution.py:513
  19.0 0.1 shard_map.108
  19.1 0.6 %collective-permute-start.5 = (f32[2,1,8,1440]{3,2,1,0:T(8,128)S(1)}, f32[2,1,8,1440]{3,2,1,0:T(8,128)S(1)}, u32[]{:S(2)}, u32[]{:S(2)}) collective-permute-start(f32[2,1,8,1440]{3,2,1,0:T(8,128)S(1)} %get-tuple-element.49), channel_id=1, source_target_pairs={{0,1},{1,0},{2,3},{3,2},{4,5},{5,4},{6,7},{7,6},{8,9},{9,8},{10,11... | collective-permute-start | bytes 276488 | tf_op jit(solution)/shard_map/ppermute | solution.py:504
  19.6 1.3 %collective-permute-start.7 = (f32[2,8,2176]{2,1,0:T(8,128)S(1)}, f32[2,8,2176]{2,1,0:T(8,128)S(1)}, u32[]{:S(2)}, u32[]{:S(2)}) collective-permute-start(f32[2,8,2176]{2,1,0:T(8,128)S(1)} %get-tuple-element.45.after_ref.own_ref), channel_id=1, source_target_pairs={{0,2},{1,3},{2,0},{3,1},{4,6},{5,7},{6,4},{7,5},{8,10},{9,11},{10,... | collective-permute-start | bytes 417800 | tf_op jit(solution)/shard_map/ppermute | solution.py:507
  20.9 0.0 collective-permute-done.5.theirs_ref
  20.9 0.9 %shard_map.109 = (f32[2,8,2176]{2,1,0:T(8,128)S(1)}, f32[2,2,8,1536]{3,2,1,0:T(8,128)S(1)}) custom-call(f32[2,1,8,1440]{3,2,1,0:T(8,128)S(1)} %get-tuple-element.48.mine_ref, f32[2,1,8,1440]{3,2,1,0:T(8,128)S(1)} %collective-permute-done.5.theirs_ref, f32[18,384]{1,0:T(8,128)S(1)} %copy-done.2, bf16[384,256]{1,0:T(8,128)(2,1)S(1)} %copy-done, ...), custom_call_target="tpu_custom_call" | custom-call | flops 1 | bytes 1 | tf_op jit(solution)/shard_map/pallas_call | solution.py:473
  21.8 0.9 %collective-permute-start.6 = (f32[2,8,2176]{2,1,0:T(8,128)S(1)}, f32[2,8,2176]{2,1,0:T(8,128)S(1)}, u32[]{:S(2)}, u32[]{:S(2)}) collective-permute-start(f32[2,8,2176]{2,1,0:T(8,128)S(1)} %get-tuple-element.51.after_ref.own_ref), channel_id=1, source_target_pairs={{0,2},{1,3},{2,0},{3,1},{4,6},{5,7},{6,4},{7,5},{8,10},{9,11},{10,... | collective-permute-start | bytes 417800 | tf_op jit(solution)/shard_map/ppermute | solution.py:507
  22.7 0.6 %collective-permute-start.8 = (f32[2,2,8,1440]{3,2,1,0:T(8,128)S(1)}, f32[2,2,8,1440]{3,2,1,0:T(8,128)S(1)}, u32[]{:S(2)}, u32[]{:S(2)}) collective-permute-start(f32[2,2,8,1440]{3,2,1,0:T(8,128)S(1)} %get-tuple-element.54), channel_id=1, source_target_pairs={{0,1},{1,0},{2,3},{3,2},{4,5},{5,4},{6,7},{7,6},{8,9},{9,8},{10,11... | collective-permute-start | bytes 552968 | tf_op jit(solution)/shard_map/ppermute | solution.py:504
  23.3 0.3 shard_map.110.after_ref.moved_ref
  23.7 1.2 %collective-permute-done.7.other_ref = f32[2,8,2176]{2,1,0:T(8,128)S(1)} collective-permute-done((f32[2,8,2176]{2,1,0:T(8,128)S(1)}, f32[2,8,2176]{2,1,0:T(8,128)S(1)}, u32[]{:S(2)}, u32[]{:S(2)}) %collective-permute-start.7) | collective-permute-done | bytes 139296 | tf_op jit(solution)/shard_map/ppermute | solution.py:507
  24.9 0.6 %shard_map.111 = (f32[2,1,8,1440]{3,2,1,0:T(8,128)S(1)}, f32[2,1,8,1440]{3,2,1,0:T(8,128)S(1)}) custom-call(f32[4,8,128]{2,1,0:T(8,128)S(1)} %get-tuple-element.35.distance_ref, f32[4,8,128]{2,1,0:T(8,128)S(1)} %get-tuple-element.36.share_ref, f32[4,8,128]{2,1,0:T(8,128)S(1)} %get-tuple-element.37.keep_ref, ...), custom_call_target="tpu_custom_call" | custom-call | flops 1 | bytes 1 | tf_op jit(solution)/shard_map/pallas_call | solution.py:473
  25.5 1.4 %collective-permute-start.10 = (f32[2,1,8,1440]{3,2,1,0:T(8,128)S(1)}, f32[2,1,8,1440]{3,2,1,0:T(8,128)S(1)}, u32[]{:S(2)}, u32[]{:S(2)}) collective-permute-start(f32[2,1,8,1440]{3,2,1,0:T(8,128)S(1)} %get-tuple-element.56), channel_id=1, source_target_pairs={{0,1},{1,0},{2,3},{3,2},{4,5},{5,4},{6,7},{7,6},{8,9},{9,8},{10,11... | collective-permute-start | bytes 276488 | tf_op jit(solution)/shard_map/ppermute | solution.py:504
  26.9 1.0 %collective-permute-done.6.other_ref = f32[2,8,2176]{2,1,0:T(8,128)S(1)} collective-permute-done((f32[2,8,2176]{2,1,0:T(8,128)S(1)}, f32[2,8,2176]{2,1,0:T(8,128)S(1)}, u32[]{:S(2)}, u32[]{:S(2)}) %collective-permute-start.6) | collective-permute-done | bytes 139296 | tf_op jit(solution)/shard_map/ppermute | solution.py:507
  27.8 0.6 %shard_map.112 = (f32[2,1,8,1440]{3,2,1,0:T(8,128)S(1)}, f32[2,1,8,1440]{3,2,1,0:T(8,128)S(1)}) custom-call(f32[4,8,128]{2,1,0:T(8,128)S(1)} %get-tuple-element.35.distance_ref, f32[4,8,128]{2,1,0:T(8,128)S(1)} %get-tuple-element.36.share_ref, f32[4,8,128]{2,1,0:T(8,128)S(1)} %get-tuple-element.37.keep_ref, ...), custom_call_target="tpu_custom_call" | custom-call | flops 1 | bytes 1 | tf_op jit(solution)/shard_map/pallas_call | solution.py:473
  28.5 0.9 %collective-permute-start.9 = (f32[2,1,8,1440]{3,2,1,0:T(8,128)S(1)}, f32[2,1,8,1440]{3,2,1,0:T(8,128)S(1)}, u32[]{:S(2)}, u32[]{:S(2)}) collective-permute-start(f32[2,1,8,1440]{3,2,1,0:T(8,128)S(1)} %get-tuple-element.55), channel_id=1, source_target_pairs={{0,1},{1,0},{2,3},{3,2},{4,5},{5,4},{6,7},{7,6},{8,9},{9,8},{10,11... | collective-permute-start | bytes 276488 | tf_op jit(solution)/shard_map/ppermute | solution.py:504
  29.4 0.0 collective-permute-done.8.refs_3_
  29.4 0.0 collective-permute-done.10.refs_5_
  29.4 0.9 %collective-permute-done.9.refs_4_ = f32[2,1,8,1440]{3,2,1,0:T(8,128)S(1)} collective-permute-done((f32[2,1,8,1440]{3,2,1,0:T(8,128)S(1)}, f32[2,1,8,1440]{3,2,1,0:T(8,128)S(1)}, u32[]{:S(2)}, u32[]{:S(2)}) %collective-permute-start.9) | collective-permute-done | bytes 92192 | tf_op jit(solution)/shard_map/ppermute | solution.py:504
  30.4 1.0 %shard_map.113 = f32[4,8,4,1440]{3,2,1,0:T(4,128)} custom-call(f32[2,2,8,1440]{3,2,1,0:T(8,128)S(1)} %get-tuple-element.46.after_ref.refs_0_, f32[2,1,8,1440]{3,2,1,0:T(8,128)S(1)} %get-tuple-element.53.refs_1_, f32[2,1,8,1440]{3,2,1,0:T(8,128)S(1)} %get-tuple-element.52.after_ref.refs_2_, f32[2,2,8,1440]{3,2,1,0:T(8,128)S(1)} %collective-permute-done.8.refs_3_, ...), custom_call_target="tpu_custom_call" | custom-call | flops 1 | bytes 1 | tf_op jit(solution)/shard_map/pallas_call | solution.py:473
  (4 shorter events, 0.0 us)
Async XLA Ops:
  0.0 6.2 %copy-start = (bf16[384,256]{1,0:T(8,128)(2,1)S(1)}, bf16[384,256]{1,0:T(8,128)(2,1)}, u32[]{:S(2)}) copy-start(bf16[384,256]{1,0:T(8,128)(2,1)} %constant.10.clone.high_ref) | copy-start | bytes 589828
  0.0 6.2 %copy-start.1 = (bf16[384,256]{1,0:T(8,128)(2,1)S(1)}, bf16[384,256]{1,0:T(8,128)(2,1)}, u32[]{:S(2)}) copy-start(bf16[384,256]{1,0:T(8,128)(2,1)} %constant.11.clone.low_ref) | copy-start | bytes 589828
  0.0 6.2 %copy-start.2 = (f32[18,384]{1,0:T(8,128)S(1)}, f32[18,384]{1,0:T(8,128)}, u32[]{:S(2)}) copy-start(f32[18,384]{1,0:T(8,128)} %constant.8.clone.phase_ref) | copy-start | bytes 82948
  2.3 3.9 %collective-permute-start = (f32[2,2,8,1440]{3,2,1,0:T(8,128)S(1)}, f32[2,2,8,1440]{3,2,1,0:T(8,128)S(1)}, u32[]{:S(2)}, u32[]{:S(2)}) collective-permute-start(f32[2,2,8,1440]{3,2,1,0:T(8,128)S(1)} %get-tuple-element.32), channel_id=1, source_target_pairs={{0,1},{1,0},{2,3},{3,2},{4,5},{5,4},{6,7},{7,6},{8,9},{9,8},{10,11... | collective-permute-start | bytes 552968 | tf_op jit(solution)/shard_map/ppermute | solution.py:504
  3.0 10.4 %collective-permute-start.2 = (f32[40,1440]{1,0:T(8,128)S(1)}, f32[40,1440]{1,0:T(8,128)S(1)}, u32[]{:S(2)}, u32[]{:S(2)}) collective-permute-start(f32[40,1440]{1,0:T(8,128)S(1)} %get-tuple-element.40.own_ref), channel_id=1, source_target_pairs={{4,8},{8,4},{12,16},{16,12},{20,24},{24,20},{5,9},{9,5},{13,17},{1... | collective-permute-start | bytes 691208 | tf_op jit(solution)/shard_map/ppermute | solution.py:513
  6.3 2.8 %copy-start.3 = (f32[18,128]{1,0:T(8,128)S(1)}, f32[18,128]{1,0:T(8,128)}, u32[]{:S(2)}) copy-start(f32[18,128]{1,0:T(8,128)} %constant.9.clone.wave_ref) | copy-start | bytes 27652
  7.7 8.9 %collective-permute-start.1 = (f32[4,8,2176]{2,1,0:T(8,128)S(1)}, f32[4,8,2176]{2,1,0:T(8,128)S(1)}, u32[]{:S(2)}, u32[]{:S(2)}) collective-permute-start(f32[4,8,2176]{2,1,0:T(8,128)S(1)} %get-tuple-element.34.after_ref.own_ref), channel_id=1, source_target_pairs={{0,2},{1,3},{2,0},{3,1},{4,6},{5,7},{6,4},{7,5},{8,10},{9,11},{10,... | collective-permute-start | bytes 835592 | tf_op jit(solution)/shard_map/ppermute | solution.py:507
  9.0 0.7 %copy-start.5 = (f32[8,4]{0,1:T(4,128)S(1)}, f32[8,4]{0,1:T(4,128)}, u32[]{:S(2)}) copy-start(f32[8,4]{0,1:T(4,128)} %param.13) | copy-start | bytes 388
  9.0 0.7 %copy-start.4 = (s32[8,4]{0,1:T(4,128)S(1)}, s32[8,4]{0,1:T(4,128)}, u32[]{:S(2)}) copy-start(s32[8,4]{0,1:T(4,128)} %param.12) | copy-start | bytes 388
  9.0 10.0 %collective-permute-start.4 = (f32[40,1440]{1,0:T(8,128)S(1)}, f32[40,1440]{1,0:T(8,128)S(1)}, u32[]{:S(2)}, u32[]{:S(2)}) collective-permute-start(f32[40,1440]{1,0:T(8,128)S(1)} %get-tuple-element.47.own_ref), channel_id=1, source_target_pairs={{0,4},{4,0},{8,12},{12,8},{16,20},{20,16},{24,28},{28,24},{1,5},{5... | collective-permute-start | bytes 691208 | tf_op jit(solution)/shard_map/ppermute | solution.py:513
  9.0 0.7 %copy-start.6 = (s32[32]{0:T(128)S(1)}, s32[32]{0:T(128)}, u32[]{:S(2)}) copy-start(s32[32]{0:T(128)} %cutoff_ref.1) | copy-start | bytes 388
  9.0 0.7 %copy-start.7 = (f32[32]{0:T(128)S(1)}, f32[32]{0:T(128)}, u32[]{:S(2)}) copy-start(f32[32]{0:T(128)} %damping_ref.1) | copy-start | bytes 388
  13.5 1.9 %collective-permute-start.3 = (f32[2,1,8,1440]{3,2,1,0:T(8,128)S(1)}, f32[2,1,8,1440]{3,2,1,0:T(8,128)S(1)}, u32[]{:S(2)}, u32[]{:S(2)}) collective-permute-start(f32[2,1,8,1440]{3,2,1,0:T(8,128)S(1)} %get-tuple-element.43), channel_id=1, source_target_pairs={{0,1},{1,0},{2,3},{3,2},{4,5},{5,4},{6,7},{7,6},{8,9},{9,8},{10,11... | collective-permute-start | bytes 276488 | tf_op jit(solution)/shard_map/ppermute | solution.py:504
  19.1 1.8 %collective-permute-start.5 = (f32[2,1,8,1440]{3,2,1,0:T(8,128)S(1)}, f32[2,1,8,1440]{3,2,1,0:T(8,128)S(1)}, u32[]{:S(2)}, u32[]{:S(2)}) collective-permute-start(f32[2,1,8,1440]{3,2,1,0:T(8,128)S(1)} %get-tuple-element.49), channel_id=1, source_target_pairs={{0,1},{1,0},{2,3},{3,2},{4,5},{5,4},{6,7},{7,6},{8,9},{9,8},{10,11... | collective-permute-start | bytes 276488 | tf_op jit(solution)/shard_map/ppermute | solution.py:504
  19.6 5.3 %collective-permute-start.7 = (f32[2,8,2176]{2,1,0:T(8,128)S(1)}, f32[2,8,2176]{2,1,0:T(8,128)S(1)}, u32[]{:S(2)}, u32[]{:S(2)}) collective-permute-start(f32[2,8,2176]{2,1,0:T(8,128)S(1)} %get-tuple-element.45.after_ref.own_ref), channel_id=1, source_target_pairs={{0,2},{1,3},{2,0},{3,1},{4,6},{5,7},{6,4},{7,5},{8,10},{9,11},{10,... | collective-permute-start | bytes 417800 | tf_op jit(solution)/shard_map/ppermute | solution.py:507
  21.8 6.1 %collective-permute-start.6 = (f32[2,8,2176]{2,1,0:T(8,128)S(1)}, f32[2,8,2176]{2,1,0:T(8,128)S(1)}, u32[]{:S(2)}, u32[]{:S(2)}) collective-permute-start(f32[2,8,2176]{2,1,0:T(8,128)S(1)} %get-tuple-element.51.after_ref.own_ref), channel_id=1, source_target_pairs={{0,2},{1,3},{2,0},{3,1},{4,6},{5,7},{6,4},{7,5},{8,10},{9,11},{10,... | collective-permute-start | bytes 417800 | tf_op jit(solution)/shard_map/ppermute | solution.py:507
  22.7 6.7 %collective-permute-start.8 = (f32[2,2,8,1440]{3,2,1,0:T(8,128)S(1)}, f32[2,2,8,1440]{3,2,1,0:T(8,128)S(1)}, u32[]{:S(2)}, u32[]{:S(2)}) collective-permute-start(f32[2,2,8,1440]{3,2,1,0:T(8,128)S(1)} %get-tuple-element.54), channel_id=1, source_target_pairs={{0,1},{1,0},{2,3},{3,2},{4,5},{5,4},{6,7},{7,6},{8,9},{9,8},{10,11... | collective-permute-start | bytes 552968 | tf_op jit(solution)/shard_map/ppermute | solution.py:504
  25.5 3.9 %collective-permute-start.10 = (f32[2,1,8,1440]{3,2,1,0:T(8,128)S(1)}, f32[2,1,8,1440]{3,2,1,0:T(8,128)S(1)}, u32[]{:S(2)}, u32[]{:S(2)}) collective-permute-start(f32[2,1,8,1440]{3,2,1,0:T(8,128)S(1)} %get-tuple-element.56), channel_id=1, source_target_pairs={{0,1},{1,0},{2,3},{3,2},{4,5},{5,4},{6,7},{7,6},{8,9},{9,8},{10,11... | collective-permute-start | bytes 276488 | tf_op jit(solution)/shard_map/ppermute | solution.py:504
  28.5 1.9 %collective-permute-start.9 = (f32[2,1,8,1440]{3,2,1,0:T(8,128)S(1)}, f32[2,1,8,1440]{3,2,1,0:T(8,128)S(1)}, u32[]{:S(2)}, u32[]{:S(2)}) collective-permute-start(f32[2,1,8,1440]{3,2,1,0:T(8,128)S(1)} %get-tuple-element.55), channel_id=1, source_target_pairs={{0,1},{1,0},{2,3},{3,2},{4,5},{5,4},{6,7},{7,6},{8,9},{9,8},{10,11... | collective-permute-start | bytes 276488 | tf_op jit(solution)/shard_map/ppermute | solution.py:504

commit v10 on v9

--- a/solution.py
+++ b/solution.py
@@ -584,11 +584,11 @@
         whole(near_edge, near_got, near_part) + [(inner[0], UNREAD)],
     )
     near_theirs = swap_core(near_send)
-    near_own, near_held = forward(near_mine, near_theirs, inner[0])
+    far = inverse("far", far_held, far_moved, far_own, far_other, near_mine)
+    far_back = swap_core(far[1])
+    near_own, near_held = forward(near_mine, near_theirs, far[0])
     near_other = swap_half(near_own)
     (near_moved,) = shifted("near", near_held, near_own)
-    far = inverse("far", far_held, far_moved, far_own, far_other, near_moved)
-    far_back = swap_core(far[1])
     near = inverse("near", near_held, near_moved, near_own, near_other, far[0])
     near_back = swap_core(near[1])
     (result,) = call(

time: 31.6 us -> 32 us (1.013)
  starting transfers between devices: 11.8 us -> 13.1 us
  waiting for transfers between devices: 7.56 us -> 6.6 us
    ppermute x2, waiting for transfers between devices: 3.49 us -> 2.26 us  [swap_band(): return lax.ppermute(value, 'lat', pairs)]
    ppermute x6, starting transfers between devices: 5.17 us -> 6.16 us  [swap_core(): return lax.ppermute(value, 'lon', [(p, p ^ 1) for p in range(lon_count)])]
  transfers between devices with their start and end apart: 11 -> 11, of which waited for: 6 -> 6; matrix products, arithmetic and copies ran while one was open for 0% -> 0% of each run, Pallas kernels for 25% -> 22%
where the time goes in v10:
time: 32 us; the launch traced here: 31.6 us
  starting transfers between devices  13.1 us (41%)
  Pallas kernels  11.1 us (35%)
  waiting for transfers between devices  6.6 us (21%)
  local copies, waits for them, and re-layouts  0.69 us (2%)
    pallas_call x14, Pallas kernels, call(): pl.pallas_call(kernel, out_shape=[jax.ShapeDtypeStruct(shape, jnp.float32...  11.1 us
    ppermute x6, starting transfers between devices, swap_core(): return lax.ppermute(value, 'lon', [(p, p ^ 1) for p in range(lon_count)])  6.16 us
    ppermute x3, starting transfers between devices, swap_half(): return lax.ppermute(value, 'lon', [(p, p ^ 2) for p in range(lon_count)])  3.76 us
    ppermute x2, starting transfers between devices, swap_band(): return lax.ppermute(value, 'lat', pairs)  3.17 us
    ppermute x3, waiting for transfers between devices, swap_half(): return lax.ppermute(value, 'lon', [(p, p ^ 2) for p in range(lon_count)])  2.45 us
    ppermute x2, waiting for transfers between devices, swap_band(): return lax.ppermute(value, 'lat', pairs)  2.26 us
    ppermute x6, waiting for transfers between devices, swap_core(): return lax.ppermute(value, 'lon', [(p, p ^ 1) for p in range(lon_count)])  1.89 us
    unnamed x16, local copies, waits for them, and re-layouts  0.69 us
  transfers between devices with their start and end apart: 11, of which 6 were waited for; matrix products, arithmetic and copies ran while one was open for 0% of the time, Pallas kernels for 22%

profile of v10, /device:TPU:3, one launch (start us, length us, event | category | flops | bytes accessed | tf_op | source)
XLA Modules:
  0.0 31.6 jit_solution(9323979419315166070)
XLA Ops:
  0.0 0.0 copy-start
  0.0 0.0 copy-start.1
  0.0 2.3 %shard_map.100 = (f32[2,2,8,1440]{3,2,1,0:T(8,128)S(1)}, f32[2,2,8,1440]{3,2,1,0:T(8,128)S(1)}, f32[40,1440]{1,0:T(8,128)S(1)}, f32[40,1440]{1,0:T(8,128)S(1)}, ...) custom-call(f32[4,8,4,1440]{3,2,1,0:T(4,128)} %cells_hbm.1, f32[8,4,1440]{2,1,0:T(4,128)} %speed_hbm.1), custom_call_target="tpu_custom_call" | custom-call | flops 1 | bytes 1 | tf_op jit(solution)/shard_map/pallas_call | solution.py:473
  2.3 0.7 %collective-permute-start = (f32[2,2,8,1440]{3,2,1,0:T(8,128)S(1)}, f32[2,2,8,1440]{3,2,1,0:T(8,128)S(1)}, u32[]{:S(2)}, u32[]{:S(2)}) collective-permute-start(f32[2,2,8,1440]{3,2,1,0:T(8,128)S(1)} %get-tuple-element.32), channel_id=1, source_target_pairs={{0,1},{1,0},{2,3},{3,2},{4,5},{5,4},{6,7},{7,6},{8,9},{9,8},{10,11... | collective-permute-start | bytes 552968 | tf_op jit(solution)/shard_map/ppermute | solution.py:504
  3.0 3.2 %collective-permute-start.2 = (f32[40,1440]{1,0:T(8,128)S(1)}, f32[40,1440]{1,0:T(8,128)S(1)}, u32[]{:S(2)}, u32[]{:S(2)}) collective-permute-start(f32[40,1440]{1,0:T(8,128)S(1)} %get-tuple-element.40.own_ref), channel_id=1, source_target_pairs={{4,8},{8,4},{12,16},{16,12},{20,24},{24,20},{5,9},{9,5},{13,17},{1... | collective-permute-start | bytes 691208 | tf_op jit(solution)/shard_map/ppermute | solution.py:513
  6.2 0.0 collective-permute-done.theirs_ref
  6.2 0.0 copy-done
  6.2 0.0 copy-done.1
  6.3 0.0 copy-done.2
  6.3 0.0 copy-start.3
  6.3 1.5 %shard_map.101 = (f32[4,8,2176]{2,1,0:T(8,128)S(1)}, f32[2,4,8,1536]{3,2,1,0:T(8,128)S(1)}) custom-call(f32[2,2,8,1440]{3,2,1,0:T(8,128)S(1)} %get-tuple-element.31.mine_ref, f32[2,2,8,1440]{3,2,1,0:T(8,128)S(1)} %collective-permute-done.theirs_ref, f32[18,384]{1,0:T(8,128)S(1)} %copy-done.2, bf16[384,256]{1,0:T(8,128)(2,1)S(1)} %copy-done, ...), custom_call_target="tpu_custom_call" | custom-call | flops 1 | bytes 1 | tf_op jit(solution)/shard_map/pallas_call | solution.py:473
  7.7 1.3 %collective-permute-start.1 = (f32[4,8,2176]{2,1,0:T(8,128)S(1)}, f32[4,8,2176]{2,1,0:T(8,128)S(1)}, u32[]{:S(2)}, u32[]{:S(2)}) collective-permute-start(f32[4,8,2176]{2,1,0:T(8,128)S(1)} %get-tuple-element.34.after_ref.own_ref), channel_id=1, source_target_pairs={{0,2},{1,3},{2,0},{3,1},{4,6},{5,7},{6,4},{7,5},{8,10},{9,11},{10,... | collective-permute-start | bytes 835592 | tf_op jit(solution)/shard_map/ppermute | solution.py:507
  9.0 0.0 collective-permute-start.4
  9.0 0.0 copy-start.7
  9.0 0.0 copy-done.3
  9.0 0.6 %copy-done.5 = f32[8,4]{0,1:T(4,128)S(1)} copy-done((f32[8,4]{0,1:T(4,128)S(1)}, f32[8,4]{0,1:T(4,128)}, u32[]{:S(2)}) %copy-start.5) | copy-done | bytes 152
  9.7 0.0 copy-done.4
  9.7 0.0 copy-done.6
  9.7 0.0 copy-done.7
  9.7 0.9 %shard_map.102 = (f32[4,8,128]{2,1,0:T(8,128)S(1)}, f32[4,8,128]{2,1,0:T(8,128)S(1)}, f32[4,8,128]{2,1,0:T(8,128)S(1)}, f32[4,18,8,128]{3,2,1,0:T(8,128)S(1)}) custom-call(s32[4,8]{1,0:T(4,128)S(1)} %bitcast.2, f32[4,8]{1,0:T(4,128)S(1)} %bitcast.3, s32[32]{0:T(128)S(1)} %copy-done.6, f32[32]{0:T(128)S(1)} %copy-done.7, f32[18,128]{1,0:T(8,128)S(1)} %copy-done.3, ...), custom_call_target="tpu_custom_call" | custom-call | flops 1 | bytes 1 | tf_op jit(solution)/shard_map/pallas_call | solution.py:473
  10.6 0.7 %shard_map.103.after_ref.moved_ref = f32[4,2,8,1536]{3,2,1,0:T(8,128)S(1)} custom-call(f32[4,8,128]{2,1,0:T(8,128)S(1)} %get-tuple-element.35.distance_ref, f32[4,8,128]{2,1,0:T(8,128)S(1)} %get-tuple-element.36.share_ref, f32[2,4,8,1536]{3,2,1,0:T(8,128)S(1)} %get-tuple-element.39.held_ref, f32[4,8,2176]{2,1,0:T(8,128)S(1)} %get-tuple-element.34.after_ref.own_ref), custom_call_target="tpu_custom_call" | custom-call | flops 1 | bytes 1 | tf_op jit(solution)/shard_map/pallas_call | solution.py:473
  11.3 2.1 %collective-permute-done.2.got_ref = f32[40,1440]{1,0:T(8,128)S(1)} collective-permute-done((f32[40,1440]{1,0:T(8,128)S(1)}, f32[40,1440]{1,0:T(8,128)S(1)}, u32[]{:S(2)}, u32[]{:S(2)}) %collective-permute-start.2) | collective-permute-done | bytes 230432 | tf_op jit(solution)/shard_map/ppermute | solution.py:513
  13.4 0.1 shard_map.104
  13.5 1.0 %collective-permute-start.3 = (f32[2,1,8,1440]{3,2,1,0:T(8,128)S(1)}, f32[2,1,8,1440]{3,2,1,0:T(8,128)S(1)}, u32[]{:S(2)}, u32[]{:S(2)}) collective-permute-start(f32[2,1,8,1440]{3,2,1,0:T(8,128)S(1)} %get-tuple-element.43), channel_id=1, source_target_pairs={{0,1},{1,0},{2,3},{3,2},{4,5},{5,4},{6,7},{7,6},{8,9},{9,8},{10,11... | collective-permute-start | bytes 276488 | tf_op jit(solution)/shard_map/ppermute | solution.py:504
  14.5 0.9 %collective-permute-done.3.theirs_ref = f32[2,1,8,1440]{3,2,1,0:T(8,128)S(1)} collective-permute-done((f32[2,1,8,1440]{3,2,1,0:T(8,128)S(1)}, f32[2,1,8,1440]{3,2,1,0:T(8,128)S(1)}, u32[]{:S(2)}, u32[]{:S(2)}) %collective-permute-start.3) | collective-permute-done | bytes 92192 | tf_op jit(solution)/shard_map/ppermute | solution.py:504
  15.4 0.9 %shard_map.105 = (f32[2,8,2176]{2,1,0:T(8,128)S(1)}, f32[2,2,8,1536]{3,2,1,0:T(8,128)S(1)}) custom-call(f32[2,1,8,1440]{3,2,1,0:T(8,128)S(1)} %get-tuple-element.42.mine_ref, f32[2,1,8,1440]{3,2,1,0:T(8,128)S(1)} %collective-permute-done.3.theirs_ref, f32[18,384]{1,0:T(8,128)S(1)} %copy-done.2, bf16[384,256]{1,0:T(8,128)(2,1)S(1)} %copy-done, ...), custom_call_target="tpu_custom_call" | custom-call | flops 1 | bytes 1 | tf_op jit(solution)/shard_map/pallas_call | solution.py:473
  16.3 1.3 %collective-permute-start.6 = (f32[2,8,2176]{2,1,0:T(8,128)S(1)}, f32[2,8,2176]{2,1,0:T(8,128)S(1)}, u32[]{:S(2)}, u32[]{:S(2)}) collective-permute-start(f32[2,8,2176]{2,1,0:T(8,128)S(1)} %get-tuple-element.45.after_ref.own_ref), channel_id=1, source_target_pairs={{0,2},{1,3},{2,0},{3,1},{4,6},{5,7},{6,4},{7,5},{8,10},{9,11},{10,... | collective-permute-start | bytes 417800 | tf_op jit(solution)/shard_map/ppermute | solution.py:507
  17.5 0.3 shard_map.106.after_ref.moved_ref
  17.9 0.0 collective-permute-done.1.other_ref
  17.9 1.0 %shard_map.107 = (f32[2,2,8,1440]{3,2,1,0:T(8,128)S(1)}, f32[2,2,8,1440]{3,2,1,0:T(8,128)S(1)}) custom-call(f32[4,8,128]{2,1,0:T(8,128)S(1)} %get-tuple-element.35.distance_ref, f32[4,8,128]{2,1,0:T(8,128)S(1)} %get-tuple-element.36.share_ref, f32[4,8,128]{2,1,0:T(8,128)S(1)} %get-tuple-element.37.keep_ref, ...), custom_call_target="tpu_custom_call" | custom-call | flops 1 | bytes 1 | tf_op jit(solution)/shard_map/pallas_call | solution.py:473
  18.9 0.1 collective-permute-done.4.got_ref
  19.0 0.1 shard_map.108
  19.0 0.6 %collective-permute-start.5 = (f32[2,1,8,1440]{3,2,1,0:T(8,128)S(1)}, f32[2,1,8,1440]{3,2,1,0:T(8,128)S(1)}, u32[]{:S(2)}, u32[]{:S(2)}) collective-permute-start(f32[2,1,8,1440]{3,2,1,0:T(8,128)S(1)} %get-tuple-element.49), channel_id=1, source_target_pairs={{0,1},{1,0},{2,3},{3,2},{4,5},{5,4},{6,7},{7,6},{8,9},{9,8},{10,11... | collective-permute-start | bytes 276488 | tf_op jit(solution)/shard_map/ppermute | solution.py:504
  19.7 1.6 %collective-permute-done.6.other_ref = f32[2,8,2176]{2,1,0:T(8,128)S(1)} collective-permute-done((f32[2,8,2176]{2,1,0:T(8,128)S(1)}, f32[2,8,2176]{2,1,0:T(8,128)S(1)}, u32[]{:S(2)}, u32[]{:S(2)}) %collective-permute-start.6) | collective-permute-done | bytes 139296 | tf_op jit(solution)/shard_map/ppermute | solution.py:507
  21.2 0.6 %shard_map.109 = (f32[2,1,8,1440]{3,2,1,0:T(8,128)S(1)}, f32[2,1,8,1440]{3,2,1,0:T(8,128)S(1)}) custom-call(f32[4,8,128]{2,1,0:T(8,128)S(1)} %get-tuple-element.35.distance_ref, f32[4,8,128]{2,1,0:T(8,128)S(1)} %get-tuple-element.36.share_ref, f32[4,8,128]{2,1,0:T(8,128)S(1)} %get-tuple-element.37.keep_ref, ...), custom_call_target="tpu_custom_call" | custom-call | flops 1 | bytes 1 | tf_op jit(solution)/shard_map/pallas_call | solution.py:473
  21.9 0.0 collective-permute-done.5.theirs_ref
  21.9 0.9 %shard_map.110 = (f32[2,8,2176]{2,1,0:T(8,128)S(1)}, f32[2,2,8,1536]{3,2,1,0:T(8,128)S(1)}) custom-call(f32[2,1,8,1440]{3,2,1,0:T(8,128)S(1)} %get-tuple-element.48.after_ref.mine_ref, f32[2,1,8,1440]{3,2,1,0:T(8,128)S(1)} %collective-permute-done.5.theirs_ref, f32[18,384]{1,0:T(8,128)S(1)} %copy-done.2, bf16[384,256]{1,0:T(8,128)(2,1)S(1)} %copy-done, ...), custom_call_target="tpu_custom_call" | custom-call | flops 1 | bytes 1 | tf_op jit(solution)/shard_map/pallas_call | solution.py:473
  22.8 1.3 %collective-permute-start.7 = (f32[2,8,2176]{2,1,0:T(8,128)S(1)}, f32[2,8,2176]{2,1,0:T(8,128)S(1)}, u32[]{:S(2)}, u32[]{:S(2)}) collective-permute-start(f32[2,8,2176]{2,1,0:T(8,128)S(1)} %get-tuple-element.52.after_ref.own_ref), channel_id=1, source_target_pairs={{0,2},{1,3},{2,0},{3,1},{4,6},{5,7},{6,4},{7,5},{8,10},{9,11},{10,... | collective-permute-start | bytes 417800 | tf_op jit(solution)/shard_map/ppermute | solution.py:507
  24.0 1.5 %collective-permute-start.8 = (f32[2,2,8,1440]{3,2,1,0:T(8,128)S(1)}, f32[2,2,8,1440]{3,2,1,0:T(8,128)S(1)}, u32[]{:S(2)}, u32[]{:S(2)}) collective-permute-start(f32[2,2,8,1440]{3,2,1,0:T(8,128)S(1)} %get-tuple-element.54), channel_id=1, source_target_pairs={{0,1},{1,0},{2,3},{3,2},{4,5},{5,4},{6,7},{7,6},{8,9},{9,8},{10,11... | collective-permute-start | bytes 552968 | tf_op jit(solution)/shard_map/ppermute | solution.py:504
  25.5 0.0 collective-permute-start.10
  25.5 0.3 shard_map.111.moved_ref
  25.8 0.9 %collective-permute-done.7.other_ref = f32[2,8,2176]{2,1,0:T(8,128)S(1)} collective-permute-done((f32[2,8,2176]{2,1,0:T(8,128)S(1)}, f32[2,8,2176]{2,1,0:T(8,128)S(1)}, u32[]{:S(2)}, u32[]{:S(2)}) %collective-permute-start.7) | collective-permute-done | bytes 139296 | tf_op jit(solution)/shard_map/ppermute | solution.py:507
  26.7 0.6 %shard_map.112 = (f32[2,1,8,1440]{3,2,1,0:T(8,128)S(1)}, f32[2,1,8,1440]{3,2,1,0:T(8,128)S(1)}) custom-call(f32[4,8,128]{2,1,0:T(8,128)S(1)} %get-tuple-element.35.distance_ref, f32[4,8,128]{2,1,0:T(8,128)S(1)} %get-tuple-element.36.share_ref, f32[4,8,128]{2,1,0:T(8,128)S(1)} %get-tuple-element.37.keep_ref, ...), custom_call_target="tpu_custom_call" | custom-call | flops 1 | bytes 1 | tf_op jit(solution)/shard_map/pallas_call | solution.py:473
  27.4 2.4 %collective-permute-start.9 = (f32[2,1,8,1440]{3,2,1,0:T(8,128)S(1)}, f32[2,1,8,1440]{3,2,1,0:T(8,128)S(1)}, u32[]{:S(2)}, u32[]{:S(2)}) collective-permute-start(f32[2,1,8,1440]{3,2,1,0:T(8,128)S(1)} %get-tuple-element.55), channel_id=1, source_target_pairs={{0,1},{1,0},{2,3},{3,2},{4,5},{5,4},{6,7},{7,6},{8,9},{9,8},{10,11... | collective-permute-start | bytes 276488 | tf_op jit(solution)/shard_map/ppermute | solution.py:504
  29.7 0.0 collective-permute-done.10.refs_5_
  29.8 0.0 collective-permute-done.8.refs_3_
  29.8 0.9 %collective-permute-done.9.refs_4_ = f32[2,1,8,1440]{3,2,1,0:T(8,128)S(1)} collective-permute-done((f32[2,1,8,1440]{3,2,1,0:T(8,128)S(1)}, f32[2,1,8,1440]{3,2,1,0:T(8,128)S(1)}, u32[]{:S(2)}, u32[]{:S(2)}) %collective-permute-start.9) | collective-permute-done | bytes 92192 | tf_op jit(solution)/shard_map/ppermute | solution.py:504
  30.7 0.9 %shard_map.113 = f32[4,8,4,1440]{3,2,1,0:T(4,128)} custom-call(f32[2,2,8,1440]{3,2,1,0:T(8,128)S(1)} %get-tuple-element.46.after_ref.refs_0_, f32[2,1,8,1440]{3,2,1,0:T(8,128)S(1)} %get-tuple-element.53.refs_1_, f32[2,1,8,1440]{3,2,1,0:T(8,128)S(1)} %get-tuple-element.50.after_ref.refs_2_, f32[2,2,8,1440]{3,2,1,0:T(8,128)S(1)} %collective-permute-done.8.refs_3_, ...), custom_call_target="tpu_custom_call" | custom-call | flops 1 | bytes 1 | tf_op jit(solution)/shard_map/pallas_call | solution.py:473
  (4 shorter events, 0.0 us)
Async XLA Ops:
  0.0 6.2 %copy-start = (bf16[384,256]{1,0:T(8,128)(2,1)S(1)}, bf16[384,256]{1,0:T(8,128)(2,1)}, u32[]{:S(2)}) copy-start(bf16[384,256]{1,0:T(8,128)(2,1)} %constant.10.clone.high_ref) | copy-start | bytes 589828
  0.0 6.2 %copy-start.1 = (bf16[384,256]{1,0:T(8,128)(2,1)S(1)}, bf16[384,256]{1,0:T(8,128)(2,1)}, u32[]{:S(2)}) copy-start(bf16[384,256]{1,0:T(8,128)(2,1)} %constant.11.clone.low_ref) | copy-start | bytes 589828
  0.0 6.2 %copy-start.2 = (f32[18,384]{1,0:T(8,128)S(1)}, f32[18,384]{1,0:T(8,128)}, u32[]{:S(2)}) copy-start(f32[18,384]{1,0:T(8,128)} %constant.8.clone.phase_ref) | copy-start | bytes 82948
  2.3 3.9 %collective-permute-start = (f32[2,2,8,1440]{3,2,1,0:T(8,128)S(1)}, f32[2,2,8,1440]{3,2,1,0:T(8,128)S(1)}, u32[]{:S(2)}, u32[]{:S(2)}) collective-permute-start(f32[2,2,8,1440]{3,2,1,0:T(8,128)S(1)} %get-tuple-element.32), channel_id=1, source_target_pairs={{0,1},{1,0},{2,3},{3,2},{4,5},{5,4},{6,7},{7,6},{8,9},{9,8},{10,11... | collective-permute-start | bytes 552968 | tf_op jit(solution)/shard_map/ppermute | solution.py:504
  3.0 10.4 %collective-permute-start.2 = (f32[40,1440]{1,0:T(8,128)S(1)}, f32[40,1440]{1,0:T(8,128)S(1)}, u32[]{:S(2)}, u32[]{:S(2)}) collective-permute-start(f32[40,1440]{1,0:T(8,128)S(1)} %get-tuple-element.40.own_ref), channel_id=1, source_target_pairs={{4,8},{8,4},{12,16},{16,12},{20,24},{24,20},{5,9},{9,5},{13,17},{1... | collective-permute-start | bytes 691208 | tf_op jit(solution)/shard_map/ppermute | solution.py:513
  6.3 2.8 %copy-start.3 = (f32[18,128]{1,0:T(8,128)S(1)}, f32[18,128]{1,0:T(8,128)}, u32[]{:S(2)}) copy-start(f32[18,128]{1,0:T(8,128)} %constant.9.clone.wave_ref) | copy-start | bytes 27652
  7.7 10.1 %collective-permute-start.1 = (f32[4,8,2176]{2,1,0:T(8,128)S(1)}, f32[4,8,2176]{2,1,0:T(8,128)S(1)}, u32[]{:S(2)}, u32[]{:S(2)}) collective-permute-start(f32[4,8,2176]{2,1,0:T(8,128)S(1)} %get-tuple-element.34.after_ref.own_ref), channel_id=1, source_target_pairs={{0,2},{1,3},{2,0},{3,1},{4,6},{5,7},{6,4},{7,5},{8,10},{9,11},{10,... | collective-permute-start | bytes 835592 | tf_op jit(solution)/shard_map/ppermute | solution.py:507
  9.0 0.7 %copy-start.5 = (f32[8,4]{0,1:T(4,128)S(1)}, f32[8,4]{0,1:T(4,128)}, u32[]{:S(2)}) copy-start(f32[8,4]{0,1:T(4,128)} %param.13) | copy-start | bytes 388
  9.0 0.7 %copy-start.4 = (s32[8,4]{0,1:T(4,128)S(1)}, s32[8,4]{0,1:T(4,128)}, u32[]{:S(2)}) copy-start(s32[8,4]{0,1:T(4,128)} %param.12) | copy-start | bytes 388
  9.0 10.0 %collective-permute-start.4 = (f32[40,1440]{1,0:T(8,128)S(1)}, f32[40,1440]{1,0:T(8,128)S(1)}, u32[]{:S(2)}, u32[]{:S(2)}) collective-permute-start(f32[40,1440]{1,0:T(8,128)S(1)} %get-tuple-element.47.own_ref), channel_id=1, source_target_pairs={{0,4},{4,0},{8,12},{12,8},{16,20},{20,16},{24,28},{28,24},{1,5},{5... | collective-permute-start | bytes 691208 | tf_op jit(solution)/shard_map/ppermute | solution.py:513
  9.0 0.7 %copy-start.6 = (s32[32]{0:T(128)S(1)}, s32[32]{0:T(128)}, u32[]{:S(2)}) copy-start(s32[32]{0:T(128)} %cutoff_ref.1) | copy-start | bytes 388
  9.0 0.7 %copy-start.7 = (f32[32]{0:T(128)S(1)}, f32[32]{0:T(128)}, u32[]{:S(2)}) copy-start(f32[32]{0:T(128)} %damping_ref.1) | copy-start | bytes 388
  13.5 1.9 %collective-permute-start.3 = (f32[2,1,8,1440]{3,2,1,0:T(8,128)S(1)}, f32[2,1,8,1440]{3,2,1,0:T(8,128)S(1)}, u32[]{:S(2)}, u32[]{:S(2)}) collective-permute-start(f32[2,1,8,1440]{3,2,1,0:T(8,128)S(1)} %get-tuple-element.43), channel_id=1, source_target_pairs={{0,1},{1,0},{2,3},{3,2},{4,5},{5,4},{6,7},{7,6},{8,9},{9,8},{10,11... | collective-permute-start | bytes 276488 | tf_op jit(solution)/shard_map/ppermute | solution.py:504
  16.3 4.9 %collective-permute-start.6 = (f32[2,8,2176]{2,1,0:T(8,128)S(1)}, f32[2,8,2176]{2,1,0:T(8,128)S(1)}, u32[]{:S(2)}, u32[]{:S(2)}) collective-permute-start(f32[2,8,2176]{2,1,0:T(8,128)S(1)} %get-tuple-element.45.after_ref.own_ref), channel_id=1, source_target_pairs={{0,2},{1,3},{2,0},{3,1},{4,6},{5,7},{6,4},{7,5},{8,10},{9,11},{10,... | collective-permute-start | bytes 417800 | tf_op jit(solution)/shard_map/ppermute | solution.py:507
  19.0 2.8 %collective-permute-start.5 = (f32[2,1,8,1440]{3,2,1,0:T(8,128)S(1)}, f32[2,1,8,1440]{3,2,1,0:T(8,128)S(1)}, u32[]{:S(2)}, u32[]{:S(2)}) collective-permute-start(f32[2,1,8,1440]{3,2,1,0:T(8,128)S(1)} %get-tuple-element.49), channel_id=1, source_target_pairs={{0,1},{1,0},{2,3},{3,2},{4,5},{5,4},{6,7},{7,6},{8,9},{9,8},{10,11... | collective-permute-start | bytes 276488 | tf_op jit(solution)/shard_map/ppermute | solution.py:504
  22.8 3.9 %collective-permute-start.7 = (f32[2,8,2176]{2,1,0:T(8,128)S(1)}, f32[2,8,2176]{2,1,0:T(8,128)S(1)}, u32[]{:S(2)}, u32[]{:S(2)}) collective-permute-start(f32[2,8,2176]{2,1,0:T(8,128)S(1)} %get-tuple-element.52.after_ref.own_ref), channel_id=1, source_target_pairs={{0,2},{1,3},{2,0},{3,1},{4,6},{5,7},{6,4},{7,5},{8,10},{9,11},{10,... | collective-permute-start | bytes 417800 | tf_op jit(solution)/shard_map/ppermute | solution.py:507
  24.0 5.7 %collective-permute-start.8 = (f32[2,2,8,1440]{3,2,1,0:T(8,128)S(1)}, f32[2,2,8,1440]{3,2,1,0:T(8,128)S(1)}, u32[]{:S(2)}, u32[]{:S(2)}) collective-permute-start(f32[2,2,8,1440]{3,2,1,0:T(8,128)S(1)} %get-tuple-element.54), channel_id=1, source_target_pairs={{0,1},{1,0},{2,3},{3,2},{4,5},{5,4},{6,7},{7,6},{8,9},{9,8},{10,11... | collective-permute-start | bytes 552968 | tf_op jit(solution)/shard_map/ppermute | solution.py:504
  25.5 4.3 %collective-permute-start.10 = (f32[2,1,8,1440]{3,2,1,0:T(8,128)S(1)}, f32[2,1,8,1440]{3,2,1,0:T(8,128)S(1)}, u32[]{:S(2)}, u32[]{:S(2)}) collective-permute-start(f32[2,1,8,1440]{3,2,1,0:T(8,128)S(1)} %get-tuple-element.56), channel_id=1, source_target_pairs={{0,1},{1,0},{2,3},{3,2},{4,5},{5,4},{6,7},{7,6},{8,9},{9,8},{10,11... | collective-permute-start | bytes 276488 | tf_op jit(solution)/shard_map/ppermute | solution.py:504
  27.4 3.3 %collective-permute-start.9 = (f32[2,1,8,1440]{3,2,1,0:T(8,128)S(1)}, f32[2,1,8,1440]{3,2,1,0:T(8,128)S(1)}, u32[]{:S(2)}, u32[]{:S(2)}) collective-permute-start(f32[2,1,8,1440]{3,2,1,0:T(8,128)S(1)} %get-tuple-element.55), channel_id=1, source_target_pairs={{0,1},{1,0},{2,3},{3,2},{4,5},{5,4},{6,7},{7,6},{8,9},{9,8},{10,11... | collective-permute-start | bytes 276488 | tf_op jit(solution)/shard_map/ppermute | solution.py:504

commit v11 on v9

--- a/solution.py
+++ b/solution.py
@@ -172,7 +172,7 @@
                 far_part_ref[t, :, lanes] = jnp.where(north, south_part, north_part)
 
 
-def edge_kernel(is_near, own_ref, got_ref, part_ref, after_ref, mine_ref, send_ref):
+def edge_kernel(is_near, own_ref, got_ref, later_ref, part_ref, after_ref, mine_ref, send_ref):
     tracer_count, levels, columns = part_ref.shape
     share = tracer_count // PAIR
     total = tracer_count * levels
@@ -180,15 +180,22 @@
     lat = lax.axis_index("lat")
     north = near_is_north() if is_near else jnp.logical_not(near_is_north())
     wall = jnp.where(north, lat == lax.axis_size("lat") - 1, lat == 0)
+    urgent = is_cap(lat) | is_cap(jnp.where(north, lat + 1, lat - 1))
+
+    def got(place, lanes):
+        if not is_near:
+            return got_ref[place, lanes]
+        return jnp.where(urgent, got_ref[place, lanes], later_ref[place, lanes])
+
     for lanes in spans(columns, 3 * LANES):
-        speed = jnp.where(north, got_ref[total:, lanes], own_ref[total:, lanes])
+        speed = jnp.where(north, got(slice(total, total + levels), lanes), own_ref[total:, lanes])
         speed = jnp.where(wall, 0.0, speed)
         for which, out_ref in enumerate([mine_ref, send_ref]):
             for i in range(share):
                 t = lax.rem(core + which, PAIR) * share + i
                 place = pl.ds(pl.multiple_of(t * levels, levels), levels)
-                own, got = own_ref[place, lanes], got_ref[place, lanes]
-                flux = flux_of(speed, jnp.where(north, own, got), jnp.where(north, got, own))
+                own, other = own_ref[place, lanes], got(place, lanes)
+                flux = flux_of(speed, jnp.where(north, own, other), jnp.where(north, other, own))
                 out_ref[i, 0, :, lanes] = part_ref[t, :, lanes] + jnp.where(north, -flux, flux)
 
 
@@ -328,7 +335,11 @@
                 gain_ref[row, 2 * r + 1] = (re * mix_im + im * mix_re) * weight
 
 
-def shift_kernel(which, columns, distance_ref, share_ref, held_ref, after_ref, moved_ref):
+def shift_kernel(which, columns, distance_ref, share_ref, held_ref, after_ref, *refs):
+    relays = len(refs) // 2
+    moved_ref = refs[relays]
+    for source_ref, relay_ref in zip(refs[:relays], refs[relays + 1 :]):
+        relay_ref[...] = source_ref[...]
     _, count, levels, padded = held_ref.shape
     rows = rows_of(which, share_ref.shape[0])
     number = len(rows)
@@ -506,10 +517,13 @@
     def swap_half(value):
         return lax.ppermute(value, "lon", [(p, p ^ 2) for p in range(lon_count)])
 
-    def swap_band(value, first):
+    caps = [b for b in range(lat_count) if b < lat_count // 4 or b >= lat_count - lat_count // 4]
+
+    def swap_band(value, first, urgent=None):
         pairs = []
         for b in range(first, lat_count - 1, 2):
-            pairs += [(b, b + 1), (b + 1, b)]
+            if urgent is None or (b in caps or b + 1 in caps) == urgent:
+                pairs += [(b, b + 1), (b + 1, b)]
         return lax.ppermute(value, "lat", pairs)
 
     def set_shape(number):
@@ -524,12 +538,12 @@
             [(count * group, padded)],
         )
 
-    def shifted(which, held, after):
+    def shifted(which, held, after, *relay):
         count = held.shape[1]
         return call(
             functools.partial(shift_kernel, which, column_count),
-            [(count, PAIR, level_count, width)],
-            whole(distance, fraction, held) + [(after, UNREAD)],
+            [(count, PAIR, level_count, width)] + [v.shape for v in relay],
+            whole(distance, fraction, held) + [(after, UNREAD)] + whole(*relay),
         )
 
     def inverse(which, held, moved, own, other, after):
@@ -563,13 +577,14 @@
         + whole(wave)
         + [(inner_own, UNREAD)],
     )
-    (inner_moved,) = shifted("inner", inner_held, inner_own)
-    near_got = swap_band(near_edge, 0)
+    near_got = swap_band(near_edge, 0, True)
+    inner_moved, near_relay = shifted("inner", inner_held, inner_own, near_edge)
+    near_later = swap_band(near_relay, 0, False)
 
     far_mine, far_send = call(
         functools.partial(edge_kernel, False),
         [set_shape(1)] * 2,
-        whole(far_edge, far_got, far_part) + [(inner_moved, UNREAD)],
+        whole(far_edge, far_got) + [(far_edge, UNREAD)] + whole(far_part) + [(inner_moved, UNREAD)],
     )
     far_theirs = swap_core(far_send)
     far_own, far_held = forward(far_mine, far_theirs, inner_moved)
@@ -581,7 +596,7 @@
     near_mine, near_send = call(
         functools.partial(edge_kernel, True),
         [set_shape(1)] * 2,
-        whole(near_edge, near_got, near_part) + [(inner[0], UNREAD)],
+        whole(near_edge, near_got, near_later, near_part) + [(inner[0], UNREAD)],
     )
     near_theirs = swap_core(near_send)
     near_own, near_held = forward(near_mine, near_theirs, inner[0])

time: 31.6 us -> 32.9 us (1.041)
  the two profiles are of different devices: /device:TPU:3 before, /device:TPU:0 now
where the time goes in v11:
time: 32.9 us; the launch traced here: 32.7 us
  starting transfers between devices  12.2 us (37%)
  Pallas kernels  11.1 us (34%)
  waiting for transfers between devices  8.52 us (26%)
  local copies, waits for them, and re-layouts  0.65 us (2%)
    pallas_call x14, Pallas kernels, call(): pl.pallas_call(kernel, out_shape=[jax.ShapeDtypeStruct(shape, jnp.float32...  11.1 us
    ppermute x3, starting transfers between devices, swap_band(): return lax.ppermute(value, 'lat', pairs)  6.92 us
    ppermute x3, waiting for transfers between devices, swap_half(): return lax.ppermute(value, 'lon', [(p, p ^ 2) for p in range(lon_count)])  4.92 us
    ppermute x3, starting transfers between devices, swap_half(): return lax.ppermute(value, 'lon', [(p, p ^ 2) for p in range(lon_count)])  4.32 us
    ppermute x6, waiting for transfers between devices, swap_core(): return lax.ppermute(value, 'lon', [(p, p ^ 1) for p in range(lon_count)])  3.59 us
    ppermute x6, starting transfers between devices, swap_core(): return lax.ppermute(value, 'lon', [(p, p ^ 1) for p in range(lon_count)])  0.96 us
  transfers between devices with their start and end apart: 12, of which 6 were waited for; matrix products, arithmetic and copies ran while one was open for 0% of the time, Pallas kernels for 24%

profile of v11, /device:TPU:0, one launch (start us, length us, event | category | flops | bytes accessed | tf_op | source)
XLA Modules:
  0.0 32.7 jit_solution(9068355418424719521)
XLA Ops:
  0.0 2.3 %shard_map.100 = (f32[2,2,8,1440]{3,2,1,0:T(8,128)S(1)}, f32[2,2,8,1440]{3,2,1,0:T(8,128)S(1)}, f32[40,1440]{1,0:T(8,128)S(1)}, f32[40,1440]{1,0:T(8,128)S(1)}, ...) custom-call(f32[4,8,4,1440]{3,2,1,0:T(4,128)} %cells_hbm.1, f32[8,4,1440]{2,1,0:T(4,128)} %speed_hbm.1), custom_call_target="tpu_custom_call" | custom-call | flops 1 | bytes 1 | tf_op jit(solution)/shard_map/pallas_call | solution.py:484
  2.3 0.5 %collective-permute-start = (f32[2,2,8,1440]{3,2,1,0:T(8,128)S(1)}, f32[2,2,8,1440]{3,2,1,0:T(8,128)S(1)}, u32[]{:S(2)}, u32[]{:S(2)}) collective-permute-start(f32[2,2,8,1440]{3,2,1,0:T(8,128)S(1)} %get-tuple-element.34), channel_id=1, source_target_pairs={{0,1},{1,0},{2,3},{3,2},{4,5},{5,4},{6,7},{7,6},{8,9},{9,8},{10,11... | collective-permute-start | bytes 552968 | tf_op jit(solution)/shard_map/ppermute | solution.py:515
  2.8 0.7 %collective-permute-start.2 = (f32[40,1440]{1,0:T(8,128)S(1)}, f32[40,1440]{1,0:T(8,128)S(1)}, u32[]{:S(2)}, u32[]{:S(2)}) collective-permute-start(f32[40,1440]{1,0:T(8,128)S(1)} %get-tuple-element.44.own_ref.later_ref), channel_id=1, source_target_pairs={{4,8},{8,4},{12,16},{16,12},{20,24},{24,20},{5,9},{9,5},{13,17},{1... | collective-permute-start | bytes 691208 | tf_op jit(solution)/shard_map/ppermute | solution.py:527
  3.5 0.4 %collective-permute-done.theirs_ref = f32[2,2,8,1440]{3,2,1,0:T(8,128)S(1)} collective-permute-done((f32[2,2,8,1440]{3,2,1,0:T(8,128)S(1)}, f32[2,2,8,1440]{3,2,1,0:T(8,128)S(1)}, u32[]{:S(2)}, u32[]{:S(2)}) %collective-permute-start) | collective-permute-done | bytes 184352 | tf_op jit(solution)/shard_map/ppermute | solution.py:515
  3.9 0.0 copy-done
  3.9 0.0 copy-done.1
  3.9 0.0 copy-done.2
  3.9 1.5 %shard_map.101 = (f32[4,8,2176]{2,1,0:T(8,128)S(1)}, f32[2,4,8,1536]{3,2,1,0:T(8,128)S(1)}) custom-call(f32[2,2,8,1440]{3,2,1,0:T(8,128)S(1)} %get-tuple-element.33.mine_ref, f32[2,2,8,1440]{3,2,1,0:T(8,128)S(1)} %collective-permute-done.theirs_ref, f32[18,384]{1,0:T(8,128)S(1)} %copy-done.2, bf16[384,256]{1,0:T(8,128)(2,1)S(1)} %copy-done, ...), custom_call_target="tpu_custom_call" | custom-call | flops 1 | bytes 1 | tf_op jit(solution)/shard_map/pallas_call | solution.py:484
  5.4 2.9 %collective-permute-start.1 = (f32[4,8,2176]{2,1,0:T(8,128)S(1)}, f32[4,8,2176]{2,1,0:T(8,128)S(1)}, u32[]{:S(2)}, u32[]{:S(2)}) collective-permute-start(f32[4,8,2176]{2,1,0:T(8,128)S(1)} %get-tuple-element.36.after_ref.own_ref), channel_id=1, source_target_pairs={{0,2},{1,3},{2,0},{3,1},{4,6},{5,7},{6,4},{7,5},{8,10},{9,11},{10,... | collective-permute-start | bytes 835592 | tf_op jit(solution)/shard_map/ppermute | solution.py:518
  8.3 5.6 %collective-permute-start.4 = (f32[40,1440]{1,0:T(8,128)S(1)}, f32[40,1440]{1,0:T(8,128)S(1)}, u32[]{:S(2)}, u32[]{:S(2)}) collective-permute-start(f32[40,1440]{1,0:T(8,128)S(1)} %get-tuple-element.42.refs_0_.own_ref), channel_id=1, source_target_pairs={{0,4},{4,0},{24,28},{28,24},{1,5},{5,1},{25,29},{29,25},{2,6},{6,2... | collective-permute-start | bytes 691208 | tf_op jit(solution)/shard_map/ppermute | solution.py:527
  13.9 0.0 copy-start.6
  13.9 0.0 copy-start.7
  13.9 0.0 copy-done.3
  13.9 0.0 copy-done.5
  13.9 0.0 copy-done.4
  13.9 0.6 %copy-done.6 = s32[32]{0:T(128)S(1)} copy-done((s32[32]{0:T(128)S(1)}, s32[32]{0:T(128)}, u32[]{:S(2)}) %copy-start.6) | copy-done | bytes 152
  14.5 0.0 copy-done.7
  14.5 0.9 %shard_map.102 = (f32[4,8,128]{2,1,0:T(8,128)S(1)}, f32[4,8,128]{2,1,0:T(8,128)S(1)}, f32[4,8,128]{2,1,0:T(8,128)S(1)}, f32[4,18,8,128]{3,2,1,0:T(8,128)S(1)}) custom-call(s32[4,8]{1,0:T(4,128)S(1)} %bitcast.2, f32[4,8]{1,0:T(4,128)S(1)} %bitcast.3, s32[32]{0:T(128)S(1)} %copy-done.6, f32[32]{0:T(128)S(1)} %copy-done.7, f32[18,128]{1,0:T(8,128)S(1)} %copy-done.3, ...), custom_call_target="tpu_custom_call" | custom-call | flops 1 | bytes 1 | tf_op jit(solution)/shard_map/pallas_call | solution.py:484
  15.4 0.7 %shard_map.103 = (f32[4,2,8,1536]{3,2,1,0:T(8,128)S(1)}, f32[40,1440]{1,0:T(8,128)S(1)}) custom-call(f32[4,8,128]{2,1,0:T(8,128)S(1)} %get-tuple-element.37.distance_ref, f32[4,8,128]{2,1,0:T(8,128)S(1)} %get-tuple-element.38.share_ref, f32[2,4,8,1536]{3,2,1,0:T(8,128)S(1)} %get-tuple-element.41.held_ref, ...), custom_call_target="tpu_custom_call" | custom-call | flops 1 | bytes 1 | tf_op jit(solution)/shard_map/pallas_call | solution.py:484
  16.1 0.7 %collective-permute-start.5 = (f32[40,1440]{1,0:T(8,128)S(1)}, f32[40,1440]{1,0:T(8,128)S(1)}, u32[]{:S(2)}, u32[]{:S(2)}) collective-permute-start(f32[40,1440]{1,0:T(8,128)S(1)} %get-tuple-element.51), channel_id=1, source_target_pairs={{8,12},{12,8},{16,20},{20,16},{9,13},{13,9},{17,21},{21,17},{10,14... | collective-permute-start | bytes 691208 | tf_op jit(solution)/shard_map/ppermute | solution.py:527
  16.8 0.0 collective-permute-done.2.got_ref
  16.8 0.1 shard_map.104
  16.9 0.1 collective-permute-start.3
  17.0 1.3 %collective-permute-done.3.theirs_ref = f32[2,1,8,1440]{3,2,1,0:T(8,128)S(1)} collective-permute-done((f32[2,1,8,1440]{3,2,1,0:T(8,128)S(1)}, f32[2,1,8,1440]{3,2,1,0:T(8,128)S(1)}, u32[]{:S(2)}, u32[]{:S(2)}) %collective-permute-start.3) | collective-permute-done | bytes 92192 | tf_op jit(solution)/shard_map/ppermute | solution.py:515
  18.3 0.9 %shard_map.105 = (f32[2,8,2176]{2,1,0:T(8,128)S(1)}, f32[2,2,8,1536]{3,2,1,0:T(8,128)S(1)}) custom-call(f32[2,1,8,1440]{3,2,1,0:T(8,128)S(1)} %get-tuple-element.46.mine_ref, f32[2,1,8,1440]{3,2,1,0:T(8,128)S(1)} %collective-permute-done.3.theirs_ref, f32[18,384]{1,0:T(8,128)S(1)} %copy-done.2, bf16[384,256]{1,0:T(8,128)(2,1)S(1)} %copy-done, ...), custom_call_target="tpu_custom_call" | custom-call | flops 1 | bytes 1 | tf_op jit(solution)/shard_map/pallas_call | solution.py:484
  19.2 0.3 shard_map.106.after_ref.moved_ref
  19.5 0.0 collective-permute-done.1.other_ref
  19.5 1.0 %shard_map.107 = (f32[2,2,8,1440]{3,2,1,0:T(8,128)S(1)}, f32[2,2,8,1440]{3,2,1,0:T(8,128)S(1)}) custom-call(f32[4,8,128]{2,1,0:T(8,128)S(1)} %get-tuple-element.37.distance_ref, f32[4,8,128]{2,1,0:T(8,128)S(1)} %get-tuple-element.38.share_ref, f32[4,8,128]{2,1,0:T(8,128)S(1)} %get-tuple-element.39.keep_ref, ...), custom_call_target="tpu_custom_call" | custom-call | flops 1 | bytes 1 | tf_op jit(solution)/shard_map/pallas_call | solution.py:484
  20.5 0.0 collective-permute-done.4.got_ref
  20.5 0.0 collective-permute-done.5.later_ref
  20.5 0.1 shard_map.108
  20.6 0.2 collective-permute-start.6
  20.8 0.5 %collective-permute-start.8 = (f32[2,8,2176]{2,1,0:T(8,128)S(1)}, f32[2,8,2176]{2,1,0:T(8,128)S(1)}, u32[]{:S(2)}, u32[]{:S(2)}) collective-permute-start(f32[2,8,2176]{2,1,0:T(8,128)S(1)} %get-tuple-element.49.after_ref.own_ref), channel_id=1, source_target_pairs={{0,2},{1,3},{2,0},{3,1},{4,6},{5,7},{6,4},{7,5},{8,10},{9,11},{10,... | collective-permute-start | bytes 417800 | tf_op jit(solution)/shard_map/ppermute | solution.py:518
  21.4 0.6 %collective-permute-done.6.theirs_ref = f32[2,1,8,1440]{3,2,1,0:T(8,128)S(1)} collective-permute-done((f32[2,1,8,1440]{3,2,1,0:T(8,128)S(1)}, f32[2,1,8,1440]{3,2,1,0:T(8,128)S(1)}, u32[]{:S(2)}, u32[]{:S(2)}) %collective-permute-start.6) | collective-permute-done | bytes 92192 | tf_op jit(solution)/shard_map/ppermute | solution.py:515
  22.0 0.9 %shard_map.109 = (f32[2,8,2176]{2,1,0:T(8,128)S(1)}, f32[2,2,8,1536]{3,2,1,0:T(8,128)S(1)}) custom-call(f32[2,1,8,1440]{3,2,1,0:T(8,128)S(1)} %get-tuple-element.52.mine_ref, f32[2,1,8,1440]{3,2,1,0:T(8,128)S(1)} %collective-permute-done.6.theirs_ref, f32[18,384]{1,0:T(8,128)S(1)} %copy-done.2, bf16[384,256]{1,0:T(8,128)(2,1)S(1)} %copy-done, ...), custom_call_target="tpu_custom_call" | custom-call | flops 1 | bytes 1 | tf_op jit(solution)/shard_map/pallas_call | solution.py:484
  22.9 0.9 %collective-permute-start.7 = (f32[2,8,2176]{2,1,0:T(8,128)S(1)}, f32[2,8,2176]{2,1,0:T(8,128)S(1)}, u32[]{:S(2)}, u32[]{:S(2)}) collective-permute-start(f32[2,8,2176]{2,1,0:T(8,128)S(1)} %get-tuple-element.55.after_ref.own_ref), channel_id=1, source_target_pairs={{0,2},{1,3},{2,0},{3,1},{4,6},{5,7},{6,4},{7,5},{8,10},{9,11},{10,... | collective-permute-start | bytes 417800 | tf_op jit(solution)/shard_map/ppermute | solution.py:518
  23.8 0.0 collective-permute-start.9
  23.8 0.3 shard_map.110.after_ref.moved_ref
  24.1 3.2 %collective-permute-done.8.other_ref = f32[2,8,2176]{2,1,0:T(8,128)S(1)} collective-permute-done((f32[2,8,2176]{2,1,0:T(8,128)S(1)}, f32[2,8,2176]{2,1,0:T(8,128)S(1)}, u32[]{:S(2)}, u32[]{:S(2)}) %collective-permute-start.8) | collective-permute-done | bytes 139296 | tf_op jit(solution)/shard_map/ppermute | solution.py:518
  27.3 0.6 %shard_map.111 = (f32[2,1,8,1440]{3,2,1,0:T(8,128)S(1)}, f32[2,1,8,1440]{3,2,1,0:T(8,128)S(1)}) custom-call(f32[4,8,128]{2,1,0:T(8,128)S(1)} %get-tuple-element.37.distance_ref, f32[4,8,128]{2,1,0:T(8,128)S(1)} %get-tuple-element.38.share_ref, f32[4,8,128]{2,1,0:T(8,128)S(1)} %get-tuple-element.39.keep_ref, ...), custom_call_target="tpu_custom_call" | custom-call | flops 1 | bytes 1 | tf_op jit(solution)/shard_map/pallas_call | solution.py:484
  28.0 0.1 collective-permute-start.11
  28.1 1.7 %collective-permute-done.7.other_ref = f32[2,8,2176]{2,1,0:T(8,128)S(1)} collective-permute-done((f32[2,8,2176]{2,1,0:T(8,128)S(1)}, f32[2,8,2176]{2,1,0:T(8,128)S(1)}, u32[]{:S(2)}, u32[]{:S(2)}) %collective-permute-start.7) | collective-permute-done | bytes 139296 | tf_op jit(solution)/shard_map/ppermute | solution.py:518
  29.8 0.6 %shard_map.112 = (f32[2,1,8,1440]{3,2,1,0:T(8,128)S(1)}, f32[2,1,8,1440]{3,2,1,0:T(8,128)S(1)}) custom-call(f32[4,8,128]{2,1,0:T(8,128)S(1)} %get-tuple-element.37.distance_ref, f32[4,8,128]{2,1,0:T(8,128)S(1)} %get-tuple-element.38.share_ref, f32[4,8,128]{2,1,0:T(8,128)S(1)} %get-tuple-element.39.keep_ref, ...), custom_call_target="tpu_custom_call" | custom-call | flops 1 | bytes 1 | tf_op jit(solution)/shard_map/pallas_call | solution.py:484
  30.4 0.1 collective-permute-start.10
  30.5 0.0 collective-permute-done.9.refs_3_
  30.5 0.0 collective-permute-done.11.refs_5_
  30.5 1.3 %collective-permute-done.10.refs_4_ = f32[2,1,8,1440]{3,2,1,0:T(8,128)S(1)} collective-permute-done((f32[2,1,8,1440]{3,2,1,0:T(8,128)S(1)}, f32[2,1,8,1440]{3,2,1,0:T(8,128)S(1)}, u32[]{:S(2)}, u32[]{:S(2)}) %collective-permute-start.10) | collective-permute-done | bytes 92192 | tf_op jit(solution)/shard_map/ppermute | solution.py:515
  31.8 0.9 %shard_map.113 = f32[4,8,4,1440]{3,2,1,0:T(4,128)} custom-call(f32[2,2,8,1440]{3,2,1,0:T(8,128)S(1)} %get-tuple-element.50.after_ref.refs_0_, f32[2,1,8,1440]{3,2,1,0:T(8,128)S(1)} %get-tuple-element.57.refs_1_, f32[2,1,8,1440]{3,2,1,0:T(8,128)S(1)} %get-tuple-element.56.after_ref.refs_2_, f32[2,2,8,1440]{3,2,1,0:T(8,128)S(1)} %collective-permute-done.9.refs_3_, ...), custom_call_target="tpu_custom_call" | custom-call | flops 1 | bytes 1 | tf_op jit(solution)/shard_map/pallas_call | solution.py:484
  (6 shorter events, 0.0 us)
Async XLA Ops:
  0.0 3.9 %copy-start = (bf16[384,256]{1,0:T(8,128)(2,1)S(1)}, bf16[384,256]{1,0:T(8,128)(2,1)}, u32[]{:S(2)}) copy-start(bf16[384,256]{1,0:T(8,128)(2,1)} %constant.10.clone.high_ref) | copy-start | bytes 589828
  0.0 3.9 %copy-start.1 = (bf16[384,256]{1,0:T(8,128)(2,1)S(1)}, bf16[384,256]{1,0:T(8,128)(2,1)}, u32[]{:S(2)}) copy-start(bf16[384,256]{1,0:T(8,128)(2,1)} %constant.11.clone.low_ref) | copy-start | bytes 589828
  0.0 3.9 %copy-start.2 = (f32[18,384]{1,0:T(8,128)S(1)}, f32[18,384]{1,0:T(8,128)}, u32[]{:S(2)}) copy-start(f32[18,384]{1,0:T(8,128)} %constant.8.clone.phase_ref) | copy-start | bytes 82948
  2.3 1.6 %collective-permute-start = (f32[2,2,8,1440]{3,2,1,0:T(8,128)S(1)}, f32[2,2,8,1440]{3,2,1,0:T(8,128)S(1)}, u32[]{:S(2)}, u32[]{:S(2)}) collective-permute-start(f32[2,2,8,1440]{3,2,1,0:T(8,128)S(1)} %get-tuple-element.34), channel_id=1, source_target_pairs={{0,1},{1,0},{2,3},{3,2},{4,5},{5,4},{6,7},{7,6},{8,9},{9,8},{10,11... | collective-permute-start | bytes 552968 | tf_op jit(solution)/shard_map/ppermute | solution.py:515
  2.8 14.0 %collective-permute-start.2 = (f32[40,1440]{1,0:T(8,128)S(1)}, f32[40,1440]{1,0:T(8,128)S(1)}, u32[]{:S(2)}, u32[]{:S(2)}) collective-permute-start(f32[40,1440]{1,0:T(8,128)S(1)} %get-tuple-element.44.own_ref.later_ref), channel_id=1, source_target_pairs={{4,8},{8,4},{12,16},{16,12},{20,24},{24,20},{5,9},{9,5},{13,17},{1... | collective-permute-start | bytes 691208 | tf_op jit(solution)/shard_map/ppermute | solution.py:527
  3.9 10.0 %copy-start.3 = (f32[18,128]{1,0:T(8,128)S(1)}, f32[18,128]{1,0:T(8,128)}, u32[]{:S(2)}) copy-start(f32[18,128]{1,0:T(8,128)} %constant.9.clone.wave_ref) | copy-start | bytes 27652
  5.4 14.1 %collective-permute-start.1 = (f32[4,8,2176]{2,1,0:T(8,128)S(1)}, f32[4,8,2176]{2,1,0:T(8,128)S(1)}, u32[]{:S(2)}, u32[]{:S(2)}) collective-permute-start(f32[4,8,2176]{2,1,0:T(8,128)S(1)} %get-tuple-element.36.after_ref.own_ref), channel_id=1, source_target_pairs={{0,2},{1,3},{2,0},{3,1},{4,6},{5,7},{6,4},{7,5},{8,10},{9,11},{10,... | collective-permute-start | bytes 835592 | tf_op jit(solution)/shard_map/ppermute | solution.py:518
  8.3 5.6 %copy-start.5 = (f32[8,4]{0,1:T(4,128)S(1)}, f32[8,4]{0,1:T(4,128)}, u32[]{:S(2)}) copy-start(f32[8,4]{0,1:T(4,128)} %param.13) | copy-start | bytes 388
  8.3 5.6 %copy-start.4 = (s32[8,4]{0,1:T(4,128)S(1)}, s32[8,4]{0,1:T(4,128)}, u32[]{:S(2)}) copy-start(s32[8,4]{0,1:T(4,128)} %param.12) | copy-start | bytes 388
  8.3 12.2 %collective-permute-start.4 = (f32[40,1440]{1,0:T(8,128)S(1)}, f32[40,1440]{1,0:T(8,128)S(1)}, u32[]{:S(2)}, u32[]{:S(2)}) collective-permute-start(f32[40,1440]{1,0:T(8,128)S(1)} %get-tuple-element.42.refs_0_.own_ref), channel_id=1, source_target_pairs={{0,4},{4,0},{24,28},{28,24},{1,5},{5,1},{25,29},{29,25},{2,6},{6,2... | collective-permute-start | bytes 691208 | tf_op jit(solution)/shard_map/ppermute | solution.py:527
  13.9 0.7 %copy-start.6 = (s32[32]{0:T(128)S(1)}, s32[32]{0:T(128)}, u32[]{:S(2)}) copy-start(s32[32]{0:T(128)} %cutoff_ref.1) | copy-start | bytes 388
  13.9 0.7 %copy-start.7 = (f32[32]{0:T(128)S(1)}, f32[32]{0:T(128)}, u32[]{:S(2)}) copy-start(f32[32]{0:T(128)} %damping_ref.1) | copy-start | bytes 388
  16.1 4.4 %collective-permute-start.5 = (f32[40,1440]{1,0:T(8,128)S(1)}, f32[40,1440]{1,0:T(8,128)S(1)}, u32[]{:S(2)}, u32[]{:S(2)}) collective-permute-start(f32[40,1440]{1,0:T(8,128)S(1)} %get-tuple-element.51), channel_id=1, source_target_pairs={{8,12},{12,8},{16,20},{20,16},{9,13},{13,9},{17,21},{21,17},{10,14... | collective-permute-start | bytes 691208 | tf_op jit(solution)/shard_map/ppermute | solution.py:527
  16.9 1.4 %collective-permute-start.3 = (f32[2,1,8,1440]{3,2,1,0:T(8,128)S(1)}, f32[2,1,8,1440]{3,2,1,0:T(8,128)S(1)}, u32[]{:S(2)}, u32[]{:S(2)}) collective-permute-start(f32[2,1,8,1440]{3,2,1,0:T(8,128)S(1)} %get-tuple-element.47), channel_id=1, source_target_pairs={{0,1},{1,0},{2,3},{3,2},{4,5},{5,4},{6,7},{7,6},{8,9},{9,8},{10,11... | collective-permute-start | bytes 276488 | tf_op jit(solution)/shard_map/ppermute | solution.py:515
  20.6 1.4 %collective-permute-start.6 = (f32[2,1,8,1440]{3,2,1,0:T(8,128)S(1)}, f32[2,1,8,1440]{3,2,1,0:T(8,128)S(1)}, u32[]{:S(2)}, u32[]{:S(2)}) collective-permute-start(f32[2,1,8,1440]{3,2,1,0:T(8,128)S(1)} %get-tuple-element.53), channel_id=1, source_target_pairs={{0,1},{1,0},{2,3},{3,2},{4,5},{5,4},{6,7},{7,6},{8,9},{9,8},{10,11... | collective-permute-start | bytes 276488 | tf_op jit(solution)/shard_map/ppermute | solution.py:515
  20.8 6.5 %collective-permute-start.8 = (f32[2,8,2176]{2,1,0:T(8,128)S(1)}, f32[2,8,2176]{2,1,0:T(8,128)S(1)}, u32[]{:S(2)}, u32[]{:S(2)}) collective-permute-start(f32[2,8,2176]{2,1,0:T(8,128)S(1)} %get-tuple-element.49.after_ref.own_ref), channel_id=1, source_target_pairs={{0,2},{1,3},{2,0},{3,1},{4,6},{5,7},{6,4},{7,5},{8,10},{9,11},{10,... | collective-permute-start | bytes 417800 | tf_op jit(solution)/shard_map/ppermute | solution.py:518
  22.9 6.9 %collective-permute-start.7 = (f32[2,8,2176]{2,1,0:T(8,128)S(1)}, f32[2,8,2176]{2,1,0:T(8,128)S(1)}, u32[]{:S(2)}, u32[]{:S(2)}) collective-permute-start(f32[2,8,2176]{2,1,0:T(8,128)S(1)} %get-tuple-element.55.after_ref.own_ref), channel_id=1, source_target_pairs={{0,2},{1,3},{2,0},{3,1},{4,6},{5,7},{6,4},{7,5},{8,10},{9,11},{10,... | collective-permute-start | bytes 417800 | tf_op jit(solution)/shard_map/ppermute | solution.py:518
  23.8 6.7 %collective-permute-start.9 = (f32[2,2,8,1440]{3,2,1,0:T(8,128)S(1)}, f32[2,2,8,1440]{3,2,1,0:T(8,128)S(1)}, u32[]{:S(2)}, u32[]{:S(2)}) collective-permute-start(f32[2,2,8,1440]{3,2,1,0:T(8,128)S(1)} %get-tuple-element.58), channel_id=1, source_target_pairs={{0,1},{1,0},{2,3},{3,2},{4,5},{5,4},{6,7},{7,6},{8,9},{9,8},{10,11... | collective-permute-start | bytes 552968 | tf_op jit(solution)/shard_map/ppermute | solution.py:515
  28.0 2.5 %collective-permute-start.11 = (f32[2,1,8,1440]{3,2,1,0:T(8,128)S(1)}, f32[2,1,8,1440]{3,2,1,0:T(8,128)S(1)}, u32[]{:S(2)}, u32[]{:S(2)}) collective-permute-start(f32[2,1,8,1440]{3,2,1,0:T(8,128)S(1)} %get-tuple-element.60), channel_id=1, source_target_pairs={{0,1},{1,0},{2,3},{3,2},{4,5},{5,4},{6,7},{7,6},{8,9},{9,8},{10,11... | collective-permute-start | bytes 276488 | tf_op jit(solution)/shard_map/ppermute | solution.py:515
  30.4 1.4 %collective-permute-start.10 = (f32[2,1,8,1440]{3,2,1,0:T(8,128)S(1)}, f32[2,1,8,1440]{3,2,1,0:T(8,128)S(1)}, u32[]{:S(2)}, u32[]{:S(2)}) collective-permute-start(f32[2,1,8,1440]{3,2,1,0:T(8,128)S(1)} %get-tuple-element.59), channel_id=1, source_target_pairs={{0,1},{1,0},{2,3},{3,2},{4,5},{5,4},{6,7},{7,6},{8,9},{9,8},{10,11... | collective-permute-start | bytes 276488 | tf_op jit(solution)/shard_map/ppermute | solution.py:515

commit v12 on v8

--- a/solution.py
+++ b/solution.py
@@ -145,31 +145,32 @@
     share = tracer_count // PAIR
     core = lax.rem(lax.axis_index("lon"), PAIR)
     north = near_is_north()
-    copies = [pltpu.make_async_copy(speed_hbm, speed_ref, sems.at[tracer_count])]
-    copies += [
-        pltpu.make_async_copy(cells_hbm.at[t], cells_ref.at[t], sems.at[t]) for t in range(tracer_count)
-    ]
-    for copy in copies:
-        copy.start()
-    for copy in copies:
-        copy.wait()
-    for lanes in spans(columns, 2 * LANES):
-        speed = [speed_ref[:, j, lanes] for j in range(row_count)]
-        near_ref[tracer_count * levels :, lanes] = speed[0]
-        far_ref[tracer_count * levels :, lanes] = speed[0]
-        for which, out_ref in enumerate([mine_ref, send_ref]):
-            for i in range(share):
-                t = lax.rem(core + which, PAIR) * share + i
-                place = pl.ds(pl.multiple_of(t * levels, levels), levels)
-                x = [cells_ref[t, :, j, lanes] for j in range(row_count)]
-                flux = [flux_of(speed[j], x[j - 1], x[j]) for j in range(1, row_count)]
-                for j in range(1, row_count - 1):
-                    out_ref[i, j - 1, :, lanes] = x[j] + flux[j - 1] - flux[j]
-                near_ref[place, lanes] = jnp.where(north, x[-1], x[0])
-                far_ref[place, lanes] = jnp.where(north, x[0], x[-1])
-                south_part, north_part = x[0] - flux[0], x[-1] + flux[-1]
-                near_part_ref[t, :, lanes] = jnp.where(north, north_part, south_part)
-                far_part_ref[t, :, lanes] = jnp.where(north, south_part, north_part)
+    loads = [pltpu.make_async_copy(speed_hbm, speed_ref, sems.at[tracer_count])]
+    owners = []
+    for slot in range(tracer_count):
+        place, i = divmod(slot, share)
+        owners.append(lax.rem(core + place, PAIR) * share + i)
+        loads.append(pltpu.make_async_copy(cells_hbm.at[owners[-1]], cells_ref.at[slot], sems.at[slot]))
+    for load in loads:
+        load.start()
+    loads[0].wait()
+    near_ref[tracer_count * levels :] = speed_ref[:, 0]
+    far_ref[tracer_count * levels :] = speed_ref[:, 0]
+    for slot, t in enumerate(owners):
+        loads[slot + 1].wait()
+        out_ref, i = (mine_ref, send_ref)[slot // share], slot % share
+        place = pl.ds(pl.multiple_of(t * levels, levels), levels)
+        for lanes in spans(columns, 3 * LANES):
+            speed = [speed_ref[:, j, lanes] for j in range(row_count)]
+            x = [cells_ref[slot, :, j, lanes] for j in range(row_count)]
+            flux = [flux_of(speed[j], x[j - 1], x[j]) for j in range(1, row_count)]
+            for j in range(1, row_count - 1):
+                out_ref[i, j - 1, :, lanes] = x[j] + flux[j - 1] - flux[j]
+            near_ref[place, lanes] = jnp.where(north, x[-1], x[0])
+            far_ref[place, lanes] = jnp.where(north, x[0], x[-1])
+            south_part, north_part = x[0] - flux[0], x[-1] + flux[-1]
+            near_part_ref[t, :, lanes] = jnp.where(north, north_part, south_part)
+            far_part_ref[t, :, lanes] = jnp.where(north, south_part, north_part)
 
 
 def edge_kernel(is_near, own_ref, got_ref, part_ref, after_ref, mine_ref, send_ref):
@@ -193,8 +194,13 @@
 
 
 def forward_kernel(
-    mine_ref, theirs_ref, phase_ref, high_ref, low_ref, after_ref, message_ref, held_ref, stack_ref
+    mine_ref, theirs_ref, phase_ref, high_ref, low_ref, after_ref, *refs
 ):
+    *refs, stack_ref = refs
+    relays = len(refs) // 3
+    message_ref, held_ref = refs[relays : relays + 2]
+    for source_ref, relay_ref in zip(refs[:relays], refs[relays + 2 :]):
+        relay_ref[...] = source_ref[...]
     share, number, levels, columns = mine_ref.shape
     piece = columns * PAIR // HALF
     padded = stack_ref.shape[1]
@@ -328,12 +334,7 @@
                 gain_ref[row, 2 * r + 1] = (re * mix_im + im * mix_re) * weight
 
 
-def shift_kernel(which, columns, distance_ref, share_ref, held_ref, after_ref, *refs):
-    if which == "inner":
-        source_ref, moved_ref, relay_ref = refs
-        relay_ref[...] = source_ref[...]
-    else:
-        (moved_ref,) = refs
+def shift_kernel(which, columns, distance_ref, share_ref, held_ref, after_ref, moved_ref):
     _, count, levels, padded = held_ref.shape
     rows = rows_of(which, share_ref.shape[0])
     number = len(rows)
@@ -425,25 +426,22 @@
             send_ref[i, j] = pair_ref[1 - core, n, :, :columns]
 
 
-def end_kernel(*refs):
-    *refs, out_hbm, out_ref, sems = refs
-    tracer_count, levels, row_count, columns = out_ref.shape
-    share = tracer_count // PAIR
+def end_kernel(place, inner, near, far, *refs):
+    out_hbm, out_ref, sems = refs[-3:]
+    share, levels, row_count, columns = out_ref.shape
     core = lax.rem(lax.axis_index("lon"), PAIR)
     north = near_is_north()
     copies = []
-    for place, (inner, near, far) in enumerate([refs[:3], refs[3:]]):
-        for i in range(share):
-            slot = place * share + i
-            for lanes in spans(columns, 4 * LANES):
-                a, b = near[i, 0, :, lanes], far[i, 0, :, lanes]
-                out_ref[slot, :, 0, lanes] = jnp.where(north, b, a)
-                out_ref[slot, :, row_count - 1, lanes] = jnp.where(north, a, b)
-                for j in range(1, row_count - 1):
-                    out_ref[slot, :, j, lanes] = inner[i, j - 1, :, lanes]
-            t = lax.rem(core + place, PAIR) * share + i
-            copies.append(pltpu.make_async_copy(out_ref.at[slot], out_hbm.at[t], sems.at[slot]))
-            copies[-1].start()
+    for i in range(share):
+        for lanes in spans(columns, 4 * LANES):
+            a, b = near[i, 0, :, lanes], far[i, 0, :, lanes]
+            out_ref[i, :, 0, lanes] = jnp.where(north, b, a)
+            out_ref[i, :, row_count - 1, lanes] = jnp.where(north, a, b)
+            for j in range(1, row_count - 1):
+                out_ref[i, :, j, lanes] = inner[i, j - 1, :, lanes]
+        t = lax.rem(core + place, PAIR) * share + i
+        copies.append(pltpu.make_async_copy(out_ref.at[i], out_hbm.at[t], sems.at[i]))
+        copies[-1].start()
     for copy in copies:
         copy.wait()
 
@@ -474,12 +472,13 @@
 SMALL, WHOLE, UNREAD = pltpu.SMEM, pltpu.VMEM, pl.ANY
 
 
-def call(kernel, outs, operands, scratch=(), sems=0, place=None):
+def call(kernel, outs, operands, scratch=(), sems=0, place=None, aliases=None):
     return pl.pallas_call(
         kernel,
         out_shape=[jax.ShapeDtypeStruct(shape, jnp.float32) for shape in outs],
         in_specs=[pl.BlockSpec(memory_space=place) for _, place in operands],
         out_specs=[pl.BlockSpec(memory_space=place or WHOLE)] * len(outs),
+        input_output_aliases=aliases or {},
         scratch_shapes=[pltpu.VMEM(shape, jnp.float32) for shape in scratch]
         + ([pltpu.SemaphoreType.DMA((sems,))] if sems else []),
         compiler_params=pltpu.CompilerParams(vmem_limit_bytes=24 << 20),
@@ -520,21 +519,22 @@
     def set_shape(number):
         return (share, number, level_count, column_count)
 
-    def forward(mine, theirs, after):
+    def forward(mine, theirs, after, *relay):
         count = mine.shape[0] * mine.shape[1]
+        message_shape = (count, level_count, 2 * MODES + LANES)
         return call(
             forward_kernel,
-            [(count, level_count, 2 * MODES + LANES), (PAIR, count, level_count, width)],
-            whole(mine, theirs, phase, high, low) + [(after, UNREAD)],
+            [message_shape, (PAIR, count, level_count, width)] + [v.shape for v in relay],
+            whole(mine, theirs, phase, high, low) + [(after, UNREAD)] + whole(*relay),
             [(count * group, padded)],
         )
 
-    def shifted(which, held, after, *relay):
+    def shifted(which, held, after):
         count = held.shape[1]
         return call(
             functools.partial(shift_kernel, which, column_count),
-            [(count, PAIR, level_count, width)] + [v.shape for v in relay],
-            whole(distance, fraction, held) + [(after, UNREAD)] + whole(*relay),
+            [(count, PAIR, level_count, width)],
+            whole(distance, fraction, held) + [(after, UNREAD)],
         )
 
     def inverse(which, held, moved, own, other, after):
@@ -558,7 +558,8 @@
     )
     inner_theirs = swap_core(inner_send)
     near_got = swap_band(near_edge, 0)
-    inner_own, inner_held = forward(inner_mine, inner_theirs, near_part)
+    inner_own, inner_held, far_relay = forward(inner_mine, inner_theirs, near_part, far_edge)
+    far_got = swap_band(far_relay, 1)
     inner_other = swap_half(inner_own)
     row_shape = (row_count, level_count, LANES)
     distance, fraction, keep, gain = call(
@@ -568,8 +569,7 @@
         + whole(wave)
         + [(inner_own, UNREAD)],
     )
-    inner_moved, far_relay = shifted("inner", inner_held, inner_own, far_edge)
-    far_got = swap_band(far_relay, 1)
+    (inner_moved,) = shifted("inner", inner_held, inner_own)
 
     near_mine, near_send = call(
         functools.partial(edge_kernel, True),
@@ -596,13 +596,22 @@
     (far_moved,) = shifted("far", far_held, far_own)
     far = inverse("far", far_held, far_moved, far_own, far_other, far_moved)
     far_back = swap_core(far[1])
+    (half_done,) = call(
+        functools.partial(end_kernel, 0),
+        [tracers.shape],
+        whole(inner[0], near[0], far[0]),
+        [(share,) + tracers.shape[1:]],
+        share,
+        pltpu.HBM,
+    )
     (result,) = call(
-        end_kernel,
+        functools.partial(end_kernel, 1),
         [tracers.shape],
-        whole(inner[0], near[0], far[0], inner_back, near_back, far_back),
-        [tracers.shape],
-        tracer_count,
+        whole(inner_back, near_back, far_back) + [(half_done, pltpu.HBM)],
+        [(share,) + tracers.shape[1:]],
+        share,
         pltpu.HBM,
+        {3: 0},
     )
     return result
 

time: 31.3 us -> 30.9 us (0.987)
  the two profiles are of different devices: /device:TPU:3 before, /device:TPU:13 now
where the time goes in v12:
time: 30.9 us; the launch traced here: 30.7 us
  waiting for transfers between devices  11.9 us (39%)
  starting transfers between devices  11.8 us (38%)
  Pallas kernels  6.18 us (20%)
  local copies, waits for them, and re-layouts  0.65 us (2%)
    pallas_call x15, Pallas kernels, call(): pl.pallas_call(kernel, out_shape=[jax.ShapeDtypeStruct(shape, jnp.float32...  6.18 us
    ppermute x3, waiting for transfers between devices, swap_half(): return lax.ppermute(value, 'lon', [(p, p ^ 2) for p in range(lon_count)])  6.02 us
    ppermute x6, starting transfers between devices, swap_core(): return lax.ppermute(value, 'lon', [(p, p ^ 1) for p in range(lon_count)])  5.63 us
    ppermute x2, starting transfers between devices, swap_band(): return lax.ppermute(value, 'lat', pairs)  5.52 us
    ppermute x2, waiting for transfers between devices, swap_band(): return lax.ppermute(value, 'lat', pairs)  4.86 us
    ppermute x6, waiting for transfers between devices, swap_core(): return lax.ppermute(value, 'lon', [(p, p ^ 1) for p in range(lon_count)])  1.07 us
    unnamed x16, local copies, waits for them, and re-layouts  0.65 us
  transfers between devices with their start and end apart: 11, of which 5 were waited for; matrix products, arithmetic and copies ran while one was open for 0% of the time, Pallas kernels for 11%

profile of v12, /device:TPU:13, one launch (start us, length us, event | category | flops | bytes accessed | tf_op | source)
XLA Modules:
  0.0 30.7 jit_solution(645660740727481425)
XLA Ops:
  0.0 1.8 %shard_map.100 = (f32[2,2,8,1440]{3,2,1,0:T(8,128)S(1)}, f32[2,2,8,1440]{3,2,1,0:T(8,128)S(1)}, f32[40,1440]{1,0:T(8,128)S(1)}, f32[40,1440]{1,0:T(8,128)S(1)}, ...) custom-call(f32[4,8,4,1440]{3,2,1,0:T(4,128)} %cells_hbm.1, f32[8,4,1440]{2,1,0:T(4,128)} %speed_hbm.1), custom_call_target="tpu_custom_call" | custom-call | flops 1 | bytes 1 | tf_op jit(solution)/shard_map/pallas_call | solution.py:476
  1.9 0.7 %collective-permute-start = (f32[2,2,8,1440]{3,2,1,0:T(8,128)S(1)}, f32[2,2,8,1440]{3,2,1,0:T(8,128)S(1)}, u32[]{:S(2)}, u32[]{:S(2)}) collective-permute-start(f32[2,2,8,1440]{3,2,1,0:T(8,128)S(1)} %get-tuple-element.33), channel_id=1, source_target_pairs={{0,1},{1,0},{2,3},{3,2},{4,5},{5,4},{6,7},{7,6},{8,9},{9,8},{10,11... | collective-permute-start | bytes 552968 | tf_op jit(solution)/shard_map/ppermute | solution.py:508
  2.6 1.2 %collective-permute-start.2 = (f32[40,1440]{1,0:T(8,128)S(1)}, f32[40,1440]{1,0:T(8,128)S(1)}, u32[]{:S(2)}, u32[]{:S(2)}) collective-permute-start(f32[40,1440]{1,0:T(8,128)S(1)} %get-tuple-element.42.own_ref), channel_id=1, source_target_pairs={{0,4},{4,0},{8,12},{12,8},{16,20},{20,16},{24,28},{28,24},{1,5},{5... | collective-permute-start | bytes 691208 | tf_op jit(solution)/shard_map/ppermute | solution.py:517
  3.8 0.0 collective-permute-done.theirs_ref
  3.8 0.0 copy-done
  3.8 0.0 copy-done.1
  3.8 0.0 copy-done.2
  3.8 0.0 copy-start.3
  3.9 0.1 shard_map.101
  4.0 0.3 collective-permute-start.1
  4.2 4.3 %collective-permute-start.6 = (f32[40,1440]{1,0:T(8,128)S(1)}, f32[40,1440]{1,0:T(8,128)S(1)}, u32[]{:S(2)}, u32[]{:S(2)}) collective-permute-start(f32[40,1440]{1,0:T(8,128)S(1)} %get-tuple-element.48), channel_id=1, source_target_pairs={{4,8},{8,4},{12,16},{16,12},{20,24},{24,20},{5,9},{9,5},{13,17},{1... | collective-permute-start | bytes 691208 | tf_op jit(solution)/shard_map/ppermute | solution.py:517
  8.5 0.0 copy-start.6
  8.5 0.0 copy-start.7
  8.6 0.0 copy-done.3
  8.6 0.0 copy-done.5
  8.6 0.0 copy-done.4
  8.6 0.6 %copy-done.6 = s32[32]{0:T(128)S(1)} copy-done((s32[32]{0:T(128)S(1)}, s32[32]{0:T(128)}, u32[]{:S(2)}) %copy-start.6) | copy-done | bytes 152
  9.2 0.0 copy-done.7
  9.2 0.6 %shard_map.102 = (f32[4,8,128]{2,1,0:T(8,128)S(1)}, f32[4,8,128]{2,1,0:T(8,128)S(1)}, f32[4,8,128]{2,1,0:T(8,128)S(1)}, f32[4,18,8,128]{3,2,1,0:T(8,128)S(1)}) custom-call(s32[4,8]{1,0:T(4,128)S(1)} %bitcast.2, f32[4,8]{1,0:T(4,128)S(1)} %bitcast.3, s32[32]{0:T(128)S(1)} %copy-done.6, f32[32]{0:T(128)S(1)} %copy-done.7, f32[18,128]{1,0:T(8,128)S(1)} %copy-done.3, ...), custom_call_target="tpu_custom_call" | custom-call | flops 1 | bytes 1 | tf_op jit(solution)/shard_map/pallas_call | solution.py:476
  9.8 0.7 %shard_map.103.after_ref.moved_ref = f32[4,2,8,1536]{3,2,1,0:T(8,128)S(1)} custom-call(f32[4,8,128]{2,1,0:T(8,128)S(1)} %get-tuple-element.37.distance_ref, f32[4,8,128]{2,1,0:T(8,128)S(1)} %get-tuple-element.38.share_ref, f32[2,4,8,1536]{3,2,1,0:T(8,128)S(1)} %get-tuple-element.41.held_ref, f32[4,8,2176]{2,1,0:T(8,128)S(1)} %get-tuple-element.36.after_ref.own_ref), custom_call_target="tpu_custom_call" | custom-call | flops 1 | bytes 1 | tf_op jit(solution)/shard_map/pallas_call | solution.py:476
  10.5 4.9 %collective-permute-done.2.got_ref = f32[40,1440]{1,0:T(8,128)S(1)} collective-permute-done((f32[40,1440]{1,0:T(8,128)S(1)}, f32[40,1440]{1,0:T(8,128)S(1)}, u32[]{:S(2)}, u32[]{:S(2)}) %collective-permute-start.2) | collective-permute-done | bytes 230432 | tf_op jit(solution)/shard_map/ppermute | solution.py:517
  15.4 0.1 shard_map.104
  15.5 0.9 %collective-permute-start.3 = (f32[2,1,8,1440]{3,2,1,0:T(8,128)S(1)}, f32[2,1,8,1440]{3,2,1,0:T(8,128)S(1)}, u32[]{:S(2)}, u32[]{:S(2)}) collective-permute-start(f32[2,1,8,1440]{3,2,1,0:T(8,128)S(1)} %get-tuple-element.44), channel_id=1, source_target_pairs={{0,1},{1,0},{2,3},{3,2},{4,5},{5,4},{6,7},{7,6},{8,9},{9,8},{10,11... | collective-permute-start | bytes 276488 | tf_op jit(solution)/shard_map/ppermute | solution.py:508
  16.4 0.9 %collective-permute-done.3.theirs_ref = f32[2,1,8,1440]{3,2,1,0:T(8,128)S(1)} collective-permute-done((f32[2,1,8,1440]{3,2,1,0:T(8,128)S(1)}, f32[2,1,8,1440]{3,2,1,0:T(8,128)S(1)}, u32[]{:S(2)}, u32[]{:S(2)}) %collective-permute-start.3) | collective-permute-done | bytes 92192 | tf_op jit(solution)/shard_map/ppermute | solution.py:508
  17.3 0.1 shard_map.105
  17.4 0.0 collective-permute-start.5
  17.4 0.3 %shard_map.106.after_ref.moved_ref = f32[2,2,8,1536]{3,2,1,0:T(8,128)S(1)} custom-call(f32[4,8,128]{2,1,0:T(8,128)S(1)} %get-tuple-element.37.distance_ref, f32[4,8,128]{2,1,0:T(8,128)S(1)} %get-tuple-element.38.share_ref, f32[2,2,8,1536]{3,2,1,0:T(8,128)S(1)} %get-tuple-element.45.held_ref, f32[2,8,2176]{2,1,0:T(8,128)S(1)} %get-tuple-element.46.after_ref.own_ref), custom_call_target="tpu_custom_call" | custom-call | flops 1 | bytes 1 | tf_op jit(solution)/shard_map/pallas_call | solution.py:476
  17.8 0.0 collective-permute-done.1.other_ref
  17.8 0.1 shard_map.107
  17.9 0.0 collective-permute-done.6.got_ref
  17.9 0.1 shard_map.108
  18.0 0.4 %collective-permute-start.8 = (f32[2,1,8,1440]{3,2,1,0:T(8,128)S(1)}, f32[2,1,8,1440]{3,2,1,0:T(8,128)S(1)}, u32[]{:S(2)}, u32[]{:S(2)}) collective-permute-start(f32[2,1,8,1440]{3,2,1,0:T(8,128)S(1)} %get-tuple-element.53), channel_id=1, source_target_pairs={{0,1},{1,0},{2,3},{3,2},{4,5},{5,4},{6,7},{7,6},{8,9},{9,8},{10,11... | collective-permute-start | bytes 276488 | tf_op jit(solution)/shard_map/ppermute | solution.py:508
  18.4 3.9 %collective-permute-done.5.other_ref = f32[2,8,2176]{2,1,0:T(8,128)S(1)} collective-permute-done((f32[2,8,2176]{2,1,0:T(8,128)S(1)}, f32[2,8,2176]{2,1,0:T(8,128)S(1)}, u32[]{:S(2)}, u32[]{:S(2)}) %collective-permute-start.5) | collective-permute-done | bytes 139296 | tf_op jit(solution)/shard_map/ppermute | solution.py:511
  22.3 0.1 shard_map.109
  22.4 0.0 collective-permute-done.8.theirs_ref
  22.5 0.1 shard_map.110
  22.6 0.3 %collective-permute-start.9 = (f32[2,8,2176]{2,1,0:T(8,128)S(1)}, f32[2,8,2176]{2,1,0:T(8,128)S(1)}, u32[]{:S(2)}, u32[]{:S(2)}) collective-permute-start(f32[2,8,2176]{2,1,0:T(8,128)S(1)} %get-tuple-element.56.after_ref.own_ref), channel_id=1, source_target_pairs={{0,2},{1,3},{2,0},{3,1},{4,6},{5,7},{6,4},{7,5},{8,10},{9,11},{10,... | collective-permute-start | bytes 417800 | tf_op jit(solution)/shard_map/ppermute | solution.py:511
  22.9 1.1 %collective-permute-start.4 = (f32[2,2,8,1440]{3,2,1,0:T(8,128)S(1)}, f32[2,2,8,1440]{3,2,1,0:T(8,128)S(1)}, u32[]{:S(2)}, u32[]{:S(2)}) collective-permute-start(f32[2,2,8,1440]{3,2,1,0:T(8,128)S(1)} %get-tuple-element.47), channel_id=1, source_target_pairs={{0,1},{1,0},{2,3},{3,2},{4,5},{5,4},{6,7},{7,6},{8,9},{9,8},{10,11... | collective-permute-start | bytes 552968 | tf_op jit(solution)/shard_map/ppermute | solution.py:508
  24.0 0.0 collective-permute-start.7
  24.0 0.3 shard_map.111.moved_ref.after_ref
  24.3 2.1 %collective-permute-done.9.other_ref = f32[2,8,2176]{2,1,0:T(8,128)S(1)} collective-permute-done((f32[2,8,2176]{2,1,0:T(8,128)S(1)}, f32[2,8,2176]{2,1,0:T(8,128)S(1)}, u32[]{:S(2)}, u32[]{:S(2)}) %collective-permute-start.9) | collective-permute-done | bytes 139296 | tf_op jit(solution)/shard_map/ppermute | solution.py:511
  26.5 0.1 shard_map.112
  26.6 2.4 %collective-permute-start.10 = (f32[2,1,8,1440]{3,2,1,0:T(8,128)S(1)}, f32[2,1,8,1440]{3,2,1,0:T(8,128)S(1)}, u32[]{:S(2)}, u32[]{:S(2)}) collective-permute-start(f32[2,1,8,1440]{3,2,1,0:T(8,128)S(1)} %get-tuple-element.57), channel_id=1, source_target_pairs={{0,1},{1,0},{2,3},{3,2},{4,5},{5,4},{6,7},{7,6},{8,9},{9,8},{10,11... | collective-permute-start | bytes 276488 | tf_op jit(solution)/shard_map/ppermute | solution.py:508
  29.0 0.8 %shard_map.113.refs_0_ = f32[4,8,4,1440]{3,2,1,0:T(4,128)} custom-call(f32[2,2,8,1440]{3,2,1,0:T(8,128)S(1)} %get-tuple-element.50.after_ref.inner, f32[2,1,8,1440]{3,2,1,0:T(8,128)S(1)} %get-tuple-element.54.after_ref.near, f32[2,1,8,1440]{3,2,1,0:T(8,128)S(1)} %get-tuple-element.58.far), custom_call_target="tpu_custom_call" | custom-call | flops 1 | bytes 1 | tf_op jit(solution)/shard_map/pallas_call | solution.py:476
  29.8 0.0 collective-permute-done.7.near
  29.8 0.0 collective-permute-done.4.inner
  29.8 0.1 collective-permute-done.10.far
  29.9 0.8 %shard_map.114 = f32[4,8,4,1440]{3,2,1,0:T(4,128)} custom-call(f32[2,2,8,1440]{3,2,1,0:T(8,128)S(1)} %collective-permute-done.4.inner, f32[2,1,8,1440]{3,2,1,0:T(8,128)S(1)} %collective-permute-done.7.near, f32[2,1,8,1440]{3,2,1,0:T(8,128)S(1)} %collective-permute-done.10.far, f32[4,8,4,1440]{3,2,1,0:T(4,128)} %shard_map.113.refs_0_), custom_call_target="tpu_custom_call", output_to_operand_aliasing={{}: (3, {})} | custom-call | flops 1 | bytes 1 | tf_op jit(solution)/shard_map/pallas_call | solution.py:476
  (5 shorter events, 0.0 us)
Async XLA Ops:
  0.0 3.8 %copy-start = (bf16[384,256]{1,0:T(8,128)(2,1)S(1)}, bf16[384,256]{1,0:T(8,128)(2,1)}, u32[]{:S(2)}) copy-start(bf16[384,256]{1,0:T(8,128)(2,1)} %constant.10.clone.high_ref) | copy-start | bytes 589828
  0.0 3.8 %copy-start.1 = (bf16[384,256]{1,0:T(8,128)(2,1)S(1)}, bf16[384,256]{1,0:T(8,128)(2,1)}, u32[]{:S(2)}) copy-start(bf16[384,256]{1,0:T(8,128)(2,1)} %constant.11.clone.low_ref) | copy-start | bytes 589828
  0.0 3.8 %copy-start.2 = (f32[18,384]{1,0:T(8,128)S(1)}, f32[18,384]{1,0:T(8,128)}, u32[]{:S(2)}) copy-start(f32[18,384]{1,0:T(8,128)} %constant.8.clone.phase_ref) | copy-start | bytes 82948
  1.9 2.0 %collective-permute-start = (f32[2,2,8,1440]{3,2,1,0:T(8,128)S(1)}, f32[2,2,8,1440]{3,2,1,0:T(8,128)S(1)}, u32[]{:S(2)}, u32[]{:S(2)}) collective-permute-start(f32[2,2,8,1440]{3,2,1,0:T(8,128)S(1)} %get-tuple-element.33), channel_id=1, source_target_pairs={{0,1},{1,0},{2,3},{3,2},{4,5},{5,4},{6,7},{7,6},{8,9},{9,8},{10,11... | collective-permute-start | bytes 552968 | tf_op jit(solution)/shard_map/ppermute | solution.py:508
  2.6 12.8 %collective-permute-start.2 = (f32[40,1440]{1,0:T(8,128)S(1)}, f32[40,1440]{1,0:T(8,128)S(1)}, u32[]{:S(2)}, u32[]{:S(2)}) collective-permute-start(f32[40,1440]{1,0:T(8,128)S(1)} %get-tuple-element.42.own_ref), channel_id=1, source_target_pairs={{0,4},{4,0},{8,12},{12,8},{16,20},{20,16},{24,28},{28,24},{1,5},{5... | collective-permute-start | bytes 691208 | tf_op jit(solution)/shard_map/ppermute | solution.py:517
  3.8 4.7 %copy-start.3 = (f32[18,128]{1,0:T(8,128)S(1)}, f32[18,128]{1,0:T(8,128)}, u32[]{:S(2)}) copy-start(f32[18,128]{1,0:T(8,128)} %constant.9.clone.wave_ref) | copy-start | bytes 27652
  4.0 13.8 %collective-permute-start.1 = (f32[4,8,2176]{2,1,0:T(8,128)S(1)}, f32[4,8,2176]{2,1,0:T(8,128)S(1)}, u32[]{:S(2)}, u32[]{:S(2)}) collective-permute-start(f32[4,8,2176]{2,1,0:T(8,128)S(1)} %get-tuple-element.36.after_ref.own_ref), channel_id=1, source_target_pairs={{0,2},{1,3},{2,0},{3,1},{4,6},{5,7},{6,4},{7,5},{8,10},{9,11},{10,... | collective-permute-start | bytes 835592 | tf_op jit(solution)/shard_map/ppermute | solution.py:511
  4.2 4.3 %copy-start.5 = (f32[8,4]{0,1:T(4,128)S(1)}, f32[8,4]{0,1:T(4,128)}, u32[]{:S(2)}) copy-start(f32[8,4]{0,1:T(4,128)} %param.13) | copy-start | bytes 388
  4.2 4.4 %copy-start.4 = (s32[8,4]{0,1:T(4,128)S(1)}, s32[8,4]{0,1:T(4,128)}, u32[]{:S(2)}) copy-start(s32[8,4]{0,1:T(4,128)} %param.12) | copy-start | bytes 388
  4.2 13.7 %collective-permute-start.6 = (f32[40,1440]{1,0:T(8,128)S(1)}, f32[40,1440]{1,0:T(8,128)S(1)}, u32[]{:S(2)}, u32[]{:S(2)}) collective-permute-start(f32[40,1440]{1,0:T(8,128)S(1)} %get-tuple-element.48), channel_id=1, source_target_pairs={{4,8},{8,4},{12,16},{16,12},{20,24},{24,20},{5,9},{9,5},{13,17},{1... | collective-permute-start | bytes 691208 | tf_op jit(solution)/shard_map/ppermute | solution.py:517
  8.5 0.7 %copy-start.6 = (s32[32]{0:T(128)S(1)}, s32[32]{0:T(128)}, u32[]{:S(2)}) copy-start(s32[32]{0:T(128)} %cutoff_ref.1) | copy-start | bytes 388
  8.5 0.7 %copy-start.7 = (f32[32]{0:T(128)S(1)}, f32[32]{0:T(128)}, u32[]{:S(2)}) copy-start(f32[32]{0:T(128)} %damping_ref.1) | copy-start | bytes 388
  15.5 1.9 %collective-permute-start.3 = (f32[2,1,8,1440]{3,2,1,0:T(8,128)S(1)}, f32[2,1,8,1440]{3,2,1,0:T(8,128)S(1)}, u32[]{:S(2)}, u32[]{:S(2)}) collective-permute-start(f32[2,1,8,1440]{3,2,1,0:T(8,128)S(1)} %get-tuple-element.44), channel_id=1, source_target_pairs={{0,1},{1,0},{2,3},{3,2},{4,5},{5,4},{6,7},{7,6},{8,9},{9,8},{10,11... | collective-permute-start | bytes 276488 | tf_op jit(solution)/shard_map/ppermute | solution.py:508
  17.4 4.9 %collective-permute-start.5 = (f32[2,8,2176]{2,1,0:T(8,128)S(1)}, f32[2,8,2176]{2,1,0:T(8,128)S(1)}, u32[]{:S(2)}, u32[]{:S(2)}) collective-permute-start(f32[2,8,2176]{2,1,0:T(8,128)S(1)} %get-tuple-element.46.after_ref.own_ref), channel_id=1, source_target_pairs={{0,2},{1,3},{2,0},{3,1},{4,6},{5,7},{6,4},{7,5},{8,10},{9,11},{10,... | collective-permute-start | bytes 417800 | tf_op jit(solution)/shard_map/ppermute | solution.py:511
  18.0 4.4 %collective-permute-start.8 = (f32[2,1,8,1440]{3,2,1,0:T(8,128)S(1)}, f32[2,1,8,1440]{3,2,1,0:T(8,128)S(1)}, u32[]{:S(2)}, u32[]{:S(2)}) collective-permute-start(f32[2,1,8,1440]{3,2,1,0:T(8,128)S(1)} %get-tuple-element.53), channel_id=1, source_target_pairs={{0,1},{1,0},{2,3},{3,2},{4,5},{5,4},{6,7},{7,6},{8,9},{9,8},{10,11... | collective-permute-start | bytes 276488 | tf_op jit(solution)/shard_map/ppermute | solution.py:508
  22.6 3.9 %collective-permute-start.9 = (f32[2,8,2176]{2,1,0:T(8,128)S(1)}, f32[2,8,2176]{2,1,0:T(8,128)S(1)}, u32[]{:S(2)}, u32[]{:S(2)}) collective-permute-start(f32[2,8,2176]{2,1,0:T(8,128)S(1)} %get-tuple-element.56.after_ref.own_ref), channel_id=1, source_target_pairs={{0,2},{1,3},{2,0},{3,1},{4,6},{5,7},{6,4},{7,5},{8,10},{9,11},{10,... | collective-permute-start | bytes 417800 | tf_op jit(solution)/shard_map/ppermute | solution.py:511
  22.9 6.9 %collective-permute-start.4 = (f32[2,2,8,1440]{3,2,1,0:T(8,128)S(1)}, f32[2,2,8,1440]{3,2,1,0:T(8,128)S(1)}, u32[]{:S(2)}, u32[]{:S(2)}) collective-permute-start(f32[2,2,8,1440]{3,2,1,0:T(8,128)S(1)} %get-tuple-element.47), channel_id=1, source_target_pairs={{0,1},{1,0},{2,3},{3,2},{4,5},{5,4},{6,7},{7,6},{8,9},{9,8},{10,11... | collective-permute-start | bytes 552968 | tf_op jit(solution)/shard_map/ppermute | solution.py:508
  24.0 5.8 %collective-permute-start.7 = (f32[2,1,8,1440]{3,2,1,0:T(8,128)S(1)}, f32[2,1,8,1440]{3,2,1,0:T(8,128)S(1)}, u32[]{:S(2)}, u32[]{:S(2)}) collective-permute-start(f32[2,1,8,1440]{3,2,1,0:T(8,128)S(1)} %get-tuple-element.52), channel_id=1, source_target_pairs={{0,1},{1,0},{2,3},{3,2},{4,5},{5,4},{6,7},{7,6},{8,9},{9,8},{10,11... | collective-permute-start | bytes 276488 | tf_op jit(solution)/shard_map/ppermute | solution.py:508
  26.6 3.3 %collective-permute-start.10 = (f32[2,1,8,1440]{3,2,1,0:T(8,128)S(1)}, f32[2,1,8,1440]{3,2,1,0:T(8,128)S(1)}, u32[]{:S(2)}, u32[]{:S(2)}) collective-permute-start(f32[2,1,8,1440]{3,2,1,0:T(8,128)S(1)} %get-tuple-element.57), channel_id=1, source_target_pairs={{0,1},{1,0},{2,3},{3,2},{4,5},{5,4},{6,7},{7,6},{8,9},{9,8},{10,11... | collective-permute-start | bytes 276488 | tf_op jit(solution)/shard_map/ppermute | solution.py:508

commit v13 on v12

--- a/solution.py
+++ b/solution.py
@@ -197,9 +197,9 @@
     mine_ref, theirs_ref, phase_ref, high_ref, low_ref, after_ref, *refs
 ):
     *refs, stack_ref = refs
-    relays = len(refs) // 3
-    message_ref, held_ref = refs[relays : relays + 2]
-    for source_ref, relay_ref in zip(refs[:relays], refs[relays + 2 :]):
+    relays = (len(refs) - 3) // 2
+    message_ref, held_ref, rim_ref = refs[relays : relays + 3]
+    for source_ref, relay_ref in zip(refs[:relays], refs[relays + 3 :]):
         relay_ref[...] = source_ref[...]
     share, number, levels, columns = mine_ref.shape
     piece = columns * PAIR // HALF
@@ -214,7 +214,8 @@
         held_ref[1 - core, n, :, :columns] = theirs_ref[i, j]
         for pos in range(PAIR):
             held_ref[pos, n, :, columns:] = jnp.zeros((levels, held_ref.shape[3] - columns), jnp.float32)
-        message_ref[n, :, 2 * MODES :] = held_ref[PAIR - 1, n, :, columns - LANES : columns]
+        rim_ref[n] = held_ref[PAIR - 1, n, :, columns - LANES : columns]
+        message_ref[n, :, 2 * MODES :] = rim_ref[n]
 
     @pl.when(is_cap(lax.axis_index("lat")))
     def _():
@@ -350,7 +351,7 @@
 
 def inverse_kernel(
     which, columns, distance_ref, share_ref, keep_ref, gain_ref, phase_ref, high_ref, low_ref,
-    held_ref, moved_ref, own_ref, other_ref, after_ref, mine_ref, send_ref,
+    held_ref, moved_ref, own_ref, other_ref, rim_ref, after_ref, mine_ref, send_ref,
     stack_ref, back_ref, pair_ref,
 ):
     _, count, levels, _ = held_ref.shape
@@ -365,7 +366,8 @@
     for j, row in enumerate(rows):
         distance, share = distance_ref[row].astype(jnp.int32), share_ref[row]
         for n in range(j, count, number):
-            tiles = [other_ref[n, :, 2 * MODES :], held_ref[0, n, :, :LANES]]
+            rim = jnp.where(cap, other_ref[n, :, 2 * MODES :], rim_ref[n])
+            tiles = [rim, held_ref[0, n, :, :LANES]]
             (moved_ref[n, 0, :, :LANES],) = displaced(tiles, distance, share)
 
     @pl.when(jnp.logical_not(cap))
@@ -507,8 +509,16 @@
     def swap_core(value):
         return lax.ppermute(value, "lon", [(p, p ^ 1) for p in range(lon_count)])
 
-    def swap_half(value):
-        return lax.ppermute(value, "lon", [(p, p ^ 2) for p in range(lon_count)])
+    quarter = lat_count // 4
+    caps = [b for b in range(lat_count) if b < quarter or b >= lat_count - quarter]
+
+    def swap_half(message, rim):
+        def pairs(bands):
+            return [(b * lon_count + p, b * lon_count + (p ^ 2)) for b in bands for p in range(lon_count)]
+
+        others = [b for b in range(lat_count) if b not in caps]
+        axes = ("lat", "lon")
+        return lax.ppermute(message, axes, pairs(caps)), lax.ppermute(rim, axes, pairs(others))
 
     def swap_band(value, first):
         pairs = []
@@ -524,7 +534,8 @@
         message_shape = (count, level_count, 2 * MODES + LANES)
         return call(
             forward_kernel,
-            [message_shape, (PAIR, count, level_count, width)] + [v.shape for v in relay],
+            [message_shape, (PAIR, count, level_count, width), (count, level_count, LANES)]
+            + [v.shape for v in relay],
             whole(mine, theirs, phase, high, low) + [(after, UNREAD)] + whole(*relay),
             [(count * group, padded)],
         )
@@ -537,12 +548,12 @@
             whole(distance, fraction, held) + [(after, UNREAD)],
         )
 
-    def inverse(which, held, moved, own, other, after):
+    def inverse(which, held, moved, own, others, after):
         count = held.shape[1]
         return call(
             functools.partial(inverse_kernel, which, column_count),
             [set_shape(count // share)] * 2,
-            whole(distance, fraction, keep, gain, phase, high, low, held, moved, own, other)
+            whole(distance, fraction, keep, gain, phase, high, low, held, moved, own, *others)
             + [(after, UNREAD)],
             [(count * group, padded), (count * group, double), (PAIR, count, level_count, width)],
         )
@@ -558,9 +569,9 @@
     )
     inner_theirs = swap_core(inner_send)
     near_got = swap_band(near_edge, 0)
-    inner_own, inner_held, far_relay = forward(inner_mine, inner_theirs, near_part, far_edge)
+    inner_own, inner_held, inner_rim, far_relay = forward(inner_mine, inner_theirs, near_part, far_edge)
     far_got = swap_band(far_relay, 1)
-    inner_other = swap_half(inner_own)
+    inner_others = swap_half(inner_own, inner_rim)
     row_shape = (row_count, level_count, LANES)
     distance, fraction, keep, gain = call(
         functools.partial(row_kernel, column_count),
@@ -577,10 +588,10 @@
         whole(near_edge, near_got, near_part) + [(inner_moved, UNREAD)],
     )
     near_theirs = swap_core(near_send)
-    near_own, near_held = forward(near_mine, near_theirs, inner_moved)
-    near_other = swap_half(near_own)
+    near_own, near_held, near_rim = forward(near_mine, near_theirs, inner_moved)
+    near_others = swap_half(near_own, near_rim)
     (near_moved,) = shifted("near", near_held, near_own)
-    inner = inverse("inner", inner_held, inner_moved, inner_own, inner_other, near_moved)
+    inner = inverse("inner", inner_held, inner_moved, inner_own, inner_others, near_moved)
     inner_back = swap_core(inner[1])
 
     far_mine, far_send = call(
@@ -589,12 +600,12 @@
         whole(far_edge, far_got, far_part) + [(inner[0], UNREAD)],
     )
     far_theirs = swap_core(far_send)
-    near = inverse("near", near_held, near_moved, near_own, near_other, far_mine)
+    near = inverse("near", near_held, near_moved, near_own, near_others, far_mine)
     near_back = swap_core(near[1])
-    far_own, far_held = forward(far_mine, far_theirs, near[0])
-    far_other = swap_half(far_own)
+    far_own, far_held, far_rim = forward(far_mine, far_theirs, near[0])
+    far_others = swap_half(far_own, far_rim)
     (far_moved,) = shifted("far", far_held, far_own)
-    far = inverse("far", far_held, far_moved, far_own, far_other, far_moved)
+    far = inverse("far", far_held, far_moved, far_own, far_others, far_moved)
     far_back = swap_core(far[1])
     (half_done,) = call(
         functools.partial(end_kernel, 0),

time: 30.9 us -> 38.7 us (1.25)
  the two profiles are of different devices: /device:TPU:13 before, /device:TPU:17 now
where the time goes in v13:
time: 38.7 us; the launch traced here: 38.4 us
  starting transfers between devices  26.8 us (69%)
  Pallas kernels  6.19 us (16%)
  waiting for transfers between devices  4.47 us (12%)
  local copies, waits for them, and re-layouts  0.66 us (2%)
    ppermute x6, starting transfers between devices, swap_core(): return lax.ppermute(value, 'lon', [(p, p ^ 1) for p in range(lon_count)])  11.3 us
    ppermute x3, starting transfers between devices, swap_half(): lax.ppermute(rim, axes, pairs(others))  9.42 us
    pallas_call x15, Pallas kernels, call(): pl.pallas_call(kernel, out_shape=[jax.ShapeDtypeStruct(shape, jnp.float32...  6.19 us
    ppermute x2, starting transfers between devices, swap_band(): return lax.ppermute(value, 'lat', pairs)  4.06 us
    ppermute x3, waiting for transfers between devices, swap_half(): lax.ppermute(rim, axes, pairs(others))  2.81 us
    ppermute x3, starting transfers between devices, swap_half(): lax.ppermute(message, axes, pairs(caps))  2.02 us
    ppermute x6, waiting for transfers between devices, swap_core(): return lax.ppermute(value, 'lon', [(p, p ^ 1) for p in range(lon_count)])  1.07 us
  transfers between devices with their start and end apart: 14, of which 6 were waited for; matrix products, arithmetic and copies ran while one was open for 0% of the time, Pallas kernels for 9%

profile of v13, /device:TPU:17, one launch (start us, length us, event | category | flops | bytes accessed | tf_op | source)
XLA Modules:
  0.0 38.4 jit_solution(434971153830100329)
XLA Ops:
  0.0 1.8 %shard_map.100 = (f32[2,2,8,1440]{3,2,1,0:T(8,128)S(1)}, f32[2,2,8,1440]{3,2,1,0:T(8,128)S(1)}, f32[40,1440]{1,0:T(8,128)S(1)}, f32[40,1440]{1,0:T(8,128)S(1)}, ...) custom-call(f32[4,8,4,1440]{3,2,1,0:T(4,128)} %cells_hbm.1, f32[8,4,1440]{2,1,0:T(4,128)} %speed_hbm.1), custom_call_target="tpu_custom_call" | custom-call | flops 1 | bytes 1 | tf_op jit(solution)/shard_map/pallas_call | solution.py:478
  1.9 0.7 %collective-permute-start = (f32[2,2,8,1440]{3,2,1,0:T(8,128)S(1)}, f32[2,2,8,1440]{3,2,1,0:T(8,128)S(1)}, u32[]{:S(2)}, u32[]{:S(2)}) collective-permute-start(f32[2,2,8,1440]{3,2,1,0:T(8,128)S(1)} %get-tuple-element.36), channel_id=1, source_target_pairs={{0,1},{1,0},{2,3},{3,2},{4,5},{5,4},{6,7},{7,6},{8,9},{9,8},{10,11... | collective-permute-start | bytes 552968 | tf_op jit(solution)/shard_map/ppermute | solution.py:510
  2.6 1.2 %collective-permute-start.3 = (f32[40,1440]{1,0:T(8,128)S(1)}, f32[40,1440]{1,0:T(8,128)S(1)}, u32[]{:S(2)}, u32[]{:S(2)}) collective-permute-start(f32[40,1440]{1,0:T(8,128)S(1)} %get-tuple-element.46.own_ref), channel_id=1, source_target_pairs={{0,4},{4,0},{8,12},{12,8},{16,20},{20,16},{24,28},{28,24},{1,5},{5... | collective-permute-start | bytes 691208 | tf_op jit(solution)/shard_map/ppermute | solution.py:527
  3.8 0.0 collective-permute-done.theirs_ref
  3.8 0.0 copy-start.3
  3.9 0.1 shard_map.101
  4.0 0.7 %collective-permute-start.1 = (f32[4,8,2176]{2,1,0:T(8,128)S(1)}, f32[4,8,2176]{2,1,0:T(8,128)S(1)}, u32[]{:S(2)}, u32[]{:S(2)}) collective-permute-start(f32[4,8,2176]{2,1,0:T(8,128)S(1)} %get-tuple-element.39.after_ref.own_ref), channel_id=1, source_target_pairs={{0,2},{1,3},{2,0},{3,1},{4,6},{5,7},{6,4},{7,5},{24,26},{25,27},{2... | collective-permute-start | bytes 835592 | tf_op jit(solution)/shard_map/ppermute | solution.py:521
  4.7 0.0 copy-start.5
  4.7 0.0 copy-start.4
  4.7 2.8 %collective-permute-start.8 = (f32[40,1440]{1,0:T(8,128)S(1)}, f32[40,1440]{1,0:T(8,128)S(1)}, u32[]{:S(2)}, u32[]{:S(2)}) collective-permute-start(f32[40,1440]{1,0:T(8,128)S(1)} %get-tuple-element.53), channel_id=1, source_target_pairs={{4,8},{8,4},{12,16},{16,12},{20,24},{24,20},{5,9},{9,5},{13,17},{1... | collective-permute-start | bytes 691208 | tf_op jit(solution)/shard_map/ppermute | solution.py:527
  7.5 0.0 copy-start.6
  7.5 0.0 copy-start.7
  7.6 0.6 %copy-done.6 = s32[32]{0:T(128)S(1)} copy-done((s32[32]{0:T(128)S(1)}, s32[32]{0:T(128)}, u32[]{:S(2)}) %copy-start.6) | copy-done | bytes 152
  8.2 0.0 copy-done.7
  8.2 0.6 %shard_map.102 = (f32[4,8,128]{2,1,0:T(8,128)S(1)}, f32[4,8,128]{2,1,0:T(8,128)S(1)}, f32[4,8,128]{2,1,0:T(8,128)S(1)}, f32[4,18,8,128]{3,2,1,0:T(8,128)S(1)}) custom-call(s32[4,8]{1,0:T(4,128)S(1)} %bitcast.2, f32[4,8]{1,0:T(4,128)S(1)} %bitcast.3, s32[32]{0:T(128)S(1)} %copy-done.6, f32[32]{0:T(128)S(1)} %copy-done.7, f32[18,128]{1,0:T(8,128)S(1)} %copy-done.3, ...), custom_call_target="tpu_custom_call" | custom-call | flops 1 | bytes 1 | tf_op jit(solution)/shard_map/pallas_call | solution.py:478
  8.9 0.7 %shard_map.103.after_ref.moved_ref = f32[4,2,8,1536]{3,2,1,0:T(8,128)S(1)} custom-call(f32[4,8,128]{2,1,0:T(8,128)S(1)} %get-tuple-element.40.distance_ref, f32[4,8,128]{2,1,0:T(8,128)S(1)} %get-tuple-element.41.share_ref, f32[2,4,8,1536]{3,2,1,0:T(8,128)S(1)} %get-tuple-element.44.held_ref, f32[4,8,2176]{2,1,0:T(8,128)S(1)} %get-tuple-element.39.after_ref.own_ref), custom_call_target="tpu_custom_call" | custom-call | flops 1 | bytes 1 | tf_op jit(solution)/shard_map/pallas_call | solution.py:478
  9.5 0.6 %collective-permute-done.3.got_ref = f32[40,1440]{1,0:T(8,128)S(1)} collective-permute-done((f32[40,1440]{1,0:T(8,128)S(1)}, f32[40,1440]{1,0:T(8,128)S(1)}, u32[]{:S(2)}, u32[]{:S(2)}) %collective-permute-start.3) | collective-permute-done | bytes 230432 | tf_op jit(solution)/shard_map/ppermute | solution.py:527
  10.1 0.1 shard_map.104
  10.2 6.2 %collective-permute-start.4 = (f32[2,1,8,1440]{3,2,1,0:T(8,128)S(1)}, f32[2,1,8,1440]{3,2,1,0:T(8,128)S(1)}, u32[]{:S(2)}, u32[]{:S(2)}) collective-permute-start(f32[2,1,8,1440]{3,2,1,0:T(8,128)S(1)} %get-tuple-element.48), channel_id=1, source_target_pairs={{0,1},{1,0},{2,3},{3,2},{4,5},{5,4},{6,7},{7,6},{8,9},{9,8},{10,11... | collective-permute-start | bytes 276488 | tf_op jit(solution)/shard_map/ppermute | solution.py:510
  16.4 0.9 %collective-permute-done.4.theirs_ref = f32[2,1,8,1440]{3,2,1,0:T(8,128)S(1)} collective-permute-done((f32[2,1,8,1440]{3,2,1,0:T(8,128)S(1)}, f32[2,1,8,1440]{3,2,1,0:T(8,128)S(1)}, u32[]{:S(2)}, u32[]{:S(2)}) %collective-permute-start.4) | collective-permute-done | bytes 92192 | tf_op jit(solution)/shard_map/ppermute | solution.py:510
  17.3 0.1 shard_map.105
  17.4 0.7 %collective-permute-start.6 = (f32[2,8,2176]{2,1,0:T(8,128)S(1)}, f32[2,8,2176]{2,1,0:T(8,128)S(1)}, u32[]{:S(2)}, u32[]{:S(2)}) collective-permute-start(f32[2,8,2176]{2,1,0:T(8,128)S(1)} %get-tuple-element.50.after_ref.own_ref), channel_id=1, source_target_pairs={{0,2},{1,3},{2,0},{3,1},{4,6},{5,7},{6,4},{7,5},{24,26},{25,27},{2... | collective-permute-start | bytes 417800 | tf_op jit(solution)/shard_map/ppermute | solution.py:521
  18.1 3.1 %collective-permute-start.2 = (f32[4,8,128]{2,1,0:T(8,128)S(1)}, f32[4,8,128]{2,1,0:T(8,128)S(1)}, u32[]{:S(2)}, u32[]{:S(2)}) collective-permute-start(f32[4,8,128]{2,1,0:T(8,128)S(1)} %get-tuple-element.45), channel_id=1, source_target_pairs={{8,10},{9,11},{10,8},{11,9},{12,14},{13,15},{14,12},{15,13},{16,18... | collective-permute-start | bytes 49160 | tf_op jit(solution)/shard_map/ppermute | solution.py:521
  21.3 0.3 shard_map.106.after_ref.moved_ref
  21.6 1.0 %collective-permute-done.2.rim_ref = f32[4,8,128]{2,1,0:T(8,128)S(1)} collective-permute-done((f32[4,8,128]{2,1,0:T(8,128)S(1)}, f32[4,8,128]{2,1,0:T(8,128)S(1)}, u32[]{:S(2)}, u32[]{:S(2)}) %collective-permute-start.2) | collective-permute-done | bytes 16416 | tf_op jit(solution)/shard_map/ppermute | solution.py:521
  22.6 0.0 collective-permute-done.1.other_ref
  22.6 0.1 shard_map.107
  22.7 0.0 collective-permute-done.8.got_ref
  22.7 0.1 shard_map.108
  22.8 1.6 %collective-permute-start.10 = (f32[2,1,8,1440]{3,2,1,0:T(8,128)S(1)}, f32[2,1,8,1440]{3,2,1,0:T(8,128)S(1)}, u32[]{:S(2)}, u32[]{:S(2)}) collective-permute-start(f32[2,1,8,1440]{3,2,1,0:T(8,128)S(1)} %get-tuple-element.58), channel_id=1, source_target_pairs={{0,1},{1,0},{2,3},{3,2},{4,5},{5,4},{6,7},{7,6},{8,9},{9,8},{10,11... | collective-permute-start | bytes 276488 | tf_op jit(solution)/shard_map/ppermute | solution.py:510
  24.4 3.1 %collective-permute-start.7 = (f32[2,8,128]{2,1,0:T(8,128)S(1)}, f32[2,8,128]{2,1,0:T(8,128)S(1)}, u32[]{:S(2)}, u32[]{:S(2)}) collective-permute-start(f32[2,8,128]{2,1,0:T(8,128)S(1)} %get-tuple-element.52), channel_id=1, source_target_pairs={{8,10},{9,11},{10,8},{11,9},{12,14},{13,15},{14,12},{15,13},{16,18... | collective-permute-start | bytes 24584 | tf_op jit(solution)/shard_map/ppermute | solution.py:521
  27.5 1.2 %collective-permute-done.7.rim_ref = f32[2,8,128]{2,1,0:T(8,128)S(1)} collective-permute-done((f32[2,8,128]{2,1,0:T(8,128)S(1)}, f32[2,8,128]{2,1,0:T(8,128)S(1)}, u32[]{:S(2)}, u32[]{:S(2)}) %collective-permute-start.7) | collective-permute-done | bytes 8224 | tf_op jit(solution)/shard_map/ppermute | solution.py:521
  28.8 0.0 collective-permute-done.6.other_ref
  28.8 0.1 shard_map.109
  28.9 0.0 collective-permute-done.10.theirs_ref
  28.9 0.1 shard_map.110
  29.0 0.7 %collective-permute-start.11 = (f32[2,8,2176]{2,1,0:T(8,128)S(1)}, f32[2,8,2176]{2,1,0:T(8,128)S(1)}, u32[]{:S(2)}, u32[]{:S(2)}) collective-permute-start(f32[2,8,2176]{2,1,0:T(8,128)S(1)} %get-tuple-element.61.after_ref.own_ref), channel_id=1, source_target_pairs={{0,2},{1,3},{2,0},{3,1},{4,6},{5,7},{6,4},{7,5},{24,26},{25,27},{2... | collective-permute-start | bytes 417800 | tf_op jit(solution)/shard_map/ppermute | solution.py:521
  29.7 1.2 %collective-permute-start.5 = (f32[2,2,8,1440]{3,2,1,0:T(8,128)S(1)}, f32[2,2,8,1440]{3,2,1,0:T(8,128)S(1)}, u32[]{:S(2)}, u32[]{:S(2)}) collective-permute-start(f32[2,2,8,1440]{3,2,1,0:T(8,128)S(1)} %get-tuple-element.51), channel_id=1, source_target_pairs={{0,1},{1,0},{2,3},{3,2},{4,5},{5,4},{6,7},{7,6},{8,9},{9,8},{10,11... | collective-permute-start | bytes 552968 | tf_op jit(solution)/shard_map/ppermute | solution.py:510
  30.9 3.1 %collective-permute-start.12 = (f32[2,8,128]{2,1,0:T(8,128)S(1)}, f32[2,8,128]{2,1,0:T(8,128)S(1)}, u32[]{:S(2)}, u32[]{:S(2)}) collective-permute-start(f32[2,8,128]{2,1,0:T(8,128)S(1)} %get-tuple-element.62), channel_id=1, source_target_pairs={{8,10},{9,11},{10,8},{11,9},{12,14},{13,15},{14,12},{15,13},{16,18... | collective-permute-start | bytes 24584 | tf_op jit(solution)/shard_map/ppermute | solution.py:521
  34.1 0.4 collective-permute-start.9
  34.4 0.3 shard_map.111.moved_ref.after_ref
  34.7 0.6 %collective-permute-done.12.rim_ref = f32[2,8,128]{2,1,0:T(8,128)S(1)} collective-permute-done((f32[2,8,128]{2,1,0:T(8,128)S(1)}, f32[2,8,128]{2,1,0:T(8,128)S(1)}, u32[]{:S(2)}, u32[]{:S(2)}) %collective-permute-start.12) | collective-permute-done | bytes 8224 | tf_op jit(solution)/shard_map/ppermute | solution.py:521
  35.3 0.1 shard_map.112
  35.4 1.2 %collective-permute-start.13 = (f32[2,1,8,1440]{3,2,1,0:T(8,128)S(1)}, f32[2,1,8,1440]{3,2,1,0:T(8,128)S(1)}, u32[]{:S(2)}, u32[]{:S(2)}) collective-permute-start(f32[2,1,8,1440]{3,2,1,0:T(8,128)S(1)} %get-tuple-element.63), channel_id=1, source_target_pairs={{0,1},{1,0},{2,3},{3,2},{4,5},{5,4},{6,7},{7,6},{8,9},{9,8},{10,11... | collective-permute-start | bytes 276488 | tf_op jit(solution)/shard_map/ppermute | solution.py:510
  36.7 0.8 %shard_map.113.refs_0_ = f32[4,8,4,1440]{3,2,1,0:T(4,128)} custom-call(f32[2,2,8,1440]{3,2,1,0:T(8,128)S(1)} %get-tuple-element.55.after_ref.inner, f32[2,1,8,1440]{3,2,1,0:T(8,128)S(1)} %get-tuple-element.59.after_ref.near, f32[2,1,8,1440]{3,2,1,0:T(8,128)S(1)} %get-tuple-element.64.far), custom_call_target="tpu_custom_call" | custom-call | flops 1 | bytes 1 | tf_op jit(solution)/shard_map/pallas_call | solution.py:478
  37.5 0.0 collective-permute-done.9.near
  37.5 0.1 collective-permute-done.13.far
  37.6 0.8 %shard_map.114 = f32[4,8,4,1440]{3,2,1,0:T(4,128)} custom-call(f32[2,2,8,1440]{3,2,1,0:T(8,128)S(1)} %collective-permute-done.5.inner, f32[2,1,8,1440]{3,2,1,0:T(8,128)S(1)} %collective-permute-done.9.near, f32[2,1,8,1440]{3,2,1,0:T(8,128)S(1)} %collective-permute-done.13.far, f32[4,8,4,1440]{3,2,1,0:T(4,128)} %shard_map.113.refs_0_), custom_call_target="tpu_custom_call", output_to_operand_aliasing={{}: (3, {})} | custom-call | flops 1 | bytes 1 | tf_op jit(solution)/shard_map/pallas_call | solution.py:478
  (11 shorter events, 0.0 us)
Async XLA Ops:
  0.0 3.8 %copy-start = (bf16[384,256]{1,0:T(8,128)(2,1)S(1)}, bf16[384,256]{1,0:T(8,128)(2,1)}, u32[]{:S(2)}) copy-start(bf16[384,256]{1,0:T(8,128)(2,1)} %constant.10.clone.high_ref) | copy-start | bytes 589828
  0.0 3.8 %copy-start.1 = (bf16[384,256]{1,0:T(8,128)(2,1)S(1)}, bf16[384,256]{1,0:T(8,128)(2,1)}, u32[]{:S(2)}) copy-start(bf16[384,256]{1,0:T(8,128)(2,1)} %constant.11.clone.low_ref) | copy-start | bytes 589828
  0.0 3.8 %copy-start.2 = (f32[18,384]{1,0:T(8,128)S(1)}, f32[18,384]{1,0:T(8,128)}, u32[]{:S(2)}) copy-start(f32[18,384]{1,0:T(8,128)} %constant.8.clone.phase_ref) | copy-start | bytes 82948
  1.9 2.0 %collective-permute-start = (f32[2,2,8,1440]{3,2,1,0:T(8,128)S(1)}, f32[2,2,8,1440]{3,2,1,0:T(8,128)S(1)}, u32[]{:S(2)}, u32[]{:S(2)}) collective-permute-start(f32[2,2,8,1440]{3,2,1,0:T(8,128)S(1)} %get-tuple-element.36), channel_id=1, source_target_pairs={{0,1},{1,0},{2,3},{3,2},{4,5},{5,4},{6,7},{7,6},{8,9},{9,8},{10,11... | collective-permute-start | bytes 552968 | tf_op jit(solution)/shard_map/ppermute | solution.py:510
  2.6 7.5 %collective-permute-start.3 = (f32[40,1440]{1,0:T(8,128)S(1)}, f32[40,1440]{1,0:T(8,128)S(1)}, u32[]{:S(2)}, u32[]{:S(2)}) collective-permute-start(f32[40,1440]{1,0:T(8,128)S(1)} %get-tuple-element.46.own_ref), channel_id=1, source_target_pairs={{0,4},{4,0},{8,12},{12,8},{16,20},{20,16},{24,28},{28,24},{1,5},{5... | collective-permute-start | bytes 691208 | tf_op jit(solution)/shard_map/ppermute | solution.py:527
  3.8 3.7 %copy-start.3 = (f32[18,128]{1,0:T(8,128)S(1)}, f32[18,128]{1,0:T(8,128)}, u32[]{:S(2)}) copy-start(f32[18,128]{1,0:T(8,128)} %constant.9.clone.wave_ref) | copy-start | bytes 27652
  4.0 18.6 %collective-permute-start.1 = (f32[4,8,2176]{2,1,0:T(8,128)S(1)}, f32[4,8,2176]{2,1,0:T(8,128)S(1)}, u32[]{:S(2)}, u32[]{:S(2)}) collective-permute-start(f32[4,8,2176]{2,1,0:T(8,128)S(1)} %get-tuple-element.39.after_ref.own_ref), channel_id=1, source_target_pairs={{0,2},{1,3},{2,0},{3,1},{4,6},{5,7},{6,4},{7,5},{24,26},{25,27},{2... | collective-permute-start | bytes 835592 | tf_op jit(solution)/shard_map/ppermute | solution.py:521
  4.7 2.9 %copy-start.5 = (f32[8,4]{0,1:T(4,128)S(1)}, f32[8,4]{0,1:T(4,128)}, u32[]{:S(2)}) copy-start(f32[8,4]{0,1:T(4,128)} %param.13) | copy-start | bytes 388
  4.7 2.9 %copy-start.4 = (s32[8,4]{0,1:T(4,128)S(1)}, s32[8,4]{0,1:T(4,128)}, u32[]{:S(2)}) copy-start(s32[8,4]{0,1:T(4,128)} %param.12) | copy-start | bytes 388
  4.7 18.0 %collective-permute-start.8 = (f32[40,1440]{1,0:T(8,128)S(1)}, f32[40,1440]{1,0:T(8,128)S(1)}, u32[]{:S(2)}, u32[]{:S(2)}) collective-permute-start(f32[40,1440]{1,0:T(8,128)S(1)} %get-tuple-element.53), channel_id=1, source_target_pairs={{4,8},{8,4},{12,16},{16,12},{20,24},{24,20},{5,9},{9,5},{13,17},{1... | collective-permute-start | bytes 691208 | tf_op jit(solution)/shard_map/ppermute | solution.py:527
  7.5 0.7 %copy-start.6 = (s32[32]{0:T(128)S(1)}, s32[32]{0:T(128)}, u32[]{:S(2)}) copy-start(s32[32]{0:T(128)} %cutoff_ref.1) | copy-start | bytes 388
  7.5 0.7 %copy-start.7 = (f32[32]{0:T(128)S(1)}, f32[32]{0:T(128)}, u32[]{:S(2)}) copy-start(f32[32]{0:T(128)} %damping_ref.1) | copy-start | bytes 388
  10.2 7.1 %collective-permute-start.4 = (f32[2,1,8,1440]{3,2,1,0:T(8,128)S(1)}, f32[2,1,8,1440]{3,2,1,0:T(8,128)S(1)}, u32[]{:S(2)}, u32[]{:S(2)}) collective-permute-start(f32[2,1,8,1440]{3,2,1,0:T(8,128)S(1)} %get-tuple-element.48), channel_id=1, source_target_pairs={{0,1},{1,0},{2,3},{3,2},{4,5},{5,4},{6,7},{7,6},{8,9},{9,8},{10,11... | collective-permute-start | bytes 276488 | tf_op jit(solution)/shard_map/ppermute | solution.py:510
  17.4 11.4 %collective-permute-start.6 = (f32[2,8,2176]{2,1,0:T(8,128)S(1)}, f32[2,8,2176]{2,1,0:T(8,128)S(1)}, u32[]{:S(2)}, u32[]{:S(2)}) collective-permute-start(f32[2,8,2176]{2,1,0:T(8,128)S(1)} %get-tuple-element.50.after_ref.own_ref), channel_id=1, source_target_pairs={{0,2},{1,3},{2,0},{3,1},{4,6},{5,7},{6,4},{7,5},{24,26},{25,27},{2... | collective-permute-start | bytes 417800 | tf_op jit(solution)/shard_map/ppermute | solution.py:521
  18.1 4.5 %collective-permute-start.2 = (f32[4,8,128]{2,1,0:T(8,128)S(1)}, f32[4,8,128]{2,1,0:T(8,128)S(1)}, u32[]{:S(2)}, u32[]{:S(2)}) collective-permute-start(f32[4,8,128]{2,1,0:T(8,128)S(1)} %get-tuple-element.45), channel_id=1, source_target_pairs={{8,10},{9,11},{10,8},{11,9},{12,14},{13,15},{14,12},{15,13},{16,18... | collective-permute-start | bytes 49160 | tf_op jit(solution)/shard_map/ppermute | solution.py:521
  22.8 6.1 %collective-permute-start.10 = (f32[2,1,8,1440]{3,2,1,0:T(8,128)S(1)}, f32[2,1,8,1440]{3,2,1,0:T(8,128)S(1)}, u32[]{:S(2)}, u32[]{:S(2)}) collective-permute-start(f32[2,1,8,1440]{3,2,1,0:T(8,128)S(1)} %get-tuple-element.58), channel_id=1, source_target_pairs={{0,1},{1,0},{2,3},{3,2},{4,5},{5,4},{6,7},{7,6},{8,9},{9,8},{10,11... | collective-permute-start | bytes 276488 | tf_op jit(solution)/shard_map/ppermute | solution.py:510
  24.4 4.4 %collective-permute-start.7 = (f32[2,8,128]{2,1,0:T(8,128)S(1)}, f32[2,8,128]{2,1,0:T(8,128)S(1)}, u32[]{:S(2)}, u32[]{:S(2)}) collective-permute-start(f32[2,8,128]{2,1,0:T(8,128)S(1)} %get-tuple-element.52), channel_id=1, source_target_pairs={{8,10},{9,11},{10,8},{11,9},{12,14},{13,15},{14,12},{15,13},{16,18... | collective-permute-start | bytes 24584 | tf_op jit(solution)/shard_map/ppermute | solution.py:521
  29.0 6.3 %collective-permute-start.11 = (f32[2,8,2176]{2,1,0:T(8,128)S(1)}, f32[2,8,2176]{2,1,0:T(8,128)S(1)}, u32[]{:S(2)}, u32[]{:S(2)}) collective-permute-start(f32[2,8,2176]{2,1,0:T(8,128)S(1)} %get-tuple-element.61.after_ref.own_ref), channel_id=1, source_target_pairs={{0,2},{1,3},{2,0},{3,1},{4,6},{5,7},{6,4},{7,5},{24,26},{25,27},{2... | collective-permute-start | bytes 417800 | tf_op jit(solution)/shard_map/ppermute | solution.py:521
  29.7 7.8 %collective-permute-start.5 = (f32[2,2,8,1440]{3,2,1,0:T(8,128)S(1)}, f32[2,2,8,1440]{3,2,1,0:T(8,128)S(1)}, u32[]{:S(2)}, u32[]{:S(2)}) collective-permute-start(f32[2,2,8,1440]{3,2,1,0:T(8,128)S(1)} %get-tuple-element.51), channel_id=1, source_target_pairs={{0,1},{1,0},{2,3},{3,2},{4,5},{5,4},{6,7},{7,6},{8,9},{9,8},{10,11... | collective-permute-start | bytes 552968 | tf_op jit(solution)/shard_map/ppermute | solution.py:510
  30.9 4.4 %collective-permute-start.12 = (f32[2,8,128]{2,1,0:T(8,128)S(1)}, f32[2,8,128]{2,1,0:T(8,128)S(1)}, u32[]{:S(2)}, u32[]{:S(2)}) collective-permute-start(f32[2,8,128]{2,1,0:T(8,128)S(1)} %get-tuple-element.62), channel_id=1, source_target_pairs={{8,10},{9,11},{10,8},{11,9},{12,14},{13,15},{14,12},{15,13},{16,18... | collective-permute-start | bytes 24584 | tf_op jit(solution)/shard_map/ppermute | solution.py:521
  34.1 3.4 %collective-permute-start.9 = (f32[2,1,8,1440]{3,2,1,0:T(8,128)S(1)}, f32[2,1,8,1440]{3,2,1,0:T(8,128)S(1)}, u32[]{:S(2)}, u32[]{:S(2)}) collective-permute-start(f32[2,1,8,1440]{3,2,1,0:T(8,128)S(1)} %get-tuple-element.57), channel_id=1, source_target_pairs={{0,1},{1,0},{2,3},{3,2},{4,5},{5,4},{6,7},{7,6},{8,9},{9,8},{10,11... | collective-permute-start | bytes 276488 | tf_op jit(solution)/shard_map/ppermute | solution.py:510
  35.4 2.2 %collective-permute-start.13 = (f32[2,1,8,1440]{3,2,1,0:T(8,128)S(1)}, f32[2,1,8,1440]{3,2,1,0:T(8,128)S(1)}, u32[]{:S(2)}, u32[]{:S(2)}) collective-permute-start(f32[2,1,8,1440]{3,2,1,0:T(8,128)S(1)} %get-tuple-element.63), channel_id=1, source_target_pairs={{0,1},{1,0},{2,3},{3,2},{4,5},{5,4},{6,7},{7,6},{8,9},{9,8},{10,11... | collective-permute-start | bytes 276488 | tf_op jit(solution)/shard_map/ppermute | solution.py:510

commit v14 on v12

--- a/solution.py
+++ b/solution.py
@@ -194,13 +194,8 @@
 
 
 def forward_kernel(
-    mine_ref, theirs_ref, phase_ref, high_ref, low_ref, after_ref, *refs
+    mine_ref, theirs_ref, phase_ref, high_ref, low_ref, after_ref, message_ref, held_ref, stack_ref
 ):
-    *refs, stack_ref = refs
-    relays = len(refs) // 3
-    message_ref, held_ref = refs[relays : relays + 2]
-    for source_ref, relay_ref in zip(refs[:relays], refs[relays + 2 :]):
-        relay_ref[...] = source_ref[...]
     share, number, levels, columns = mine_ref.shape
     piece = columns * PAIR // HALF
     padded = stack_ref.shape[1]
@@ -292,9 +287,10 @@
 
 
 def row_kernel(
-    columns, shift_ref, fraction_ref, cutoff_ref, damping_ref, wave_ref, after_ref,
-    distance_ref, share_ref, keep_ref, gain_ref,
+    columns, shift_ref, fraction_ref, cutoff_ref, damping_ref, wave_ref, after_ref, source_ref,
+    distance_ref, share_ref, keep_ref, gain_ref, relay_ref,
 ):
+    relay_ref[...] = source_ref[...]
     row_count, levels = shift_ref.shape
     lon_cells = columns * PAIR * PAIR
     modes = gain_ref.shape[3]
@@ -511,21 +507,22 @@
         return lax.ppermute(value, "lon", [(p, p ^ 2) for p in range(lon_count)])
 
     def swap_band(value, first):
-        pairs = []
+        pairs = [(b, b) for b in range(first)]
         for b in range(first, lat_count - 1, 2):
             pairs += [(b, b + 1), (b + 1, b)]
+        pairs += [(b, b) for b in range(len(pairs), lat_count)]
         return lax.ppermute(value, "lat", pairs)
 
     def set_shape(number):
         return (share, number, level_count, column_count)
 
-    def forward(mine, theirs, after, *relay):
+    def forward(mine, theirs, after):
         count = mine.shape[0] * mine.shape[1]
         message_shape = (count, level_count, 2 * MODES + LANES)
         return call(
             forward_kernel,
-            [message_shape, (PAIR, count, level_count, width)] + [v.shape for v in relay],
-            whole(mine, theirs, phase, high, low) + [(after, UNREAD)] + whole(*relay),
+            [message_shape, (PAIR, count, level_count, width)],
+            whole(mine, theirs, phase, high, low) + [(after, UNREAD)],
             [(count * group, padded)],
         )
 
@@ -558,17 +555,18 @@
     )
     inner_theirs = swap_core(inner_send)
     near_got = swap_band(near_edge, 0)
-    inner_own, inner_held, far_relay = forward(inner_mine, inner_theirs, near_part, far_edge)
-    far_got = swap_band(far_relay, 1)
+    inner_own, inner_held = forward(inner_mine, inner_theirs, near_part)
     inner_other = swap_half(inner_own)
     row_shape = (row_count, level_count, LANES)
-    distance, fraction, keep, gain = call(
+    distance, fraction, keep, gain, far_relay = call(
         functools.partial(row_kernel, column_count),
-        [row_shape] * 3 + [(row_count, 2 * (HALF + 1), level_count, double // 2)],
+        [row_shape] * 3 + [(row_count, 2 * (HALF + 1), level_count, double // 2), edge_shape],
         [(v, SMALL) for v in (shift_rows, fraction_rows, cutoff, damping)]
         + whole(wave)
-        + [(inner_own, UNREAD)],
-    )
+        + [(inner_own, UNREAD)]
+        + whole(far_edge),
+    )
+    far_got = swap_band(far_relay, 1)
     (inner_moved,) = shifted("inner", inner_held, inner_own)
 
     near_mine, near_send = call(

time: 30.9 us -> 30.1 us (0.974)
  the two profiles are of different devices: /device:TPU:13 before, /device:TPU:3 now
where the time goes in v14:
time: 30.1 us; the launch traced here: 29.7 us
  Pallas kernels  11.3 us (38%)
  starting transfers between devices  9.44 us (31%)
  waiting for transfers between devices  8.1 us (27%)
  local copies, waits for them, and re-layouts  0.7 us (2%)
    pallas_call x15, Pallas kernels, call(): pl.pallas_call(kernel, out_shape=[jax.ShapeDtypeStruct(shape, jnp.float32...  11.3 us
    ppermute x6, starting transfers between devices, swap_core(): return lax.ppermute(value, 'lon', [(p, p ^ 1) for p in range(lon_count)])  5.17 us
    ppermute x3, waiting for transfers between devices, swap_half(): return lax.ppermute(value, 'lon', [(p, p ^ 2) for p in range(lon_count)])  3.58 us
    ppermute x6, waiting for transfers between devices, swap_core(): return lax.ppermute(value, 'lon', [(p, p ^ 1) for p in range(lon_count)])  2.42 us
    ppermute x3, starting transfers between devices, swap_half(): return lax.ppermute(value, 'lon', [(p, p ^ 2) for p in range(lon_count)])  2.34 us
    ppermute x2, waiting for transfers between devices, swap_band(): return lax.ppermute(value, 'lat', pairs)  2.1 us
    ppermute x2, starting transfers between devices, swap_band(): return lax.ppermute(value, 'lat', pairs)  1.92 us
    unnamed x16, local copies, waits for them, and re-layouts  0.7 us
  transfers between devices with their start and end apart: 11, of which 6 were waited for; matrix products, arithmetic and copies ran while one was open for 0% of the time, Pallas kernels for 26%

profile of v14, /device:TPU:3, one launch (start us, length us, event | category | flops | bytes accessed | tf_op | source)
XLA Modules:
  0.0 29.7 jit_solution(11185173984339462884)
XLA Ops:
  0.0 0.0 copy-start
  0.0 0.0 copy-start.1
  0.0 0.0 copy-start.2
  0.0 1.8 %shard_map.100 = (f32[2,2,8,1440]{3,2,1,0:T(8,128)S(1)}, f32[2,2,8,1440]{3,2,1,0:T(8,128)S(1)}, f32[40,1440]{1,0:T(8,128)S(1)}, f32[40,1440]{1,0:T(8,128)S(1)}, ...) custom-call(f32[4,8,4,1440]{3,2,1,0:T(4,128)} %cells_hbm.1, f32[8,4,1440]{2,1,0:T(4,128)} %speed_hbm.1), custom_call_target="tpu_custom_call" | custom-call | flops 1 | bytes 1 | tf_op jit(solution)/shard_map/pallas_call | solution.py:472
  1.9 0.7 %collective-permute-start = (f32[2,2,8,1440]{3,2,1,0:T(8,128)S(1)}, f32[2,2,8,1440]{3,2,1,0:T(8,128)S(1)}, u32[]{:S(2)}, u32[]{:S(2)}) collective-permute-start(f32[2,2,8,1440]{3,2,1,0:T(8,128)S(1)} %get-tuple-element.33), channel_id=1, source_target_pairs={{0,1},{1,0},{2,3},{3,2},{4,5},{5,4},{6,7},{7,6},{8,9},{9,8},{10,11... | collective-permute-start | bytes 552968 | tf_op jit(solution)/shard_map/ppermute | solution.py:504
  2.6 0.0 collective-permute-start.2
  2.6 1.1 %collective-permute-done.theirs_ref = f32[2,2,8,1440]{3,2,1,0:T(8,128)S(1)} collective-permute-done((f32[2,2,8,1440]{3,2,1,0:T(8,128)S(1)}, f32[2,2,8,1440]{3,2,1,0:T(8,128)S(1)}, u32[]{:S(2)}, u32[]{:S(2)}) %collective-permute-start) | collective-permute-done | bytes 184352 | tf_op jit(solution)/shard_map/ppermute | solution.py:504
  3.7 0.0 copy-done
  3.7 0.0 copy-done.1
  3.7 0.0 copy-done.2
  3.7 1.5 %shard_map.101 = (f32[4,8,2176]{2,1,0:T(8,128)S(1)}, f32[2,4,8,1536]{3,2,1,0:T(8,128)S(1)}) custom-call(f32[2,2,8,1440]{3,2,1,0:T(8,128)S(1)} %get-tuple-element.32.mine_ref, f32[2,2,8,1440]{3,2,1,0:T(8,128)S(1)} %collective-permute-done.theirs_ref, f32[18,384]{1,0:T(8,128)S(1)} %copy-done.2, bf16[384,256]{1,0:T(8,128)(2,1)S(1)} %copy-done, ...), custom_call_target="tpu_custom_call" | custom-call | flops 1 | bytes 1 | tf_op jit(solution)/shard_map/pallas_call | solution.py:472
  5.1 1.2 %collective-permute-start.1 = (f32[4,8,2176]{2,1,0:T(8,128)S(1)}, f32[4,8,2176]{2,1,0:T(8,128)S(1)}, u32[]{:S(2)}, u32[]{:S(2)}) collective-permute-start(f32[4,8,2176]{2,1,0:T(8,128)S(1)} %get-tuple-element.35.after_ref.own_ref), channel_id=1, source_target_pairs={{0,2},{1,3},{2,0},{3,1},{4,6},{5,7},{6,4},{7,5},{8,10},{9,11},{10,... | collective-permute-start | bytes 835592 | tf_op jit(solution)/shard_map/ppermute | solution.py:507
  6.4 0.0 copy-done.3
  6.4 0.7 %copy-done.5 = f32[8,4]{0,1:T(4,128)S(1)} copy-done((f32[8,4]{0,1:T(4,128)S(1)}, f32[8,4]{0,1:T(4,128)}, u32[]{:S(2)}) %copy-start.5) | copy-done | bytes 152
  7.1 0.0 copy-done.4
  7.1 0.0 copy-done.6
  7.1 0.0 copy-done.7
  7.1 0.9 %shard_map.102 = (f32[4,8,128]{2,1,0:T(8,128)S(1)}, f32[4,8,128]{2,1,0:T(8,128)S(1)}, f32[4,8,128]{2,1,0:T(8,128)S(1)}, f32[4,18,8,128]{3,2,1,0:T(8,128)S(1)}, f32[40,1440]{1,0:T(8,128)S(1)}) custom-call(s32[4,8]{1,0:T(4,128)S(1)} %bitcast.2, f32[4,8]{1,0:T(4,128)S(1)} %bitcast.3, s32[32]{0:T(128)S(1)} %copy-done.6, f32[32]{0:T(128)S(1)} %copy-done.7, ...), custom_call_target="tpu_custom_call" | custom-call | flops 1 | bytes 1 | tf_op jit(solution)/shard_map/pallas_call | solution.py:472
  8.0 1.9 %collective-permute-start.6 = (f32[40,1440]{1,0:T(8,128)S(1)}, f32[40,1440]{1,0:T(8,128)S(1)}, u32[]{:S(2)}, u32[]{:S(2)}) collective-permute-start(f32[40,1440]{1,0:T(8,128)S(1)} %get-tuple-element.48), channel_id=1, source_target_pairs={{0,0},{4,8},{8,4},{12,16},{16,12},{20,24},{24,20},{28,28},{1,1},{5... | collective-permute-start | bytes 691208 | tf_op jit(solution)/shard_map/ppermute | solution.py:514
  9.9 0.7 %shard_map.103.after_ref.moved_ref = f32[4,2,8,1536]{3,2,1,0:T(8,128)S(1)} custom-call(f32[4,8,128]{2,1,0:T(8,128)S(1)} %get-tuple-element.37.distance_ref, f32[4,8,128]{2,1,0:T(8,128)S(1)} %get-tuple-element.38.share_ref, f32[2,4,8,1536]{3,2,1,0:T(8,128)S(1)} %get-tuple-element.41.held_ref, f32[4,8,2176]{2,1,0:T(8,128)S(1)} %get-tuple-element.35.after_ref.own_ref), custom_call_target="tpu_custom_call" | custom-call | flops 1 | bytes 1 | tf_op jit(solution)/shard_map/pallas_call | solution.py:472
  10.6 0.0 collective-permute-done.2.got_ref
  10.6 0.1 shard_map.104
  10.7 0.8 %collective-permute-start.3 = (f32[2,1,8,1440]{3,2,1,0:T(8,128)S(1)}, f32[2,1,8,1440]{3,2,1,0:T(8,128)S(1)}, u32[]{:S(2)}, u32[]{:S(2)}) collective-permute-start(f32[2,1,8,1440]{3,2,1,0:T(8,128)S(1)} %get-tuple-element.44), channel_id=1, source_target_pairs={{0,1},{1,0},{2,3},{3,2},{4,5},{5,4},{6,7},{7,6},{8,9},{9,8},{10,11... | collective-permute-start | bytes 276488 | tf_op jit(solution)/shard_map/ppermute | solution.py:504
  11.5 0.9 %collective-permute-done.3.theirs_ref = f32[2,1,8,1440]{3,2,1,0:T(8,128)S(1)} collective-permute-done((f32[2,1,8,1440]{3,2,1,0:T(8,128)S(1)}, f32[2,1,8,1440]{3,2,1,0:T(8,128)S(1)}, u32[]{:S(2)}, u32[]{:S(2)}) %collective-permute-start.3) | collective-permute-done | bytes 92192 | tf_op jit(solution)/shard_map/ppermute | solution.py:504
  12.5 0.9 %shard_map.105 = (f32[2,8,2176]{2,1,0:T(8,128)S(1)}, f32[2,2,8,1536]{3,2,1,0:T(8,128)S(1)}) custom-call(f32[2,1,8,1440]{3,2,1,0:T(8,128)S(1)} %get-tuple-element.43.mine_ref, f32[2,1,8,1440]{3,2,1,0:T(8,128)S(1)} %collective-permute-done.3.theirs_ref, f32[18,384]{1,0:T(8,128)S(1)} %copy-done.2, bf16[384,256]{1,0:T(8,128)(2,1)S(1)} %copy-done, ...), custom_call_target="tpu_custom_call" | custom-call | flops 1 | bytes 1 | tf_op jit(solution)/shard_map/pallas_call | solution.py:472
  13.4 0.8 %collective-permute-start.5 = (f32[2,8,2176]{2,1,0:T(8,128)S(1)}, f32[2,8,2176]{2,1,0:T(8,128)S(1)}, u32[]{:S(2)}, u32[]{:S(2)}) collective-permute-start(f32[2,8,2176]{2,1,0:T(8,128)S(1)} %get-tuple-element.46.after_ref.own_ref), channel_id=1, source_target_pairs={{0,2},{1,3},{2,0},{3,1},{4,6},{5,7},{6,4},{7,5},{8,10},{9,11},{10,... | collective-permute-start | bytes 417800 | tf_op jit(solution)/shard_map/ppermute | solution.py:507
  14.2 0.3 %shard_map.106.after_ref.moved_ref = f32[2,2,8,1536]{3,2,1,0:T(8,128)S(1)} custom-call(f32[4,8,128]{2,1,0:T(8,128)S(1)} %get-tuple-element.37.distance_ref, f32[4,8,128]{2,1,0:T(8,128)S(1)} %get-tuple-element.38.share_ref, f32[2,2,8,1536]{3,2,1,0:T(8,128)S(1)} %get-tuple-element.45.held_ref, f32[2,8,2176]{2,1,0:T(8,128)S(1)} %get-tuple-element.46.after_ref.own_ref), custom_call_target="tpu_custom_call" | custom-call | flops 1 | bytes 1 | tf_op jit(solution)/shard_map/pallas_call | solution.py:472
  14.5 0.0 collective-permute-done.1.other_ref
  14.5 1.0 %shard_map.107 = (f32[2,2,8,1440]{3,2,1,0:T(8,128)S(1)}, f32[2,2,8,1440]{3,2,1,0:T(8,128)S(1)}) custom-call(f32[4,8,128]{2,1,0:T(8,128)S(1)} %get-tuple-element.37.distance_ref, f32[4,8,128]{2,1,0:T(8,128)S(1)} %get-tuple-element.38.share_ref, f32[4,8,128]{2,1,0:T(8,128)S(1)} %get-tuple-element.39.keep_ref, ...), custom_call_target="tpu_custom_call" | custom-call | flops 1 | bytes 1 | tf_op jit(solution)/shard_map/pallas_call | solution.py:472
  15.5 2.1 %collective-permute-done.6.got_ref = f32[40,1440]{1,0:T(8,128)S(1)} collective-permute-done((f32[40,1440]{1,0:T(8,128)S(1)}, f32[40,1440]{1,0:T(8,128)S(1)}, u32[]{:S(2)}, u32[]{:S(2)}) %collective-permute-start.6) | collective-permute-done | bytes 230432 | tf_op jit(solution)/shard_map/ppermute | solution.py:514
  17.6 0.1 shard_map.108
  17.7 1.6 %collective-permute-start.8 = (f32[2,1,8,1440]{3,2,1,0:T(8,128)S(1)}, f32[2,1,8,1440]{3,2,1,0:T(8,128)S(1)}, u32[]{:S(2)}, u32[]{:S(2)}) collective-permute-start(f32[2,1,8,1440]{3,2,1,0:T(8,128)S(1)} %get-tuple-element.53), channel_id=1, source_target_pairs={{0,1},{1,0},{2,3},{3,2},{4,5},{5,4},{6,7},{7,6},{8,9},{9,8},{10,11... | collective-permute-start | bytes 276488 | tf_op jit(solution)/shard_map/ppermute | solution.py:504
  19.3 0.0 collective-permute-done.5.other_ref
  19.3 0.6 %shard_map.109 = (f32[2,1,8,1440]{3,2,1,0:T(8,128)S(1)}, f32[2,1,8,1440]{3,2,1,0:T(8,128)S(1)}) custom-call(f32[4,8,128]{2,1,0:T(8,128)S(1)} %get-tuple-element.37.distance_ref, f32[4,8,128]{2,1,0:T(8,128)S(1)} %get-tuple-element.38.share_ref, f32[4,8,128]{2,1,0:T(8,128)S(1)} %get-tuple-element.39.keep_ref, ...), custom_call_target="tpu_custom_call" | custom-call | flops 1 | bytes 1 | tf_op jit(solution)/shard_map/pallas_call | solution.py:472
  20.0 0.3 collective-permute-done.8.theirs_ref
  20.2 0.9 %shard_map.110 = (f32[2,8,2176]{2,1,0:T(8,128)S(1)}, f32[2,2,8,1536]{3,2,1,0:T(8,128)S(1)}) custom-call(f32[2,1,8,1440]{3,2,1,0:T(8,128)S(1)} %get-tuple-element.51.after_ref.mine_ref, f32[2,1,8,1440]{3,2,1,0:T(8,128)S(1)} %collective-permute-done.8.theirs_ref, f32[18,384]{1,0:T(8,128)S(1)} %copy-done.2, bf16[384,256]{1,0:T(8,128)(2,1)S(1)} %copy-done, ...), custom_call_target="tpu_custom_call" | custom-call | flops 1 | bytes 1 | tf_op jit(solution)/shard_map/pallas_call | solution.py:472
  21.1 0.2 collective-permute-start.9
  21.4 0.8 %collective-permute-start.4 = (f32[2,2,8,1440]{3,2,1,0:T(8,128)S(1)}, f32[2,2,8,1440]{3,2,1,0:T(8,128)S(1)}, u32[]{:S(2)}, u32[]{:S(2)}) collective-permute-start(f32[2,2,8,1440]{3,2,1,0:T(8,128)S(1)} %get-tuple-element.47), channel_id=1, source_target_pairs={{0,1},{1,0},{2,3},{3,2},{4,5},{5,4},{6,7},{7,6},{8,9},{9,8},{10,11... | collective-permute-start | bytes 552968 | tf_op jit(solution)/shard_map/ppermute | solution.py:504
  22.2 0.0 collective-permute-start.7
  22.2 0.3 %shard_map.111.moved_ref.after_ref = f32[2,2,8,1536]{3,2,1,0:T(8,128)S(1)} custom-call(f32[4,8,128]{2,1,0:T(8,128)S(1)} %get-tuple-element.37.distance_ref, f32[4,8,128]{2,1,0:T(8,128)S(1)} %get-tuple-element.38.share_ref, f32[2,2,8,1536]{3,2,1,0:T(8,128)S(1)} %get-tuple-element.55.held_ref, f32[2,8,2176]{2,1,0:T(8,128)S(1)} %get-tuple-element.56.after_ref.own_ref), custom_call_target="tpu_custom_call" | custom-call | flops 1 | bytes 1 | tf_op jit(solution)/shard_map/pallas_call | solution.py:472
  22.5 3.6 %collective-permute-done.9.other_ref = f32[2,8,2176]{2,1,0:T(8,128)S(1)} collective-permute-done((f32[2,8,2176]{2,1,0:T(8,128)S(1)}, f32[2,8,2176]{2,1,0:T(8,128)S(1)}, u32[]{:S(2)}, u32[]{:S(2)}) %collective-permute-start.9) | collective-permute-done | bytes 139296 | tf_op jit(solution)/shard_map/ppermute | solution.py:507
  26.1 0.6 %shard_map.112 = (f32[2,1,8,1440]{3,2,1,0:T(8,128)S(1)}, f32[2,1,8,1440]{3,2,1,0:T(8,128)S(1)}) custom-call(f32[4,8,128]{2,1,0:T(8,128)S(1)} %get-tuple-element.37.distance_ref, f32[4,8,128]{2,1,0:T(8,128)S(1)} %get-tuple-element.38.share_ref, f32[4,8,128]{2,1,0:T(8,128)S(1)} %get-tuple-element.39.keep_ref, ...), custom_call_target="tpu_custom_call" | custom-call | flops 1 | bytes 1 | tf_op jit(solution)/shard_map/pallas_call | solution.py:472
  26.7 1.3 %collective-permute-start.10 = (f32[2,1,8,1440]{3,2,1,0:T(8,128)S(1)}, f32[2,1,8,1440]{3,2,1,0:T(8,128)S(1)}, u32[]{:S(2)}, u32[]{:S(2)}) collective-permute-start(f32[2,1,8,1440]{3,2,1,0:T(8,128)S(1)} %get-tuple-element.57), channel_id=1, source_target_pairs={{0,1},{1,0},{2,3},{3,2},{4,5},{5,4},{6,7},{7,6},{8,9},{9,8},{10,11... | collective-permute-start | bytes 276488 | tf_op jit(solution)/shard_map/ppermute | solution.py:504
  28.0 0.8 %shard_map.113.refs_0_ = f32[4,8,4,1440]{3,2,1,0:T(4,128)} custom-call(f32[2,2,8,1440]{3,2,1,0:T(8,128)S(1)} %get-tuple-element.50.after_ref.inner, f32[2,1,8,1440]{3,2,1,0:T(8,128)S(1)} %get-tuple-element.54.after_ref.near, f32[2,1,8,1440]{3,2,1,0:T(8,128)S(1)} %get-tuple-element.58.far), custom_call_target="tpu_custom_call" | custom-call | flops 1 | bytes 1 | tf_op jit(solution)/shard_map/pallas_call | solution.py:472
  28.8 0.0 collective-permute-done.7.near
  28.8 0.0 collective-permute-done.4.inner
  28.8 0.1 collective-permute-done.10.far
  28.9 0.8 %shard_map.114 = f32[4,8,4,1440]{3,2,1,0:T(4,128)} custom-call(f32[2,2,8,1440]{3,2,1,0:T(8,128)S(1)} %collective-permute-done.4.inner, f32[2,1,8,1440]{3,2,1,0:T(8,128)S(1)} %collective-permute-done.7.near, f32[2,1,8,1440]{3,2,1,0:T(8,128)S(1)} %collective-permute-done.10.far, f32[4,8,4,1440]{3,2,1,0:T(4,128)} %shard_map.113.refs_0_), custom_call_target="tpu_custom_call", output_to_operand_aliasing={{}: (3, {})} | custom-call | flops 1 | bytes 1 | tf_op jit(solution)/shard_map/pallas_call | solution.py:472
  (5 shorter events, 0.0 us)
Async XLA Ops:
  0.0 3.7 %copy-start = (bf16[384,256]{1,0:T(8,128)(2,1)S(1)}, bf16[384,256]{1,0:T(8,128)(2,1)}, u32[]{:S(2)}) copy-start(bf16[384,256]{1,0:T(8,128)(2,1)} %constant.10.clone.high_ref) | copy-start | bytes 589828
  0.0 3.7 %copy-start.1 = (bf16[384,256]{1,0:T(8,128)(2,1)S(1)}, bf16[384,256]{1,0:T(8,128)(2,1)}, u32[]{:S(2)}) copy-start(bf16[384,256]{1,0:T(8,128)(2,1)} %constant.11.clone.low_ref) | copy-start | bytes 589828
  0.0 3.7 %copy-start.2 = (f32[18,384]{1,0:T(8,128)S(1)}, f32[18,384]{1,0:T(8,128)}, u32[]{:S(2)}) copy-start(f32[18,384]{1,0:T(8,128)} %constant.8.clone.phase_ref) | copy-start | bytes 82948
  1.9 1.8 %collective-permute-start = (f32[2,2,8,1440]{3,2,1,0:T(8,128)S(1)}, f32[2,2,8,1440]{3,2,1,0:T(8,128)S(1)}, u32[]{:S(2)}, u32[]{:S(2)}) collective-permute-start(f32[2,2,8,1440]{3,2,1,0:T(8,128)S(1)} %get-tuple-element.33), channel_id=1, source_target_pairs={{0,1},{1,0},{2,3},{3,2},{4,5},{5,4},{6,7},{7,6},{8,9},{9,8},{10,11... | collective-permute-start | bytes 552968 | tf_op jit(solution)/shard_map/ppermute | solution.py:504
  2.6 8.0 %collective-permute-start.2 = (f32[40,1440]{1,0:T(8,128)S(1)}, f32[40,1440]{1,0:T(8,128)S(1)}, u32[]{:S(2)}, u32[]{:S(2)}) collective-permute-start(f32[40,1440]{1,0:T(8,128)S(1)} %get-tuple-element.42.own_ref), channel_id=1, source_target_pairs={{0,4},{4,0},{8,12},{12,8},{16,20},{20,16},{24,28},{28,24},{1,5},{5... | collective-permute-start | bytes 691208 | tf_op jit(solution)/shard_map/ppermute | solution.py:514
  3.7 2.7 %copy-start.3 = (f32[18,128]{1,0:T(8,128)S(1)}, f32[18,128]{1,0:T(8,128)}, u32[]{:S(2)}) copy-start(f32[18,128]{1,0:T(8,128)} %constant.9.clone.wave_ref) | copy-start | bytes 27652
  5.1 9.4 %collective-permute-start.1 = (f32[4,8,2176]{2,1,0:T(8,128)S(1)}, f32[4,8,2176]{2,1,0:T(8,128)S(1)}, u32[]{:S(2)}, u32[]{:S(2)}) collective-permute-start(f32[4,8,2176]{2,1,0:T(8,128)S(1)} %get-tuple-element.35.after_ref.own_ref), channel_id=1, source_target_pairs={{0,2},{1,3},{2,0},{3,1},{4,6},{5,7},{6,4},{7,5},{8,10},{9,11},{10,... | collective-permute-start | bytes 835592 | tf_op jit(solution)/shard_map/ppermute | solution.py:507
  6.4 0.7 %copy-start.5 = (f32[8,4]{0,1:T(4,128)S(1)}, f32[8,4]{0,1:T(4,128)}, u32[]{:S(2)}) copy-start(f32[8,4]{0,1:T(4,128)} %param.13) | copy-start | bytes 388
  6.4 0.7 %copy-start.4 = (s32[8,4]{0,1:T(4,128)S(1)}, s32[8,4]{0,1:T(4,128)}, u32[]{:S(2)}) copy-start(s32[8,4]{0,1:T(4,128)} %param.12) | copy-start | bytes 388
  6.4 0.7 %copy-start.6 = (s32[32]{0:T(128)S(1)}, s32[32]{0:T(128)}, u32[]{:S(2)}) copy-start(s32[32]{0:T(128)} %cutoff_ref.1) | copy-start | bytes 388
  6.4 0.7 %copy-start.7 = (f32[32]{0:T(128)S(1)}, f32[32]{0:T(128)}, u32[]{:S(2)}) copy-start(f32[32]{0:T(128)} %damping_ref.1) | copy-start | bytes 388
  8.0 9.6 %collective-permute-start.6 = (f32[40,1440]{1,0:T(8,128)S(1)}, f32[40,1440]{1,0:T(8,128)S(1)}, u32[]{:S(2)}, u32[]{:S(2)}) collective-permute-start(f32[40,1440]{1,0:T(8,128)S(1)} %get-tuple-element.48), channel_id=1, source_target_pairs={{0,0},{4,8},{8,4},{12,16},{16,12},{20,24},{24,20},{28,28},{1,1},{5... | collective-permute-start | bytes 691208 | tf_op jit(solution)/shard_map/ppermute | solution.py:514
  10.7 1.8 %collective-permute-start.3 = (f32[2,1,8,1440]{3,2,1,0:T(8,128)S(1)}, f32[2,1,8,1440]{3,2,1,0:T(8,128)S(1)}, u32[]{:S(2)}, u32[]{:S(2)}) collective-permute-start(f32[2,1,8,1440]{3,2,1,0:T(8,128)S(1)} %get-tuple-element.44), channel_id=1, source_target_pairs={{0,1},{1,0},{2,3},{3,2},{4,5},{5,4},{6,7},{7,6},{8,9},{9,8},{10,11... | collective-permute-start | bytes 276488 | tf_op jit(solution)/shard_map/ppermute | solution.py:504
  13.4 5.9 %collective-permute-start.5 = (f32[2,8,2176]{2,1,0:T(8,128)S(1)}, f32[2,8,2176]{2,1,0:T(8,128)S(1)}, u32[]{:S(2)}, u32[]{:S(2)}) collective-permute-start(f32[2,8,2176]{2,1,0:T(8,128)S(1)} %get-tuple-element.46.after_ref.own_ref), channel_id=1, source_target_pairs={{0,2},{1,3},{2,0},{3,1},{4,6},{5,7},{6,4},{7,5},{8,10},{9,11},{10,... | collective-permute-start | bytes 417800 | tf_op jit(solution)/shard_map/ppermute | solution.py:507
  17.7 2.5 %collective-permute-start.8 = (f32[2,1,8,1440]{3,2,1,0:T(8,128)S(1)}, f32[2,1,8,1440]{3,2,1,0:T(8,128)S(1)}, u32[]{:S(2)}, u32[]{:S(2)}) collective-permute-start(f32[2,1,8,1440]{3,2,1,0:T(8,128)S(1)} %get-tuple-element.53), channel_id=1, source_target_pairs={{0,1},{1,0},{2,3},{3,2},{4,5},{5,4},{6,7},{7,6},{8,9},{9,8},{10,11... | collective-permute-start | bytes 276488 | tf_op jit(solution)/shard_map/ppermute | solution.py:504
  21.1 4.9 %collective-permute-start.9 = (f32[2,8,2176]{2,1,0:T(8,128)S(1)}, f32[2,8,2176]{2,1,0:T(8,128)S(1)}, u32[]{:S(2)}, u32[]{:S(2)}) collective-permute-start(f32[2,8,2176]{2,1,0:T(8,128)S(1)} %get-tuple-element.56.after_ref.own_ref), channel_id=1, source_target_pairs={{0,2},{1,3},{2,0},{3,1},{4,6},{5,7},{6,4},{7,5},{8,10},{9,11},{10,... | collective-permute-start | bytes 417800 | tf_op jit(solution)/shard_map/ppermute | solution.py:507
  21.4 7.4 %collective-permute-start.4 = (f32[2,2,8,1440]{3,2,1,0:T(8,128)S(1)}, f32[2,2,8,1440]{3,2,1,0:T(8,128)S(1)}, u32[]{:S(2)}, u32[]{:S(2)}) collective-permute-start(f32[2,2,8,1440]{3,2,1,0:T(8,128)S(1)} %get-tuple-element.47), channel_id=1, source_target_pairs={{0,1},{1,0},{2,3},{3,2},{4,5},{5,4},{6,7},{7,6},{8,9},{9,8},{10,11... | collective-permute-start | bytes 552968 | tf_op jit(solution)/shard_map/ppermute | solution.py:504
  22.2 6.6 %collective-permute-start.7 = (f32[2,1,8,1440]{3,2,1,0:T(8,128)S(1)}, f32[2,1,8,1440]{3,2,1,0:T(8,128)S(1)}, u32[]{:S(2)}, u32[]{:S(2)}) collective-permute-start(f32[2,1,8,1440]{3,2,1,0:T(8,128)S(1)} %get-tuple-element.52), channel_id=1, source_target_pairs={{0,1},{1,0},{2,3},{3,2},{4,5},{5,4},{6,7},{7,6},{8,9},{9,8},{10,11... | collective-permute-start | bytes 276488 | tf_op jit(solution)/shard_map/ppermute | solution.py:504
  26.7 2.2 %collective-permute-start.10 = (f32[2,1,8,1440]{3,2,1,0:T(8,128)S(1)}, f32[2,1,8,1440]{3,2,1,0:T(8,128)S(1)}, u32[]{:S(2)}, u32[]{:S(2)}) collective-permute-start(f32[2,1,8,1440]{3,2,1,0:T(8,128)S(1)} %get-tuple-element.57), channel_id=1, source_target_pairs={{0,1},{1,0},{2,3},{3,2},{4,5},{5,4},{6,7},{7,6},{8,9},{9,8},{10,11... | collective-permute-start | bytes 276488 | tf_op jit(solution)/shard_map/ppermute | solution.py:504

commit v15 on v14

--- a/solution.py
+++ b/solution.py
@@ -173,7 +173,7 @@
             far_part_ref[t, :, lanes] = jnp.where(north, south_part, north_part)
 
 
-def edge_kernel(is_near, own_ref, got_ref, part_ref, after_ref, mine_ref, send_ref):
+def edge_kernel(is_near, own_ref, got_ref, part_ref, after_ref, gain_ref, mine_ref, send_ref):
     tracer_count, levels, columns = part_ref.shape
     share = tracer_count // PAIR
     total = tracer_count * levels
@@ -287,18 +287,25 @@
 
 
 def row_kernel(
-    columns, shift_ref, fraction_ref, cutoff_ref, damping_ref, wave_ref, after_ref, source_ref,
-    distance_ref, share_ref, keep_ref, gain_ref, relay_ref,
+    shift_ref, fraction_ref, cutoff_ref, damping_ref, after_ref, source_ref,
+    distance_ref, share_ref, keep_ref, limit_ref, relay_ref,
 ):
     relay_ref[...] = source_ref[...]
     row_count, levels = shift_ref.shape
-    lon_cells = columns * PAIR * PAIR
-    modes = gain_ref.shape[3]
     lat = lax.axis_index("lat")
     for row in range(row_count):
         distance_ref[row] = row_vector(shift_ref, row, levels).astype(jnp.float32)
         share_ref[row] = row_vector(fraction_ref, row, levels)
         keep_ref[row] = jnp.full((levels, LANES), damping_ref[lat * row_count + row])
+        limit = jnp.full((levels, LANES), cutoff_ref[lat * row_count + row])
+        limit_ref[row] = limit.astype(jnp.float32)
+
+
+def gain_kernel(columns, distance_ref, share_ref, limit_ref, wave_ref, gain_ref):
+    row_count, levels = distance_ref.shape[:2]
+    lon_cells = columns * PAIR * PAIR
+    modes = gain_ref.shape[3]
+    lat = lax.axis_index("lat")
 
     @pl.when(is_cap(lat))
     def _():
@@ -307,7 +314,7 @@
         for row in range(row_count):
             distance = distance_ref[row].astype(jnp.int32)
             share = share_ref[row]
-            limit = cutoff_ref[lat * row_count + row]
+            limit = limit_ref[row].astype(jnp.int32)
             wide = wave_angle(RADIX * mode * distance, lon_cells)
             wide_re, wide_im = jnp.cos(wide), -jnp.sin(wide)
             fine = wave_angle(lane * distance, lon_cells)
@@ -558,13 +565,17 @@
     inner_own, inner_held = forward(inner_mine, inner_theirs, near_part)
     inner_other = swap_half(inner_own)
     row_shape = (row_count, level_count, LANES)
-    distance, fraction, keep, gain, far_relay = call(
-        functools.partial(row_kernel, column_count),
-        [row_shape] * 3 + [(row_count, 2 * (HALF + 1), level_count, double // 2), edge_shape],
+    distance, fraction, keep, limit, far_relay = call(
+        row_kernel,
+        [row_shape] * 4 + [edge_shape],
         [(v, SMALL) for v in (shift_rows, fraction_rows, cutoff, damping)]
-        + whole(wave)
         + [(inner_own, UNREAD)]
         + whole(far_edge),
+    )
+    (gain,) = call(
+        functools.partial(gain_kernel, column_count),
+        [(row_count, 2 * (HALF + 1), level_count, double // 2)],
+        whole(distance, fraction, limit, wave),
     )
     far_got = swap_band(far_relay, 1)
     (inner_moved,) = shifted("inner", inner_held, inner_own)
@@ -572,7 +583,7 @@
     near_mine, near_send = call(
         functools.partial(edge_kernel, True),
         [set_shape(1)] * 2,
-        whole(near_edge, near_got, near_part) + [(inner_moved, UNREAD)],
+        whole(near_edge, near_got, near_part) + [(inner_moved, UNREAD), (gain, UNREAD)],
     )
     near_theirs = swap_core(near_send)
     near_own, near_held = forward(near_mine, near_theirs, inner_moved)
@@ -584,7 +595,7 @@
     far_mine, far_send = call(
         functools.partial(edge_kernel, False),
         [set_shape(1)] * 2,
-        whole(far_edge, far_got, far_part) + [(inner[0], UNREAD)],
+        whole(far_edge, far_got, far_part) + [(inner[0], UNREAD), (gain, UNREAD)],
     )
     far_theirs = swap_core(far_send)
     near = inverse("near", near_held, near_moved, near_own, near_other, far_mine)

time: 30.1 us -> 29.9 us (level)
  waiting for transfers between devices: 8.1 us -> 7.51 us
  starting transfers between devices: 9.44 us -> 9.76 us
    ppermute x6, starting transfers between devices: 5.17 us -> 5.68 us  [swap_core(): return lax.ppermute(value, 'lon', [(p, p ^ 1) for p in range(lon_count)])]
    ppermute x3, waiting for transfers between devices: 3.58 us -> 3.24 us  [swap_half(): return lax.ppermute(value, 'lon', [(p, p ^ 2) for p in range(lon_count)])]
    pallas_call x15 -> x16, Pallas kernels: 11.3 us -> 11.3 us  [call(): pl.pallas_call(kernel, out_shape=[jax.ShapeDtypeStruct(shape, jnp.float32...]
where the time goes in v15:
time: 29.9 us; the launch traced here: 29.4 us
  Pallas kernels  11.3 us (38%)
  starting transfers between devices  9.76 us (33%)
  waiting for transfers between devices  7.51 us (25%)
  local copies, waits for them, and re-layouts  0.72 us (2%)
    pallas_call x16, Pallas kernels, call(): pl.pallas_call(kernel, out_shape=[jax.ShapeDtypeStruct(shape, jnp.float32...  11.3 us
    ppermute x6, starting transfers between devices, swap_core(): return lax.ppermute(value, 'lon', [(p, p ^ 1) for p in range(lon_count)])  5.68 us
    ppermute x3, waiting for transfers between devices, swap_half(): return lax.ppermute(value, 'lon', [(p, p ^ 2) for p in range(lon_count)])  3.24 us
    ppermute x6, waiting for transfers between devices, swap_core(): return lax.ppermute(value, 'lon', [(p, p ^ 1) for p in range(lon_count)])  2.42 us
    ppermute x3, starting transfers between devices, swap_half(): return lax.ppermute(value, 'lon', [(p, p ^ 2) for p in range(lon_count)])  2.06 us
    ppermute x2, starting transfers between devices, swap_band(): return lax.ppermute(value, 'lat', pairs)  2.02 us
    ppermute x2, waiting for transfers between devices, swap_band(): return lax.ppermute(value, 'lat', pairs)  1.84 us
    unnamed x16, local copies, waits for them, and re-layouts  0.72 us
  transfers between devices with their start and end apart: 11, of which 6 were waited for; matrix products, arithmetic and copies ran while one was open for 0% of the time, Pallas kernels for 26%

profile of v15, /device:TPU:3, one launch (start us, length us, event | category | flops | bytes accessed | tf_op | source)
XLA Modules:
  0.0 29.4 jit_solution(7392393395890414476)
XLA Ops:
  0.0 0.0 copy-start
  0.0 1.8 %shard_map.100 = (f32[2,2,8,1440]{3,2,1,0:T(8,128)S(1)}, f32[2,2,8,1440]{3,2,1,0:T(8,128)S(1)}, f32[40,1440]{1,0:T(8,128)S(1)}, f32[40,1440]{1,0:T(8,128)S(1)}, ...) custom-call(f32[4,8,4,1440]{3,2,1,0:T(4,128)} %cells_hbm.1, f32[8,4,1440]{2,1,0:T(4,128)} %speed_hbm.1), custom_call_target="tpu_custom_call" | custom-call | flops 1 | bytes 1 | tf_op jit(solution)/shard_map/pallas_call | solution.py:479
  1.9 0.7 %collective-permute-start = (f32[2,2,8,1440]{3,2,1,0:T(8,128)S(1)}, f32[2,2,8,1440]{3,2,1,0:T(8,128)S(1)}, u32[]{:S(2)}, u32[]{:S(2)}) collective-permute-start(f32[2,2,8,1440]{3,2,1,0:T(8,128)S(1)} %get-tuple-element.33), channel_id=1, source_target_pairs={{0,1},{1,0},{2,3},{3,2},{4,5},{5,4},{6,7},{7,6},{8,9},{9,8},{10,11... | collective-permute-start | bytes 552968 | tf_op jit(solution)/shard_map/ppermute | solution.py:511
  2.6 0.0 collective-permute-start.2
  2.6 1.1 %collective-permute-done.theirs_ref = f32[2,2,8,1440]{3,2,1,0:T(8,128)S(1)} collective-permute-done((f32[2,2,8,1440]{3,2,1,0:T(8,128)S(1)}, f32[2,2,8,1440]{3,2,1,0:T(8,128)S(1)}, u32[]{:S(2)}, u32[]{:S(2)}) %collective-permute-start) | collective-permute-done | bytes 184352 | tf_op jit(solution)/shard_map/ppermute | solution.py:511
  3.7 0.0 copy-done
  3.7 0.0 copy-done.1
  3.7 0.0 copy-done.2
  3.7 1.4 %shard_map.101 = (f32[4,8,2176]{2,1,0:T(8,128)S(1)}, f32[2,4,8,1536]{3,2,1,0:T(8,128)S(1)}) custom-call(f32[2,2,8,1440]{3,2,1,0:T(8,128)S(1)} %get-tuple-element.32.mine_ref, f32[2,2,8,1440]{3,2,1,0:T(8,128)S(1)} %collective-permute-done.theirs_ref, f32[18,384]{1,0:T(8,128)S(1)} %copy-done.2, bf16[384,256]{1,0:T(8,128)(2,1)S(1)} %copy-done, ...), custom_call_target="tpu_custom_call" | custom-call | flops 1 | bytes 1 | tf_op jit(solution)/shard_map/pallas_call | solution.py:479
  5.1 1.3 %collective-permute-start.1 = (f32[4,8,2176]{2,1,0:T(8,128)S(1)}, f32[4,8,2176]{2,1,0:T(8,128)S(1)}, u32[]{:S(2)}, u32[]{:S(2)}) collective-permute-start(f32[4,8,2176]{2,1,0:T(8,128)S(1)} %get-tuple-element.35.after_ref.own_ref), channel_id=1, source_target_pairs={{0,2},{1,3},{2,0},{3,1},{4,6},{5,7},{6,4},{7,5},{8,10},{9,11},{10,... | collective-permute-start | bytes 835592 | tf_op jit(solution)/shard_map/ppermute | solution.py:514
  6.4 0.7 %copy-done.5 = f32[8,4]{0,1:T(4,128)S(1)} copy-done((f32[8,4]{0,1:T(4,128)S(1)}, f32[8,4]{0,1:T(4,128)}, u32[]{:S(2)}) %copy-start.5) | copy-done | bytes 152
  7.1 0.0 copy-done.4
  7.1 0.0 copy-done.6
  7.1 0.0 copy-done.7
  7.1 0.6 %shard_map.102 = (f32[4,8,128]{2,1,0:T(8,128)S(1)}, f32[4,8,128]{2,1,0:T(8,128)S(1)}, f32[4,8,128]{2,1,0:T(8,128)S(1)}, f32[4,8,128]{2,1,0:T(8,128)S(1)}, f32[40,1440]{1,0:T(8,128)S(1)}) custom-call(s32[4,8]{1,0:T(4,128)S(1)} %bitcast.2, f32[4,8]{1,0:T(4,128)S(1)} %bitcast.3, s32[32]{0:T(128)S(1)} %copy-done.6, f32[32]{0:T(128)S(1)} %copy-done.7, ...), custom_call_target="tpu_custom_call" | custom-call | flops 1 | bytes 1 | tf_op jit(solution)/shard_map/pallas_call | solution.py:479
  7.7 2.0 %collective-permute-start.6 = (f32[40,1440]{1,0:T(8,128)S(1)}, f32[40,1440]{1,0:T(8,128)S(1)}, u32[]{:S(2)}, u32[]{:S(2)}) collective-permute-start(f32[40,1440]{1,0:T(8,128)S(1)} %get-tuple-element.48), channel_id=1, source_target_pairs={{0,0},{4,8},{8,4},{12,16},{16,12},{20,24},{24,20},{28,28},{1,1},{5... | collective-permute-start | bytes 691208 | tf_op jit(solution)/shard_map/ppermute | solution.py:521
  9.8 0.0 copy-start.3
  9.8 0.7 %shard_map.104.after_ref.moved_ref = f32[4,2,8,1536]{3,2,1,0:T(8,128)S(1)} custom-call(f32[4,8,128]{2,1,0:T(8,128)S(1)} %get-tuple-element.37.distance_ref, f32[4,8,128]{2,1,0:T(8,128)S(1)} %get-tuple-element.38.share_ref, f32[2,4,8,1536]{3,2,1,0:T(8,128)S(1)} %get-tuple-element.41.held_ref, f32[4,8,2176]{2,1,0:T(8,128)S(1)} %get-tuple-element.35.after_ref.own_ref), custom_call_target="tpu_custom_call" | custom-call | flops 1 | bytes 1 | tf_op jit(solution)/shard_map/pallas_call | solution.py:479
  10.5 0.0 copy-done.3
  10.5 0.3 shard_map.103.gain_ref
  10.7 0.0 collective-permute-done.2.got_ref
  10.7 0.1 shard_map.105
  10.8 1.0 %collective-permute-start.3 = (f32[2,1,8,1440]{3,2,1,0:T(8,128)S(1)}, f32[2,1,8,1440]{3,2,1,0:T(8,128)S(1)}, u32[]{:S(2)}, u32[]{:S(2)}) collective-permute-start(f32[2,1,8,1440]{3,2,1,0:T(8,128)S(1)} %get-tuple-element.44), channel_id=1, source_target_pairs={{0,1},{1,0},{2,3},{3,2},{4,5},{5,4},{6,7},{7,6},{8,9},{9,8},{10,11... | collective-permute-start | bytes 276488 | tf_op jit(solution)/shard_map/ppermute | solution.py:511
  11.8 0.9 %collective-permute-done.3.theirs_ref = f32[2,1,8,1440]{3,2,1,0:T(8,128)S(1)} collective-permute-done((f32[2,1,8,1440]{3,2,1,0:T(8,128)S(1)}, f32[2,1,8,1440]{3,2,1,0:T(8,128)S(1)}, u32[]{:S(2)}, u32[]{:S(2)}) %collective-permute-start.3) | collective-permute-done | bytes 92192 | tf_op jit(solution)/shard_map/ppermute | solution.py:511
  12.7 0.9 %shard_map.106 = (f32[2,8,2176]{2,1,0:T(8,128)S(1)}, f32[2,2,8,1536]{3,2,1,0:T(8,128)S(1)}) custom-call(f32[2,1,8,1440]{3,2,1,0:T(8,128)S(1)} %get-tuple-element.43.mine_ref, f32[2,1,8,1440]{3,2,1,0:T(8,128)S(1)} %collective-permute-done.3.theirs_ref, f32[18,384]{1,0:T(8,128)S(1)} %copy-done.2, bf16[384,256]{1,0:T(8,128)(2,1)S(1)} %copy-done, ...), custom_call_target="tpu_custom_call" | custom-call | flops 1 | bytes 1 | tf_op jit(solution)/shard_map/pallas_call | solution.py:479
  13.6 0.6 %collective-permute-start.5 = (f32[2,8,2176]{2,1,0:T(8,128)S(1)}, f32[2,8,2176]{2,1,0:T(8,128)S(1)}, u32[]{:S(2)}, u32[]{:S(2)}) collective-permute-start(f32[2,8,2176]{2,1,0:T(8,128)S(1)} %get-tuple-element.46.after_ref.own_ref), channel_id=1, source_target_pairs={{0,2},{1,3},{2,0},{3,1},{4,6},{5,7},{6,4},{7,5},{8,10},{9,11},{10,... | collective-permute-start | bytes 417800 | tf_op jit(solution)/shard_map/ppermute | solution.py:514
  14.2 0.3 %shard_map.107.after_ref.moved_ref = f32[2,2,8,1536]{3,2,1,0:T(8,128)S(1)} custom-call(f32[4,8,128]{2,1,0:T(8,128)S(1)} %get-tuple-element.37.distance_ref, f32[4,8,128]{2,1,0:T(8,128)S(1)} %get-tuple-element.38.share_ref, f32[2,2,8,1536]{3,2,1,0:T(8,128)S(1)} %get-tuple-element.45.held_ref, f32[2,8,2176]{2,1,0:T(8,128)S(1)} %get-tuple-element.46.after_ref.own_ref), custom_call_target="tpu_custom_call" | custom-call | flops 1 | bytes 1 | tf_op jit(solution)/shard_map/pallas_call | solution.py:479
  14.5 0.0 collective-permute-done.1.other_ref
  14.5 1.0 %shard_map.108 = (f32[2,2,8,1440]{3,2,1,0:T(8,128)S(1)}, f32[2,2,8,1440]{3,2,1,0:T(8,128)S(1)}) custom-call(f32[4,8,128]{2,1,0:T(8,128)S(1)} %get-tuple-element.37.distance_ref, f32[4,8,128]{2,1,0:T(8,128)S(1)} %get-tuple-element.38.share_ref, f32[4,8,128]{2,1,0:T(8,128)S(1)} %get-tuple-element.39.keep_ref, f32[4,18,8,128]{3,2,1,0:T(8,128)S(1)} %shard_map.103.gain_ref, ...), custom_call_target="tpu_custom_call" | custom-call | flops 1 | bytes 1 | tf_op jit(solution)/shard_map/pallas_call | solution.py:479
  15.5 1.8 %collective-permute-done.6.got_ref = f32[40,1440]{1,0:T(8,128)S(1)} collective-permute-done((f32[40,1440]{1,0:T(8,128)S(1)}, f32[40,1440]{1,0:T(8,128)S(1)}, u32[]{:S(2)}, u32[]{:S(2)}) %collective-permute-start.6) | collective-permute-done | bytes 230432 | tf_op jit(solution)/shard_map/ppermute | solution.py:521
  17.4 0.1 shard_map.109
  17.4 1.6 %collective-permute-start.8 = (f32[2,1,8,1440]{3,2,1,0:T(8,128)S(1)}, f32[2,1,8,1440]{3,2,1,0:T(8,128)S(1)}, u32[]{:S(2)}, u32[]{:S(2)}) collective-permute-start(f32[2,1,8,1440]{3,2,1,0:T(8,128)S(1)} %get-tuple-element.53), channel_id=1, source_target_pairs={{0,1},{1,0},{2,3},{3,2},{4,5},{5,4},{6,7},{7,6},{8,9},{9,8},{10,11... | collective-permute-start | bytes 276488 | tf_op jit(solution)/shard_map/ppermute | solution.py:511
  19.0 0.0 collective-permute-done.5.other_ref
  19.0 0.6 %shard_map.110 = (f32[2,1,8,1440]{3,2,1,0:T(8,128)S(1)}, f32[2,1,8,1440]{3,2,1,0:T(8,128)S(1)}) custom-call(f32[4,8,128]{2,1,0:T(8,128)S(1)} %get-tuple-element.37.distance_ref, f32[4,8,128]{2,1,0:T(8,128)S(1)} %get-tuple-element.38.share_ref, f32[4,8,128]{2,1,0:T(8,128)S(1)} %get-tuple-element.39.keep_ref, f32[4,18,8,128]{3,2,1,0:T(8,128)S(1)} %shard_map.103.gain_ref, ...), custom_call_target="tpu_custom_call" | custom-call | flops 1 | bytes 1 | tf_op jit(solution)/shard_map/pallas_call | solution.py:479
  19.7 0.3 collective-permute-done.8.theirs_ref
  20.0 0.9 %shard_map.111 = (f32[2,8,2176]{2,1,0:T(8,128)S(1)}, f32[2,2,8,1536]{3,2,1,0:T(8,128)S(1)}) custom-call(f32[2,1,8,1440]{3,2,1,0:T(8,128)S(1)} %get-tuple-element.51.after_ref.mine_ref, f32[2,1,8,1440]{3,2,1,0:T(8,128)S(1)} %collective-permute-done.8.theirs_ref, f32[18,384]{1,0:T(8,128)S(1)} %copy-done.2, bf16[384,256]{1,0:T(8,128)(2,1)S(1)} %copy-done, ...), custom_call_target="tpu_custom_call" | custom-call | flops 1 | bytes 1 | tf_op jit(solution)/shard_map/pallas_call | solution.py:479
  20.9 0.2 collective-permute-start.9
  21.1 1.0 %collective-permute-start.4 = (f32[2,2,8,1440]{3,2,1,0:T(8,128)S(1)}, f32[2,2,8,1440]{3,2,1,0:T(8,128)S(1)}, u32[]{:S(2)}, u32[]{:S(2)}) collective-permute-start(f32[2,2,8,1440]{3,2,1,0:T(8,128)S(1)} %get-tuple-element.47), channel_id=1, source_target_pairs={{0,1},{1,0},{2,3},{3,2},{4,5},{5,4},{6,7},{7,6},{8,9},{9,8},{10,11... | collective-permute-start | bytes 552968 | tf_op jit(solution)/shard_map/ppermute | solution.py:511
  22.2 0.0 collective-permute-start.7
  22.2 0.3 %shard_map.112.moved_ref.after_ref = f32[2,2,8,1536]{3,2,1,0:T(8,128)S(1)} custom-call(f32[4,8,128]{2,1,0:T(8,128)S(1)} %get-tuple-element.37.distance_ref, f32[4,8,128]{2,1,0:T(8,128)S(1)} %get-tuple-element.38.share_ref, f32[2,2,8,1536]{3,2,1,0:T(8,128)S(1)} %get-tuple-element.55.held_ref, f32[2,8,2176]{2,1,0:T(8,128)S(1)} %get-tuple-element.56.after_ref.own_ref), custom_call_target="tpu_custom_call" | custom-call | flops 1 | bytes 1 | tf_op jit(solution)/shard_map/pallas_call | solution.py:479
  22.5 3.2 %collective-permute-done.9.other_ref = f32[2,8,2176]{2,1,0:T(8,128)S(1)} collective-permute-done((f32[2,8,2176]{2,1,0:T(8,128)S(1)}, f32[2,8,2176]{2,1,0:T(8,128)S(1)}, u32[]{:S(2)}, u32[]{:S(2)}) %collective-permute-start.9) | collective-permute-done | bytes 139296 | tf_op jit(solution)/shard_map/ppermute | solution.py:514
  25.7 0.6 %shard_map.113 = (f32[2,1,8,1440]{3,2,1,0:T(8,128)S(1)}, f32[2,1,8,1440]{3,2,1,0:T(8,128)S(1)}) custom-call(f32[4,8,128]{2,1,0:T(8,128)S(1)} %get-tuple-element.37.distance_ref, f32[4,8,128]{2,1,0:T(8,128)S(1)} %get-tuple-element.38.share_ref, f32[4,8,128]{2,1,0:T(8,128)S(1)} %get-tuple-element.39.keep_ref, f32[4,18,8,128]{3,2,1,0:T(8,128)S(1)} %shard_map.103.gain_ref, ...), custom_call_target="tpu_custom_call" | custom-call | flops 1 | bytes 1 | tf_op jit(solution)/shard_map/pallas_call | solution.py:479
  26.4 1.3 %collective-permute-start.10 = (f32[2,1,8,1440]{3,2,1,0:T(8,128)S(1)}, f32[2,1,8,1440]{3,2,1,0:T(8,128)S(1)}, u32[]{:S(2)}, u32[]{:S(2)}) collective-permute-start(f32[2,1,8,1440]{3,2,1,0:T(8,128)S(1)} %get-tuple-element.57), channel_id=1, source_target_pairs={{0,1},{1,0},{2,3},{3,2},{4,5},{5,4},{6,7},{7,6},{8,9},{9,8},{10,11... | collective-permute-start | bytes 276488 | tf_op jit(solution)/shard_map/ppermute | solution.py:511
  27.7 0.8 %shard_map.114.refs_0_ = f32[4,8,4,1440]{3,2,1,0:T(4,128)} custom-call(f32[2,2,8,1440]{3,2,1,0:T(8,128)S(1)} %get-tuple-element.50.after_ref.inner, f32[2,1,8,1440]{3,2,1,0:T(8,128)S(1)} %get-tuple-element.54.after_ref.near, f32[2,1,8,1440]{3,2,1,0:T(8,128)S(1)} %get-tuple-element.58.far), custom_call_target="tpu_custom_call" | custom-call | flops 1 | bytes 1 | tf_op jit(solution)/shard_map/pallas_call | solution.py:479
  28.5 0.0 collective-permute-done.7.near
  28.5 0.0 collective-permute-done.4.inner
  28.5 0.1 collective-permute-done.10.far
  28.6 0.8 %shard_map.115 = f32[4,8,4,1440]{3,2,1,0:T(4,128)} custom-call(f32[2,2,8,1440]{3,2,1,0:T(8,128)S(1)} %collective-permute-done.4.inner, f32[2,1,8,1440]{3,2,1,0:T(8,128)S(1)} %collective-permute-done.7.near, f32[2,1,8,1440]{3,2,1,0:T(8,128)S(1)} %collective-permute-done.10.far, f32[4,8,4,1440]{3,2,1,0:T(4,128)} %shard_map.114.refs_0_), custom_call_target="tpu_custom_call", output_to_operand_aliasing={{}: (3, {})} | custom-call | flops 1 | bytes 1 | tf_op jit(solution)/shard_map/pallas_call | solution.py:479
  (6 shorter events, 0.0 us)
Async XLA Ops:
  0.0 3.7 %copy-start = (bf16[384,256]{1,0:T(8,128)(2,1)S(1)}, bf16[384,256]{1,0:T(8,128)(2,1)}, u32[]{:S(2)}) copy-start(bf16[384,256]{1,0:T(8,128)(2,1)} %constant.10.clone.high_ref) | copy-start | bytes 589828
  0.0 3.7 %copy-start.1 = (bf16[384,256]{1,0:T(8,128)(2,1)S(1)}, bf16[384,256]{1,0:T(8,128)(2,1)}, u32[]{:S(2)}) copy-start(bf16[384,256]{1,0:T(8,128)(2,1)} %constant.11.clone.low_ref) | copy-start | bytes 589828
  0.0 3.7 %copy-start.2 = (f32[18,384]{1,0:T(8,128)S(1)}, f32[18,384]{1,0:T(8,128)}, u32[]{:S(2)}) copy-start(f32[18,384]{1,0:T(8,128)} %constant.8.clone.phase_ref) | copy-start | bytes 82948
  1.9 1.8 %collective-permute-start = (f32[2,2,8,1440]{3,2,1,0:T(8,128)S(1)}, f32[2,2,8,1440]{3,2,1,0:T(8,128)S(1)}, u32[]{:S(2)}, u32[]{:S(2)}) collective-permute-start(f32[2,2,8,1440]{3,2,1,0:T(8,128)S(1)} %get-tuple-element.33), channel_id=1, source_target_pairs={{0,1},{1,0},{2,3},{3,2},{4,5},{5,4},{6,7},{7,6},{8,9},{9,8},{10,11... | collective-permute-start | bytes 552968 | tf_op jit(solution)/shard_map/ppermute | solution.py:511
  2.6 8.1 %collective-permute-start.2 = (f32[40,1440]{1,0:T(8,128)S(1)}, f32[40,1440]{1,0:T(8,128)S(1)}, u32[]{:S(2)}, u32[]{:S(2)}) collective-permute-start(f32[40,1440]{1,0:T(8,128)S(1)} %get-tuple-element.42.own_ref), channel_id=1, source_target_pairs={{0,4},{4,0},{8,12},{12,8},{16,20},{20,16},{24,28},{28,24},{1,5},{5... | collective-permute-start | bytes 691208 | tf_op jit(solution)/shard_map/ppermute | solution.py:521
  5.1 9.4 %collective-permute-start.1 = (f32[4,8,2176]{2,1,0:T(8,128)S(1)}, f32[4,8,2176]{2,1,0:T(8,128)S(1)}, u32[]{:S(2)}, u32[]{:S(2)}) collective-permute-start(f32[4,8,2176]{2,1,0:T(8,128)S(1)} %get-tuple-element.35.after_ref.own_ref), channel_id=1, source_target_pairs={{0,2},{1,3},{2,0},{3,1},{4,6},{5,7},{6,4},{7,5},{8,10},{9,11},{10,... | collective-permute-start | bytes 835592 | tf_op jit(solution)/shard_map/ppermute | solution.py:514
  6.4 0.7 %copy-start.5 = (f32[8,4]{0,1:T(4,128)S(1)}, f32[8,4]{0,1:T(4,128)}, u32[]{:S(2)}) copy-start(f32[8,4]{0,1:T(4,128)} %param.13) | copy-start | bytes 388
  6.4 0.7 %copy-start.4 = (s32[8,4]{0,1:T(4,128)S(1)}, s32[8,4]{0,1:T(4,128)}, u32[]{:S(2)}) copy-start(s32[8,4]{0,1:T(4,128)} %param.12) | copy-start | bytes 388
  6.4 0.7 %copy-start.6 = (s32[32]{0:T(128)S(1)}, s32[32]{0:T(128)}, u32[]{:S(2)}) copy-start(s32[32]{0:T(128)} %cutoff_ref.1) | copy-start | bytes 388
  6.4 0.7 %copy-start.7 = (f32[32]{0:T(128)S(1)}, f32[32]{0:T(128)}, u32[]{:S(2)}) copy-start(f32[32]{0:T(128)} %damping_ref.1) | copy-start | bytes 388
  7.7 9.6 %collective-permute-start.6 = (f32[40,1440]{1,0:T(8,128)S(1)}, f32[40,1440]{1,0:T(8,128)S(1)}, u32[]{:S(2)}, u32[]{:S(2)}) collective-permute-start(f32[40,1440]{1,0:T(8,128)S(1)} %get-tuple-element.48), channel_id=1, source_target_pairs={{0,0},{4,8},{8,4},{12,16},{16,12},{20,24},{24,20},{28,28},{1,1},{5... | collective-permute-start | bytes 691208 | tf_op jit(solution)/shard_map/ppermute | solution.py:521
  9.8 0.7 %copy-start.3 = (f32[18,128]{1,0:T(8,128)S(1)}, f32[18,128]{1,0:T(8,128)}, u32[]{:S(2)}) copy-start(f32[18,128]{1,0:T(8,128)} %constant.9.clone.wave_ref) | copy-start | bytes 27652
  10.8 1.9 %collective-permute-start.3 = (f32[2,1,8,1440]{3,2,1,0:T(8,128)S(1)}, f32[2,1,8,1440]{3,2,1,0:T(8,128)S(1)}, u32[]{:S(2)}, u32[]{:S(2)}) collective-permute-start(f32[2,1,8,1440]{3,2,1,0:T(8,128)S(1)} %get-tuple-element.44), channel_id=1, source_target_pairs={{0,1},{1,0},{2,3},{3,2},{4,5},{5,4},{6,7},{7,6},{8,9},{9,8},{10,11... | collective-permute-start | bytes 276488 | tf_op jit(solution)/shard_map/ppermute | solution.py:511
  13.6 5.4 %collective-permute-start.5 = (f32[2,8,2176]{2,1,0:T(8,128)S(1)}, f32[2,8,2176]{2,1,0:T(8,128)S(1)}, u32[]{:S(2)}, u32[]{:S(2)}) collective-permute-start(f32[2,8,2176]{2,1,0:T(8,128)S(1)} %get-tuple-element.46.after_ref.own_ref), channel_id=1, source_target_pairs={{0,2},{1,3},{2,0},{3,1},{4,6},{5,7},{6,4},{7,5},{8,10},{9,11},{10,... | collective-permute-start | bytes 417800 | tf_op jit(solution)/shard_map/ppermute | solution.py:514
  17.4 2.5 %collective-permute-start.8 = (f32[2,1,8,1440]{3,2,1,0:T(8,128)S(1)}, f32[2,1,8,1440]{3,2,1,0:T(8,128)S(1)}, u32[]{:S(2)}, u32[]{:S(2)}) collective-permute-start(f32[2,1,8,1440]{3,2,1,0:T(8,128)S(1)} %get-tuple-element.53), channel_id=1, source_target_pairs={{0,1},{1,0},{2,3},{3,2},{4,5},{5,4},{6,7},{7,6},{8,9},{9,8},{10,11... | collective-permute-start | bytes 276488 | tf_op jit(solution)/shard_map/ppermute | solution.py:511
  20.9 4.8 %collective-permute-start.9 = (f32[2,8,2176]{2,1,0:T(8,128)S(1)}, f32[2,8,2176]{2,1,0:T(8,128)S(1)}, u32[]{:S(2)}, u32[]{:S(2)}) collective-permute-start(f32[2,8,2176]{2,1,0:T(8,128)S(1)} %get-tuple-element.56.after_ref.own_ref), channel_id=1, source_target_pairs={{0,2},{1,3},{2,0},{3,1},{4,6},{5,7},{6,4},{7,5},{8,10},{9,11},{10,... | collective-permute-start | bytes 417800 | tf_op jit(solution)/shard_map/ppermute | solution.py:514
  21.1 7.4 %collective-permute-start.4 = (f32[2,2,8,1440]{3,2,1,0:T(8,128)S(1)}, f32[2,2,8,1440]{3,2,1,0:T(8,128)S(1)}, u32[]{:S(2)}, u32[]{:S(2)}) collective-permute-start(f32[2,2,8,1440]{3,2,1,0:T(8,128)S(1)} %get-tuple-element.47), channel_id=1, source_target_pairs={{0,1},{1,0},{2,3},{3,2},{4,5},{5,4},{6,7},{7,6},{8,9},{9,8},{10,11... | collective-permute-start | bytes 552968 | tf_op jit(solution)/shard_map/ppermute | solution.py:511
  22.2 6.4 %collective-permute-start.7 = (f32[2,1,8,1440]{3,2,1,0:T(8,128)S(1)}, f32[2,1,8,1440]{3,2,1,0:T(8,128)S(1)}, u32[]{:S(2)}, u32[]{:S(2)}) collective-permute-start(f32[2,1,8,1440]{3,2,1,0:T(8,128)S(1)} %get-tuple-element.52), channel_id=1, source_target_pairs={{0,1},{1,0},{2,3},{3,2},{4,5},{5,4},{6,7},{7,6},{8,9},{9,8},{10,11... | collective-permute-start | bytes 276488 | tf_op jit(solution)/shard_map/ppermute | solution.py:511
  26.4 2.3 %collective-permute-start.10 = (f32[2,1,8,1440]{3,2,1,0:T(8,128)S(1)}, f32[2,1,8,1440]{3,2,1,0:T(8,128)S(1)}, u32[]{:S(2)}, u32[]{:S(2)}) collective-permute-start(f32[2,1,8,1440]{3,2,1,0:T(8,128)S(1)} %get-tuple-element.57), channel_id=1, source_target_pairs={{0,1},{1,0},{2,3},{3,2},{4,5},{5,4},{6,7},{7,6},{8,9},{9,8},{10,11... | collective-permute-start | bytes 276488 | tf_op jit(solution)/shard_map/ppermute | solution.py:511
